TPU v7x, 32 devices: a whole 2x2x4 slice. The times are simulated.
32 devices in a mesh: dp: 16 (over z, x, core), mp: 2 (over y).
Axes of the slice: x: 2, y: 2, z: 4, core: 2. Of those that a mesh axis runs over, the one named last changes fastest.
Arguments:
- tokens: bfloat16 [4096, 2048], P('dp', 'mp'), may hold values from -6 to 6
- gain_rnn: bfloat16 [2048], replicated, may hold values from 0.5 to 1.5
- rnn_in: bfloat16 [2048, 2, 2816], P('dp', None, 'mp'), may hold values from -0.125 to 0.125
- gate_recur: bfloat16 [16, 176, 176], P('mp'), may hold values from -0.4375 to 0.4375
- gate_input: bfloat16 [16, 176, 176], P('mp'), may hold values from -0.4375 to 0.4375
- bias_recur: float32 [2816], P('mp'), may hold values from -3 to 3
- bias_input: float32 [2816], P('mp'), may hold values from -3 to 3
- decay_param: float32 [2816], P('mp'), may hold values from -1 to 7
- conv_weight: float32 [4, 2816], P(None, 'mp'), may hold values from -3 to 3
- conv_bias: float32 [2816], P('mp'), may hold values from -2 to 2
- rnn_out: bfloat16 [2048, 2816], P('dp', 'mp'), may hold values from -0.4375 to 0.4375
- gain_mlp: bfloat16 [2048], replicated, may hold values from 0.5 to 1.5
- mlp_in: bfloat16 [2048, 2, 6144], P('dp', None, 'mp'), may hold values from -0.125 to 0.125
- mlp_out: bfloat16 [2048, 6144], P('dp', 'mp'), may hold values from -0.15625 to 0.15625
- lengths: int32 [16, 4], P('dp'), may hold values from 1 to 153, 256 in all within a row
- out_grad: bfloat16 [4096, 2048], P('dp', 'mp'), may hold values from -6 to 6
Outputs:
- layer_output: bfloat16 [4096, 2048], P('dp', 'mp')
- tokens_grad: bfloat16 [4096, 2048], P('dp', 'mp')
- gain_rnn_grad: float32 [2048], P('mp')
- rnn_in_grad: float32 [2048, 2, 2816], P('dp', None, 'mp')
- gate_recur_grad: float32 [16, 176, 176], P('mp')
- gate_input_grad: float32 [16, 176, 176], P('mp')
- bias_recur_grad: float32 [2816], P('mp')
- bias_input_grad: float32 [2816], P('mp')
- decay_param_grad: float32 [2816], P('mp')
- conv_weight_grad: float32 [4, 2816], P(None, 'mp')
- conv_bias_grad: float32 [2816], P('mp')
- rnn_out_grad: float32 [2048, 2816], P('dp', 'mp')
- gain_mlp_grad: float32 [2048], P('mp')
- mlp_in_grad: float32 [2048, 2, 6144], P('dp', None, 'mp')
- mlp_out_grad: float32 [2048, 6144], P('dp', 'mp')
Inputs may be any that keep to these rules, and one draw needn't show every extreme that they name: `lengths`: row b lists the pieces of buffer b in order: 3 sequences, then the padding at the buffer's end; together they fill all 256 slots, and every row has a piece of exactly 153.
All inputs are finite; a program needn't handle non-finite values.
Results may differ from a plain program's by a relative error of at most 0.012.
Values may be sent and summed in bfloat16 or wider, within the bound.
A program may use at most 256 MiB of HBM per device.

v0:
```python
import jax
import jax.numpy as jnp
from jax import lax
from jax.sharding import PartitionSpec as P

norm_eps = 1e-06
root_eps = 0.001
contract_cols = (((1,), (1,)), ((), ()))
contract_rows = (((0,), (0,)), ((), ()))


def segment_info(length_row, length_total):
    ends = jnp.cumsum(length_row)
    starts = ends - length_row
    places = jnp.arange(length_total, dtype=jnp.int32)
    inside = (places[:, None] >= starts[None, :]) & (places[:, None] < ends[None, :])
    first_place = jnp.sum(jnp.where(inside, starts[None, :], 0), axis=1)
    live_mask = (places < ends[-2]).astype(jnp.float32)[:, None]
    keep_mask = (places != first_place).astype(jnp.float32)[:, None]
    return (places, first_place, live_mask, keep_mask)


def rms_scale(values):
    return lax.rsqrt(jnp.mean(values * values, axis=1, keepdims=True) + norm_eps)


def combine(earlier, later):
    return (earlier[0] * later[0], later[0] * earlier[1] + later[1])


def norm_back(source, scale_rows, gain, grad_rows):
    weighted = grad_rows * gain
    inner_mean = jnp.mean(weighted * source, axis=1, keepdims=True)
    cubed = scale_rows * scale_rows * scale_rows
    back_rows = scale_rows * weighted - source * cubed * inner_mean
    gain_term = jnp.sum(grad_rows * source * scale_rows, axis=0)
    return (back_rows, gain_term)


def features(half_rows):
    return lax.all_gather(half_rows, "mp", axis=1, tiled=True)


def project_in(normed, weight):
    width_all = weight.shape[1] * weight.shape[2]
    piece = lax.all_gather(weight, "dp", axis=0, tiled=True)
    return jnp.dot(
        normed, piece.reshape(piece.shape[0], width_all), preferred_element_type=jnp.float32
    )


def project_out(mixed_low, weight):
    partial_value = lax.dot_general(
        mixed_low,
        lax.all_gather(weight, "dp", axis=0, tiled=True),
        contract_cols,
        preferred_element_type=jnp.float32,
    )
    return lax.psum_scatter(partial_value, "mp", scatter_dimension=1, tiled=True)


def back_out(grad_low, weight):
    return jnp.dot(
        grad_low,
        lax.all_gather(weight, "dp", axis=0, tiled=True),
        preferred_element_type=jnp.float32,
    )


def back_in(d_both, weight, source, scale_rows, gain):
    width_all = weight.shape[1] * weight.shape[2]
    piece = lax.all_gather(weight, "dp", axis=0, tiled=True)
    partial_value = lax.dot_general(
        d_both,
        piece.reshape(piece.shape[0], width_all),
        contract_cols,
        preferred_element_type=jnp.float32,
    )
    back_rows, gain_term = norm_back(source, scale_rows, gain, partial_value)
    return (
        lax.psum_scatter(back_rows, "mp", scatter_dimension=1, tiled=True),
        lax.psum_scatter(gain_term, "mp", scatter_dimension=0, tiled=True),
    )


def weight_grads(normed, d_both, grad_low, mixed_low, rows_here):
    half_width = d_both.shape[1] // 2
    part = normed
    in_sum = lax.psum_scatter(
        lax.dot_general(part, d_both, contract_rows, preferred_element_type=jnp.float32),
        "dp",
        scatter_dimension=0,
        tiled=True,
    )
    part = grad_low
    out_sum = lax.psum_scatter(
        lax.dot_general(part, mixed_low, contract_rows, preferred_element_type=jnp.float32),
        "dp",
        scatter_dimension=0,
        tiled=True,
    )
    return (in_sum.reshape(rows_here, 2, half_width), out_sum)


def local(
    tokens,
    gain_rnn,
    rnn_in,
    gate_recur,
    gate_input,
    bias_recur,
    bias_input,
    decay_param,
    conv_weight,
    conv_bias,
    rnn_out,
    gain_mlp,
    mlp_in,
    mlp_out,
    lengths,
    out_grad,
):
    tokens_here = tokens.shape[0]
    heads_here = gate_recur.shape[0]
    head_size = gate_recur.shape[1]
    channels = rnn_in.shape[2]
    hidden_units = mlp_in.shape[2]
    rows_here = rnn_in.shape[0]
    taps = conv_weight.shape[0]
    places, first_place, live_mask, keep_mask = segment_info(lengths[0], tokens_here)
    gain_one = gain_rnn.astype(jnp.float32)
    gain_two = gain_mlp.astype(jnp.float32)
    source = features(tokens).astype(jnp.float32)
    scale_one = rms_scale(source)
    normed = (source * scale_one * gain_one).astype(jnp.bfloat16)
    both_proj = project_in(normed, rnn_in)
    inner_branch = both_proj[:, :channels]
    gate_value, gate_pull = jax.vjp(jax.nn.gelu, both_proj[:, channels:])
    conv_out = conv_bias + conv_weight[0] * inner_branch
    for offset in range(1, taps):
        moved = jnp.concatenate(
            [jnp.zeros((offset, channels), jnp.float32), inner_branch[:-offset]], axis=0
        )
        valid = (places - offset >= first_place).astype(jnp.float32)[:, None]
        conv_out = conv_out + conv_weight[offset] * moved * valid
    heads_in = conv_out.astype(jnp.bfloat16).reshape(tokens_here, heads_here, head_size)
    pre_recur = (
        jnp.einsum(
            "thi,hij->thj", heads_in, gate_recur, preferred_element_type=jnp.float32
        ).reshape(tokens_here, channels)
        + bias_recur
    )
    pre_input = (
        jnp.einsum(
            "thi,hij->thj", heads_in, gate_input, preferred_element_type=jnp.float32
        ).reshape(tokens_here, channels)
        + bias_input
    )
    rate_gate = jax.nn.sigmoid(pre_recur)
    input_gate = jax.nn.sigmoid(pre_input)
    softened = jax.nn.softplus(-decay_param)
    decay_step = jnp.exp(-8.0 * rate_gate * softened)
    root_scale = jnp.sqrt(1.0 - decay_step * decay_step + root_eps)
    push_term = root_scale * input_gate * conv_out
    carry_coef = decay_step * keep_mask
    hidden_state = lax.associative_scan(combine, (carry_coef, push_term), axis=0)[1]
    mixed_low = (hidden_state * gate_value).astype(jnp.bfloat16)
    middle = tokens.astype(jnp.float32) + project_out(mixed_low, rnn_out)
    whole_mid = features(middle.astype(jnp.bfloat16)).astype(jnp.float32)
    scale_two = rms_scale(whole_mid)
    normed_two = (whole_mid * scale_two * gain_two).astype(jnp.bfloat16)
    pair_proj = project_in(normed_two, mlp_in)
    gate_mlp_value, gate_mlp_pull = jax.vjp(jax.nn.gelu, pair_proj[:, :hidden_units])
    up_value = pair_proj[:, hidden_units:]
    activation = (gate_mlp_value * up_value).astype(jnp.bfloat16)
    branch_two = project_out(activation, mlp_out)
    layer_output = (live_mask * (middle + branch_two)).astype(jnp.bfloat16)
    grad_low = features(out_grad) * live_mask.astype(jnp.bfloat16)
    d_activation = back_out(grad_low, mlp_out)
    d_gate_mlp = gate_mlp_pull(d_activation * up_value)[0]
    d_pair = jnp.concatenate([d_gate_mlp, d_activation * gate_mlp_value], axis=1).astype(
        jnp.bfloat16
    )
    back_two, gain_two_half = back_in(d_pair, mlp_in, whole_mid, scale_two, gain_two)
    mlp_in_grad, mlp_out_grad = weight_grads(normed_two, d_pair, grad_low, activation, rows_here)
    d_middle = live_mask * out_grad.astype(jnp.float32) + back_two
    branch_grad = features(d_middle.astype(jnp.bfloat16))
    d_mixed = back_out(branch_grad, rnn_out)
    d_hidden = d_mixed * gate_value
    d_gate_pre = gate_pull(d_mixed * hidden_state)[0]
    coef_next = jnp.concatenate([carry_coef[1:], jnp.zeros((1, channels), jnp.float32)], axis=0)
    d_push = lax.associative_scan(combine, (coef_next, d_hidden), reverse=True, axis=0)[1]
    state_before = jnp.concatenate(
        [jnp.zeros((1, channels), jnp.float32), hidden_state[:-1]], axis=0
    )
    d_root = d_push * input_gate * conv_out
    d_input_gate = d_push * root_scale * conv_out
    d_conv = d_push * root_scale * input_gate
    d_decay = d_push * keep_mask * state_before - d_root * decay_step / root_scale
    d_log = d_decay * decay_step
    d_pre_recur = d_log * (-8.0 * softened) * rate_gate * (1.0 - rate_gate)
    d_pre_input = d_input_gate * input_gate * (1.0 - input_gate)
    decay_grad = 8.0 * jax.nn.sigmoid(-decay_param) * jnp.sum(d_log * rate_gate, axis=0)
    bias_recur_term = jnp.sum(d_pre_recur, axis=0)
    bias_input_term = jnp.sum(d_pre_input, axis=0)
    recur_low = d_pre_recur.astype(jnp.bfloat16).reshape(tokens_here, heads_here, head_size)
    input_low = d_pre_input.astype(jnp.bfloat16).reshape(tokens_here, heads_here, head_size)
    recur_term = jnp.einsum("thi,thj->hij", heads_in, recur_low, preferred_element_type=jnp.float32)
    input_term = jnp.einsum("thi,thj->hij", heads_in, input_low, preferred_element_type=jnp.float32)
    gate_back = jnp.einsum(
        "thj,hij->thi", recur_low, gate_recur, preferred_element_type=jnp.float32
    )
    gate_back = gate_back + jnp.einsum(
        "thj,hij->thi", input_low, gate_input, preferred_element_type=jnp.float32
    )
    d_conv = d_conv + gate_back.reshape(tokens_here, channels)
    d_inner = conv_weight[0] * d_conv
    conv_terms = [jnp.sum(d_conv * inner_branch, axis=0)]
    for offset in range(1, taps):
        moved = jnp.concatenate(
            [jnp.zeros((offset, channels), jnp.float32), inner_branch[:-offset]], axis=0
        )
        valid = (places - offset >= first_place).astype(jnp.float32)[:, None]
        conv_terms.append(jnp.sum(d_conv * moved * valid, axis=0))
        later = jnp.concatenate(
            [(d_conv * valid)[offset:], jnp.zeros((offset, channels), jnp.float32)], axis=0
        )
        d_inner = d_inner + conv_weight[offset] * later
    conv_bias_term = jnp.sum(d_conv, axis=0)
    d_both = jnp.concatenate([d_inner, d_gate_pre], axis=1).astype(jnp.bfloat16)
    back_one, gain_one_half = back_in(d_both, rnn_in, source, scale_one, gain_one)
    rnn_in_grad, rnn_out_grad = weight_grads(normed, d_both, branch_grad, mixed_low, rows_here)
    tokens_grad = (d_middle + back_one).astype(jnp.bfloat16)
    summed = lax.psum(
        (
            gain_one_half,
            recur_term,
            input_term,
            bias_recur_term,
            bias_input_term,
            decay_grad,
            jnp.stack(conv_terms),
            conv_bias_term,
            gain_two_half,
        ),
        "dp",
    )
    return (
        layer_output,
        tokens_grad,
        summed[0],
        rnn_in_grad,
        summed[1],
        summed[2],
        summed[3],
        summed[4],
        summed[5],
        summed[6],
        summed[7],
        rnn_out_grad,
        summed[8],
        mlp_in_grad,
        mlp_out_grad,
    )


def solution(mesh):
    return jax.shard_map(
        local,
        mesh=mesh,
        in_specs=(
            P("dp", "mp"),
            P(),
            P("dp", None, "mp"),
            P("mp", None, None),
            P("mp", None, None),
            P("mp"),
            P("mp"),
            P("mp"),
            P(None, "mp"),
            P("mp"),
            P("dp", "mp"),
            P(),
            P("dp", None, "mp"),
            P("dp", "mp"),
            P("dp", None),
            P("dp", "mp"),
        ),
        out_specs=(
            P("dp", "mp"),
            P("dp", "mp"),
            P("mp"),
            P("dp", None, "mp"),
            P("mp", None, None),
            P("mp", None, None),
            P("mp"),
            P("mp"),
            P("mp"),
            P(None, "mp"),
            P("mp"),
            P("dp", "mp"),
            P("mp"),
            P("dp", None, "mp"),
            P("dp", "mp"),
        ),
        check_vma=False,
    )
```

profile of v0, /device:TPU:0, one launch (start us, length us, event | category | flops | bytes accessed | tf_op | source)
XLA Modules:
  0.0 2017.2 jit_solution(6098510089343708558)
XLA Ops:
  10.6 23.1 %all-gather.9.cloned.1.call-done = bf16[256,2048]{1,0:T(8,128)(2,1)} async-done(((bf16[256,1024]{1,0:T(8,128)(2,1)}), bf16[256,2048]{1,0:T(8,128)(2,1)}) %all-gather.9.cloned.1.call-update) | async-done | bytes 1048592 | tf_op jit(solution)/shard_map/all_gather | solution.py:41
  35.8 94.5 %all-gather.11.cloned.1.call-done = bf16[2048,2,1408]{2,1,0:T(2,128)(2,1)} async-done(((bf16[128,2,1408]{2,1,0:T(2,128)(2,1)}), bf16[2048,2,1408]{2,1,0:T(2,128)(2,1)}) %all-gather.11.cloned.1.call-update) | async-done | bytes 11534352 | tf_op jit(solution)/shard_map/all_gather | solution.py:46
  130.3 7.6 copy.70
  155.7 4.7 fusion.33
  160.4 4.2 slice.462
  164.7 4.3 slice.458
  168.9 4.3 slice.457
  174.7 4.3 slice.514
  179.0 4.2 slice.460
  183.3 4.3 slice.459
  225.8 5.0 pad.120
  238.6 5.8 fusion.100
  244.4 30.1 %reduce-scatter.9.cloned.1.call-done = f32[256,1024]{1,0:T(8,128)} async-done(((f32[256,2048]{1,0:T(8,128)}), f32[256,1024]{1,0:T(8,128)}) %reduce-scatter.9.cloned.1.call-update) | async-done | bytes 1048592 | tf_op jit(solution)/shard_map/reduce_scatter | solution.py:59
  280.1 18.0 all-gather.15.cloned.1.call-done
  299.7 128.6 %all-gather.17.cloned.1.call-done = bf16[2048,2,3072]{2,1,0:T(2,128)(2,1)} async-done(((bf16[128,2,3072]{2,1,0:T(2,128)(2,1)}), bf16[2048,2,3072]{2,1,0:T(2,128)(2,1)}) %all-gather.17.cloned.1.call-update) | async-done | bytes 25165840 | tf_op jit(solution)/shard_map/all_gather | solution.py:46
  428.3 25.5 %copy.71 = bf16[256,8,2,3072]{3,1,2,0:T(8,128)(2,1)} copy(bf16[256,8,2,3072]{3,2,1,0:T(2,128)(2,1)} %bitcast.52) | data formatting | bytes 50331648
  453.8 14.7 fusion.52
  468.4 86.1 %all-gather.19.cloned.1.call-done = bf16[2048,3072]{1,0:T(8,128)(2,1)} async-done(((bf16[128,3072]{1,0:T(8,128)(2,1)}), bf16[2048,3072]{1,0:T(8,128)(2,1)}) %all-gather.19.cloned.1.call-update) | async-done | bytes 12582928 | tf_op jit(solution)/shard_map/all_gather | solution.py:55
  554.6 11.3 fusion.6
  565.8 14.4 fusion.22
  589.9 4.2 slice.529
  597.2 4.3 slice.520
  601.5 6.2 slice.530
  607.8 6.3 slice.521
  623.3 10.2 reduce-scatter.11.cloned.1.call-start
  633.5 9.8 fusion.101
  643.4 7.1 fusion.46
  652.2 4.3 slice.582
  659.6 4.3 slice.524
  663.9 6.3 slice.525
  709.8 3.9 slice.583
  729.0 5.0 pad.136
  740.0 11.8 rev.2
  751.8 5.2 fusion.80
  769.3 5.6 fusion.79
  778.1 5.9 fusion.14
  787.5 11.2 fusion.34
  800.0 21.6 %fusion.23 = f32[2048,6144]{1,0:T(8,128)} fusion(bf16[256,3072]{1,0:T(8,128)(2,1)} %get-tuple-element.50, bf16[256,3072]{1,0:T(8,128)(2,1)} %get-tuple-element.49, bf16[256,2048]{1,0:T(8,128)(2,1)S(1)} %copy-done.11, f32[2048]{0:T(1024)S(1)} %convert_element_type.115, f32[256]{0:T(256)S(1)} %copy-done.52), kind=kOutput, calls=%fused_computation.41 | convolution fusion | flops 6450839552 | bytes 54535168 | tf_op jit(solution)/shard_map/dot_general | solution.py:90
  827.3 8.3 fusion.104
  837.0 17.4 fusion.36
  856.4 7.9 all-reduce.44
  864.3 63.4 %all-reduce.42 = (f32[1024]{0:T(1024)}, f32[1408]{0:T(1024)}, f32[1408]{0:T(1024)}, f32[1408]{0:T(1024)}, f32[4,1408]{1,0:T(4,128)}, /*index=5*/f32[1408]{0:T(1024)}, f32[1024]{0:T(1024)}) all-reduce(f32[1024]{0:T(1024)S(1)} %dynamic-slice.1, f32[1408]{0:T(1024)S(1)} %get-tuple-element.52, ...), channel_id=1, replica_groups=mesh['dp'=16,'mp'=2] {'dp'}, use_global_device_ids=true, to_apply=%region_12.13 | all-reduce | flops 13312 | bytes 106496 | tf_op jit(solution)/shard_map/psum | solution.py:234
  930.9 119.9 %reduce-scatter.17.cloned.1.call-done = f32[128,2816]{1,0:T(8,128)} async-done(((f32[2048,2816]{1,0:T(8,128)}), f32[128,2816]{1,0:T(8,128)}) %reduce-scatter.17.cloned.1.call-update) | async-done | bytes 1441808 | tf_op jit(solution)/shard_map/reduce_scatter | solution.py:89
  1053.8 468.0 %reduce-scatter.21.cloned.1.call-done = f32[128,6144]{1,0:T(8,128)} async-done(((f32[2048,6144]{1,0:T(8,128)}), f32[128,6144]{1,0:T(8,128)}) %reduce-scatter.21.cloned.1.call-update) | async-done | bytes 3145744 | tf_op jit(solution)/shard_map/reduce_scatter | solution.py:89
  1521.8 5.4 reshape.168
  1527.3 100.1 %all-reduce.47.cloned.1.call-done = (f32[8,176,176]{2,1,0:T(8,128)}, f32[8,176,176]{2,1,0:T(8,128)}) async-done(((f32[8,176,176]{2,1,0:T(8,128)}, f32[8,176,176]{2,1,0:T(8,128)}), (f32[8,176,176]{2,1,0:T(8,128)}, f32[8,176,176]{2,1,0:T(8,128)})) %all-reduce.47.cloned.1.call-update) | async-done | bytes 1982480 | tf_op jit(solution)/shard_map/psum | solution.py:234
  1627.3 130.3 %reduce-scatter.19.cloned.1.call-done = f32[128,1408]{1,0:T(8,128)} async-done(((f32[2048,1408]{1,0:T(8,128)}), f32[128,1408]{1,0:T(8,128)}) %reduce-scatter.19.cloned.1.call-update) | async-done | bytes 720912 | tf_op jit(solution)/shard_map/reduce_scatter | solution.py:96
  1757.7 248.7 %reduce-scatter.23.cloned.1.call-done = f32[128,3072]{1,0:T(8,128)} async-done(((f32[2048,3072]{1,0:T(8,128)}), f32[128,3072]{1,0:T(8,128)}) %reduce-scatter.23.cloned.1.call-update) | async-done | bytes 1572880 | tf_op jit(solution)/shard_map/reduce_scatter | solution.py:96
  (462 shorter events, 202.8 us)
Async XLA Ops:
  7.2 142.2 %copy-start = (bf16[8,176,176]{2,1,0:T(8,128)(2,1)S(1)}, bf16[8,176,176]{2,1,0:T(8,128)(2,1)}, u32[]{:S(2)}) copy-start(bf16[8,176,176]{2,1,0:T(8,128)(2,1)} %param.19) | copy-start | bytes 1486852
  7.2 26.4 %all-gather.9.cloned.1.call-start = ((), (), s32[]{:S(2)}) async-start(), calls=%async_computation.8 | async-start | bytes 1572864 | tf_op jit(solution)/shard_map/all_gather | solution.py:41
  8.0 122.3 %all-gather.11.cloned.1.call-start = ((), (), s32[]{:S(2)}) async-start(), calls=%async_computation.9 | async-start | bytes 12255232 | tf_op jit(solution)/shard_map/all_gather | solution.py:46
  8.7 229.0 %all-gather.13.cloned.1.call-start = ((), (), s32[]{:S(2)}) async-start(), calls=%async_computation.10 | async-start | bytes 6127616 | tf_op jit(solution)/shard_map/all_gather | solution.py:55
  9.5 265.1 %reduce-scatter.9.cloned.1.call-start = ((), (), s32[]{:S(2)}) async-start(), calls=%async_computation.11 | async-start | bytes 3145728 | tf_op jit(solution)/shard_map/reduce_scatter | solution.py:59
  10.4 132.1 %copy-start.65 = (f32[256]{0:T(256)}, f32[256]{0:T(256)S(1)}, u32[]{:S(2)}) copy-start(f32[256]{0:T(256)S(1)} %get-tuple-element.98) | copy-start | bytes 3076
  10.4 132.1 %copy-start.68 = (f32[256]{0:T(256)}, f32[256]{0:T(256)S(1)}, u32[]{:S(2)}) copy-start(f32[256]{0:T(256)S(1)} %get-tuple-element.99) | copy-start | bytes 3076
  10.4 132.1 %copy-start.71 = (f32[256]{0:T(256)}, f32[256]{0:T(256)S(1)}, u32[]{:S(2)}) copy-start(f32[256]{0:T(256)S(1)} %get-tuple-element.100) | copy-start | bytes 3076
  10.4 145.3 %copy-start.74 = (f32[256]{0:T(256)}, f32[256]{0:T(256)S(1)}, u32[]{:S(2)}) copy-start(f32[256]{0:T(256)S(1)} %get-tuple-element.97) | copy-start | bytes 3076
  10.5 132.0 %copy-start.43 = (f32[1408]{0:T(1024)}, f32[1408]{0:T(1024)S(1)}, u32[]{:S(2)}) copy-start(f32[1408]{0:T(1024)S(1)} %get-tuple-element.26) | copy-start | bytes 16900
  10.5 132.0 %copy-start.45 = (f32[1408]{0:T(1024)}, f32[1408]{0:T(1024)S(1)}, u32[]{:S(2)}) copy-start(f32[1408]{0:T(1024)S(1)} %get-tuple-element.27) | copy-start | bytes 16900
  10.6 132.0 %copy-start.47 = (f32[1408]{0:T(1024)}, f32[1408]{0:T(1024)S(1)}, u32[]{:S(2)}) copy-start(f32[1408]{0:T(1024)S(1)} %get-tuple-element.28) | copy-start | bytes 16900
  10.6 132.0 %copy-start.49 = (f32[1408]{0:T(1024)}, f32[1408]{0:T(1024)S(1)}, u32[]{:S(2)}) copy-start(f32[1408]{0:T(1024)S(1)} %get-tuple-element.29) | copy-start | bytes 16900
  35.8 102.2 %copy-start.55 = (f32[256]{0:T(256)}, f32[256]{0:T(256)S(1)}, u32[]{:S(2)}) copy-start(f32[256]{0:T(256)S(1)} %get-tuple-element.94) | copy-start | bytes 3076
  130.3 7.7 copy-start.8
  142.5 4.2 copy-start.6
  225.7 5.0 copy-start.28
  244.3 30.2 %copy-start.15 = (bf16[256,1024]{1,0:T(8,128)(2,1)S(1)}, bf16[256,1024]{1,0:T(8,128)(2,1)}, u32[]{:S(2)}) copy-start(bf16[256,1024]{1,0:T(8,128)(2,1)} %param.16) | copy-start | bytes 1572868
  244.4 53.8 %all-gather.15.cloned.1.call-start = ((), (), s32[]{:S(2)}) async-start(), calls=%async_computation.12 | async-start | bytes 1572864 | tf_op jit(solution)/shard_map/all_gather | solution.py:41
  276.7 151.6 %all-gather.17.cloned.1.call-start = ((), (), s32[]{:S(2)}) async-start(), calls=%async_computation.13 | async-start | bytes 26738688 | tf_op jit(solution)/shard_map/all_gather | solution.py:46
  277.3 191.1 %all-gather.21.cloned.1.call-start = ((), (), s32[]{:S(2)}) async-start(), calls=%async_computation.16 | async-start | bytes 1572864 | tf_op jit(solution)/shard_map/all_gather | solution.py:41
  278.1 276.5 %all-gather.19.cloned.1.call-start = ((), (), s32[]{:S(2)}) async-start(), calls=%async_computation.14 | async-start | bytes 13369344 | tf_op jit(solution)/shard_map/all_gather | solution.py:55
  278.8 342.2 %reduce-scatter.13.cloned.1.call-start = ((), (), s32[]{:S(2)}) async-start(), calls=%async_computation.17 | async-start | bytes 3145728 | tf_op jit(solution)/shard_map/reduce_scatter | solution.py:81
  280.1 274.5 %copy-start.78 = (bf16[256]{0:T(256)(128)(2,1)}, bf16[256]{0:T(256)(128)(2,1)S(1)}, u32[]{:S(2)}) copy-start(bf16[256]{0:T(256)(128)(2,1)S(1)} %fusion.74) | copy-start | bytes 1540
  299.7 280.6 %copy-start.51 = (f32[256]{0:T(256)}, f32[256]{0:T(256)S(1)}, u32[]{:S(2)}) copy-start(f32[256]{0:T(256)S(1)} %get-tuple-element.96) | copy-start | bytes 3076
  428.3 25.5 %copy-start.10 = (bf16[256,2048]{1,0:T(8,128)(2,1)S(1)}, bf16[256,2048]{1,0:T(8,128)(2,1)}, u32[]{:S(2)}) copy-start(bf16[256,2048]{1,0:T(8,128)(2,1)} %all-gather.15.cloned.1.call-done) | copy-start | bytes 3145732
  583.7 59.7 %all-gather.23.cloned.1.call-start = ((), (), s32[]{:S(2)}) async-start(), calls=%async_computation.18 | async-start | bytes 1572864 | tf_op jit(solution)/shard_map/all_gather | solution.py:41
  586.9 34.2 %copy-start.85 = (f32[256]{0:T(256)}, f32[256]{0:T(256)S(1)}, u32[]{:S(2)}) copy-start(f32[256]{0:T(256)S(1)} %compare_convert_fusion.4) | copy-start | bytes 3076
  623.3 304.4 %reduce-scatter.11.cloned.1.call-start = ((), (), s32[]{:S(2)}) async-start(), calls=%async_computation.15 | async-start | bytes 3145728 | tf_op jit(solution)/shard_map/reduce_scatter | solution.py:59
  643.4 284.3 %reduce-scatter.15.cloned.1.call-start = ((), (), s32[]{:S(2)}) async-start(), calls=%async_computation.19 | async-start | bytes 3145728 | tf_op jit(solution)/shard_map/reduce_scatter | solution.py:81
  696.6 13.1 copy-start.29
  709.8 7.8 copy-start.40
  729.0 5.0 copy-start.27
  740.0 11.8 copy-start.75
  769.3 5.6 copy-start.82
  769.3 8.6 slice-start
  769.3 8.6 slice-start.1
  778.1 5.9 copy-start.87
  787.5 263.4 %reduce-scatter.17.cloned.1.call-start = ((), (), s32[]{:S(2)}) async-start(), calls=%async_computation.20 | async-start | bytes 24510464 | tf_op jit(solution)/shard_map/reduce_scatter | solution.py:89
  798.8 723.1 %reduce-scatter.21.cloned.1.call-start = ((), (), s32[]{:S(2)}) async-start(), calls=%async_computation.22 | async-start | bytes 53477376 | tf_op jit(solution)/shard_map/reduce_scatter | solution.py:89
  821.6 805.7 %all-reduce.47.cloned.1.call-start = ((), (), s32[]{:S(2)}) async-start(), calls=%async_computation.24 | async-start | bytes 5767168 | tf_op jit(solution)/shard_map/psum | solution.py:234
  825.9 931.8 %reduce-scatter.19.cloned.1.call-start = ((), (), s32[]{:S(2)}) async-start(), calls=%async_computation.21 | async-start | bytes 12255232 | tf_op jit(solution)/shard_map/reduce_scatter | solution.py:96
  835.6 1170.8 %reduce-scatter.23.cloned.1.call-start = ((), (), s32[]{:S(2)}) async-start(), calls=%async_computation.23 | async-start | bytes 26738688 | tf_op jit(solution)/shard_map/reduce_scatter | solution.py:96
  854.4 9.8 copy-start.54
  854.4 73.3 %copy-start.16 = (bf16[256,1024]{1,0:T(8,128)(2,1)S(1)}, bf16[256,1024]{1,0:T(8,128)(2,1)}, u32[]{:S(2)}) copy-start(bf16[256,1024]{1,0:T(8,128)(2,1)} %param.16) | copy-start | bytes 1572868
  854.4 73.3 %copy-start.18 = (bf16[256,1024]{1,0:T(8,128)(2,1)S(1)}, bf16[256,1024]{1,0:T(8,128)(2,1)}, u32[]{:S(2)}) copy-start(bf16[256,1024]{1,0:T(8,128)(2,1)} %param.31) | copy-start | bytes 1572868
  854.4 73.3 %copy-start.19 = (f32[256,1024]{1,0:T(8,128)S(1)}, f32[256,1024]{1,0:T(8,128)}, u32[]{:S(2)}) copy-start(f32[256,1024]{1,0:T(8,128)} %reduce-scatter.9.cloned.1.call-done) | copy-start | bytes 3145732
  854.4 73.3 %copy-start.86 = (f32[256]{0:T(256)S(1)}, f32[256]{0:T(256)}, u32[]{:S(2)}) copy-start(f32[256]{0:T(256)} %copy-done.85) | copy-start | bytes 3076
  (64 other events, 119.2 us)
Sparse Core Ops, SparseCore 0:
  9.6 24.0 all-gather.8
  35.9 94.3 all-gather.10
  132.6 57.1 all-gather.12
  244.5 29.9 reduce-scatter.8
  276.8 21.2 all-gather.14
  299.7 128.5 all-gather.16
  429.9 21.2 all-gather.20
  453.8 100.7 all-gather.18
  583.8 30.0 reduce-scatter.12
  623.4 19.2 all-gather.22
  644.9 31.8 reduce-scatter.10
  787.6 31.1 reduce-scatter.14
  822.8 227.9 reduce-scatter.16
  1054.9 466.8 reduce-scatter.20
  1526.0 101.2 all-reduce.46
  1631.9 125.7 reduce-scatter.18
  1762.7 243.5 reduce-scatter.22
where the time goes:
time: 2030 us; the launch traced here: 2020 us
  waiting for transfers between devices  1450 us (71%)
  local copies, waits for them, and re-layouts  243 us (12%)
  matrix products  140 us (7%)
  other arithmetic  84 us (4%)
  blocking collectives  71.3 us (4%)
    reduce_scatter x2, waiting for transfers between devices, weight_grads(): lax.psum_scatter(lax.dot_general(part, d_both, contract_rows, preferred_e...  588 us
    reduce_scatter x2, waiting for transfers between devices, weight_grads(): lax.psum_scatter(lax.dot_general(part, mixed_low, contract_rows, preferre...  379 us
    all_gather x2, waiting for transfers between devices, project_in(): piece = lax.all_gather(weight, 'dp', axis=0, tiled=True)  223 us
    psum x1, waiting for transfers between devices, local(): lax.psum((gain_one_half, recur_term, input_term, bias_recur_term, bias_in...  100 us
    all_gather x2, waiting for transfers between devices, project_out(): lax.all_gather(weight, 'dp', axis=0, tiled=True)  86.2 us
    slice x52, local copies, waits for them, and re-layouts, local(): lax.associative_scan(combine, (coef_next, d_hidden), reverse=True, axis=0)  81.4 us
    psum x1, blocking collectives, local(): lax.psum((gain_one_half, recur_term, input_term, bias_recur_term, bias_in...  63.4 us
    unnamed x197, local copies, waits for them, and re-layouts  53.4 us
  transfers between devices with their start and end apart: 17, of which 11 were waited for; matrix products, arithmetic and copies ran while one was open for 20% of the time, Pallas kernels for 0%

commit v1 on v0

v1 whole, which is shorter than its diff:
```python
import functools

import jax
import jax.numpy as jnp
from jax import lax
from jax.experimental import pallas as pl
from jax.experimental.pallas import tpu as pltpu
from jax.sharding import PartitionSpec as P

norm_eps = 1e-06
root_eps = 0.001
bf16 = jnp.bfloat16
f32 = jnp.float32
contract_cols = (((1,), (1,)), ((), ()))
contract_rows = (((0,), (0,)), ((), ()))
gelu_scale = 0.7978845608028654
gelu_cubic = 0.044715
held_buffers = 4
scan_unroll = 8
lanes = 128


def pairs(n_dp, move):
    found = []
    for i in range(n_dp):
        target = move((i // 4) % 4, (i // 2) % 2, i % 2)
        if target is not None:
            z, x, c = target
            found.append((i, i // 16 * 16 + z * 4 + x * 2 + c))
    return found


def gelu_parts(v):
    tanh_value = jnp.tanh(gelu_scale * (v + gelu_cubic * v * v * v))
    value = 0.5 * v * (1.0 + tanh_value)
    slope = 0.5 * (1.0 + tanh_value) + 0.5 * v * (1.0 - tanh_value * tanh_value) * (
        gelu_scale * (1.0 + 3.0 * gelu_cubic * v * v)
    )
    return value, slope


def shifted(value, offset):
    return pltpu.roll(value, offset % value.shape[0], 0)


def store_lanes(ref, at, value):
    chunks = ref.shape[0]
    spare = chunks * lanes - value.shape[1]
    if spare:
        value = jnp.concatenate([value, jnp.zeros((value.shape[0], spare), f32)], axis=1)
    for i in range(chunks):
        ref[i, at, :] = value[:, i * lanes : (i + 1) * lanes]


def load_lanes(ref, at, width):
    return jnp.concatenate([ref[i, at, :] for i in range(ref.shape[0])], axis=1)[:, :width]


def scan_rows(coef_ref, push_ref, rows, reverse):
    chunks = coef_ref.shape[0]

    def step(i, carried):
        carried = list(carried)
        for j in range(scan_unroll):
            t = i * scan_unroll + j
            at = pl.ds(rows - 1 - t if reverse else t, held_buffers, stride=rows)
            for k in range(chunks):
                if reverse:
                    value = push_ref[k, at, :] + carried[k]
                    carried[k] = coef_ref[k, at, :] * value
                else:
                    value = coef_ref[k, at, :] * carried[k] + push_ref[k, at, :]
                    carried[k] = value
                push_ref[k, at, :] = value
        return tuple(carried)

    start = tuple(jnp.zeros((held_buffers, lanes), f32) for _ in range(chunks))
    lax.fori_loop(0, rows // scan_unroll, step, start)


def recur_forward(
    both_ref, mask_ref, vec_ref, wr_ref, wi_ref,
    mixed_ref, state_ref, conv_ref, rate_ref, igate_ref,
    coef_ref, push_ref,
):
    width = state_ref.shape[1]
    rows = both_ref.shape[0] // held_buffers

    def gates(b, carry):
        at = pl.ds(b * rows, rows)
        inner = both_ref[at, :width]
        mask = mask_ref[at, :]
        conv = vec_ref[4:5, :] + vec_ref[0:1, :] * inner
        for k in range(1, 4):
            conv = conv + vec_ref[k : k + 1, :] * (shifted(inner, k) * mask[:, k : k + 1])
        conv_low = conv.astype(bf16)
        rate = jax.nn.sigmoid(
            jnp.dot(conv_low, wr_ref[...], preferred_element_type=f32) + vec_ref[5:6, :]
        )
        igate = jax.nn.sigmoid(
            jnp.dot(conv_low, wi_ref[...], preferred_element_type=f32) + vec_ref[6:7, :]
        )
        decay = jnp.exp(-8.0 * rate * vec_ref[7:8, :])
        root = jnp.sqrt(1.0 - decay * decay + root_eps)
        store_lanes(coef_ref, at, decay * mask[:, 0:1])
        store_lanes(push_ref, at, root * igate * conv)
        conv_ref[at, :] = conv
        rate_ref[at, :] = rate
        igate_ref[at, :] = igate
        return carry

    lax.fori_loop(0, held_buffers, gates, 0)

    scan_rows(coef_ref, push_ref, rows, False)

    def mix(b, carry):
        at = pl.ds(b * rows, rows)
        gate = gelu_parts(both_ref[at, width:])[0]
        state = load_lanes(push_ref, at, width)
        state_ref[at, :] = state
        mixed_ref[at, :] = (state * gate).astype(bf16)
        return carry

    lax.fori_loop(0, held_buffers, mix, 0)


def recur_backward(
    dmix_ref, both_ref, state_ref, conv_ref, rate_ref, igate_ref, mask_ref, vec_ref, wr_ref, wi_ref,
    dboth_ref, sums_ref, gr_ref, gi_ref,
    coef_ref, push_ref,
):
    width = state_ref.shape[1]
    rows = both_ref.shape[0] // held_buffers

    def first(b, carry):
        at = pl.ds(b * rows, rows)
        gate, slope = gelu_parts(both_ref[at, width:])
        d_mixed = dmix_ref[at, :]
        store_lanes(push_ref, at, d_mixed * gate)
        dboth_ref[at, width:] = (slope * d_mixed * state_ref[at, :]).astype(bf16)
        store_lanes(
            coef_ref, at, jnp.exp(-8.0 * rate_ref[at, :] * vec_ref[7:8, :]) * mask_ref[at, 0:1]
        )
        return carry

    lax.fori_loop(0, held_buffers, first, 0)

    scan_rows(coef_ref, push_ref, rows, True)
    sums_ref[...] = jnp.zeros_like(sums_ref)
    gr_ref[...] = jnp.zeros_like(gr_ref)
    gi_ref[...] = jnp.zeros_like(gi_ref)

    def add_sum(k, value):
        sums_ref[k : k + 1, :] += jnp.sum(value, axis=0, keepdims=True)

    def last(b, carry):
        at = pl.ds(b * rows, rows)
        inner = both_ref[at, :width]
        mask = mask_ref[at, :]
        keep = mask[:, 0:1]
        softened = vec_ref[7:8, :]
        rate, igate, conv = rate_ref[at, :], igate_ref[at, :], conv_ref[at, :]
        d_push = load_lanes(push_ref, at, width)
        decay = jnp.exp(-8.0 * rate * softened)
        square = 1.0 - decay * decay + root_eps
        root = jnp.sqrt(square)
        d_root = d_push * igate * conv
        d_igate = d_push * root * conv
        before = shifted(state_ref[at, :], 1) * keep
        d_decay = d_push * before - d_root * decay / root
        d_log = d_decay * decay
        slow = d_log * rate
        d_pre_recur = (-8.0 * softened) * slow * (1.0 - rate)
        d_pre_input = d_igate * igate * (1.0 - igate)
        add_sum(7, slow)
        add_sum(5, d_pre_recur)
        add_sum(6, d_pre_input)
        low_recur = d_pre_recur.astype(bf16)
        low_input = d_pre_input.astype(bf16)
        conv_low = conv.astype(bf16)
        gr_ref[...] += lax.dot_general(
            conv_low, low_recur, contract_rows, preferred_element_type=f32
        )
        gi_ref[...] += lax.dot_general(
            conv_low, low_input, contract_rows, preferred_element_type=f32
        )
        d_conv = d_push * root * igate
        d_conv = d_conv + lax.dot_general(
            low_recur, wr_ref[...], contract_cols, preferred_element_type=f32
        )
        d_conv = d_conv + lax.dot_general(
            low_input, wi_ref[...], contract_cols, preferred_element_type=f32
        )
        add_sum(4, d_conv)
        add_sum(0, d_conv * inner)
        d_inner = vec_ref[0:1, :] * d_conv
        for k in range(1, 4):
            kept = d_conv * mask[:, k : k + 1]
            add_sum(k, kept * shifted(inner, k))
            d_inner = d_inner + vec_ref[k : k + 1, :] * shifted(kept, -k)
        dboth_ref[at, :width] = d_inner.astype(bf16)
        return carry

    lax.fori_loop(0, held_buffers, last, 0)


def whole_vmem(count):
    return [pl.BlockSpec(memory_space=pltpu.VMEM)] * count


def run_recur_forward(both, mask, vectors, wr, wi):
    rows, width = both.shape[0], both.shape[1] // 2
    wide = jax.ShapeDtypeStruct((rows, width), f32)
    return pl.pallas_call(
        recur_forward,
        out_shape=(jax.ShapeDtypeStruct((rows, width), bf16), wide, wide, wide, wide),
        in_specs=whole_vmem(5),
        out_specs=whole_vmem(5),
        scratch_shapes=[pltpu.VMEM((pl.cdiv(width, lanes), rows, lanes), f32)] * 2,
        compiler_params=pltpu.CompilerParams(vmem_limit_bytes=56 * 2**20),
        cost_estimate=pl.CostEstimate(
            flops=4 * rows * width * width, bytes_accessed=rows * width * 30, transcendentals=rows * width * 5
        ),
        name="recur_forward",
    )(both, mask, vectors, wr, wi)


def run_recur_backward(d_mixed, both, state, conv, rate, igate, mask, vectors, wr, wi):
    rows, width = state.shape
    square = jax.ShapeDtypeStruct((width, width), f32)
    return pl.pallas_call(
        recur_backward,
        out_shape=(
            jax.ShapeDtypeStruct((rows, 2 * width), bf16),
            jax.ShapeDtypeStruct((8, width), f32),
            square,
            square,
        ),
        in_specs=whole_vmem(10),
        out_specs=whole_vmem(4),
        scratch_shapes=[pltpu.VMEM((pl.cdiv(width, lanes), rows, lanes), f32)] * 2,
        compiler_params=pltpu.CompilerParams(vmem_limit_bytes=56 * 2**20),
        cost_estimate=pl.CostEstimate(
            flops=8 * rows * width * width, bytes_accessed=rows * width * 40, transcendentals=rows * width * 5
        ),
        name="recur_backward",
    )(d_mixed, both, state, conv, rate, igate, mask, vectors, wr, wi)


def block_diagonal(blocks):
    count, size = blocks.shape[0], blocks.shape[1]
    rows = [
        jnp.pad(blocks[h], ((0, 0), (h * size, (count - 1 - h) * size))) for h in range(count)
    ]
    return jnp.concatenate(rows, axis=0)


def diagonal_blocks(square, count):
    size = square.shape[0] // count
    return jnp.stack(
        [square[h * size : (h + 1) * size, h * size : (h + 1) * size] for h in range(count)]
    )


def masks_of(lengths, rows):
    ends = jnp.cumsum(lengths, axis=1)
    starts = ends - lengths
    places = jnp.arange(rows, dtype=jnp.int32)[None, :, None]
    inside = (places >= starts[:, None, :]) & (places < ends[:, None, :])
    first_place = jnp.sum(jnp.where(inside, starts[:, None, :], 0), axis=2)
    places = places[:, :, 0]
    live = (places < ends[:, 2:3]).astype(f32)
    columns = [(places != first_place).astype(f32)]
    for k in range(1, 4):
        columns.append((places - k >= first_place).astype(f32))
    columns += [live] + [jnp.zeros_like(live)] * 3
    return jnp.stack(columns, axis=2).reshape(lengths.shape[0] * rows, 8), live


def local(
    n_dp,
    tokens,
    gain_rnn,
    rnn_in,
    gate_recur,
    gate_input,
    bias_recur,
    bias_input,
    decay_param,
    conv_weight,
    conv_bias,
    rnn_out,
    gain_mlp,
    mlp_in,
    mlp_out,
    lengths,
    out_grad,
):
    outer_count = n_dp // 16
    rows_here = rnn_in.shape[0]
    model = gain_rnn.shape[0]
    half_model = model // 2
    buffer_rows = tokens.shape[0]
    own_rows = 2 * buffer_rows
    index = lax.axis_index("dp")
    y = lax.axis_index("mp")
    c = index % 2
    x = (index // 2) % 2
    z = (index // 4) % 4
    outer = jnp.where(z < 2, 0, 3)
    far = 3 - z
    far_outer = 3 - outer
    worker = (z == 1) | (z == 2)

    def mover(move):
        table = pairs(n_dp, move)
        return lambda value: lax.ppermute(value, "dp", table)

    swap_c = mover(lambda z, x, c: (z, x, 1 - c))
    swap_x = mover(lambda z, x, c: (z, 1 - x, c))
    swap_x_work = mover(lambda z, x, c: (z, 1 - x, c) if z in (1, 2) else None)
    swap_x_ends = mover(lambda z, x, c: (z, 1 - x, c) if z in (0, 3) else None)
    inward = mover(lambda z, x, c: {0: (1, x, c), 3: (2, x, c)}.get(z))
    outward = mover(lambda z, x, c: {1: (0, x, c), 2: (3, x, c)}.get(z))
    across = mover(lambda z, x, c: {1: (2, x, c), 2: (1, x, c)}.get(z))

    def swap_y(value):
        return lax.ppermute(value, "mp", [(0, 1), (1, 0)])

    def pick_c(first, second):
        return jnp.where(c == 0, first, second)

    def pick_y(first, second):
        return jnp.where(y == 0, first, second)

    group_rows = outer_count * rows_here
    block_rows = 2 * group_rows

    def over_outer(value):
        if outer_count == 1:
            return value
        groups = [[w * 16 + i for w in range(outer_count)] for i in range(16)]
        return lax.all_gather(value, "dp", axis_index_groups=groups, axis=0, tiled=True)

    def offset_of(z_at, x_at):
        z_place = z_at ^ (2 * y) if outer_count == 1 else z_at
        return (z_place * 2 + x_at) * block_rows

    def gather_weight(first_quarter, second_quarter):
        first_quarter, second_quarter = over_outer(first_quarter), over_outer(second_quarter)
        arrived = swap_c(pick_c(second_quarter, first_quarter))
        own = pick_c(
            jnp.concatenate([first_quarter, arrived], axis=0),
            jnp.concatenate([arrived, second_quarter], axis=0),
        )
        own_x = swap_x(own)
        from_outer = inward(own)
        from_outer_x = inward(own_x)
        from_far = across(own)
        from_far_outer = across(from_outer)
        from_far_x = swap_x_work(from_far)
        from_far_outer_x = across(from_outer_x)
        whole = jnp.zeros((model, own.shape[1]), bf16)
        for piece, z_at, x_at in (
            (own, z, x),
            (own_x, z, 1 - x),
            (from_outer, outer, x),
            (from_outer_x, outer, 1 - x),
            (from_far, far, x),
            (from_far_x, far, 1 - x),
            (from_far_outer, far_outer, x),
            (from_far_outer_x, far_outer, 1 - x),
        ):
            whole = lax.dynamic_update_slice(whole, piece, (offset_of(z_at, x_at), 0))
        if outer_count > 1:
            whole = whole.reshape(16, outer_count, rows_here, -1).swapaxes(0, 1)
            whole = whole.reshape(model, -1)
            whole = pick_y(whole, jnp.roll(whole, half_model, axis=0))
        return whole

    def scatter_grad(partial):
        if outer_count > 1:
            partial = pick_y(partial, jnp.roll(partial, half_model, axis=0))
            partial = partial.reshape(outer_count, 16, rows_here, -1).swapaxes(0, 1)
            partial = partial.reshape(model, -1)

        def block(z_at, x_at):
            start = (offset_of(z_at, x_at), 0)
            return lax.dynamic_slice(partial, start, (block_rows, partial.shape[1])).astype(f32)

        def sum_x(z_at):
            return block(z_at, x) + swap_x_work(block(z_at, 1 - x).astype(bf16)).astype(f32)

        to_far_outer = across(sum_x(far_outer).astype(bf16)).astype(f32)
        to_far = across(sum_x(far).astype(bf16)).astype(f32)
        out_x = outward((block(outer, x) + to_far_outer).astype(bf16)).astype(f32)
        out_other = outward(block(outer, 1 - x).astype(bf16))
        worker_total = sum_x(z) + to_far
        end_total = out_x + swap_x_ends(out_other).astype(f32)
        total = jnp.where(worker, worker_total, end_total).astype(bf16)
        top, bottom = total[:group_rows], total[group_rows:]
        mine = pick_c(top, bottom)
        arrived = swap_c(pick_c(bottom, top))
        first, second = pick_c(mine, arrived).astype(f32), pick_c(arrived, mine).astype(f32)
        if outer_count > 1:
            groups = [[w * 16 + i for w in range(outer_count)] for i in range(16)]
            first, second = (
                lax.psum_scatter(
                    v, "dp", axis_index_groups=groups, scatter_dimension=0, tiled=True
                )
                for v in (first, second)
            )
        return first, second

    def whole_features(half_rows):
        return jnp.concatenate([half_rows, swap_y(half_rows)], axis=1)

    def all_rows(rows_value):
        return jnp.concatenate([rows_value, swap_c(rows_value)], axis=0)

    def sum_partials(product):
        theirs = product(slice(own_rows, 2 * own_rows)).astype(bf16)
        theirs = swap_c(theirs)
        mine = product(slice(0, own_rows)) + theirs.astype(f32)
        arrived = swap_y(mine[:, half_model:].astype(bf16))
        return mine[:, :half_model] + arrived.astype(f32)

    def relative(vector):
        first, second = vector[:half_model], vector[half_model:]
        return jnp.concatenate([pick_y(first, second), pick_y(second, first)])

    def scale_of(rows_value):
        return lax.rsqrt(jnp.mean(rows_value * rows_value, axis=1, keepdims=True) + norm_eps)

    def norm_back(source, scale_rows, gain, grad_rows):
        weighted = grad_rows * gain
        part = jnp.sum(weighted * source, axis=1, keepdims=True)
        inner_mean = (part + swap_y(part)) / model
        back_rows = scale_rows * weighted - source * (scale_rows * scale_rows * scale_rows) * inner_mean
        return back_rows, jnp.sum(grad_rows * source * scale_rows, axis=0)

    def quarters(value, axis):
        size = value.shape[axis] // 2
        return (
            lax.slice_in_dim(value, 0, size, axis=axis),
            lax.slice_in_dim(value, size, 2 * size, axis=axis),
        )

    def pair_quarters(weight):
        first, second = quarters(weight, 2)
        return tuple(jnp.concatenate([v[:, 0], v[:, 1]], axis=1) for v in (first, second))

    def quarter(value, axis=0):
        return pick_c(*quarters(value, axis))

    gain_one, gain_two = relative(gain_rnn.astype(f32)), relative(gain_mlp.astype(f32))
    tokens_two = jnp.concatenate([tokens, inward(tokens)], axis=0)
    lengths_two = jnp.concatenate([lengths, inward(lengths)], axis=0)
    mask, live = masks_of(jnp.concatenate([lengths_two, swap_c(lengths_two)], axis=0), buffer_rows)
    live = live.reshape(-1, 1)[:own_rows]

    rnn_in_all = gather_weight(*pair_quarters(rnn_in))
    source = whole_features(tokens_two).astype(f32)
    scale_one = scale_of(source)
    normed = all_rows((source * scale_one * gain_one).astype(bf16))
    rnn_out_all = gather_weight(*quarters(rnn_out, 1))
    mlp_in_all = gather_weight(*pair_quarters(mlp_in))
    mlp_out_all = gather_weight(*quarters(mlp_out, 1))
    grad_two = jnp.concatenate([out_grad, inward(out_grad)], axis=0)
    live_grad = live * grad_two.astype(f32)
    grad_low = all_rows(whole_features(live_grad.astype(bf16)))

    both = jnp.dot(normed, rnn_in_all, preferred_element_type=f32)
    softened = jax.nn.softplus(-quarter(decay_param))
    vectors = jnp.concatenate(
        [
            quarter(conv_weight, 1),
            jnp.stack([quarter(conv_bias), quarter(bias_recur), quarter(bias_input), softened]),
        ],
        axis=0,
    )
    heads = gate_recur.shape[0] // 2
    wr = block_diagonal(quarter(gate_recur))
    wi = block_diagonal(quarter(gate_input))
    mixed, state, conv, rate, igate = run_recur_forward(both, mask, vectors, wr, wi)
    branch = sum_partials(
        lambda at: lax.dot_general(
            mixed[at], rnn_out_all, contract_cols, preferred_element_type=f32
        )
    )
    middle = tokens_two.astype(f32) + branch
    middle_low = middle.astype(bf16)
    middle_all = whole_features(middle_low).astype(f32)
    scale_two = scale_of(middle_all)
    normed_two = all_rows((middle_all * scale_two * gain_two).astype(bf16))
    pair = jnp.dot(normed_two, mlp_in_all, preferred_element_type=f32)
    hidden = pair.shape[1] // 2
    gate_mlp, up = pair[:, :hidden], pair[:, hidden:]
    gate_mlp_value, gate_mlp_slope = gelu_parts(gate_mlp)
    act = (gate_mlp_value * up).astype(bf16)
    mlp_out_partial = lax.dot_general(grad_low, act, contract_rows, preferred_element_type=f32)
    mlp_out_grad = scatter_grad(mlp_out_partial.astype(bf16))
    d_act = jnp.dot(grad_low, mlp_out_all, preferred_element_type=f32)
    d_pair = jnp.concatenate(
        [(gate_mlp_slope * d_act * up).astype(bf16), (d_act * gate_mlp_value).astype(bf16)], axis=1
    )
    e_two = sum_partials(
        lambda at: lax.dot_general(
            d_pair[at], mlp_in_all, contract_cols, preferred_element_type=f32
        )
    )
    mlp_in_partial = lax.dot_general(normed_two, d_pair, contract_rows, preferred_element_type=f32)
    mlp_in_grad = scatter_grad(mlp_in_partial.astype(bf16))
    back_two, gain_two_term = norm_back(
        middle_low.astype(f32), scale_two, gain_two[:half_model], e_two
    )
    d_middle = live_grad + back_two
    d_branch = all_rows(whole_features(d_middle.astype(bf16)))
    d_mixed = jnp.dot(d_branch, rnn_out_all, preferred_element_type=f32)
    rnn_out_partial = lax.dot_general(d_branch, mixed, contract_rows, preferred_element_type=f32)
    rnn_out_grad = scatter_grad(rnn_out_partial.astype(bf16))
    branch_two = sum_partials(
        lambda at: lax.dot_general(act[at], mlp_out_all, contract_cols, preferred_element_type=f32)
    )
    output_two = (live * (middle + branch_two)).astype(bf16)

    d_both, sums, square_recur, square_input = run_recur_backward(
        d_mixed, both, state, conv, rate, igate, mask, vectors, wr, wi
    )
    rnn_in_partial = lax.dot_general(normed, d_both, contract_rows, preferred_element_type=f32)
    rnn_in_grad = scatter_grad(rnn_in_partial.astype(bf16))
    e_one = sum_partials(
        lambda at: lax.dot_general(
            d_both[at], rnn_in_all, contract_cols, preferred_element_type=f32
        )
    )
    back_one, gain_one_term = norm_back(
        tokens_two.astype(f32), scale_one, gain_one[:half_model], e_one
    )
    tokens_grad_two = (d_middle + back_one).astype(bf16)

    def settle(two):
        return jnp.where(worker, two[:buffer_rows], outward(two[buffer_rows:]))

    layer_output = settle(output_two)
    tokens_grad = settle(tokens_grad_two)

    def total(value, dtype=f32):
        value = jnp.where(worker, value, 0).astype(dtype)
        if outer_count > 1:
            groups = [[w * 16 + i for w in range(outer_count)] for i in range(16)]
            value = lax.psum(value, "dp", axis_index_groups=groups)
        value = value + swap_x(value)
        value = value + across(value)
        return jnp.where(worker, value, outward(value))

    def both_quarters(value, axis=0):
        arrived = swap_c(value)
        return pick_c(
            jnp.concatenate([value, arrived], axis=axis), jnp.concatenate([arrived, value], axis=axis)
        )

    sums = both_quarters(total(sums), 1)
    blocks = jnp.concatenate(
        [diagonal_blocks(square_recur, heads), diagonal_blocks(square_input, heads)], axis=2
    )
    blocks = both_quarters(total(blocks, bf16)).astype(f32)
    gains = total(jnp.stack([gain_one_term, gain_two_term]))
    gains = gains + swap_c(gains)
    size = gate_recur.shape[1]

    def pair_layout(halves):
        columns = halves[0].shape[1] // 2
        return jnp.stack(
            [
                jnp.concatenate([v[:, k * columns : (k + 1) * columns] for v in halves], axis=1)
                for k in range(2)
            ],
            axis=1,
        )

    return (
        layer_output,
        tokens_grad,
        gains[0],
        pair_layout(rnn_in_grad),
        blocks[:, :, :size],
        blocks[:, :, size:],
        sums[5],
        sums[6],
        8.0 * jax.nn.sigmoid(-decay_param) * sums[7],
        sums[:4],
        sums[4],
        jnp.concatenate(rnn_out_grad, axis=1),
        gains[1],
        pair_layout(mlp_in_grad),
        jnp.concatenate(mlp_out_grad, axis=1),
    )


def solution(mesh):
    return jax.shard_map(
        functools.partial(local, mesh.shape["dp"]),
        mesh=mesh,
        in_specs=(
            P("dp", "mp"),
            P(),
            P("dp", None, "mp"),
            P("mp", None, None),
            P("mp", None, None),
            P("mp"),
            P("mp"),
            P("mp"),
            P(None, "mp"),
            P("mp"),
            P("dp", "mp"),
            P(),
            P("dp", None, "mp"),
            P("dp", "mp"),
            P("dp", None),
            P("dp", "mp"),
        ),
        out_specs=(
            P("dp", "mp"),
            P("dp", "mp"),
            P("mp"),
            P("dp", None, "mp"),
            P("mp", None, None),
            P("mp", None, None),
            P("mp"),
            P("mp"),
            P("mp"),
            P(None, "mp"),
            P("mp"),
            P("dp", "mp"),
            P("mp"),
            P("dp", None, "mp"),
            P("dp", "mp"),
        ),
        check_vma=False,
    )
```

time: 2030 us -> 942 us (0.46)
  waiting for transfers between devices: 1450 us -> 416 us
  local copies, waits for them, and re-layouts: 243 us -> 80.4 us
  starting transfers between devices: 10.9 us -> 165 us
  blocking collectives: 71.3 us -> 0 us
  Pallas kernels: 0 us -> 57.7 us
  other arithmetic: 84 us -> 60.5 us
    reduce_scatter x8 -> x0, waiting for transfers between devices: 997 us -> none  [the longest x2 588 us: weight_grads(): lax.psum_scatter(lax.dot_general(part, d_both, contract_rows, preferred_e...]
    ppermute x0 -> x104, waiting for transfers between devices: none -> 416 us  [the longest x94 383 us: mover(): return lambda value: lax.ppermute(value, 'dp', table)]
    all_gather x8 -> x0, waiting for transfers between devices: 350 us -> none  [the longest x2 223 us: project_in(): piece = lax.all_gather(weight, 'dp', axis=0, tiled=True)]
    ppermute x0 -> x104, starting transfers between devices: none -> 165 us  [the longest x94 155 us: mover(): return lambda value: lax.ppermute(value, 'dp', table)]
    slice x107 -> x19, local copies, waits for them, and re-layouts: 132 us -> 15.3 us  [the longest x2 5.55 us: pair_quarters(): v[:, 0]]
    psum x1 -> x0, waiting for transfers between devices: 100 us -> none  [local(): lax.psum((gain_one_half, recur_term, input_term, bias_recur_term, bias_in...]
    psum x1 -> x0, blocking collectives: 63.4 us -> none  [local(): lax.psum((gain_one_half, recur_term, input_term, bias_recur_term, bias_in...]
    pallas_call x0 -> x2, Pallas kernels: none -> 57.7 us  [the longest x1 35.6 us: run_recur_backward(): pl.pallas_call(recur_backward, out_shape=(jax.ShapeDtypeStruct((rows, 2 *...]
  transfers between devices with their start and end apart: 17 -> 104, of which waited for: 11 -> 34; matrix products, arithmetic and copies ran while one was open for 20% -> 25% of each run, Pallas kernels for 0% -> 2%
where the time goes in v1:
time: 942 us; the launch traced here: 935 us
  waiting for transfers between devices  416 us (44%)
  starting transfers between devices  165 us (18%)
  matrix products  151 us (16%)
  local copies, waits for them, and re-layouts  80.4 us (9%)
  other arithmetic  60.5 us (6%)
  Pallas kernels  57.7 us (6%)
    ppermute x94, waiting for transfers between devices, mover(): return lambda value: lax.ppermute(value, 'dp', table)  383 us
    ppermute x94, starting transfers between devices, mover(): return lambda value: lax.ppermute(value, 'dp', table)  155 us
    pallas_call x1, Pallas kernels, run_recur_backward(): pl.pallas_call(recur_backward, out_shape=(jax.ShapeDtypeStruct((rows, 2 *...  35.6 us
    ppermute x10, waiting for transfers between devices, swap_y(): return lax.ppermute(value, 'mp', [(0, 1), (1, 0)])  32.8 us
    dot_general x1, matrix products, local(): d_act = jnp.dot(grad_low, mlp_out_all, preferred_element_type=f32)  23.9 us
    dot_general x2, matrix products, local(): lax.dot_general(d_pair[at], mlp_in_all, contract_cols, preferred_element_...  23.1 us
    pallas_call x1, Pallas kernels, run_recur_forward(): pl.pallas_call(recur_forward, out_shape=(jax.ShapeDtypeStruct((rows, widt...  22.1 us
    unnamed x243, local copies, waits for them, and re-layouts  21.8 us
  transfers between devices with their start and end apart: 104, of which 34 were waited for; matrix products, arithmetic and copies ran while one was open for 25% of the time, Pallas kernels for 2%

profile of v1, /device:TPU:0, one launch (start us, length us, event | category | flops | bytes accessed | tf_op | source)
XLA Modules:
  0.0 934.6 jit_solution(5981029197691218447)
XLA Ops:
  0.7 5.6 collective-permute-start
  60.7 6.3 collective-permute-done.16
  76.6 24.0 %collective-permute-start.8 = (bf16[256,1408]{0,1:T(8,128)(2,1)S(1)}, bf16[256,1408]{0,1:T(8,128)(2,1)S(1)}, u32[]{:S(2)}, u32[]{:S(2)}) collective-permute-start(bf16[256,1408]{0,1:T(8,128)(2,1)S(1)} %collective-permute-done.6), channel_id=1, source_target_pairs={{0,8},{2,10},{4,12},{6,14},{24,16},{26,18},{28,20},{30,22},{1,9},{... | collective-permute-start | bytes 2162696 | tf_op jit(solution)/shard_map/ppermute | solution.py:317
  104.5 12.6 %collective-permute-done.8 = bf16[256,1408]{0,1:T(8,128)(2,1)S(1)} collective-permute-done((bf16[256,1408]{0,1:T(8,128)(2,1)S(1)}, bf16[256,1408]{0,1:T(8,128)(2,1)S(1)}, u32[]{:S(2)}, u32[]{:S(2)}) %collective-permute-start.8) | collective-permute-done | bytes 720928 | tf_op jit(solution)/shard_map/ppermute | solution.py:317
  122.6 9.2 fusion.27.both_ref
  131.8 22.1 %recur_forward.1 = (bf16[1024,704]{1,0:T(8,128)(2,1)}, f32[1024,704]{1,0:T(8,128)}, f32[1024,704]{1,0:T(8,128)}, f32[1024,704]{1,0:T(8,128)}, f32[1024,704]{1,0:T(8,128)}) custom-call(f32[1024,1408]{1,0:T(8,128)} %fusion.27.both_ref, f32[1024,8]{1,0:T(8,128)} %copy.98.mask_ref, f32[8,704]{1,0:T(8,128)} %concatenate.145.vec_ref, ...), custom_call_target="tpu_custom_call" | custom-call | flops 2030043136 | bytes 21626880 | tf_op jit(solution)/shard_map/recur_forward/pallas_call | solution.py:214
  153.9 4.4 convolution_convert_fusion.5
  167.5 20.6 %collective-permute-start.35 = (bf16[256,1536]{0,1:T(8,128)(2,1)}, bf16[256,1536]{0,1:T(8,128)(2,1)}, u32[]{:S(2)}, u32[]{:S(2)}) collective-permute-start(bf16[256,1536]{0,1:T(8,128)(2,1)} %get-tuple-element.110), channel_id=1, source_target_pairs={{0,8},{2,10},{4,12},{6,14},{24,16},{26,18},{28,20},{30,22},{1,9},{... | collective-permute-start | bytes 2359304 | tf_op jit(solution)/shard_map/ppermute | solution.py:317
  191.7 6.1 broadcast_in_dim.53
  202.0 5.0 collective-permute-start.36
  207.1 3.6 convert_add_fusion.3
  217.4 13.5 %collective-permute-start.27 = (bf16[256,3072]{1,0:T(8,128)(2,1)S(1)}, bf16[256,3072]{1,0:T(8,128)(2,1)S(1)}, u32[]{:S(2)}, u32[]{:S(2)}) collective-permute-start(bf16[256,3072]{1,0:T(8,128)(2,1)S(1)} %get-tuple-element.108), channel_id=1, source_target_pairs={{0,8},{2,10},{4,12},{6,14},{24,16},{26,18},{28,20},{30,22},{1,9},{... | collective-permute-start | bytes 4718600 | tf_op jit(solution)/shard_map/ppermute | solution.py:317
  238.3 8.0 collective-permute-start.28
  249.7 9.1 collective-permute-done.27
  260.6 29.9 %collective-permute-done.28 = bf16[256,3072]{1,0:T(8,128)(2,1)S(1)} collective-permute-done((bf16[256,3072]{1,0:T(8,128)(2,1)S(1)}, bf16[256,3072]{1,0:T(8,128)(2,1)S(1)}, u32[]{:S(2)}, u32[]{:S(2)}) %collective-permute-start.28) | collective-permute-done | bytes 1572896 | tf_op jit(solution)/shard_map/ppermute | solution.py:317
  297.9 15.7 %fusion.26 = f32[1024,3072]{1,0:T(8,128)} fusion(bf16[2048,3072]{1,0:T(8,128)(2,1)S(1)} %constant_dynamic-update-slice_fusion.8, bf16[512,2048]{1,0:T(8,128)(2,1)S(1)} %collective-permute-done.24, bf16[512,2048]{1,0:T(8,128)(2,1)S(1)} %fusion.14), kind=kOutput, calls=%fused_computation.65 | convolution fusion | flops 12893290496 | bytes 29360128 | tf_op jit(solution)/shard_map/dot_general | solution.py:496
  313.6 23.9 %multiply_convert_fusion = (bf16[1024,1536]{1,0:T(8,128)(2,1)}, bf16[1024,1536]{1,0:T(8,128)(2,1)}, bf16[1024,1536]{1,0:T(8,128)(2,1)}) fusion(f32[1024,3072]{1,0:T(8,128)} %fusion.26, bf16[2048,1536]{0,1:T(8,128)(2,1)} %constant_dynamic-update-slice_fusion, bf16[512,2048]{1,0:T(8,128)(2,1)} %collective-permute-done.46, ...), kind=kOutput, calls=%fused_computation.19 | convolution fusion | flops 6494355456 | bytes 32505856 | tf_op jit(solution)/shard_map/dot_general | solution.py:503
  337.5 12.2 %fusion.23 = bf16[512,2048]{1,0:T(8,128)(2,1)} fusion(bf16[2048,3072]{1,0:T(8,128)(2,1)} %copy-done.4, bf16[1024,1536]{1,0:T(8,128)(2,1)} %get-tuple-element.112, bf16[1024,1536]{1,0:T(8,128)(2,1)} %get-tuple-element.111), kind=kOutput, calls=%fused_computation.64 | convolution fusion | flops 6449790976 | bytes 20971520 | tf_op jit(solution)/shard_map/dot_general | solution.py:508
  349.9 18.5 %convolution_convert_fusion = bf16[2048,3072]{1,0:T(8,128)(2,1)} fusion(bf16[1024,1536]{1,0:T(8,128)(2,1)} %get-tuple-element.111, bf16[1024,1536]{1,0:T(8,128)(2,1)} %get-tuple-element.112, bf16[512,2048]{1,0:T(8,128)(2,1)S(1)} %copy-done.94, bf16[512,2048]{1,0:T(8,128)(2,1)S(1)} %copy-done.33), kind=kOutput, calls=%fused_computation | convolution fusion | flops 12912164864 | bytes 23068672 | tf_op jit(solution)/shard_map/dot_general | solution.py:512
  368.4 5.3 constant_dynamic-slice_fusion.7
  375.2 8.6 convolution_convert_fusion.1
  388.0 8.3 convolution_convert_fusion.4
  408.2 10.9 %convert_add_fusion.1 = f32[512,2048]{1,0:T(8,128)S(1)} fusion(bf16[512,2048]{1,0:T(8,128)(2,1)} %collective-permute-done.47, bf16[2048,3072]{1,0:T(8,128)(2,1)} %copy-done.4, bf16[1024,1536]{1,0:T(8,128)(2,1)} %get-tuple-element.112, bf16[1024,1536]{1,0:T(8,128)(2,1)} %get-tuple-element.111), kind=kOutput, calls=%fused_computation.37 | convolution fusion | flops 6450839552 | bytes 25165824 | tf_op jit(solution)/shard_map/dot_general | solution.py:508
  419.8 152.7 %collective-permute-done.101 = bf16[256,1536]{0,1:T(8,128)(2,1)} collective-permute-done((bf16[256,1536]{0,1:T(8,128)(2,1)}, bf16[256,1536]{0,1:T(8,128)(2,1)}, u32[]{:S(2)}, u32[]{:S(2)}) %collective-permute-start.101) | collective-permute-done | bytes 786464 | tf_op jit(solution)/shard_map/ppermute | solution.py:317
  576.8 7.3 convert_add_fusion.2
  589.4 24.2 %collective-permute-done.92 = bf16[256,3072]{1,0:T(8,128)(2,1)} collective-permute-done((bf16[256,3072]{1,0:T(8,128)(2,1)}, bf16[256,3072]{1,0:T(8,128)(2,1)}, u32[]{:S(2)}, u32[]{:S(2)}) %collective-permute-start.92) | collective-permute-done | bytes 1572896 | tf_op jit(solution)/shard_map/ppermute | solution.py:317
  618.4 9.7 %collective-permute-done.100 = bf16[256,1536]{0,1:T(8,128)(2,1)S(1)} collective-permute-done((bf16[256,1536]{0,1:T(8,128)(2,1)}, bf16[256,1536]{0,1:T(8,128)(2,1)S(1)}, u32[]{:S(2)}, u32[]{:S(2)}) %collective-permute-start.100) | collective-permute-done | bytes 786464 | tf_op jit(solution)/shard_map/ppermute | solution.py:317
  635.9 3.7 fusion.85
  640.6 8.7 collective-permute-done.93
  649.3 18.9 %collective-permute-done.91 = bf16[256,3072]{1,0:T(8,128)(2,1)S(1)} collective-permute-done((bf16[256,3072]{1,0:T(8,128)(2,1)S(1)}, bf16[256,3072]{1,0:T(8,128)(2,1)S(1)}, u32[]{:S(2)}, u32[]{:S(2)}) %collective-permute-start.91) | collective-permute-done | bytes 1572896 | tf_op jit(solution)/shard_map/ppermute | solution.py:317
  676.6 4.1 copy.111
  680.7 7.4 fusion.51.dmix_ref
  688.2 35.6 %recur_backward.1 = (bf16[1024,1408]{1,0:T(8,128)(2,1)}, f32[8,704]{1,0:T(8,128)}, f32[704,704]{1,0:T(8,128)}, f32[704,704]{1,0:T(8,128)}) custom-call(f32[1024,704]{1,0:T(8,128)} %fusion.51.dmix_ref, f32[1024,1408]{1,0:T(8,128)} %fusion.27.both_ref, f32[1024,704]{1,0:T(8,128)} %get-tuple-element.25.state_ref, f32[1024,704]{1,0:T(8,128)} %get-tuple-element.26.conv_ref, ...), custom_call_target="tpu_custom_call" | custom-call | flops 4060086272 | bytes 28835840 | tf_op jit(solution)/shard_map/recur_backward/pallas_call | solution.py:231
  729.1 4.9 convolution_convert_fusion.3
  737.8 6.6 convolution_convert_fusion.2
  745.8 4.6 convolution_convert_fusion.6
  750.4 6.8 collective-permute-done.75
  771.5 5.0 collective-permute-done.84
  778.6 28.2 %collective-permute-done.82 = bf16[256,704]{0,1:T(8,128)(2,1)S(1)} collective-permute-done((bf16[256,704]{0,1:T(8,128)(2,1)S(1)}, bf16[256,704]{0,1:T(8,128)(2,1)S(1)}, u32[]{:S(2)}, u32[]{:S(2)}) %collective-permute-start.82) | collective-permute-done | bytes 360480 | tf_op jit(solution)/shard_map/ppermute | solution.py:317
  809.2 14.0 %collective-permute-done.66 = bf16[256,1408]{0,1:T(8,128)(2,1)} collective-permute-done((bf16[256,1408]{0,1:T(8,128)(2,1)S(1)}, bf16[256,1408]{0,1:T(8,128)(2,1)}, u32[]{:S(2)}, u32[]{:S(2)}) %collective-permute-start.66) | collective-permute-done | bytes 720928 | tf_op jit(solution)/shard_map/ppermute | solution.py:317
  824.0 9.8 %collective-permute-done.71 = bf16[4,176,352]{2,1,0:T(8,128)(2,1)S(1)} collective-permute-done((bf16[4,176,352]{2,1,0:T(8,128)(2,1)S(1)}, bf16[4,176,352]{2,1,0:T(8,128)(2,1)S(1)}, u32[]{:S(2)}, u32[]{:S(2)}) %collective-permute-start.71) | collective-permute-done | bytes 495648 | tf_op jit(solution)/shard_map/ppermute | solution.py:317
  846.4 6.7 collective-permute-done.67
  853.2 6.0 collective-permute-done.65
  861.4 5.0 convert_add_fusion
  868.0 25.1 %collective-permute-done.53 = bf16[512,1024]{1,0:T(8,128)(2,1)S(1)} collective-permute-done((bf16[512,1024]{1,0:T(8,128)(2,1)S(1)}, bf16[512,1024]{1,0:T(8,128)(2,1)S(1)}, u32[]{:S(2)}, u32[]{:S(2)}) %collective-permute-start.53) | collective-permute-done | bytes 1048608 | tf_op jit(solution)/shard_map/ppermute | solution.py:328
  905.8 3.6 collective-permute-done.58
  912.2 13.2 %collective-permute-done.43 = bf16[256,1024]{1,0:T(8,128)(2,1)} collective-permute-done((bf16[256,1024]{1,0:T(8,128)(2,1)}, bf16[256,1024]{1,0:T(8,128)(2,1)}, u32[]{:S(2)}, u32[]{:S(2)}) %collective-permute-start.43) | collective-permute-done | bytes 524320 | tf_op jit(solution)/shard_map/ppermute | solution.py:317
  927.2 5.3 collective-permute-done.55
  (588 shorter events, 230.2 us)
Async XLA Ops:
  0.7 36.9 %collective-permute-start = (s32[1,4]{1,0:T(1,128)}, s32[1,4]{1,0:T(1,128)}, u32[]{:S(2)}, u32[]{:S(2)}) collective-permute-start(s32[1,4]{1,0:T(1,128)} %param.30), channel_id=1, source_target_pairs={{0,8},{2,10},{4,12},{6,14},{24,16},{26,18},{28,20},{30,22},{1,9},{... | collective-permute-start | bytes 56 | tf_op jit(solution)/shard_map/ppermute | solution.py:317
  8.5 32.7 %collective-permute-start.13 = (bf16[128,704]{0,1:T(8,128)(2,1)}, bf16[128,704]{0,1:T(8,128)(2,1)}, u32[]{:S(2)}, u32[]{:S(2)}) collective-permute-start(bf16[128,704]{0,1:T(8,128)(2,1)} %broadcast_select_fusion.14), channel_id=1, source_target_pairs={{0,2},{2,0},{4,6},{6,4},{8,10},{10,8},{12,14},{14,12},{16,18},{18,... | collective-permute-start | bytes 540680 | tf_op jit(solution)/shard_map/ppermute | solution.py:317
  8.5 36.4 %collective-permute-start.2 = (bf16[256,1024]{1,0:T(8,128)(2,1)}, bf16[256,1024]{1,0:T(8,128)(2,1)}, u32[]{:S(2)}, u32[]{:S(2)}) collective-permute-start(bf16[256,1024]{1,0:T(8,128)(2,1)} %param.16), channel_id=1, source_target_pairs={{0,8},{2,10},{4,12},{6,14},{24,16},{26,18},{28,20},{30,22},{1,9},{... | collective-permute-start | bytes 1572872 | tf_op jit(solution)/shard_map/ppermute | solution.py:317
  16.1 39.4 %collective-permute-start.5 = (bf16[128,1408]{0,1:T(8,128)(2,1)}, bf16[128,1408]{0,1:T(8,128)(2,1)}, u32[]{:S(2)}, u32[]{:S(2)}) collective-permute-start(bf16[128,1408]{0,1:T(8,128)(2,1)} %maximum_select_fusion.6), channel_id=1, source_target_pairs={{0,2},{2,0},{4,6},{6,4},{8,10},{10,8},{12,14},{14,12},{16,18},{18,... | collective-permute-start | bytes 1081352 | tf_op jit(solution)/shard_map/ppermute | solution.py:317
  57.7 43.1 %collective-permute-start.7 = (bf16[256,1408]{0,1:T(8,128)(2,1)S(1)}, bf16[256,1408]{0,1:T(8,128)(2,1)S(1)}, u32[]{:S(2)}, u32[]{:S(2)}) collective-permute-start(bf16[256,1408]{0,1:T(8,128)(2,1)S(1)} %get-tuple-element.104), channel_id=1, source_target_pairs={{0,8},{2,10},{4,12},{6,14},{24,16},{26,18},{28,20},{30,22},{1,9},{... | collective-permute-start | bytes 2162696 | tf_op jit(solution)/shard_map/ppermute | solution.py:317
  67.1 35.8 %collective-permute-start.9 = (bf16[256,1408]{0,1:T(8,128)(2,1)S(1)}, bf16[256,1408]{0,1:T(8,128)(2,1)S(1)}, u32[]{:S(2)}, u32[]{:S(2)}) collective-permute-start(bf16[256,1408]{0,1:T(8,128)(2,1)S(1)} %get-tuple-element.104), channel_id=1, source_target_pairs={{8,16},{10,18},{12,20},{14,22},{16,8},{18,10},{20,12},{22,14},{9,1... | collective-permute-start | bytes 2162696 | tf_op jit(solution)/shard_map/ppermute | solution.py:317
  73.4 45.3 %collective-permute-start.4 = (bf16[512,2048]{1,0:T(8,128)(2,1)S(1)}, bf16[512,2048]{1,0:T(8,128)(2,1)S(1)}, u32[]{:S(2)}, u32[]{:S(2)}) collective-permute-start(bf16[512,2048]{1,0:T(8,128)(2,1)S(1)} %fusion.11), channel_id=1, source_target_pairs={{0,2},{2,0},{4,6},{6,4},{8,10},{10,8},{12,14},{14,12},{16,18},{18,... | collective-permute-start | bytes 6291464 | tf_op jit(solution)/shard_map/ppermute | solution.py:317
  73.6 30.1 %collective-permute-start.20 = (bf16[256,704]{0,1:T(8,128)(2,1)S(1)}, bf16[256,704]{0,1:T(8,128)(2,1)S(1)}, u32[]{:S(2)}, u32[]{:S(2)}) collective-permute-start(bf16[256,704]{0,1:T(8,128)(2,1)S(1)} %collective-permute-done.16), channel_id=1, source_target_pairs={{8,16},{10,18},{12,20},{14,22},{16,8},{18,10},{20,12},{22,14},{9,1... | collective-permute-start | bytes 1081352 | tf_op jit(solution)/shard_map/ppermute | solution.py:317
  76.6 40.6 %collective-permute-start.8 = (bf16[256,1408]{0,1:T(8,128)(2,1)S(1)}, bf16[256,1408]{0,1:T(8,128)(2,1)S(1)}, u32[]{:S(2)}, u32[]{:S(2)}) collective-permute-start(bf16[256,1408]{0,1:T(8,128)(2,1)S(1)} %collective-permute-done.6), channel_id=1, source_target_pairs={{0,8},{2,10},{4,12},{6,14},{24,16},{26,18},{28,20},{30,22},{1,9},{... | collective-permute-start | bytes 2162696 | tf_op jit(solution)/shard_map/ppermute | solution.py:317
  100.8 87.4 %collective-permute-start.44 = (bf16[256,1024]{1,0:T(8,128)(2,1)}, bf16[256,1024]{1,0:T(8,128)(2,1)}, u32[]{:S(2)}, u32[]{:S(2)}) collective-permute-start(bf16[256,1024]{1,0:T(8,128)(2,1)} %param.31), channel_id=1, source_target_pairs={{0,8},{2,10},{4,12},{6,14},{24,16},{26,18},{28,20},{30,22},{1,9},{... | collective-permute-start | bytes 1572872 | tf_op jit(solution)/shard_map/ppermute | solution.py:317
  118.3 42.3 %collective-permute-start.33 = (bf16[128,1536]{0,1:T(8,128)(2,1)}, bf16[128,1536]{0,1:T(8,128)(2,1)}, u32[]{:S(2)}, u32[]{:S(2)}) collective-permute-start(bf16[128,1536]{0,1:T(8,128)(2,1)} %broadcast_select_fusion.7), channel_id=1, source_target_pairs={{0,2},{2,0},{4,6},{6,4},{8,10},{10,8},{12,14},{14,12},{16,18},{18,... | collective-permute-start | bytes 1179656 | tf_op jit(solution)/shard_map/ppermute | solution.py:317
  158.3 43.7 %collective-permute-start.21 = (bf16[512,2048]{1,0:T(8,128)(2,1)}, bf16[512,2048]{1,0:T(8,128)(2,1)}, u32[]{:S(2)}, u32[]{:S(2)}) collective-permute-start(bf16[512,2048]{1,0:T(8,128)(2,1)} %convolution_convert_fusion.5), channel_id=1, source_target_pairs={{0,2},{2,0},{4,6},{6,4},{8,10},{10,8},{12,14},{14,12},{16,18},{18,... | collective-permute-start | bytes 6291464 | tf_op jit(solution)/shard_map/ppermute | solution.py:317
  160.0 31.2 %collective-permute-start.25 = (bf16[128,3072]{1,0:T(8,128)(2,1)}, bf16[128,3072]{1,0:T(8,128)(2,1)}, u32[]{:S(2)}, u32[]{:S(2)}) collective-permute-start(bf16[128,3072]{1,0:T(8,128)(2,1)} %maximum_select_fusion.3), channel_id=1, source_target_pairs={{0,2},{2,0},{4,6},{6,4},{8,10},{10,8},{12,14},{14,12},{16,18},{18,... | collective-permute-start | bytes 2359304 | tf_op jit(solution)/shard_map/ppermute | solution.py:317
  166.6 34.4 %collective-permute-start.34 = (bf16[256,1536]{0,1:T(8,128)(2,1)}, bf16[256,1536]{0,1:T(8,128)(2,1)}, u32[]{:S(2)}, u32[]{:S(2)}) collective-permute-start(bf16[256,1536]{0,1:T(8,128)(2,1)} %get-tuple-element.110), channel_id=1, source_target_pairs={{0,4},{2,6},{4,0},{6,2},{8,12},{10,14},{12,8},{14,10},{16,20},{18,... | collective-permute-start | bytes 2359304 | tf_op jit(solution)/shard_map/ppermute | solution.py:317
  167.5 43.3 %collective-permute-start.35 = (bf16[256,1536]{0,1:T(8,128)(2,1)}, bf16[256,1536]{0,1:T(8,128)(2,1)}, u32[]{:S(2)}, u32[]{:S(2)}) collective-permute-start(bf16[256,1536]{0,1:T(8,128)(2,1)} %get-tuple-element.110), channel_id=1, source_target_pairs={{0,8},{2,10},{4,12},{6,14},{24,16},{26,18},{28,20},{30,22},{1,9},{... | collective-permute-start | bytes 2359304 | tf_op jit(solution)/shard_map/ppermute | solution.py:317
  188.2 42.9 %collective-permute-start.37 = (bf16[256,1536]{0,1:T(8,128)(2,1)}, bf16[256,1536]{0,1:T(8,128)(2,1)}, u32[]{:S(2)}, u32[]{:S(2)}) collective-permute-start(bf16[256,1536]{0,1:T(8,128)(2,1)} %get-tuple-element.110), channel_id=1, source_target_pairs={{8,16},{10,18},{12,20},{14,22},{16,8},{18,10},{20,12},{22,14},{9,1... | collective-permute-start | bytes 2359304 | tf_op jit(solution)/shard_map/ppermute | solution.py:317
  201.0 35.5 %collective-permute-start.26 = (bf16[256,3072]{1,0:T(8,128)(2,1)S(1)}, bf16[256,3072]{1,0:T(8,128)(2,1)S(1)}, u32[]{:S(2)}, u32[]{:S(2)}) collective-permute-start(bf16[256,3072]{1,0:T(8,128)(2,1)S(1)} %get-tuple-element.108), channel_id=1, source_target_pairs={{0,4},{2,6},{4,0},{6,2},{8,12},{10,14},{12,8},{14,10},{16,20},{18,... | collective-permute-start | bytes 4718600 | tf_op jit(solution)/shard_map/ppermute | solution.py:317
  202.0 29.9 %collective-permute-start.36 = (bf16[256,1536]{0,1:T(8,128)(2,1)}, bf16[256,1536]{0,1:T(8,128)(2,1)S(1)}, u32[]{:S(2)}, u32[]{:S(2)}) collective-permute-start(bf16[256,1536]{0,1:T(8,128)(2,1)} %collective-permute-done.34), channel_id=1, source_target_pairs={{0,8},{2,10},{4,12},{6,14},{24,16},{26,18},{28,20},{30,22},{1,9},{... | collective-permute-start | bytes 2359304 | tf_op jit(solution)/shard_map/ppermute | solution.py:317
  217.4 41.5 %collective-permute-start.27 = (bf16[256,3072]{1,0:T(8,128)(2,1)S(1)}, bf16[256,3072]{1,0:T(8,128)(2,1)S(1)}, u32[]{:S(2)}, u32[]{:S(2)}) collective-permute-start(bf16[256,3072]{1,0:T(8,128)(2,1)S(1)} %get-tuple-element.108), channel_id=1, source_target_pairs={{0,8},{2,10},{4,12},{6,14},{24,16},{26,18},{28,20},{30,22},{1,9},{... | collective-permute-start | bytes 4718600 | tf_op jit(solution)/shard_map/ppermute | solution.py:317
  238.3 52.2 %collective-permute-start.28 = (bf16[256,3072]{1,0:T(8,128)(2,1)S(1)}, bf16[256,3072]{1,0:T(8,128)(2,1)S(1)}, u32[]{:S(2)}, u32[]{:S(2)}) collective-permute-start(bf16[256,3072]{1,0:T(8,128)(2,1)S(1)} %collective-permute-done.26), channel_id=1, source_target_pairs={{0,8},{2,10},{4,12},{6,14},{24,16},{26,18},{28,20},{30,22},{1,9},{... | collective-permute-start | bytes 4718600 | tf_op jit(solution)/shard_map/ppermute | solution.py:317
  246.9 44.3 %collective-permute-start.23 = (bf16[512,1024]{1,0:T(8,128)(2,1)S(1)}, bf16[512,1024]{1,0:T(8,128)(2,1)S(1)}, u32[]{:S(2)}, u32[]{:S(2)}) collective-permute-start(bf16[512,1024]{1,0:T(8,128)(2,1)S(1)} %fusion.71), channel_id=1, source_target_pairs={{0,1},{1,0},{2,3},{3,2},{4,5},{5,4},{6,7},{7,6},{8,9},{9,8},{10,11... | collective-permute-start | bytes 3145736 | tf_op jit(solution)/shard_map/ppermute | solution.py:328
  248.5 65.1 %collective-permute-start.46 = (bf16[512,2048]{1,0:T(8,128)(2,1)S(1)}, bf16[512,2048]{1,0:T(8,128)(2,1)}, u32[]{:S(2)}, u32[]{:S(2)}) collective-permute-start(bf16[512,2048]{1,0:T(8,128)(2,1)S(1)} %pad_maximum_fusion.13), channel_id=1, source_target_pairs={{0,2},{2,0},{4,6},{6,4},{8,10},{10,8},{12,14},{14,12},{16,18},{18,... | collective-permute-start | bytes 6291464 | tf_op jit(solution)/shard_map/ppermute | solution.py:317
  258.9 34.8 %collective-permute-start.40 = (bf16[256,1536]{0,1:T(8,128)(2,1)S(1)}, bf16[256,1536]{0,1:T(8,128)(2,1)S(1)}, u32[]{:S(2)}, u32[]{:S(2)}) collective-permute-start(bf16[256,1536]{0,1:T(8,128)(2,1)S(1)} %collective-permute-done.36), channel_id=1, source_target_pairs={{8,16},{10,18},{12,20},{14,22},{16,8},{18,10},{20,12},{22,14},{9,1... | collective-permute-start | bytes 2359304 | tf_op jit(solution)/shard_map/ppermute | solution.py:317
  259.8 35.6 %collective-permute-start.31 = (bf16[256,3072]{1,0:T(8,128)(2,1)S(1)}, bf16[256,3072]{1,0:T(8,128)(2,1)S(1)}, u32[]{:S(2)}, u32[]{:S(2)}) collective-permute-start(bf16[256,3072]{1,0:T(8,128)(2,1)S(1)} %collective-permute-done.27), channel_id=1, source_target_pairs={{8,16},{10,18},{12,20},{14,22},{16,8},{18,10},{20,12},{22,14},{9,1... | collective-permute-start | bytes 4718600 | tf_op jit(solution)/shard_map/ppermute | solution.py:317
  349.7 56.6 %collective-permute-start.47 = (bf16[512,2048]{1,0:T(8,128)(2,1)}, bf16[512,2048]{1,0:T(8,128)(2,1)}, u32[]{:S(2)}, u32[]{:S(2)}) collective-permute-start(bf16[512,2048]{1,0:T(8,128)(2,1)} %fusion.23), channel_id=1, source_target_pairs={{0,2},{2,0},{4,6},{6,4},{8,10},{10,8},{12,14},{14,12},{16,18},{18,... | collective-permute-start | bytes 6291464 | tf_op jit(solution)/shard_map/ppermute | solution.py:317
  396.4 179.2 %collective-permute-start.41 = (bf16[512,2048]{1,0:T(8,128)(2,1)}, bf16[512,2048]{1,0:T(8,128)(2,1)}, u32[]{:S(2)}, u32[]{:S(2)}) collective-permute-start(bf16[512,2048]{1,0:T(8,128)(2,1)} %convolution_convert_fusion.4), channel_id=1, source_target_pairs={{0,2},{2,0},{4,6},{6,4},{8,10},{10,8},{12,14},{14,12},{16,18},{18,... | collective-permute-start | bytes 6291464 | tf_op jit(solution)/shard_map/ppermute | solution.py:317
  399.0 173.5 %collective-permute-start.101 = (bf16[256,1536]{0,1:T(8,128)(2,1)}, bf16[256,1536]{0,1:T(8,128)(2,1)}, u32[]{:S(2)}, u32[]{:S(2)}) collective-permute-start(bf16[256,1536]{0,1:T(8,128)(2,1)} %get-tuple-element.121), channel_id=1, source_target_pairs={{8,0},{10,2},{12,4},{14,6},{16,24},{18,26},{20,28},{22,30},{9,1},{... | collective-permute-start | bytes 2359304 | tf_op jit(solution)/shard_map/ppermute | solution.py:317
  403.8 209.8 %collective-permute-start.92 = (bf16[256,3072]{1,0:T(8,128)(2,1)}, bf16[256,3072]{1,0:T(8,128)(2,1)}, u32[]{:S(2)}, u32[]{:S(2)}) collective-permute-start(bf16[256,3072]{1,0:T(8,128)(2,1)} %get-tuple-element.114), channel_id=1, source_target_pairs={{8,0},{10,2},{12,4},{14,6},{16,24},{18,26},{20,28},{22,30},{9,1},{... | collective-permute-start | bytes 4718600 | tf_op jit(solution)/shard_map/ppermute | solution.py:317
  406.3 180.1 %collective-permute-start.90 = (bf16[256,3072]{1,0:T(8,128)(2,1)}, bf16[256,3072]{1,0:T(8,128)(2,1)}, u32[]{:S(2)}, u32[]{:S(2)}) collective-permute-start(bf16[256,3072]{1,0:T(8,128)(2,1)} %get-tuple-element.118), channel_id=1, source_target_pairs={{8,16},{10,18},{12,20},{14,22},{16,8},{18,10},{20,12},{22,14},{9,1... | collective-permute-start | bytes 4718600 | tf_op jit(solution)/shard_map/ppermute | solution.py:317
  419.1 196.2 %collective-permute-start.97 = (bf16[256,1536]{0,1:T(8,128)(2,1)}, bf16[256,1536]{0,1:T(8,128)(2,1)S(1)}, u32[]{:S(2)}, u32[]{:S(2)}) collective-permute-start(bf16[256,1536]{0,1:T(8,128)(2,1)} %get-tuple-element.124), channel_id=1, source_target_pairs={{8,16},{10,18},{12,20},{14,22},{16,8},{18,10},{20,12},{22,14},{9,1... | collective-permute-start | bytes 2359304 | tf_op jit(solution)/shard_map/ppermute | solution.py:317
  572.5 41.9 %collective-permute-start.102 = (bf16[256,1536]{0,1:T(8,128)(2,1)}, bf16[256,1536]{0,1:T(8,128)(2,1)S(1)}, u32[]{:S(2)}, u32[]{:S(2)}) collective-permute-start(bf16[256,1536]{0,1:T(8,128)(2,1)} %collective-permute-done.101), channel_id=1, source_target_pairs={{0,4},{2,6},{4,0},{6,2},{24,28},{26,30},{28,24},{30,26},{1,5},{3,7... | collective-permute-start | bytes 2359304 | tf_op jit(solution)/shard_map/ppermute | solution.py:317
  575.5 52.5 %collective-permute-start.100 = (bf16[256,1536]{0,1:T(8,128)(2,1)}, bf16[256,1536]{0,1:T(8,128)(2,1)S(1)}, u32[]{:S(2)}, u32[]{:S(2)}) collective-permute-start(bf16[256,1536]{0,1:T(8,128)(2,1)} %add_convert_fusion.3), channel_id=1, source_target_pairs={{8,0},{10,2},{12,4},{14,6},{16,24},{18,26},{20,28},{22,30},{9,1},{... | collective-permute-start | bytes 2359304 | tf_op jit(solution)/shard_map/ppermute | solution.py:317
  586.4 44.9 %collective-permute-start.48 = (bf16[512,1024]{1,0:T(8,128)(2,1)S(1)}, bf16[512,1024]{1,0:T(8,128)(2,1)S(1)}, u32[]{:S(2)}, u32[]{:S(2)}) collective-permute-start(bf16[512,1024]{1,0:T(8,128)(2,1)S(1)} %slice.631), channel_id=1, source_target_pairs={{0,1},{1,0},{2,3},{3,2},{4,5},{5,4},{6,7},{7,6},{8,9},{9,8},{10,11... | collective-permute-start | bytes 3145736 | tf_op jit(solution)/shard_map/ppermute | solution.py:328
  614.4 34.9 %collective-permute-start.88 = (bf16[256,3072]{1,0:T(8,128)(2,1)S(1)}, bf16[256,3072]{1,0:T(8,128)(2,1)S(1)}, u32[]{:S(2)}, u32[]{:S(2)}) collective-permute-start(bf16[256,3072]{1,0:T(8,128)(2,1)S(1)} %copy-done.46), channel_id=1, source_target_pairs={{8,16},{10,18},{12,20},{14,22},{16,8},{18,10},{20,12},{22,14},{9,1... | collective-permute-start | bytes 4718600 | tf_op jit(solution)/shard_map/ppermute | solution.py:317
  615.3 34.0 %collective-permute-start.93 = (bf16[256,3072]{1,0:T(8,128)(2,1)}, bf16[256,3072]{1,0:T(8,128)(2,1)S(1)}, u32[]{:S(2)}, u32[]{:S(2)}) collective-permute-start(bf16[256,3072]{1,0:T(8,128)(2,1)} %collective-permute-done.92), channel_id=1, source_target_pairs={{0,4},{2,6},{4,0},{6,2},{24,28},{26,30},{28,24},{30,26},{1,5},{3,7... | collective-permute-start | bytes 4718600 | tf_op jit(solution)/shard_map/ppermute | solution.py:317
  628.1 40.2 %collective-permute-start.91 = (bf16[256,3072]{1,0:T(8,128)(2,1)S(1)}, bf16[256,3072]{1,0:T(8,128)(2,1)S(1)}, u32[]{:S(2)}, u32[]{:S(2)}) collective-permute-start(bf16[256,3072]{1,0:T(8,128)(2,1)S(1)} %add_convert_fusion), channel_id=1, source_target_pairs={{8,0},{10,2},{12,4},{14,6},{16,24},{18,26},{20,28},{22,30},{9,1},{... | collective-permute-start | bytes 4718600 | tf_op jit(solution)/shard_map/ppermute | solution.py:317
  635.9 34.6 %collective-permute-start.103 = (bf16[128,1536]{0,1:T(8,128)(2,1)S(1)}, bf16[128,1536]{0,1:T(8,128)(2,1)S(1)}, u32[]{:S(2)}, u32[]{:S(2)}) collective-permute-start(bf16[128,1536]{0,1:T(8,128)(2,1)S(1)} %broadcast_select_fusion.5), channel_id=1, source_target_pairs={{0,2},{2,0},{4,6},{6,4},{8,10},{10,8},{12,14},{14,12},{16,18},{18,... | collective-permute-start | bytes 1179656 | tf_op jit(solution)/shard_map/ppermute | solution.py:317
  639.7 32.7 %collective-permute-start.50 = (bf16[512,1024]{1,0:T(8,128)(2,1)}, bf16[512,1024]{1,0:T(8,128)(2,1)}, u32[]{:S(2)}, u32[]{:S(2)}) collective-permute-start(bf16[512,1024]{1,0:T(8,128)(2,1)} %get-tuple-element.101), channel_id=1, source_target_pairs={{0,1},{1,0},{2,3},{3,2},{4,5},{5,4},{6,7},{7,6},{8,9},{9,8},{10,11... | collective-permute-start | bytes 3145736 | tf_op jit(solution)/shard_map/ppermute | solution.py:328
  728.1 34.1 %collective-permute-start.69 = (bf16[4,176,352]{2,1,0:T(8,128)(2,1)S(1)}, bf16[4,176,352]{2,1,0:T(8,128)(2,1)S(1)}, u32[]{:S(2)}, u32[]{:S(2)}) collective-permute-start(bf16[4,176,352]{2,1,0:T(8,128)(2,1)S(1)} %fusion.67), channel_id=1, source_target_pairs={{0,4},{2,6},{4,0},{6,2},{8,12},{10,14},{12,8},{14,10},{16,20},{18,... | collective-permute-start | bytes 1486856 | tf_op jit(solution)/shard_map/ppermute | solution.py:317
  734.2 28.9 %collective-permute-start.83 = (bf16[256,704]{0,1:T(8,128)(2,1)S(1)}, bf16[256,704]{0,1:T(8,128)(2,1)S(1)}, u32[]{:S(2)}, u32[]{:S(2)}) collective-permute-start(bf16[256,704]{0,1:T(8,128)(2,1)S(1)} %get-tuple-element.133), channel_id=1, source_target_pairs={{8,0},{10,2},{12,4},{14,6},{16,24},{18,26},{20,28},{22,30},{9,1},{... | collective-permute-start | bytes 1081352 | tf_op jit(solution)/shard_map/ppermute | solution.py:317
  767.7 39.1 %collective-permute-start.82 = (bf16[256,704]{0,1:T(8,128)(2,1)S(1)}, bf16[256,704]{0,1:T(8,128)(2,1)S(1)}, u32[]{:S(2)}, u32[]{:S(2)}) collective-permute-start(bf16[256,704]{0,1:T(8,128)(2,1)S(1)} %add_convert_fusion.9), channel_id=1, source_target_pairs={{8,0},{10,2},{12,4},{14,6},{16,24},{18,26},{20,28},{22,30},{9,1},{... | collective-permute-start | bytes 1081352 | tf_op jit(solution)/shard_map/ppermute | solution.py:317
  769.6 91.7 %collective-permute-start.52 = (bf16[512,2048]{1,0:T(8,128)(2,1)}, bf16[512,2048]{1,0:T(8,128)(2,1)}, u32[]{:S(2)}, u32[]{:S(2)}) collective-permute-start(bf16[512,2048]{1,0:T(8,128)(2,1)} %convolution_convert_fusion.6), channel_id=1, source_target_pairs={{0,2},{2,0},{4,6},{6,4},{8,10},{10,8},{12,14},{14,12},{16,18},{18,... | collective-permute-start | bytes 6291464 | tf_op jit(solution)/shard_map/ppermute | solution.py:317
  770.2 53.0 %collective-permute-start.66 = (bf16[256,1408]{0,1:T(8,128)(2,1)S(1)}, bf16[256,1408]{0,1:T(8,128)(2,1)}, u32[]{:S(2)}, u32[]{:S(2)}) collective-permute-start(bf16[256,1408]{0,1:T(8,128)(2,1)S(1)} %get-tuple-element.127), channel_id=1, source_target_pairs={{8,0},{10,2},{12,4},{14,6},{16,24},{18,26},{20,28},{22,30},{9,1},{... | collective-permute-start | bytes 2162696 | tf_op jit(solution)/shard_map/ppermute | solution.py:317
  776.6 60.2 %collective-permute-start.64 = (bf16[256,1408]{0,1:T(8,128)(2,1)S(1)}, bf16[256,1408]{0,1:T(8,128)(2,1)S(1)}, u32[]{:S(2)}, u32[]{:S(2)}) collective-permute-start(bf16[256,1408]{0,1:T(8,128)(2,1)S(1)} %get-tuple-element.131), channel_id=1, source_target_pairs={{8,16},{10,18},{12,20},{14,22},{16,8},{18,10},{20,12},{22,14},{9,1... | collective-permute-start | bytes 2162696 | tf_op jit(solution)/shard_map/ppermute | solution.py:317
  777.3 56.5 %collective-permute-start.71 = (bf16[4,176,352]{2,1,0:T(8,128)(2,1)S(1)}, bf16[4,176,352]{2,1,0:T(8,128)(2,1)S(1)}, u32[]{:S(2)}, u32[]{:S(2)}) collective-permute-start(bf16[4,176,352]{2,1,0:T(8,128)(2,1)S(1)} %fusion.115), channel_id=1, source_target_pairs={{8,0},{10,2},{12,4},{14,6},{16,24},{18,26},{20,28},{22,30},{9,1},{... | collective-permute-start | bytes 1486856 | tf_op jit(solution)/shard_map/ppermute | solution.py:317
  808.5 36.8 %collective-permute-start.60 = (bf16[256,1408]{0,1:T(8,128)(2,1)}, bf16[256,1408]{0,1:T(8,128)(2,1)S(1)}, u32[]{:S(2)}, u32[]{:S(2)}) collective-permute-start(bf16[256,1408]{0,1:T(8,128)(2,1)} %get-tuple-element.126), channel_id=1, source_target_pairs={{8,12},{10,14},{12,8},{14,10},{16,20},{18,22},{20,16},{22,18},{9,1... | collective-permute-start | bytes 2162696 | tf_op jit(solution)/shard_map/ppermute | solution.py:317
  823.3 29.9 %collective-permute-start.62 = (bf16[256,1408]{0,1:T(8,128)(2,1)S(1)}, bf16[256,1408]{0,1:T(8,128)(2,1)S(1)}, u32[]{:S(2)}, u32[]{:S(2)}) collective-permute-start(bf16[256,1408]{0,1:T(8,128)(2,1)S(1)} %get-tuple-element.130), channel_id=1, source_target_pairs={{8,16},{10,18},{12,20},{14,22},{16,8},{18,10},{20,12},{22,14},{9,1... | collective-permute-start | bytes 2162696 | tf_op jit(solution)/shard_map/ppermute | solution.py:317
  845.3 54.7 %collective-permute-start.42 = (bf16[512,1024]{1,0:T(8,128)(2,1)S(1)}, bf16[512,1024]{1,0:T(8,128)(2,1)S(1)}, u32[]{:S(2)}, u32[]{:S(2)}) collective-permute-start(bf16[512,1024]{1,0:T(8,128)(2,1)S(1)} %copy-done.48), channel_id=1, source_target_pairs={{0,1},{1,0},{2,3},{3,2},{4,5},{5,4},{6,7},{7,6},{8,9},{9,8},{10,11... | collective-permute-start | bytes 3145736 | tf_op jit(solution)/shard_map/ppermute | solution.py:328
  (165 other events, 2264.1 us)

commit v2 on v1

v2 whole, which is shorter than its diff:
```python
import functools

import jax
import jax.numpy as jnp
from jax import lax
from jax.experimental import pallas as pl
from jax.experimental.pallas import tpu as pltpu
from jax.sharding import PartitionSpec as P

norm_eps = 1e-06
root_eps = 0.001
bf16 = jnp.bfloat16
f32 = jnp.float32
contract_cols = (((1,), (1,)), ((), ()))
contract_rows = (((0,), (0,)), ((), ()))
gelu_scale = 0.7978845608028654
gelu_cubic = 0.044715
held_buffers = 4
scan_unroll = 8
blocks = 8
chunk_rows = 256
lanes = 128
by_mesh = pl.DeviceIdType.MESH


def pairs(n_dp, move):
    count = n_dp // 16
    found = []
    for i in range(n_dp):
        w, c, x, z = i % count, i // count % 2, i // count // 2 % 2, i // count // 4
        target = move(z, x, c)
        if target is not None:
            z, x, c = target
            found.append((i, ((z * 2 + x) * 2 + c) * count + w))
    return found


def gelu_parts(v):
    tanh_value = jnp.tanh(gelu_scale * (v + gelu_cubic * v * v * v))
    value = 0.5 * v * (1.0 + tanh_value)
    slope = 0.5 * (1.0 + tanh_value) + 0.5 * v * (1.0 - tanh_value * tanh_value) * (
        gelu_scale * (1.0 + 3.0 * gelu_cubic * v * v)
    )
    return value, slope


def shifted(value, offset):
    return pltpu.roll(value, offset % value.shape[0], 0)


def store_lanes(ref, at, value):
    chunks = ref.shape[0]
    spare = chunks * lanes - value.shape[1]
    if spare:
        value = jnp.concatenate([value, jnp.zeros((value.shape[0], spare), f32)], axis=1)
    for i in range(chunks):
        ref[i, at, :] = value[:, i * lanes : (i + 1) * lanes]


def load_lanes(ref, at, width):
    return jnp.concatenate([ref[i, at, :] for i in range(ref.shape[0])], axis=1)[:, :width]


def scan_rows(coef_ref, push_ref, rows, reverse):
    chunks = coef_ref.shape[0]

    def step(i, carried):
        carried = list(carried)
        for j in range(scan_unroll):
            t = i * scan_unroll + j
            at = pl.ds(rows - 1 - t if reverse else t, held_buffers, stride=rows)
            for k in range(chunks):
                if reverse:
                    value = push_ref[k, at, :] + carried[k]
                    carried[k] = coef_ref[k, at, :] * value
                else:
                    value = coef_ref[k, at, :] * carried[k] + push_ref[k, at, :]
                    carried[k] = value
                push_ref[k, at, :] = value
        return tuple(carried)

    start = tuple(jnp.zeros((held_buffers, lanes), f32) for _ in range(chunks))
    lax.fori_loop(0, rows // scan_unroll, step, start)


def columns_at(cols_ref, b, size):
    return pl.ds(pl.multiple_of(cols_ref[b], size), size)


def gathered(ref, at, cols_ref, size):
    return jnp.concatenate([ref[at, columns_at(cols_ref, b, size)] for b in range(blocks)], axis=1)


def stacked(refs, columns=slice(None)):
    return jnp.concatenate([ref[:, columns] for ref in refs], axis=0)


def project(mine_ref, theirs_ref, weight_refs, cols_ref, use):
    size = weight_refs[0].shape[0]
    own = mine_ref.shape[0]
    for part, ref in enumerate((mine_ref, theirs_ref)):

        def chunk(i, carry, part=part, ref=ref):
            at = pl.ds(pl.multiple_of(i * chunk_rows, chunk_rows), chunk_rows)
            rows = gathered(ref, at, cols_ref, size)
            use(
                pl.multiple_of(part * own + i * chunk_rows, chunk_rows),
                jnp.dot(rows, stacked(weight_refs), preferred_element_type=f32),
            )
            return carry

        lax.fori_loop(0, own // chunk_rows, chunk, 0)


def columns_at(cols, b, size):
    return pl.ds(pl.multiple_of(cols[b], size), size)


def gathered(ref, at, cols, size):
    return jnp.concatenate([ref[at, columns_at(cols, b, size)] for b in range(blocks)], axis=1)


def stacked(weight_ref):
    return weight_ref[...].reshape(-1, weight_ref.shape[2])


def project(mine_ref, theirs_ref, weight_ref, cols, use):
    size = weight_ref.shape[1]
    own = mine_ref.shape[0]
    for part, ref in enumerate((mine_ref, theirs_ref)):

        def chunk(i, carry, part=part, ref=ref):
            at = pl.ds(pl.multiple_of(i * chunk_rows, chunk_rows), chunk_rows)
            rows = gathered(ref, at, cols, size)
            use(
                pl.multiple_of(part * own + i * chunk_rows, chunk_rows),
                jnp.dot(rows, stacked(weight_ref), preferred_element_type=f32),
            )
            return carry

        lax.fori_loop(0, own // chunk_rows, chunk, 0)


def buffer_rows_at(b, rows):
    return pl.ds(pl.multiple_of(b * rows, rows), rows)


def conv_of(inner, mask, vec_ref):
    conv = vec_ref[4:5, :] + vec_ref[0:1, :] * inner
    for k in range(1, 4):
        conv = conv + vec_ref[k : k + 1, :] * (shifted(inner, k) * mask[:, k : k + 1])
    return conv


def gates_of(conv_low, vec_ref, wr_ref, wi_ref):
    rate = jax.nn.sigmoid(
        jnp.dot(conv_low, wr_ref[...], preferred_element_type=f32) + vec_ref[5:6, :]
    )
    igate = jax.nn.sigmoid(
        jnp.dot(conv_low, wi_ref[...], preferred_element_type=f32) + vec_ref[6:7, :]
    )
    return rate, igate


def recur_state(both_ref, mask_ref, vec_ref, wr_ref, wi_ref, coef_ref, push_ref):
    width = both_ref.shape[1] // 2
    rows = both_ref.shape[0] // held_buffers

    def gates(b, carry):
        at = buffer_rows_at(b, rows)
        mask = mask_ref[at, :]
        conv = conv_of(both_ref[at, :width], mask, vec_ref)
        rate, igate = gates_of(conv.astype(bf16), vec_ref, wr_ref, wi_ref)
        decay = jnp.exp(-8.0 * rate * vec_ref[7:8, :])
        root = jnp.sqrt(1.0 - decay * decay + root_eps)
        store_lanes(coef_ref, at, decay * mask[:, 0:1])
        store_lanes(push_ref, at, root * igate * conv)
        return carry

    lax.fori_loop(0, held_buffers, gates, 0)
    scan_rows(coef_ref, push_ref, rows, False)


def recur_mixed(both_ref, state_ref, mixed_ref):
    width = both_ref.shape[1] // 2
    rows = both_ref.shape[0] // held_buffers

    def mix(b, carry):
        at = buffer_rows_at(b, rows)
        gate = gelu_parts(both_ref[at, width:])[0]
        mixed_ref[at, :] = (load_lanes(state_ref, at, width) * gate).astype(bf16)
        return carry

    lax.fori_loop(0, held_buffers, mix, 0)


class Place:
    def __init__(self, count):
        self.me = lax.axis_index("dp")
        self.y = lax.axis_index("mp")
        self.c = self.me // count % 2
        self.x = self.me // (2 * count) % 2
        self.z = self.me // (4 * count)
        self.core = {"dp": self.me + (1 - 2 * self.c) * count}
        self.beside = {"dp": self.me + (1 - 2 * self.x) * 2 * count}
        self.over_y = {"mp": 1 - self.y}
        sign = 1 - 2 * (self.z // 2)
        self.ahead = {"dp": self.me + sign * 4 * count}
        self.behind = {"dp": self.me - sign * 4 * count}
        self.works = (self.z + 1) // 2 == 1
        self.serves = (self.z + 1) // 2 != 1

    def columns(self, size):
        outer = self.z // 2 * 3
        far, far_outer = 3 - self.z, 3 - outer
        return [
            ((at_z + 2 * self.y) % 4 * 2 + at_x) * size
            for at_z in (self.z, outer, far, far_outer)
            for at_x in (self.x, 1 - self.x)
        ]

    def meet(self):
        barrier = pltpu.get_barrier_semaphore()

        def greet(partners):
            for partner in partners:
                pl.semaphore_signal(barrier, inc=1, device_id=partner, device_id_type=by_mesh)
            pl.semaphore_wait(barrier, len(partners))

        @pl.when(self.works)
        def _():
            greet((self.core, self.beside, self.over_y, self.ahead, self.behind))

        @pl.when(self.serves)
        def _():
            greet((self.core, self.beside, self.ahead))


def remote(src, dst, send, recv, where):
    return pltpu.make_async_remote_copy(
        src_ref=src,
        dst_ref=dst,
        send_sem=send,
        recv_sem=recv,
        device_id=where,
        device_id_type=by_mesh,
    )


def normed_rows(source_ref, gain_ref, gain_row, scale_ref, scale_row, out_ref, first, count):
    size = 128

    def chunk(i, carry):
        at = pl.ds(pl.multiple_of(first + i * size, size), size)
        rows = source_ref[at, :].astype(f32)
        scale = lax.rsqrt(jnp.mean(rows * rows, axis=1, keepdims=True) + norm_eps)
        scale_ref[scale_row, at, :] = jnp.broadcast_to(scale, (size, lanes))
        out_ref[at, :] = (rows * scale * gain_ref[gain_row : gain_row + 1, :]).astype(bf16)
        return carry

    lax.fori_loop(0, count // size, chunk, 0)


def forward_kernel(
    count,
    keep_ri, keep_ro, keep_mi, keep_mo, give_ri, give_ro, give_mi, give_mo,
    tokens_ref, grad_ref, mask_in, gain_ref, vec_ref, wr_ref, wi_ref,
    g_ri, g_ro, g_mi, g_mo,
    both_ref, state_ref, mixed_ref, mask_ref, middle_ref, tok_ref,
    one_mine, one_theirs, two_mine, two_theirs, low_mine, low_theirs, scale_ref,
    coef_ref, w_ri, w_ro, grad_all, part_out, part_in, part_sum, y_out, y_in, mid_ref,
    w_send, w_recv, w_local, load_sem, m_send, m_recv, m_local,
):
    at = Place(count)
    half_rows = keep_ri.shape[0]
    size = 2 * half_rows
    model = tok_ref.shape[1]
    half_model = model // 2
    rows = tokens_ref.shape[0]
    own = 2 * rows
    cols = at.columns(size)
    whole, keeps, gives = (g_ri, g_ro, g_mi, g_mo), (keep_ri, keep_ro, keep_mi, keep_mo), (
        give_ri, give_ro, give_mi, give_mo,
    )
    ri, ro, mi, mo = range(4)
    top, bottom = pl.ds(0, half_rows), pl.ds(half_rows, half_rows)
    core_rows = pl.ds(pl.multiple_of(at.c * half_rows, half_rows), half_rows)

    def hop(w, k):
        g = whole[w]
        src, dst, where = (
            (gives[w], g.at[0, core_rows], at.core),
            (g.at[0], g.at[1], at.beside),
            (g.at[0], g.at[2], at.ahead),
            (g.at[1], g.at[3], at.ahead),
            (g.at[0], g.at[4], at.ahead),
            (g.at[4], g.at[5], at.beside),
            (g.at[2], g.at[6], at.ahead),
            (g.at[3, top], g.at[7, top], at.ahead),
            (g.at[6, bottom], g.at[7, bottom], at.beside),
        )[k]
        return remote(src, dst, w_send.at[w, k], w_recv.at[w, k], where)

    def kept(w):
        return pltpu.make_async_copy(keeps[w], whole[w].at[0, core_rows], w_local.at[w])

    def begin(w):
        kept(w).start()
        hop(w, 0).start()

    def own_block(w, hops):
        kept(w).wait()
        hop(w, 0).wait()
        for k in hops:
            hop(w, k).start()

    def pass_on(w, arrived, sent):
        hop(w, arrived).wait_recv()
        hop(w, sent).start()

    def move(k, src, dst, where):
        return remote(src, dst, m_send.at[k], m_recv.at[k], where)

    first, second = pl.ds(0, rows), pl.ds(rows, rows)
    left, right = pl.ds(0, half_model), pl.ds(half_model, half_model)
    mine_rows, their_rows = pl.ds(0, own), pl.ds(own, own)
    token_in = move(0, tokens_ref, tok_ref.at[second, left], at.ahead)
    token_y = move(1, tokens_ref, tok_ref.at[first, right], at.over_y)
    token_y_two = move(2, tok_ref.at[second, left], tok_ref.at[second, right], at.over_y)
    grad_in = move(3, grad_ref, grad_all.at[second, left], at.ahead)
    grad_y = move(4, grad_ref, grad_all.at[first, right], at.over_y)
    grad_y_two = move(5, grad_all.at[second, left], grad_all.at[second, right], at.over_y)
    mask_move = move(6, mask_in, mask_ref.at[second], at.ahead)
    mask_core = move(7, mask_ref.at[mine_rows], mask_ref.at[their_rows], at.core)
    one_core = move(8, one_mine, one_theirs, at.core)
    low_core = move(9, low_mine, low_theirs, at.core)
    halves = (first, second)
    part_core = [move(10 + i, part_out.at[h], part_in.at[h], at.core) for i, h in enumerate(halves)]
    part_y = [move(12 + i, y_out.at[h], y_in.at[h], at.over_y) for i, h in enumerate(halves)]
    mid_y = [
        move(14 + i, mid_ref.at[h, left], mid_ref.at[h, right], at.over_y)
        for i, h in enumerate(halves)
    ]
    two_core = [move(16 + i, two_mine.at[h], two_theirs.at[h], at.core) for i, h in enumerate(halves)]
    token_here = pltpu.make_async_copy(tokens_ref, tok_ref.at[first, left], m_local.at[0])
    grad_here = pltpu.make_async_copy(grad_ref, grad_all.at[first, left], m_local.at[1])
    mask_here = pltpu.make_async_copy(mask_in, mask_ref.at[first], m_local.at[2])

    def load(w, target, b):
        return pltpu.make_async_copy(whole[w].at[b], target.at[b], load_sem.at[w, b])

    at.meet()

    @pl.when(at.serves)
    def _():
        mask_move.start()
        token_in.start()
        for w in (ri, ro, mi, mo):
            begin(w)
        for w in (ri, ro):
            own_block(w, (1, 2))
        for w in (ri, ro):
            pass_on(w, 1, 3)
        grad_in.start()
        for w in (mi, mo):
            own_block(w, (1, 2))
        for w in (mi, mo):
            pass_on(w, 1, 3)
        for w in (ri, ro, mi, mo):
            for k in (1, 2, 3):
                hop(w, k).wait_send()
        for moved in (mask_move, token_in, grad_in):
            moved.wait_send()

    @pl.when(at.works)
    def _():
        token_here.start()
        mask_here.start()
        token_y.start()
        begin(ri)
        begin(ro)
        grad_here.start()
        begin(mi)
        begin(mo)
        own_block(ri, (1, 4))
        own_block(ro, (1, 4))
        mask_here.wait()
        mask_move.wait_recv()
        mask_core.start()
        token_in.wait_recv()
        token_y_two.start()
        pass_on(ri, 2, 6)
        pass_on(ri, 4, 5)
        token_here.wait()
        token_y.wait_recv()
        normed_rows(tok_ref, gain_ref, 0, scale_ref, 0, one_mine, 0, rows)
        token_y_two.wait_recv()
        normed_rows(tok_ref, gain_ref, 0, scale_ref, 0, one_mine, rows, rows)
        one_core.start()
        pass_on(ro, 2, 6)
        pass_on(ro, 4, 5)
        pass_on(ri, 3, 7)
        pass_on(ri, 6, 8)
        own_block(mi, (1, 4))
        pass_on(ro, 3, 7)
        pass_on(ro, 6, 8)
        grad_y.start()
        for w, target in ((ri, w_ri), (ro, w_ro)):
            hop(w, 1).wait_recv()
            for k in (5, 7, 8):
                hop(w, k).wait_recv()
            for b in range(blocks):
                load(w, target, b).start()
        for b in range(blocks):
            load(ri, w_ri, b).wait()
        one_core.wait_recv()
        mask_core.wait_recv()

        def keep_both(start, value):
            both_ref[pl.ds(start, chunk_rows), :] = value

        project(one_mine, one_theirs, w_ri, cols, keep_both)
        grad_in.wait_recv()
        grad_y_two.start()
        recur_state(both_ref, mask_ref, vec_ref, wr_ref, wi_ref, coef_ref, state_ref)
        pass_on(mi, 2, 6)
        pass_on(mi, 4, 5)
        own_block(mo, (1, 4))
        recur_mixed(both_ref, state_ref, mixed_ref)
        for b in range(blocks):
            load(ro, w_ro, b).wait()

        def branch(start, out_ref, out_at):
            for b in range(blocks):
                out_ref[out_at, columns_at(cols, b, size)] = lax.dot_general(
                    mixed_ref[pl.ds(start, rows), :],
                    w_ro[b],
                    contract_cols,
                    preferred_element_type=f32,
                ).astype(out_ref.dtype)

        for i, h in enumerate(halves):
            branch(own + i * rows, part_out, h)
            part_core[i].start()
        for i, h in enumerate(halves):
            branch(i * rows, part_sum, first)
            part_core[i].wait_recv()
            middle_ref[h, :] = part_sum[:, left] + part_in[h, left].astype(f32)
            y_out[h, :] = (part_sum[:, right] + part_in[h, right].astype(f32)).astype(bf16)
            part_y[i].start()
        pass_on(mi, 3, 7)
        grad_here.wait()
        grad_y.wait_recv()
        grad_y_two.wait_recv()
        low_mine[...] = (grad_all[...].astype(f32) * mask_ref[mine_rows, 4:5]).astype(bf16)
        low_core.start()
        for i, h in enumerate(halves):
            part_y[i].wait_recv()
            middle = middle_ref[h, :] + y_in[h, :].astype(f32) + tok_ref[h, left].astype(f32)
            middle_ref[h, :] = middle
            mid_ref[h, left] = middle.astype(bf16)
            mid_y[i].start()
        pass_on(mi, 6, 8)
        pass_on(mo, 2, 6)
        pass_on(mo, 4, 5)
        for i, h in enumerate(halves):
            mid_y[i].wait_recv()
            normed_rows(mid_ref, gain_ref, 1, scale_ref, 1, two_mine, i * rows, rows)
            two_core[i].start()
        pass_on(mo, 3, 7)
        pass_on(mo, 6, 8)
        for w in (mi, mo):
            for k in (1, 5, 7, 8):
                hop(w, k).wait_recv()
        low_core.wait_recv()
        for moved in two_core:
            moved.wait_recv()
        for w in (ri, ro, mi, mo):
            for k in (1, 4, 5, 6, 7, 8):
                hop(w, k).wait_send()
        for moved in (
            token_y, token_y_two, grad_y, grad_y_two, mask_core, one_core, low_core,
            *part_core, *part_y, *mid_y, *two_core,
        ):
            moved.wait_send()


def recur_backward(
    mine_ref, theirs_ref, weight_ref, cols_ref,
    both_ref, state_ref, mask_ref, vec_ref, wr_ref, wi_ref,
    dboth_ref, sums_ref, gr_ref, gi_ref,
    coef_ref, push_ref, dmix_ref,
):
    def keep_mixed(start, value):
        dmix_ref[pl.ds(start, chunk_rows), :] = value

    project(mine_ref, theirs_ref, weight_ref, cols_ref, keep_mixed)
    width = dmix_ref.shape[1]
    rows = both_ref.shape[0] // held_buffers

    def first(b, carry):
        at = buffer_rows_at(b, rows)
        gate, slope = gelu_parts(both_ref[at, width:])
        d_mixed = dmix_ref[at, :]
        mask = mask_ref[at, :]
        conv_low = conv_of(both_ref[at, :width], mask, vec_ref).astype(bf16)
        rate = gates_of(conv_low, vec_ref, wr_ref, wi_ref)[0]
        store_lanes(push_ref, at, d_mixed * gate)
        dboth_ref[at, width:] = (slope * d_mixed * load_lanes(state_ref, at, width)).astype(bf16)
        store_lanes(coef_ref, at, jnp.exp(-8.0 * rate * vec_ref[7:8, :]) * mask[:, 0:1])
        return carry

    lax.fori_loop(0, held_buffers, first, 0)

    scan_rows(coef_ref, push_ref, rows, True)
    sums_ref[...] = jnp.zeros_like(sums_ref)
    gr_ref[...] = jnp.zeros_like(gr_ref)
    gi_ref[...] = jnp.zeros_like(gi_ref)

    def add_sum(k, value):
        sums_ref[k : k + 1, :] += jnp.sum(value, axis=0, keepdims=True)

    def last(b, carry):
        at = buffer_rows_at(b, rows)
        inner = both_ref[at, :width]
        mask = mask_ref[at, :]
        keep = mask[:, 0:1]
        softened = vec_ref[7:8, :]
        conv = conv_of(inner, mask, vec_ref)
        conv_low = conv.astype(bf16)
        rate, igate = gates_of(conv_low, vec_ref, wr_ref, wi_ref)
        d_push = load_lanes(push_ref, at, width)
        decay = jnp.exp(-8.0 * rate * softened)
        square = 1.0 - decay * decay + root_eps
        root = jnp.sqrt(square)
        d_root = d_push * igate * conv
        d_igate = d_push * root * conv
        before = shifted(load_lanes(state_ref, at, width), 1) * keep
        d_decay = d_push * before - d_root * decay / root
        d_log = d_decay * decay
        slow = d_log * rate
        d_pre_recur = (-8.0 * softened) * slow * (1.0 - rate)
        d_pre_input = d_igate * igate * (1.0 - igate)
        add_sum(7, slow)
        add_sum(5, d_pre_recur)
        add_sum(6, d_pre_input)
        low_recur = d_pre_recur.astype(bf16)
        low_input = d_pre_input.astype(bf16)
        gr_ref[...] += lax.dot_general(
            conv_low, low_recur, contract_rows, preferred_element_type=f32
        )
        gi_ref[...] += lax.dot_general(
            conv_low, low_input, contract_rows, preferred_element_type=f32
        )
        d_conv = d_push * root * igate
        d_conv = d_conv + lax.dot_general(
            low_recur, wr_ref[...], contract_cols, preferred_element_type=f32
        )
        d_conv = d_conv + lax.dot_general(
            low_input, wi_ref[...], contract_cols, preferred_element_type=f32
        )
        add_sum(4, d_conv)
        add_sum(0, d_conv * inner)
        d_inner = vec_ref[0:1, :] * d_conv
        for k in range(1, 4):
            kept = d_conv * mask[:, k : k + 1]
            add_sum(k, kept * shifted(inner, k))
            d_inner = d_inner + vec_ref[k : k + 1, :] * shifted(kept, -k)
        dboth_ref[at, :width] = d_inner.astype(bf16)
        return carry

    lax.fori_loop(0, held_buffers, last, 0)


def mlp_forward(mine_ref, theirs_ref, gate_weight, up_weight, cols_ref, act_ref, slope_ref, value_ref):
    size = gate_weight.shape[1]
    own = mine_ref.shape[0]
    for part, ref in enumerate((mine_ref, theirs_ref)):

        def chunk(i, carry, part=part, ref=ref):
            rows = gathered(
                ref, pl.ds(pl.multiple_of(i * chunk_rows, chunk_rows), chunk_rows), cols_ref, size
            )
            gate = jnp.dot(rows, stacked(gate_weight), preferred_element_type=f32)
            up = jnp.dot(rows, stacked(up_weight), preferred_element_type=f32)
            value, slope = gelu_parts(gate)
            at = pl.ds(pl.multiple_of(part * own + i * chunk_rows, chunk_rows), chunk_rows)
            act_ref[at, :] = (value * up).astype(bf16)
            slope_ref[at, :] = (slope * up).astype(bf16)
            value_ref[at, :] = value.astype(bf16)
            return carry

        lax.fori_loop(0, own // chunk_rows, chunk, 0)


def mlp_backward(mine_ref, theirs_ref, weight_ref, cols_ref, slope_ref, value_ref, d_gate_ref, d_up_ref):
    def use(start, d_act):
        at = pl.ds(start, chunk_rows)
        d_gate_ref[at, :] = (d_act * slope_ref[at, :].astype(f32)).astype(bf16)
        d_up_ref[at, :] = (d_act * value_ref[at, :].astype(f32)).astype(bf16)

    project(mine_ref, theirs_ref, weight_ref, cols_ref, use)


def rows_back(part_tiles, *refs):
    count = len(part_tiles)
    row_refs, (weight_ref, cols_ref, out_ref, total_ref) = refs[:count], refs[count:]
    size = weight_ref.shape[1]
    step = pl.program_id(0)

    @pl.when(step == 0)
    def _():
        total_ref[...] = jnp.zeros_like(total_ref)

    first = 0
    for tiles, row_ref in zip(part_tiles, row_refs):

        @pl.when((step >= first) & (step < first + tiles))
        def _(row_ref=row_ref):
            for b in range(blocks):
                total_ref[:, columns_at(cols_ref, b, size)] += lax.dot_general(
                    row_ref[...], weight_ref[b], contract_cols, preferred_element_type=f32
                )

        first += tiles

    @pl.when(step == first - 1)
    def _():
        out_ref[...] = total_ref[...].astype(out_ref.dtype)


def weight_partial(part_tiles, mine_ref, theirs_ref, cols_ref, *refs):
    count = len(part_tiles)
    column_refs, out_ref = refs[:count], refs[count]
    size = out_ref.shape[1]
    own = mine_ref.shape[0]
    step = pl.program_id(0)
    first = 0
    for tiles, column_ref in zip(part_tiles, column_refs):

        @pl.when((step >= first) & (step < first + tiles))
        def _(column_ref=column_ref):
            for b in range(blocks):
                at = columns_at(cols_ref, b, size)
                total = lax.dot_general(
                    mine_ref[:, at], column_ref[:own, :], contract_rows, preferred_element_type=f32
                )
                total = total + lax.dot_general(
                    theirs_ref[:, at], column_ref[own:, :], contract_rows, preferred_element_type=f32
                )
                out_ref[b] = total.astype(bf16)

        first += tiles


in_vmem = pl.BlockSpec(memory_space=pltpu.VMEM)
in_smem = pl.BlockSpec(memory_space=pltpu.SMEM)
in_any = pl.BlockSpec(memory_space=pl.ANY)
no_cost = pl.CostEstimate(flops=0, bytes_accessed=0, transcendentals=0)
kernel_params = pltpu.CompilerParams(vmem_limit_bytes=60 * 2**20)
copy_sem = pltpu.SemaphoreType.DMA


def lane_shape(rows, width):
    return (pl.cdiv(width, lanes), rows, lanes)


def run_forward(count, keeps, gives, tokens, out_grad, mask, gains, vectors, wr, wi):
    rows, half_model = tokens.shape
    own, model, width = 2 * rows, 2 * half_model, wr.shape[0]
    size = 2 * keeps[0].shape[0]
    shape = jax.ShapeDtypeStruct
    gathered_shapes = [shape((blocks, size, v.shape[1]), bf16) for v in keeps]
    wide = shape((own, model), bf16)
    return pl.pallas_call(
        functools.partial(forward_kernel, count),
        out_shape=(
            *gathered_shapes,
            shape((2 * own, 2 * width), f32),
            shape(lane_shape(2 * own, width), f32),
            shape((2 * own, width), bf16),
            shape((2 * own, lanes), f32),
            shape((own, half_model), f32),
            *[wide] * 7,
            shape((2, own, lanes), f32),
        ),
        in_specs=[in_any] * 11 + [in_vmem] * 4,
        out_specs=[in_any] * 4 + [in_vmem] * 13,
        scratch_shapes=[
            pltpu.VMEM(lane_shape(2 * own, width), f32),
            pltpu.VMEM((blocks, size, 2 * width), bf16),
            pltpu.VMEM((blocks, size, width), bf16),
            pltpu.VMEM((own, model), bf16),
            pltpu.VMEM((own, model), bf16),
            pltpu.VMEM((own, model), bf16),
            pltpu.VMEM((rows, model), f32),
            pltpu.VMEM((own, half_model), bf16),
            pltpu.VMEM((own, half_model), bf16),
            pltpu.VMEM((own, model), bf16),
            copy_sem((4, 9)),
            copy_sem((4, 9)),
            copy_sem((4,)),
            copy_sem((2, blocks)),
            copy_sem((18,)),
            copy_sem((18,)),
            copy_sem((3,)),
        ],
        compiler_params=pltpu.CompilerParams(
            vmem_limit_bytes=60 * 2**20, collective_id=0, has_side_effects=True
        ),
        cost_estimate=no_cost,
        name="gather_and_recur",
    )(*keeps, *gives, tokens, out_grad, mask, gains, vectors, wr, wi)


def run_recur_backward(d_branch, weight, cols, both, state, mask, vectors, wr, wi):
    rows, width = both.shape[0], wr.shape[0]
    square = jax.ShapeDtypeStruct((width, width), f32)
    return pl.pallas_call(
        recur_backward,
        out_shape=(
            jax.ShapeDtypeStruct((rows, 2 * width), bf16),
            jax.ShapeDtypeStruct((8, width), f32),
            square,
            square,
        ),
        in_specs=[in_vmem] * 3 + [in_smem] + [in_vmem] * 6,
        out_specs=[in_vmem] * 4,
        scratch_shapes=[pltpu.VMEM(lane_shape(rows, width), f32)] * 2
        + [pltpu.VMEM((rows, width), f32)],
        compiler_params=kernel_params,
        cost_estimate=no_cost,
        name="recur_backward",
    )(*d_branch, weight, cols, both, state, mask, vectors, wr, wi)


def run_mlp_forward(normed, weight, cols):
    own, model = normed[0].shape
    size, hidden = weight.shape[1], weight.shape[2] // 2
    tile = 256
    tiles = hidden // tile
    out = jax.ShapeDtypeStruct((2 * own, hidden), bf16)
    return pl.pallas_call(
        mlp_forward,
        grid=(tiles,),
        out_shape=(out, out, out),
        in_specs=[pl.BlockSpec((own, model), lambda n: (0, 0))] * 2
        + [pl.BlockSpec((blocks, size, tile), lambda n: (0, 0, n))]
        + [pl.BlockSpec((blocks, size, tile), lambda n: (0, 0, n + tiles))]
        + [in_smem],
        out_specs=[pl.BlockSpec((2 * own, tile), lambda n: (0, n))] * 3,
        compiler_params=kernel_params,
        cost_estimate=no_cost,
        name="mlp_forward",
    )(*normed, weight, weight, cols)


def run_mlp_backward(grad_low, weight, cols, slope, value):
    own, model = grad_low[0].shape
    size, hidden = weight.shape[1:]
    tile = 256
    out = jax.ShapeDtypeStruct((2 * own, hidden), bf16)
    column = pl.BlockSpec((2 * own, tile), lambda n: (0, n))
    return pl.pallas_call(
        mlp_backward,
        grid=(hidden // tile,),
        out_shape=(out, out),
        in_specs=[pl.BlockSpec((own, model), lambda n: (0, 0))] * 2
        + [pl.BlockSpec((blocks, size, tile), lambda n: (0, 0, n))]
        + [in_smem, column, column],
        out_specs=[column, column],
        compiler_params=kernel_params,
        cost_estimate=no_cost,
        name="mlp_backward",
    )(*grad_low, weight, cols, slope, value)


def tile_of(width):
    return 512 if width % 512 == 0 else width


def part_specs(parts, rows, row_block, tile):
    specs, tiles, first = [], [], 0
    for part in parts:
        count = part.shape[1] // tile

        def index(n, first=first, count=count):
            return (row_block, jnp.clip(n - first, 0, count - 1))

        specs.append(pl.BlockSpec((rows, tile), index))
        tiles.append(count)
        first += count
    return specs, tuple(tiles)


def run_rows_back(name, parts, weight, cols, row_block, dtype):
    own = parts[0].shape[0] // 2
    size = weight.shape[1]
    tile = tile_of(parts[0].shape[1])
    specs, tiles = part_specs(parts, own, row_block, tile)
    return pl.pallas_call(
        functools.partial(rows_back, tiles),
        grid=(sum(tiles),),
        out_shape=jax.ShapeDtypeStruct((own, size * blocks), dtype),
        in_specs=specs
        + [pl.BlockSpec((blocks, size, tile), lambda n: (0, 0, n)), in_smem],
        out_specs=pl.BlockSpec((own, size * blocks), lambda n: (0, 0)),
        scratch_shapes=[pltpu.VMEM((own, size * blocks), f32)],
        compiler_params=kernel_params,
        cost_estimate=no_cost,
        name=name,
    )(*parts, weight, cols)


def run_weight_partial(name, rows, parts, cols):
    own, model = rows[0].shape
    size = model // blocks
    tile = tile_of(parts[0].shape[1])
    specs, tiles = part_specs(parts, 2 * own, 0, tile)
    return pl.pallas_call(
        functools.partial(weight_partial, tiles),
        grid=(sum(tiles),),
        out_shape=jax.ShapeDtypeStruct((blocks, size, sum(tiles) * tile), bf16),
        in_specs=[pl.BlockSpec((own, model), lambda n: (0, 0))] * 2 + [in_smem] + specs,
        out_specs=pl.BlockSpec((blocks, size, tile), lambda n: (0, 0, n)),
        compiler_params=kernel_params,
        cost_estimate=no_cost,
        name=name,
    )(*rows, cols, *parts)


def block_diagonal(blocks):
    count, size = blocks.shape[0], blocks.shape[1]
    rows = [
        jnp.pad(blocks[h], ((0, 0), (h * size, (count - 1 - h) * size))) for h in range(count)
    ]
    return jnp.concatenate(rows, axis=0)


def diagonal_blocks(square, count):
    size = square.shape[0] // count
    return jnp.stack(
        [square[h * size : (h + 1) * size, h * size : (h + 1) * size] for h in range(count)]
    )


def masks_of(lengths, rows):
    ends = jnp.cumsum(lengths, axis=1)
    starts = ends - lengths
    places = jnp.arange(rows, dtype=jnp.int32)[None, :, None]
    inside = (places >= starts[:, None, :]) & (places < ends[:, None, :])
    first_place = jnp.sum(jnp.where(inside, starts[:, None, :], 0), axis=2)
    places = places[:, :, 0]
    live = (places < ends[:, 2:3]).astype(f32)
    columns = [(places != first_place).astype(f32)]
    for k in range(1, 4):
        columns.append((places - k >= first_place).astype(f32))
    columns += [live] + [jnp.zeros_like(live)] * 3
    return jnp.stack(columns, axis=2).reshape(lengths.shape[0] * rows, 8), live


def local(
    n_dp,
    tokens,
    gain_rnn,
    rnn_in,
    gate_recur,
    gate_input,
    bias_recur,
    bias_input,
    decay_param,
    conv_weight,
    conv_bias,
    rnn_out,
    gain_mlp,
    mlp_in,
    mlp_out,
    lengths,
    out_grad,
):
    outer_count = n_dp // 16
    rows_here = rnn_in.shape[0]
    model = gain_rnn.shape[0]
    half_model = model // 2
    buffer_rows = tokens.shape[0]
    own_rows = 2 * buffer_rows
    index = lax.axis_index("dp")
    y = lax.axis_index("mp")
    c = index // outer_count % 2
    x = index // (2 * outer_count) % 2
    z = index // (4 * outer_count)
    outer = jnp.where(z < 2, 0, 3)
    far = 3 - z
    far_outer = 3 - outer
    worker = (z == 1) | (z == 2)

    def mover(move):
        table = pairs(n_dp, move)
        return lambda value: lax.ppermute(value, "dp", table)

    swap_c = mover(lambda z, x, c: (z, x, 1 - c))
    swap_x = mover(lambda z, x, c: (z, 1 - x, c))
    swap_x_work = mover(lambda z, x, c: (z, 1 - x, c) if z in (1, 2) else None)
    swap_x_ends = mover(lambda z, x, c: (z, 1 - x, c) if z in (0, 3) else None)
    inward = mover(lambda z, x, c: {0: (1, x, c), 3: (2, x, c)}.get(z))
    outward = mover(lambda z, x, c: {1: (0, x, c), 2: (3, x, c)}.get(z))
    across = mover(lambda z, x, c: {1: (2, x, c), 2: (1, x, c)}.get(z))

    def swap_y(value):
        return lax.ppermute(value, "mp", [(0, 1), (1, 0)])

    def pick_c(first, second):
        return jnp.where(c == 0, first, second)

    def pick_y(first, second):
        return jnp.where(y == 0, first, second)

    group_rows = outer_count * rows_here
    block_rows = 2 * group_rows

    outer_groups = [[i * outer_count + w for w in range(outer_count)] for i in range(16)]

    def over_outer(value):
        if outer_count == 1:
            return value
        return lax.all_gather(value, "dp", axis_index_groups=outer_groups, axis=0, tiled=True)

    cols = jnp.stack(
        [
            ((at_z + 2 * y) % 4 * 2 + at_x) * block_rows
            for at_z in (z, outer, far, far_outer)
            for at_x in (x, 1 - x)
        ]
    ).astype(jnp.int32)

    def added(*values):
        return sum(v.astype(f32) for v in values).astype(bf16)

    def scatter_grad(pieces, by_x):
        own, own_x, near, near_x, across_one, across_x, across_near, across_near_x = pieces
        if by_x:
            across_near = added(across_near, swap_x_work(across_near_x))
            across_one = added(across_one, swap_x_work(across_x))
        else:
            near_x = added(near_x, across(across_near_x))
            across_one = added(across_one, swap_x_work(across_x))
        near = added(near, across(across_near))
        out_other = outward(near_x)
        own_sum = swap_x_work(own_x)
        far_sum = across(across_one)
        out_near = outward(near)
        worker_total = own.astype(f32) + own_sum.astype(f32) + far_sum.astype(f32)
        end_total = out_near.astype(f32) + swap_x_ends(out_other).astype(f32)
        total = jnp.where(worker, worker_total, end_total).astype(bf16)
        top, bottom = total[:group_rows], total[group_rows:]
        mine = pick_c(top, bottom)
        arrived = swap_c(pick_c(bottom, top))
        first, second = pick_c(mine, arrived).astype(f32), pick_c(arrived, mine).astype(f32)
        if outer_count > 1:
            first, second = (
                lax.psum_scatter(
                    v, "dp", axis_index_groups=outer_groups, scatter_dimension=0, tiled=True
                )
                for v in (first, second)
            )
        return first, second

    def whole_features(half_rows):
        return jnp.concatenate([half_rows, swap_y(half_rows)], axis=1)

    def both_cores(rows_value):
        return rows_value, swap_c(rows_value)

    def sum_partials(name, parts, weight):
        theirs = swap_c(run_rows_back(name + "_theirs", parts, weight, cols, 1, bf16))
        mine = run_rows_back(name + "_mine", parts, weight, cols, 0, f32) + theirs.astype(f32)
        arrived = swap_y(mine[:, half_model:].astype(bf16))
        return mine[:, :half_model] + arrived.astype(f32)

    def relative(vector):
        first, second = vector[:half_model], vector[half_model:]
        return jnp.concatenate([pick_y(first, second), pick_y(second, first)])

    def norm_back(source, scale_rows, gain, grad_rows):
        weighted = grad_rows * gain
        part = jnp.sum(weighted * source, axis=1, keepdims=True)
        inner_mean = (part + swap_y(part)) / model
        back_rows = scale_rows * weighted - source * (scale_rows * scale_rows * scale_rows) * inner_mean
        return back_rows, jnp.sum(grad_rows * source * scale_rows, axis=0)

    def quarters(value, axis):
        size = value.shape[axis] // 2
        return (
            lax.slice_in_dim(value, 0, size, axis=axis),
            lax.slice_in_dim(value, size, 2 * size, axis=axis),
        )

    def pair_quarters(weight):
        first, second = quarters(weight, 2)
        return tuple(jnp.concatenate([v[:, 0], v[:, 1]], axis=1) for v in (first, second))

    def quarter(value, axis=0):
        return pick_c(*quarters(value, axis))

    gain_one, gain_two = relative(gain_rnn.astype(f32)), relative(gain_mlp.astype(f32))
    mask, _ = masks_of(lengths, buffer_rows)
    mask = jnp.pad(mask, ((0, 0), (0, lanes - mask.shape[1])))
    softened = jax.nn.softplus(-quarter(decay_param))
    vectors = jnp.concatenate(
        [
            quarter(conv_weight, 1),
            jnp.stack([quarter(conv_bias), quarter(bias_recur), quarter(bias_input), softened]),
        ],
        axis=0,
    )
    heads = gate_recur.shape[0] // 2
    wr = block_diagonal(quarter(gate_recur))
    wi = block_diagonal(quarter(gate_input))
    split = (
        pair_quarters(rnn_in),
        quarters(rnn_out, 1),
        pair_quarters(mlp_in),
        quarters(mlp_out, 1),
    )
    split = [(over_outer(first), over_outer(second)) for first, second in split]
    keeps = [pick_c(first, second) for first, second in split]
    gives = [pick_c(second, first) for first, second in split]
    gains = jnp.stack([gain_one, gain_two])
    (
        rnn_in_all, rnn_out_all, mlp_in_all, mlp_out_all,
        both, state, mixed, mask, middle, tokens_all,
        *rows_kept, scales,
    ) = run_forward(outer_count, keeps, gives, tokens, out_grad, mask, gains, vectors, wr, wi)
    normed, normed_two, grad_low = rows_kept[0:2], rows_kept[2:4], rows_kept[4:6]
    scale_one, scale_two = scales[0, :, :1], scales[1, :, :1]
    tokens_two = tokens_all[:, :half_model]
    live = mask[:own_rows, 4:5]
    live_grad = grad_low[0][:, :half_model].astype(f32)
    middle_low = middle.astype(bf16)

    act, gate_slope, gate_value = run_mlp_forward(normed_two, mlp_in_all, cols)
    mlp_out_grad = scatter_grad(
        run_weight_partial("mlp_out_partial", grad_low, (act,), cols), True
    )
    d_pair = run_mlp_backward(grad_low, mlp_out_all, cols, gate_slope, gate_value)
    e_two = sum_partials("mlp_in_back", d_pair, mlp_in_all)
    mlp_in_grad = scatter_grad(
        run_weight_partial("mlp_in_partial", normed_two, d_pair, cols), False
    )
    back_two, gain_two_term = norm_back(
        middle_low.astype(f32), scale_two, gain_two[:half_model], e_two
    )
    d_middle = live_grad + back_two
    d_branch = both_cores(whole_features(d_middle.astype(bf16)))
    rnn_out_grad = scatter_grad(
        run_weight_partial("rnn_out_partial", d_branch, (mixed,), cols), True
    )
    branch_two = sum_partials("mlp_out", (act,), mlp_out_all)
    output_two = (live * (middle + branch_two)).astype(bf16)

    d_both, sums, square_recur, square_input = run_recur_backward(
        d_branch, rnn_out_all, cols, both, state, mask, vectors, wr, wi
    )
    rnn_in_grad = scatter_grad(run_weight_partial("rnn_in_partial", normed, (d_both,), cols), True)
    e_one = sum_partials("rnn_in_back", (d_both,), rnn_in_all)
    back_one, gain_one_term = norm_back(
        tokens_two.astype(f32), scale_one, gain_one[:half_model], e_one
    )
    tokens_grad_two = (d_middle + back_one).astype(bf16)

    def settle(two):
        return jnp.where(worker, two[:buffer_rows], outward(two[buffer_rows:]))

    layer_output = settle(output_two)
    tokens_grad = settle(tokens_grad_two)

    def total(value, dtype=f32):
        value = jnp.where(worker, value, 0).astype(dtype)
        if outer_count > 1:
            value = lax.psum(value, "dp", axis_index_groups=outer_groups)
        value = value + swap_x(value)
        value = value + across(value)
        return jnp.where(worker, value, outward(value))

    def both_quarters(value, axis=0):
        arrived = swap_c(value)
        return pick_c(
            jnp.concatenate([value, arrived], axis=axis), jnp.concatenate([arrived, value], axis=axis)
        )

    sums = both_quarters(total(sums), 1)
    gate_grads = jnp.concatenate(
        [diagonal_blocks(square_recur, heads), diagonal_blocks(square_input, heads)], axis=2
    )
    gate_grads = both_quarters(total(gate_grads, bf16)).astype(f32)
    gains = total(jnp.stack([gain_one_term, gain_two_term]))
    gains = gains + swap_c(gains)
    size = gate_recur.shape[1]

    def pair_layout(halves):
        columns = halves[0].shape[1] // 2
        return jnp.stack(
            [
                jnp.concatenate([v[:, k * columns : (k + 1) * columns] for v in halves], axis=1)
                for k in range(2)
            ],
            axis=1,
        )

    return (
        layer_output,
        tokens_grad,
        gains[0],
        pair_layout(rnn_in_grad),
        gate_grads[:, :, :size],
        gate_grads[:, :, size:],
        sums[5],
        sums[6],
        8.0 * jax.nn.sigmoid(-decay_param) * sums[7],
        sums[:4],
        sums[4],
        jnp.concatenate(rnn_out_grad, axis=1),
        gains[1],
        pair_layout(mlp_in_grad),
        jnp.concatenate(mlp_out_grad, axis=1),
    )


def solution(mesh):
    return jax.shard_map(
        functools.partial(local, mesh.shape["dp"]),
        mesh=mesh,
        in_specs=(
            P("dp", "mp"),
            P(),
            P("dp", None, "mp"),
            P("mp", None, None),
            P("mp", None, None),
            P("mp"),
            P("mp"),
            P("mp"),
            P(None, "mp"),
            P("mp"),
            P("dp", "mp"),
            P(),
            P("dp", None, "mp"),
            P("dp", "mp"),
            P("dp", None),
            P("dp", "mp"),
        ),
        out_specs=(
            P("dp", "mp"),
            P("dp", "mp"),
            P("mp"),
            P("dp", None, "mp"),
            P("mp", None, None),
            P("mp", None, None),
            P("mp"),
            P("mp"),
            P("mp"),
            P(None, "mp"),
            P("mp"),
            P("dp", "mp"),
            P("mp"),
            P("dp", None, "mp"),
            P("dp", "mp"),
        ),
        check_vma=False,
    )
```

time: 942 us -> 845 us (0.90)
  Pallas kernels: 57.7 us -> 395 us
  matrix products: 151 us -> 0 us
  waiting for transfers between devices: 416 us -> 275 us
  starting transfers between devices: 165 us -> 65.3 us
  local copies, waits for them, and re-layouts: 80.4 us -> 50.6 us
  other arithmetic: 60.5 us -> 50.6 us
    pallas_call x1 -> x13, Pallas kernels: 22.1 us -> 351 us  [the longest x1 197 us: run_forward(): pl.pallas_call(functools.partial(forward_kernel, count), out_shape=(*gath...]
    ppermute x94 -> x54, waiting for transfers between devices: 383 us -> 210 us  [mover(): return lambda value: lax.ppermute(value, 'dp', table)]
    dot_general x16 -> x0, matrix products: 151 us -> none  [the longest x1 23.9 us: local(): d_act = jnp.dot(grad_low, mlp_out_all, preferred_element_type=f32)]
    ppermute x94 -> x54, starting transfers between devices: 155 us -> 56 us  [mover(): return lambda value: lax.ppermute(value, 'dp', table)]
    ppermute x10 -> x6, waiting for transfers between devices: 32.8 us -> 64.8 us  [swap_y(): return lax.ppermute(value, 'mp', [(0, 1), (1, 0)])]
    another operation x0 -> x5, local copies, waits for them, and re-layouts: none -> 15.1 us  [the longest x4 14.5 us: scatter_grad(): own, own_x, near, near_x, across_one, across_x, across_near, across_near_...]
    dynamic_update_slice x28 -> x0, local copies, waits for them, and re-layouts: 13.3 us -> none  [gather_weight(): whole = lax.dynamic_update_slice(whole, piece, (offset_of(z_at, x_at), 0))]
    broadcast_in_dim x4 -> x0, local copies, waits for them, and re-layouts: 10.5 us -> none  [gather_weight(): whole = jnp.zeros((model, own.shape[1]), bf16)]
  transfers between devices with their start and end apart: 104 -> 60, of which waited for: 34 -> 26; matrix products, arithmetic and copies ran while one was open for 25% -> 7% of each run, Pallas kernels for 2% -> 13%
where the time goes in v2:
time: 845 us; the launch traced here: 838 us
  Pallas kernels  395 us (47%)
  waiting for transfers between devices  275 us (33%)
  starting transfers between devices  65.3 us (8%)
  local copies, waits for them, and re-layouts  50.6 us (6%)
  other arithmetic  50.6 us (6%)
    ppermute x54, waiting for transfers between devices, mover(): return lambda value: lax.ppermute(value, 'dp', table)  210 us
    pallas_call x1, Pallas kernels, run_forward(): pl.pallas_call(functools.partial(forward_kernel, count), out_shape=(*gath...  197 us
    ppermute x6, waiting for transfers between devices, swap_y(): return lax.ppermute(value, 'mp', [(0, 1), (1, 0)])  64.8 us
    pallas_call x6, Pallas kernels, run_rows_back(): pl.pallas_call(functools.partial(rows_back, tiles), grid=(sum(tiles),), o...  63.5 us
    ppermute x54, starting transfers between devices, mover(): return lambda value: lax.ppermute(value, 'dp', table)  56 us
    pallas_call x4, Pallas kernels, run_weight_partial(): pl.pallas_call(functools.partial(weight_partial, tiles), grid=(sum(tiles)...  50.9 us
    pallas_call x1, Pallas kernels, run_recur_backward(): pl.pallas_call(recur_backward, out_shape=(jax.ShapeDtypeStruct((rows, 2 *...  43.2 us
    pallas_call x1, Pallas kernels, run_mlp_forward(): pl.pallas_call(mlp_forward, grid=(tiles,), out_shape=(out, out, out), in_...  24.9 us
  transfers between devices with their start and end apart: 60, of which 26 were waited for; matrix products, arithmetic and copies ran while one was open for 7% of the time, Pallas kernels for 13%

profile of v2, /device:TPU:0, one launch (start us, length us, event | category | flops | bytes accessed | tf_op | source)
XLA Modules:
  0.0 838.0 jit_solution(4685355310551820648)
XLA Ops:
  2.8 4.4 fusion.67
  7.2 3.1 fusion.64
  30.8 196.7 %gather_and_recur.1 = (bf16[8,256,1408]{2,1,0:T(8,128)(2,1)}, bf16[8,256,704]{2,1,0:T(8,128)(2,1)}, bf16[8,256,3072]{2,1,0:T(8,128)(2,1)}, bf16[8,256,1536]{2,1,...) custom-call(bf16[128,1408]{1,0:T(8,128)(2,1)} %get-tuple-element.194, ...), custom_call_target="tpu_custom_call" | custom-call | tf_op jit(solution)/shard_map/gather_and_recur/pallas_call | solution.py:675
  227.5 24.9 %mlp_forward.1 = (bf16[1024,1536]{1,0:T(8,128)(2,1)}, bf16[1024,1536]{1,0:T(8,128)(2,1)}, bf16[1024,1536]{1,0:T(8,128)(2,1)}) custom-call(bf16[512,2048]{1,0:T(8,128)(2,1)} %get-tuple-element.43.mine_ref, bf16[512,2048]{1,0:T(8,128)(2,1)} %get-tuple-element.44.theirs_ref, bf16[8,256,3072]{2,1,0:T(8,128)(2,1)} %get-tuple-element.45.gate_weight.up_weight.refs_2_, ...), custom_call_target="tpu_custom_call" | custom-call | tf_op jit(solution)/shard_map/mlp_forward/pallas_call | solution.py:743
  252.4 11.3 %mlp_out_partial.1 = bf16[8,256,1536]{2,1,0:T(8,128)(2,1)} custom-call(bf16[512,2048]{1,0:T(8,128)(2,1)} %get-tuple-element.48.mine_ref, bf16[512,2048]{1,0:T(8,128)(2,1)} %get-tuple-element.50.theirs_ref, s32[8]{0:T(128)} %stack.133.cols_ref.refs_2_.refs_3_, bf16[1024,1536]{1,0:T(8,128)(2,1)} %get-tuple-element.46.refs_0_), custom_call_target="tpu_custom_call" | custom-call | tf_op jit(solution)/shard_map/mlp_out_partial/pallas_call | solution.py:820
  263.7 2.9 slice_bitcast_fusion.14
  269.0 15.4 %mlp_backward.1 = (bf16[1024,1536]{1,0:T(8,128)(2,1)}, bf16[1024,1536]{1,0:T(8,128)(2,1)}) custom-call(bf16[512,2048]{1,0:T(8,128)(2,1)} %get-tuple-element.48.mine_ref, bf16[512,2048]{1,0:T(8,128)(2,1)} %get-tuple-element.50.theirs_ref, bf16[8,256,1536]{2,1,0:T(8,128)(2,1)} %get-tuple-element.47.refs_1_.weight_ref, s32[8]{0:T(128)} %stack.133.cols_ref.refs_2_.refs_3_, ...), custom_call_target="tpu_custom_call" | custom-call | tf_op jit(solution)/shard_map/mlp_backward/pallas_call | solution.py:764
  284.3 19.3 %mlp_in_partial.1 = bf16[8,256,3072]{2,1,0:T(8,128)(2,1)} custom-call(bf16[512,2048]{1,0:T(8,128)(2,1)} %get-tuple-element.43.mine_ref, bf16[512,2048]{1,0:T(8,128)(2,1)} %get-tuple-element.44.theirs_ref, s32[8]{0:T(128)} %stack.133.cols_ref.refs_2_.refs_3_, bf16[1024,1536]{1,0:T(8,128)(2,1)} %get-tuple-element.53.refs_0_, ...), custom_call_target="tpu_custom_call" | custom-call | tf_op jit(solution)/shard_map/mlp_in_partial/pallas_call | solution.py:820
  303.6 3.2 fusion.34
  308.4 5.7 slice_bitcast_fusion.6
  320.1 13.6 %mlp_in_back_theirs.1 = bf16[512,2048]{1,0:T(8,128)(2,1)} custom-call(bf16[1024,1536]{1,0:T(8,128)(2,1)} %get-tuple-element.53.refs_0_, bf16[1024,1536]{1,0:T(8,128)(2,1)} %get-tuple-element.54.refs_1_, bf16[8,256,3072]{2,1,0:T(8,128)(2,1)} %get-tuple-element.45.gate_weight.up_weight.refs_2_, s32[8]{0:T(128)} %stack.133.cols_ref.refs_2_.refs_3_), custom_call_target="tpu_custom_call" | custom-call | tf_op jit(solution)/shard_map/mlp_in_back_theirs/pallas_call | solution.py:801
  335.2 14.3 %mlp_in_back_mine.1 = f32[512,2048]{1,0:T(8,128)} custom-call(bf16[1024,1536]{1,0:T(8,128)(2,1)} %get-tuple-element.53.refs_0_, bf16[1024,1536]{1,0:T(8,128)(2,1)} %get-tuple-element.54.refs_1_, bf16[8,256,3072]{2,1,0:T(8,128)(2,1)} %get-tuple-element.45.gate_weight.up_weight.refs_2_, s32[8]{0:T(128)} %stack.133.cols_ref.refs_2_.refs_3_), custom_call_target="tpu_custom_call" | custom-call | tf_op jit(solution)/shard_map/mlp_in_back_mine/pallas_call | solution.py:801
  349.6 9.2 %mlp_out_mine.1 = f32[512,2048]{1,0:T(8,128)} custom-call(bf16[1024,1536]{1,0:T(8,128)(2,1)} %get-tuple-element.46.refs_0_, bf16[8,256,1536]{2,1,0:T(8,128)(2,1)} %get-tuple-element.47.refs_1_.weight_ref, s32[8]{0:T(128)} %stack.133.cols_ref.refs_2_.refs_3_), custom_call_target="tpu_custom_call" | custom-call | tf_op jit(solution)/shard_map/mlp_out_mine/pallas_call | solution.py:801
  358.7 8.5 %mlp_out_theirs.1 = bf16[512,2048]{1,0:T(8,128)(2,1)} custom-call(bf16[1024,1536]{1,0:T(8,128)(2,1)} %get-tuple-element.46.refs_0_, bf16[8,256,1536]{2,1,0:T(8,128)(2,1)} %get-tuple-element.47.refs_1_.weight_ref, s32[8]{0:T(128)} %stack.133.cols_ref.refs_2_.refs_3_), custom_call_target="tpu_custom_call" | custom-call | tf_op jit(solution)/shard_map/mlp_out_theirs/pallas_call | solution.py:801
  368.8 33.9 %collective-permute-done.57 = bf16[256,1536]{1,0:T(8,128)(2,1)} collective-permute-done((bf16[256,1536]{1,0:T(8,128)(2,1)}, bf16[256,1536]{1,0:T(8,128)(2,1)}, u32[]{:S(2)}, u32[]{:S(2)}) %collective-permute-start.57) | collective-permute-done | bytes 786464 | tf_op jit(solution)/shard_map/ppermute | solution.py:899
  404.3 3.3 collective-permute-start.58
  409.1 5.8 fusion.2
  417.8 7.9 collective-permute-done.58
  428.5 25.0 %collective-permute-done.56 = bf16[256,1536]{1,0:T(8,128)(2,1)S(1)} collective-permute-done((bf16[256,1536]{1,0:T(8,128)(2,1)S(1)}, bf16[256,1536]{1,0:T(8,128)(2,1)S(1)}, u32[]{:S(2)}, u32[]{:S(2)}) %collective-permute-start.56) | collective-permute-done | bytes 786464 | tf_op jit(solution)/shard_map/ppermute | solution.py:899
  458.0 14.4 %collective-permute-done.4 = bf16[512,1024]{1,0:T(8,128)(2,1)S(1)} collective-permute-done((bf16[512,1024]{1,0:T(8,128)(2,1)S(1)}, bf16[512,1024]{1,0:T(8,128)(2,1)S(1)}, u32[]{:S(2)}, u32[]{:S(2)}) %collective-permute-start.4) | collective-permute-done | bytes 1048608 | tf_op jit(solution)/shard_map/ppermute | solution.py:910
  476.6 13.9 %collective-permute-done.48 = bf16[256,3072]{1,0:T(8,128)(2,1)} collective-permute-done((bf16[256,3072]{1,0:T(8,128)(2,1)S(1)}, bf16[256,3072]{1,0:T(8,128)(2,1)}, u32[]{:S(2)}, u32[]{:S(2)}) %collective-permute-start.48) | collective-permute-done | bytes 1572896 | tf_op jit(solution)/shard_map/ppermute | solution.py:899
  494.7 20.1 %collective-permute-done.1 = bf16[512,1024]{1,0:T(8,128)(2,1)S(1)} collective-permute-done((bf16[512,1024]{1,0:T(8,128)(2,1)S(1)}, bf16[512,1024]{1,0:T(8,128)(2,1)S(1)}, u32[]{:S(2)}, u32[]{:S(2)}) %collective-permute-start.1) | collective-permute-done | bytes 1048608 | tf_op jit(solution)/shard_map/ppermute | solution.py:910
  520.2 3.9 collective-permute-done.46
  524.1 5.3 collective-permute-done.49
  529.4 2.7 fusion.5
  535.8 6.3 collective-permute-done.6
  544.3 4.1 copy.76
  549.8 43.2 %recur_backward.1 = (bf16[1024,1408]{1,0:T(8,128)(2,1)}, f32[8,704]{1,0:T(8,128)}, f32[704,704]{1,0:T(8,128)}, f32[704,704]{1,0:T(8,128)}) custom-call(bf16[512,2048]{1,0:T(8,128)(2,1)} %copy-done, bf16[512,2048]{1,0:T(8,128)(2,1)} %copy-done.6, bf16[8,256,704]{2,1,0:T(8,128)(2,1)} %get-tuple-element.55.weight_ref, s32[8]{0:T(128)} %stack.133.cols_ref.refs_2_.refs_3_, ...), custom_call_target="tpu_custom_call" | custom-call | tf_op jit(solution)/shard_map/recur_backward/pallas_call | solution.py:719
  593.0 12.3 %rnn_in_partial.1 = bf16[8,256,1408]{2,1,0:T(8,128)(2,1)} custom-call(bf16[512,2048]{1,0:T(8,128)(2,1)} %get-tuple-element.61.mine_ref, bf16[512,2048]{1,0:T(8,128)(2,1)} %get-tuple-element.62.theirs_ref, s32[8]{0:T(128)} %stack.133.cols_ref.refs_2_.refs_3_, bf16[1024,1408]{1,0:T(8,128)(2,1)} %get-tuple-element.58.refs_0_), custom_call_target="tpu_custom_call" | custom-call | tf_op jit(solution)/shard_map/rnn_in_partial/pallas_call | solution.py:820
  605.3 3.4 slice_bitcast_fusion.22
  609.2 7.9 rnn_out_partial.1
  617.2 2.5 slice_bitcast_fusion.30
  627.4 3.8 collective-permute-done.31
  632.2 9.3 %rnn_in_back_mine.1 = f32[512,2048]{1,0:T(8,128)} custom-call(bf16[1024,1408]{1,0:T(8,128)(2,1)} %get-tuple-element.58.refs_0_, bf16[8,256,1408]{2,1,0:T(8,128)(2,1)} %get-tuple-element.59.refs_1_, s32[8]{0:T(128)} %stack.133.cols_ref.refs_2_.refs_3_), custom_call_target="tpu_custom_call" | custom-call | tf_op jit(solution)/shard_map/rnn_in_back_mine/pallas_call | solution.py:801
  641.5 8.6 %rnn_in_back_theirs.1 = bf16[512,2048]{1,0:T(8,128)(2,1)} custom-call(bf16[1024,1408]{1,0:T(8,128)(2,1)} %get-tuple-element.58.refs_0_, bf16[8,256,1408]{2,1,0:T(8,128)(2,1)} %get-tuple-element.59.refs_1_, s32[8]{0:T(128)} %stack.133.cols_ref.refs_2_.refs_3_), custom_call_target="tpu_custom_call" | custom-call | tf_op jit(solution)/shard_map/rnn_in_back_theirs/pallas_call | solution.py:801
  657.7 9.0 %collective-permute-done.25 = bf16[4,176,352]{2,1,0:T(8,128)(2,1)S(1)} collective-permute-done((bf16[4,176,352]{2,1,0:T(8,128)(2,1)}, bf16[4,176,352]{2,1,0:T(8,128)(2,1)S(1)}, u32[]{:S(2)}, u32[]{:S(2)}) %collective-permute-start.25) | collective-permute-done | bytes 495648 | tf_op jit(solution)/shard_map/ppermute | solution.py:899
  667.6 6.6 collective-permute-done.39
  674.9 2.7 collective-permute-start.40
  684.0 2.9 collective-permute-done.40
  688.9 34.4 %collective-permute-done.38 = bf16[256,704]{1,0:T(8,128)(2,1)S(1)} collective-permute-done((bf16[256,704]{1,0:T(8,128)(2,1)S(1)}, bf16[256,704]{1,0:T(8,128)(2,1)S(1)}, u32[]{:S(2)}, u32[]{:S(2)}) %collective-permute-start.38) | collective-permute-done | bytes 360480 | tf_op jit(solution)/shard_map/ppermute | solution.py:899
  725.9 23.8 %collective-permute-done.22 = bf16[256,1408]{1,0:T(8,128)(2,1)S(1)} collective-permute-done((bf16[256,1408]{1,0:T(8,128)(2,1)S(1)}, bf16[256,1408]{1,0:T(8,128)(2,1)S(1)}, u32[]{:S(2)}, u32[]{:S(2)}) %collective-permute-start.22) | collective-permute-done | bytes 720928 | tf_op jit(solution)/shard_map/ppermute | solution.py:899
  750.4 10.7 %collective-permute-done.27 = bf16[4,176,352]{2,1,0:T(8,128)(2,1)S(1)} collective-permute-done((bf16[4,176,352]{2,1,0:T(8,128)(2,1)S(1)}, bf16[4,176,352]{2,1,0:T(8,128)(2,1)S(1)}, u32[]{:S(2)}, u32[]{:S(2)}) %collective-permute-start.27) | collective-permute-done | bytes 495648 | tf_op jit(solution)/shard_map/ppermute | solution.py:899
  761.1 2.7 collective-permute-start.23
  770.8 10.2 %collective-permute-done.23 = bf16[256,1408]{1,0:T(8,128)(2,1)S(1)} collective-permute-done((bf16[256,1408]{1,0:T(8,128)(2,1)S(1)}, bf16[256,1408]{1,0:T(8,128)(2,1)S(1)}, u32[]{:S(2)}, u32[]{:S(2)}) %collective-permute-start.23) | collective-permute-done | bytes 720928 | tf_op jit(solution)/shard_map/ppermute | solution.py:899
  780.9 5.0 collective-permute-done.21
  791.1 23.2 %collective-permute-done.9 = bf16[512,1024]{1,0:T(8,128)(2,1)S(1)} collective-permute-done((bf16[512,1024]{1,0:T(8,128)(2,1)S(1)}, bf16[512,1024]{1,0:T(8,128)(2,1)S(1)}, u32[]{:S(2)}, u32[]{:S(2)}) %collective-permute-start.9) | collective-permute-done | bytes 1048608 | tf_op jit(solution)/shard_map/ppermute | solution.py:910
  823.7 3.3 collective-permute-done.14
  830.0 7.0 collective-permute-done.11
  (296 shorter events, 124.1 us)
Async XLA Ops:
  266.7 36.9 %collective-permute-start.52 = (bf16[256,1536]{1,0:T(8,128)(2,1)S(1)}, bf16[256,1536]{1,0:T(8,128)(2,1)S(1)}, u32[]{:S(2)}, u32[]{:S(2)}) collective-permute-start(bf16[256,1536]{1,0:T(8,128)(2,1)S(1)} %get-tuple-element.149), channel_id=1, source_target_pairs={{8,12},{10,14},{12,8},{14,10},{16,20},{18,22},{20,16},{22,18},{9,1... | collective-permute-start | bytes 2359304 | tf_op jit(solution)/shard_map/ppermute | solution.py:899
  267.4 36.2 %collective-permute-start.54 = (bf16[256,1536]{1,0:T(8,128)(2,1)S(1)}, bf16[256,1536]{1,0:T(8,128)(2,1)}, u32[]{:S(2)}, u32[]{:S(2)}) collective-permute-start(bf16[256,1536]{1,0:T(8,128)(2,1)S(1)} %get-tuple-element.148), channel_id=1, source_target_pairs={{8,12},{10,14},{12,8},{14,10},{16,20},{18,22},{20,16},{22,18},{9,1... | collective-permute-start | bytes 2359304 | tf_op jit(solution)/shard_map/ppermute | solution.py:899
  306.8 26.9 %collective-permute-start.55 = (bf16[256,1536]{1,0:T(8,128)(2,1)}, bf16[256,1536]{1,0:T(8,128)(2,1)}, u32[]{:S(2)}, u32[]{:S(2)}) collective-permute-start(bf16[256,1536]{1,0:T(8,128)(2,1)} %get-tuple-element.151), channel_id=1, source_target_pairs={{8,16},{10,18},{12,20},{14,22},{16,8},{18,10},{20,12},{22,14},{9,1... | collective-permute-start | bytes 2359304 | tf_op jit(solution)/shard_map/ppermute | solution.py:899
  314.0 89.4 %collective-permute-start.43 = (bf16[256,3072]{1,0:T(8,128)(2,1)}, bf16[256,3072]{1,0:T(8,128)(2,1)}, u32[]{:S(2)}, u32[]{:S(2)}) collective-permute-start(bf16[256,3072]{1,0:T(8,128)(2,1)} %get-tuple-element.142), channel_id=1, source_target_pairs={{8,12},{10,14},{12,8},{14,10},{16,20},{18,22},{20,16},{22,18},{9,1... | collective-permute-start | bytes 4718600 | tf_op jit(solution)/shard_map/ppermute | solution.py:899
  315.8 88.5 %collective-permute-start.47 = (bf16[256,3072]{1,0:T(8,128)(2,1)}, bf16[256,3072]{1,0:T(8,128)(2,1)}, u32[]{:S(2)}, u32[]{:S(2)}) collective-permute-start(bf16[256,3072]{1,0:T(8,128)(2,1)} %get-tuple-element.140), channel_id=1, source_target_pairs={{8,16},{10,18},{12,20},{14,22},{16,8},{18,10},{20,12},{22,14},{9,1... | collective-permute-start | bytes 4718600 | tf_op jit(solution)/shard_map/ppermute | solution.py:899
  317.7 90.0 %collective-permute-start.45 = (bf16[256,3072]{1,0:T(8,128)(2,1)}, bf16[256,3072]{1,0:T(8,128)(2,1)}, u32[]{:S(2)}, u32[]{:S(2)}) collective-permute-start(bf16[256,3072]{1,0:T(8,128)(2,1)} %get-tuple-element.141), channel_id=1, source_target_pairs={{8,16},{10,18},{12,20},{14,22},{16,8},{18,10},{20,12},{22,14},{9,1... | collective-permute-start | bytes 4718600 | tf_op jit(solution)/shard_map/ppermute | solution.py:899
  333.7 81.3 %collective-permute-start.3 = (bf16[512,2048]{1,0:T(8,128)(2,1)}, bf16[512,2048]{1,0:T(8,128)(2,1)S(1)}, u32[]{:S(2)}, u32[]{:S(2)}) collective-permute-start(bf16[512,2048]{1,0:T(8,128)(2,1)} %mlp_in_back_theirs.1), channel_id=1, source_target_pairs={{0,2},{2,0},{4,6},{6,4},{8,10},{10,8},{12,14},{14,12},{16,18},{18,... | collective-permute-start | bytes 6291464 | tf_op jit(solution)/shard_map/ppermute | solution.py:899
  333.7 69.0 %collective-permute-start.57 = (bf16[256,1536]{1,0:T(8,128)(2,1)}, bf16[256,1536]{1,0:T(8,128)(2,1)}, u32[]{:S(2)}, u32[]{:S(2)}) collective-permute-start(bf16[256,1536]{1,0:T(8,128)(2,1)} %get-tuple-element.147), channel_id=1, source_target_pairs={{8,0},{10,2},{12,4},{14,6},{16,24},{18,26},{20,28},{22,30},{9,1},{... | collective-permute-start | bytes 2359304 | tf_op jit(solution)/shard_map/ppermute | solution.py:899
  402.7 13.1 %collective-permute-start.51 = (bf16[256,1536]{1,0:T(8,128)(2,1)S(1)}, bf16[256,1536]{1,0:T(8,128)(2,1)S(1)}, u32[]{:S(2)}, u32[]{:S(2)}) collective-permute-start(bf16[256,1536]{1,0:T(8,128)(2,1)S(1)} %get-tuple-element.146), channel_id=1, source_target_pairs={{8,12},{10,14},{12,8},{14,10},{16,20},{18,22},{20,16},{22,18},{9,1... | collective-permute-start | bytes 2359304 | tf_op jit(solution)/shard_map/ppermute | solution.py:899
  403.5 23.6 %collective-permute-start.53 = (bf16[256,1536]{1,0:T(8,128)(2,1)S(1)}, bf16[256,1536]{1,0:T(8,128)(2,1)S(1)}, u32[]{:S(2)}, u32[]{:S(2)}) collective-permute-start(bf16[256,1536]{1,0:T(8,128)(2,1)S(1)} %copy-done.17), channel_id=1, source_target_pairs={{8,16},{10,18},{12,20},{14,22},{16,8},{18,10},{20,12},{22,14},{9,1... | collective-permute-start | bytes 2359304 | tf_op jit(solution)/shard_map/ppermute | solution.py:899
  404.3 21.5 %collective-permute-start.58 = (bf16[256,1536]{1,0:T(8,128)(2,1)}, bf16[256,1536]{1,0:T(8,128)(2,1)S(1)}, u32[]{:S(2)}, u32[]{:S(2)}) collective-permute-start(bf16[256,1536]{1,0:T(8,128)(2,1)} %collective-permute-done.57), channel_id=1, source_target_pairs={{0,4},{2,6},{4,0},{6,2},{24,28},{26,30},{28,24},{30,26},{1,5},{3,7... | collective-permute-start | bytes 2359304 | tf_op jit(solution)/shard_map/ppermute | solution.py:899
  407.6 45.9 %collective-permute-start.56 = (bf16[256,1536]{1,0:T(8,128)(2,1)S(1)}, bf16[256,1536]{1,0:T(8,128)(2,1)S(1)}, u32[]{:S(2)}, u32[]{:S(2)}) collective-permute-start(bf16[256,1536]{1,0:T(8,128)(2,1)S(1)} %fusion.33), channel_id=1, source_target_pairs={{8,0},{10,2},{12,4},{14,6},{16,24},{18,26},{20,28},{22,30},{9,1},{... | collective-permute-start | bytes 2359304 | tf_op jit(solution)/shard_map/ppermute | solution.py:899
  415.0 58.2 %collective-permute-start = (bf16[512,2048]{1,0:T(8,128)(2,1)S(1)}, bf16[512,2048]{1,0:T(8,128)(2,1)S(1)}, u32[]{:S(2)}, u32[]{:S(2)}) collective-permute-start(bf16[512,2048]{1,0:T(8,128)(2,1)S(1)} %copy-done.14), channel_id=1, source_target_pairs={{0,2},{2,0},{4,6},{6,4},{8,10},{10,8},{12,14},{14,12},{16,18},{18,... | collective-permute-start | bytes 6291464 | tf_op jit(solution)/shard_map/ppermute | solution.py:899
  417.1 101.5 %collective-permute-start.42 = (bf16[256,3072]{1,0:T(8,128)(2,1)S(1)}, bf16[256,3072]{1,0:T(8,128)(2,1)S(1)}, u32[]{:S(2)}, u32[]{:S(2)}) collective-permute-start(bf16[256,3072]{1,0:T(8,128)(2,1)S(1)} %copy-done.15), channel_id=1, source_target_pairs={{8,12},{10,14},{12,8},{14,10},{16,20},{18,22},{20,16},{22,18},{9,1... | collective-permute-start | bytes 4718600 | tf_op jit(solution)/shard_map/ppermute | solution.py:899
  425.8 64.7 %collective-permute-start.48 = (bf16[256,3072]{1,0:T(8,128)(2,1)S(1)}, bf16[256,3072]{1,0:T(8,128)(2,1)}, u32[]{:S(2)}, u32[]{:S(2)}) collective-permute-start(bf16[256,3072]{1,0:T(8,128)(2,1)S(1)} %get-tuple-element.144), channel_id=1, source_target_pairs={{8,0},{10,2},{12,4},{14,6},{16,24},{18,26},{20,28},{22,30},{9,1},{... | collective-permute-start | bytes 4718600 | tf_op jit(solution)/shard_map/ppermute | solution.py:899
  427.1 97.0 %collective-permute-start.46 = (bf16[256,3072]{1,0:T(8,128)(2,1)S(1)}, bf16[256,3072]{1,0:T(8,128)(2,1)S(1)}, u32[]{:S(2)}, u32[]{:S(2)}) collective-permute-start(bf16[256,3072]{1,0:T(8,128)(2,1)S(1)} %get-tuple-element.145), channel_id=1, source_target_pairs={{8,0},{10,2},{12,4},{14,6},{16,24},{18,26},{20,28},{22,30},{9,1},{... | collective-permute-start | bytes 4718600 | tf_op jit(solution)/shard_map/ppermute | solution.py:899
  454.4 18.0 %collective-permute-start.4 = (bf16[512,1024]{1,0:T(8,128)(2,1)S(1)}, bf16[512,1024]{1,0:T(8,128)(2,1)S(1)}, u32[]{:S(2)}, u32[]{:S(2)}) collective-permute-start(bf16[512,1024]{1,0:T(8,128)(2,1)S(1)} %slice.542), channel_id=1, source_target_pairs={{0,1},{1,0},{2,3},{3,2},{4,5},{5,4},{6,7},{7,6},{8,9},{9,8},{10,11... | collective-permute-start | bytes 3145736 | tf_op jit(solution)/shard_map/ppermute | solution.py:910
  473.2 18.8 %collective-permute-start.5 = (f32[512,1]{0,1:T(1,128)S(1)}, f32[512,1]{0,1:T(1,128)S(1)}, u32[]{:S(2)}, u32[]{:S(2)}) collective-permute-start(f32[512,1]{0,1:T(1,128)S(1)} %bitcast.203), channel_id=1, source_target_pairs={{0,1},{1,0},{2,3},{3,2},{4,5},{5,4},{6,7},{7,6},{8,9},{9,8},{10,11... | collective-permute-start | bytes 6152 | tf_op jit(solution)/shard_map/ppermute | solution.py:910
  475.7 48.4 %collective-permute-start.44 = (bf16[256,3072]{1,0:T(8,128)(2,1)S(1)}, bf16[256,3072]{1,0:T(8,128)(2,1)S(1)}, u32[]{:S(2)}, u32[]{:S(2)}) collective-permute-start(bf16[256,3072]{1,0:T(8,128)(2,1)S(1)} %get-tuple-element.143), channel_id=1, source_target_pairs={{8,16},{10,18},{12,20},{14,22},{16,8},{18,10},{20,12},{22,14},{9,1... | collective-permute-start | bytes 4718600 | tf_op jit(solution)/shard_map/ppermute | solution.py:899
  490.5 24.4 %collective-permute-start.1 = (bf16[512,1024]{1,0:T(8,128)(2,1)S(1)}, bf16[512,1024]{1,0:T(8,128)(2,1)S(1)}, u32[]{:S(2)}, u32[]{:S(2)}) collective-permute-start(bf16[512,1024]{1,0:T(8,128)(2,1)S(1)} %slice.543), channel_id=1, source_target_pairs={{0,1},{1,0},{2,3},{3,2},{4,5},{5,4},{6,7},{7,6},{8,9},{9,8},{10,11... | collective-permute-start | bytes 3145736 | tf_op jit(solution)/shard_map/ppermute | solution.py:910
  492.0 37.4 %collective-permute-start.49 = (bf16[256,3072]{1,0:T(8,128)(2,1)}, bf16[256,3072]{1,0:T(8,128)(2,1)S(1)}, u32[]{:S(2)}, u32[]{:S(2)}) collective-permute-start(bf16[256,3072]{1,0:T(8,128)(2,1)} %collective-permute-done.48), channel_id=1, source_target_pairs={{0,4},{2,6},{4,0},{6,2},{24,28},{26,30},{28,24},{30,26},{1,5},{3,7... | collective-permute-start | bytes 4718600 | tf_op jit(solution)/shard_map/ppermute | solution.py:899
  517.0 17.9 %collective-permute-start.2 = (bf16[256,1024]{1,0:T(8,128)(2,1)S(1)}, bf16[256,1024]{1,0:T(8,128)(2,1)S(1)}, u32[]{:S(2)}, u32[]{:S(2)}) collective-permute-start(bf16[256,1024]{1,0:T(8,128)(2,1)S(1)} %slice.378), channel_id=1, source_target_pairs={{8,0},{10,2},{12,4},{14,6},{16,24},{18,26},{20,28},{22,30},{9,1},{... | collective-permute-start | bytes 1572872 | tf_op jit(solution)/shard_map/ppermute | solution.py:899
  518.6 23.5 %collective-permute-start.6 = (bf16[512,1024]{1,0:T(8,128)(2,1)S(1)}, bf16[512,1024]{1,0:T(8,128)(2,1)S(1)}, u32[]{:S(2)}, u32[]{:S(2)}) collective-permute-start(bf16[512,1024]{1,0:T(8,128)(2,1)S(1)} %get-tuple-element.137), channel_id=1, source_target_pairs={{0,1},{1,0},{2,3},{3,2},{4,5},{5,4},{6,7},{7,6},{8,9},{9,8},{10,11... | collective-permute-start | bytes 3145736 | tf_op jit(solution)/shard_map/ppermute | solution.py:910
  532.3 10.1 %collective-permute-start.50 = (bf16[128,3072]{1,0:T(8,128)(2,1)S(1)}, bf16[128,3072]{1,0:T(8,128)(2,1)S(1)}, u32[]{:S(2)}, u32[]{:S(2)}) collective-permute-start(bf16[128,3072]{1,0:T(8,128)(2,1)S(1)} %broadcast_select_fusion), channel_id=1, source_target_pairs={{0,2},{2,0},{4,6},{6,4},{8,10},{10,8},{12,14},{14,12},{16,18},{18,... | collective-permute-start | bytes 2359304 | tf_op jit(solution)/shard_map/ppermute | solution.py:899
  608.7 10.9 %collective-permute-start.29 = (f32[8,704]{1,0:T(8,128)S(1)}, f32[8,704]{1,0:T(8,128)S(1)}, u32[]{:S(2)}, u32[]{:S(2)}) collective-permute-start(f32[8,704]{1,0:T(8,128)S(1)} %broadcast_select_fusion.21), channel_id=1, source_target_pairs={{0,4},{2,6},{4,0},{6,2},{8,12},{10,14},{12,8},{14,10},{16,20},{18,... | collective-permute-start | bytes 67592 | tf_op jit(solution)/shard_map/ppermute | solution.py:899
  621.7 9.4 %collective-permute-start.31 = (f32[8,704]{1,0:T(8,128)S(1)}, f32[8,704]{1,0:T(8,128)S(1)}, u32[]{:S(2)}, u32[]{:S(2)}) collective-permute-start(f32[8,704]{1,0:T(8,128)S(1)} %add.289), channel_id=1, source_target_pairs={{8,0},{10,2},{12,4},{14,6},{16,24},{18,26},{20,28},{22,30},{9,1},{... | collective-permute-start | bytes 67592 | tf_op jit(solution)/shard_map/ppermute | solution.py:899
  624.4 29.3 %collective-permute-start.34 = (bf16[256,704]{1,0:T(8,128)(2,1)}, bf16[256,704]{1,0:T(8,128)(2,1)}, u32[]{:S(2)}, u32[]{:S(2)}) collective-permute-start(bf16[256,704]{1,0:T(8,128)(2,1)} %get-tuple-element.161), channel_id=1, source_target_pairs={{8,12},{10,14},{12,8},{14,10},{16,20},{18,22},{20,16},{22,18},{9,1... | collective-permute-start | bytes 1081352 | tf_op jit(solution)/shard_map/ppermute | solution.py:899
  625.8 29.2 %collective-permute-start.36 = (bf16[256,704]{1,0:T(8,128)(2,1)}, bf16[256,704]{1,0:T(8,128)(2,1)}, u32[]{:S(2)}, u32[]{:S(2)}) collective-permute-start(bf16[256,704]{1,0:T(8,128)(2,1)} %get-tuple-element.160), channel_id=1, source_target_pairs={{8,12},{10,14},{12,8},{14,10},{16,20},{18,22},{20,16},{22,18},{9,1... | collective-permute-start | bytes 1081352 | tf_op jit(solution)/shard_map/ppermute | solution.py:899
  631.2 20.5 %collective-permute-start.32 = (f32[8,704]{1,0:T(8,128)S(1)}, f32[8,704]{1,0:T(8,128)S(1)}, u32[]{:S(2)}, u32[]{:S(2)}) collective-permute-start(f32[8,704]{1,0:T(8,128)S(1)} %broadcast_select_fusion.22), channel_id=1, source_target_pairs={{0,2},{2,0},{4,6},{6,4},{8,10},{10,8},{12,14},{14,12},{16,18},{18,... | collective-permute-start | bytes 67592 | tf_op jit(solution)/shard_map/ppermute | solution.py:899
  650.1 27.6 %collective-permute-start.17 = (bf16[256,1408]{1,0:T(8,128)(2,1)}, bf16[256,1408]{1,0:T(8,128)(2,1)S(1)}, u32[]{:S(2)}, u32[]{:S(2)}) collective-permute-start(bf16[256,1408]{1,0:T(8,128)(2,1)} %get-tuple-element.155), channel_id=1, source_target_pairs={{8,12},{10,14},{12,8},{14,10},{16,20},{18,22},{20,16},{22,18},{9,1... | collective-permute-start | bytes 2162696 | tf_op jit(solution)/shard_map/ppermute | solution.py:899
  650.9 27.7 %collective-permute-start.19 = (bf16[256,1408]{1,0:T(8,128)(2,1)}, bf16[256,1408]{1,0:T(8,128)(2,1)S(1)}, u32[]{:S(2)}, u32[]{:S(2)}) collective-permute-start(bf16[256,1408]{1,0:T(8,128)(2,1)} %get-tuple-element.154), channel_id=1, source_target_pairs={{8,12},{10,14},{12,8},{14,10},{16,20},{18,22},{20,16},{22,18},{9,1... | collective-permute-start | bytes 2162696 | tf_op jit(solution)/shard_map/ppermute | solution.py:899
  651.7 15.0 %collective-permute-start.25 = (bf16[4,176,352]{2,1,0:T(8,128)(2,1)}, bf16[4,176,352]{2,1,0:T(8,128)(2,1)S(1)}, u32[]{:S(2)}, u32[]{:S(2)}) collective-permute-start(bf16[4,176,352]{2,1,0:T(8,128)(2,1)} %fusion.50), channel_id=1, source_target_pairs={{0,4},{2,6},{4,0},{6,2},{8,12},{10,14},{12,8},{14,10},{16,20},{18,... | collective-permute-start | bytes 1486856 | tf_op jit(solution)/shard_map/ppermute | solution.py:899
  653.7 20.5 %collective-permute-start.39 = (bf16[256,704]{1,0:T(8,128)(2,1)}, bf16[256,704]{1,0:T(8,128)(2,1)S(1)}, u32[]{:S(2)}, u32[]{:S(2)}) collective-permute-start(bf16[256,704]{1,0:T(8,128)(2,1)} %get-tuple-element.159), channel_id=1, source_target_pairs={{8,0},{10,2},{12,4},{14,6},{16,24},{18,26},{20,28},{22,30},{9,1},{... | collective-permute-start | bytes 1081352 | tf_op jit(solution)/shard_map/ppermute | solution.py:899
  656.3 18.6 %collective-permute-start.37 = (bf16[256,704]{1,0:T(8,128)(2,1)S(1)}, bf16[256,704]{1,0:T(8,128)(2,1)S(1)}, u32[]{:S(2)}, u32[]{:S(2)}) collective-permute-start(bf16[256,704]{1,0:T(8,128)(2,1)S(1)} %get-tuple-element.163), channel_id=1, source_target_pairs={{8,16},{10,18},{12,20},{14,22},{16,8},{18,10},{20,12},{22,14},{9,1... | collective-permute-start | bytes 1081352 | tf_op jit(solution)/shard_map/ppermute | solution.py:899
  666.6 15.4 %collective-permute-start.33 = (bf16[256,704]{1,0:T(8,128)(2,1)S(1)}, bf16[256,704]{1,0:T(8,128)(2,1)S(1)}, u32[]{:S(2)}, u32[]{:S(2)}) collective-permute-start(bf16[256,704]{1,0:T(8,128)(2,1)S(1)} %copy-done.27), channel_id=1, source_target_pairs={{8,12},{10,14},{12,8},{14,10},{16,20},{18,22},{20,16},{22,18},{9,1... | collective-permute-start | bytes 1081352 | tf_op jit(solution)/shard_map/ppermute | solution.py:899
  674.2 13.4 %collective-permute-start.35 = (bf16[256,704]{1,0:T(8,128)(2,1)S(1)}, bf16[256,704]{1,0:T(8,128)(2,1)S(1)}, u32[]{:S(2)}, u32[]{:S(2)}) collective-permute-start(bf16[256,704]{1,0:T(8,128)(2,1)S(1)} %get-tuple-element.162), channel_id=1, source_target_pairs={{8,16},{10,18},{12,20},{14,22},{16,8},{18,10},{20,12},{22,14},{9,1... | collective-permute-start | bytes 1081352 | tf_op jit(solution)/shard_map/ppermute | solution.py:899
  674.9 12.0 %collective-permute-start.40 = (bf16[256,704]{1,0:T(8,128)(2,1)S(1)}, bf16[256,704]{1,0:T(8,128)(2,1)S(1)}, u32[]{:S(2)}, u32[]{:S(2)}) collective-permute-start(bf16[256,704]{1,0:T(8,128)(2,1)S(1)} %collective-permute-done.39), channel_id=1, source_target_pairs={{0,4},{2,6},{4,0},{6,2},{24,28},{26,30},{28,24},{30,26},{1,5},{3,7... | collective-permute-start | bytes 1081352 | tf_op jit(solution)/shard_map/ppermute | solution.py:899
  678.6 44.8 %collective-permute-start.38 = (bf16[256,704]{1,0:T(8,128)(2,1)S(1)}, bf16[256,704]{1,0:T(8,128)(2,1)S(1)}, u32[]{:S(2)}, u32[]{:S(2)}) collective-permute-start(bf16[256,704]{1,0:T(8,128)(2,1)S(1)} %fusion.53), channel_id=1, source_target_pairs={{8,0},{10,2},{12,4},{14,6},{16,24},{18,26},{20,28},{22,30},{9,1},{... | collective-permute-start | bytes 1081352 | tf_op jit(solution)/shard_map/ppermute | solution.py:899
  681.6 106.0 %collective-permute-start.8 = (bf16[512,2048]{1,0:T(8,128)(2,1)S(1)}, bf16[512,2048]{1,0:T(8,128)(2,1)S(1)}, u32[]{:S(2)}, u32[]{:S(2)}) collective-permute-start(bf16[512,2048]{1,0:T(8,128)(2,1)S(1)} %copy-done.13), channel_id=1, source_target_pairs={{0,2},{2,0},{4,6},{6,4},{8,10},{10,8},{12,14},{14,12},{16,18},{18,... | collective-permute-start | bytes 6291464 | tf_op jit(solution)/shard_map/ppermute | solution.py:899
  682.7 67.0 %collective-permute-start.22 = (bf16[256,1408]{1,0:T(8,128)(2,1)S(1)}, bf16[256,1408]{1,0:T(8,128)(2,1)S(1)}, u32[]{:S(2)}, u32[]{:S(2)}) collective-permute-start(bf16[256,1408]{1,0:T(8,128)(2,1)S(1)} %copy-done.24), channel_id=1, source_target_pairs={{8,0},{10,2},{12,4},{14,6},{16,24},{18,26},{20,28},{22,30},{9,1},{... | collective-permute-start | bytes 2162696 | tf_op jit(solution)/shard_map/ppermute | solution.py:899
  686.9 76.9 %collective-permute-start.20 = (bf16[256,1408]{1,0:T(8,128)(2,1)S(1)}, bf16[256,1408]{1,0:T(8,128)(2,1)S(1)}, u32[]{:S(2)}, u32[]{:S(2)}) collective-permute-start(bf16[256,1408]{1,0:T(8,128)(2,1)S(1)} %get-tuple-element.157), channel_id=1, source_target_pairs={{8,16},{10,18},{12,20},{14,22},{16,8},{18,10},{20,12},{22,14},{9,1... | collective-permute-start | bytes 2162696 | tf_op jit(solution)/shard_map/ppermute | solution.py:899
  687.6 73.5 %collective-permute-start.27 = (bf16[4,176,352]{2,1,0:T(8,128)(2,1)S(1)}, bf16[4,176,352]{2,1,0:T(8,128)(2,1)S(1)}, u32[]{:S(2)}, u32[]{:S(2)}) collective-permute-start(bf16[4,176,352]{2,1,0:T(8,128)(2,1)S(1)} %fusion.72), channel_id=1, source_target_pairs={{8,0},{10,2},{12,4},{14,6},{16,24},{18,26},{20,28},{22,30},{9,1},{... | collective-permute-start | bytes 1486856 | tf_op jit(solution)/shard_map/ppermute | solution.py:899
  725.2 45.6 %collective-permute-start.16 = (bf16[256,1408]{1,0:T(8,128)(2,1)S(1)}, bf16[256,1408]{1,0:T(8,128)(2,1)S(1)}, u32[]{:S(2)}, u32[]{:S(2)}) collective-permute-start(bf16[256,1408]{1,0:T(8,128)(2,1)S(1)} %copy-done.23), channel_id=1, source_target_pairs={{8,12},{10,14},{12,8},{14,10},{16,20},{18,22},{20,16},{22,18},{9,1... | collective-permute-start | bytes 2162696 | tf_op jit(solution)/shard_map/ppermute | solution.py:899
  749.7 31.3 %collective-permute-start.18 = (bf16[256,1408]{1,0:T(8,128)(2,1)S(1)}, bf16[256,1408]{1,0:T(8,128)(2,1)S(1)}, u32[]{:S(2)}, u32[]{:S(2)}) collective-permute-start(bf16[256,1408]{1,0:T(8,128)(2,1)S(1)} %get-tuple-element.156), channel_id=1, source_target_pairs={{8,16},{10,18},{12,20},{14,22},{16,8},{18,10},{20,12},{22,14},{9,1... | collective-permute-start | bytes 2162696 | tf_op jit(solution)/shard_map/ppermute | solution.py:899
  761.1 19.9 %collective-permute-start.23 = (bf16[256,1408]{1,0:T(8,128)(2,1)S(1)}, bf16[256,1408]{1,0:T(8,128)(2,1)S(1)}, u32[]{:S(2)}, u32[]{:S(2)}) collective-permute-start(bf16[256,1408]{1,0:T(8,128)(2,1)S(1)} %collective-permute-done.22), channel_id=1, source_target_pairs={{0,4},{2,6},{4,0},{6,2},{24,28},{26,30},{28,24},{30,26},{1,5},{3,7... | collective-permute-start | bytes 2162696 | tf_op jit(solution)/shard_map/ppermute | solution.py:899
  765.8 20.1 %collective-permute-start.21 = (bf16[256,1408]{1,0:T(8,128)(2,1)S(1)}, bf16[256,1408]{1,0:T(8,128)(2,1)S(1)}, u32[]{:S(2)}, u32[]{:S(2)}) collective-permute-start(bf16[256,1408]{1,0:T(8,128)(2,1)S(1)} %fusion.39), channel_id=1, source_target_pairs={{8,0},{10,2},{12,4},{14,6},{16,24},{18,26},{20,28},{22,30},{9,1},{... | collective-permute-start | bytes 2162696 | tf_op jit(solution)/shard_map/ppermute | solution.py:899
  788.7 25.6 %collective-permute-start.9 = (bf16[512,1024]{1,0:T(8,128)(2,1)S(1)}, bf16[512,1024]{1,0:T(8,128)(2,1)S(1)}, u32[]{:S(2)}, u32[]{:S(2)}) collective-permute-start(bf16[512,1024]{1,0:T(8,128)(2,1)S(1)} %slice.541), channel_id=1, source_target_pairs={{0,1},{1,0},{2,3},{3,2},{4,5},{5,4},{6,7},{7,6},{8,9},{9,8},{10,11... | collective-permute-start | bytes 3145736 | tf_op jit(solution)/shard_map/ppermute | solution.py:910
  822.4 14.5 %collective-permute-start.11 = (bf16[256,1024]{1,0:T(8,128)(2,1)S(1)}, bf16[256,1024]{1,0:T(8,128)(2,1)S(1)}, u32[]{:S(2)}, u32[]{:S(2)}) collective-permute-start(bf16[256,1024]{1,0:T(8,128)(2,1)S(1)} %slice.384), channel_id=1, source_target_pairs={{8,0},{10,2},{12,4},{14,6},{16,24},{18,26},{20,28},{22,30},{9,1},{... | collective-permute-start | bytes 1572872 | tf_op jit(solution)/shard_map/ppermute | solution.py:899
  (57 other events, 472.2 us)

commit v3 on v2

--- a/solution.py
+++ b/solution.py
@@ -485,16 +485,7 @@
             moved.wait_send()
 
 
-def recur_backward(
-    mine_ref, theirs_ref, weight_ref, cols_ref,
-    both_ref, state_ref, mask_ref, vec_ref, wr_ref, wi_ref,
-    dboth_ref, sums_ref, gr_ref, gi_ref,
-    coef_ref, push_ref, dmix_ref,
-):
-    def keep_mixed(start, value):
-        dmix_ref[pl.ds(start, chunk_rows), :] = value
-
-    project(mine_ref, theirs_ref, weight_ref, cols_ref, keep_mixed)
+def recur_first(both_ref, state_ref, mask_ref, vec_ref, wr_ref, wi_ref, dmix_ref, dboth_ref, coef_ref, push_ref):
     width = dmix_ref.shape[1]
     rows = both_ref.shape[0] // held_buffers
 
@@ -512,11 +503,16 @@
 
     lax.fori_loop(0, held_buffers, first, 0)
 
-    scan_rows(coef_ref, push_ref, rows, True)
+
+def recur_last(
+    both_ref, state_ref, mask_ref, vec_ref, wr_ref, wi_ref, push_ref,
+    dboth_ref, sums_ref, gr_ref, gi_ref,
+):
+    width = both_ref.shape[1] // 2
+    rows = both_ref.shape[0] // held_buffers
     sums_ref[...] = jnp.zeros_like(sums_ref)
     gr_ref[...] = jnp.zeros_like(gr_ref)
     gi_ref[...] = jnp.zeros_like(gi_ref)
-
     def add_sum(k, value):
         sums_ref[k : k + 1, :] += jnp.sum(value, axis=0, keepdims=True)
 
@@ -653,6 +649,496 @@
         first += tiles
 
 
+class Sums:
+    def __init__(self, at, partial, land, total, send, recv):
+        self.at, self.partial, self.land, self.total = at, partial, land, total
+        self.send, self.recv = send, recv
+        self.half_rows = total.shape[1]
+        self.top = pl.ds(0, self.half_rows)
+        self.bottom = pl.ds(self.half_rows, self.half_rows)
+
+    def rows_of(self, c):
+        return pl.ds(pl.multiple_of(c * self.half_rows, self.half_rows), self.half_rows)
+
+    def hop(self, k, last=None):
+        d, land, at, top, bottom = self.partial, self.land, self.at, self.top, self.bottom
+        src, dst, where = (
+            lambda: (d.at[5], land.at[0], at.beside),
+            lambda: (d.at[7, bottom], land.at[1, top], at.beside),
+            lambda: (d.at[7, top], land.at[1, bottom], at.ahead),
+            lambda: (d.at[6, top], land.at[2, top], at.ahead),
+            lambda: (land.at[1, top], land.at[2, bottom], at.ahead),
+            lambda: (d.at[3, bottom], land.at[0, bottom], at.behind),
+            lambda: (land.at[1, bottom], land.at[0, top], at.behind),
+            lambda: (d.at[1], land.at[3], at.beside),
+            lambda: (land.at[0], land.at[4], at.ahead),
+            lambda: (land.at[2], land.at[2], at.behind),
+            lambda: (land.at[0], land.at[3], at.beside),
+            lambda: (last.at[self.rows_of(1 - at.c)], self.total.at[1], at.core),
+        )[k]()
+        return remote(src, dst, self.send.at[k], self.recv.at[k], where)
+
+    def start(self, *hops):
+        for k in hops:
+            self.hop(k).start()
+
+    def received(self, *hops):
+        for k in hops:
+            self.hop(k).wait_recv()
+
+    def sent(self, *hops):
+        for k in hops:
+            self.hop(k).wait_send()
+
+    def step(self, k, add):
+        d, land, top, bottom = self.partial, self.land, self.top, self.bottom
+        if k == 4:
+            self.received(1)
+            add(land.at[1, top], d.at[6, bottom])
+        elif k == 6:
+            self.received(2)
+            add(land.at[1, bottom], d.at[3, top])
+        elif k == 8:
+            self.received(0)
+            add(land.at[0], d.at[4])
+        elif k == 9:
+            self.received(3, 4)
+            add(land.at[2], d.at[2])
+        self.start(k)
+
+
+work_hops, serve_hops = (0, 1, 2, 3, 4, 5, 6, 7, 8, 9), (10,)
+
+
+def add_rows(into, value, other=None):
+    size = 32
+
+    def chunk(i, carry):
+        at = pl.ds(pl.multiple_of(i * size, size), size)
+        total = into[at, :].astype(f32) + value[at, :].astype(f32)
+        if other is not None:
+            total = total + other[at, :].astype(f32)
+        into[at, :] = total.astype(bf16)
+        return carry
+
+    lax.fori_loop(0, into.shape[0] // size, chunk, 0)
+
+
+def norm_sums(e_ref, y_in, source_ref, gain_ref, gain_row, mean_ref, first, count):
+    size, half = 64, e_ref.shape[1]
+
+    def chunk(i, carry):
+        at = pl.ds(pl.multiple_of(first + i * size, size), size)
+        e = e_ref[at, :] + y_in[at, :].astype(f32)
+        e_ref[at, :] = e
+        source = source_ref[at, :half].astype(bf16).astype(f32)
+        part = jnp.sum(e * gain_ref[gain_row : gain_row + 1, :half] * source, axis=1, keepdims=True)
+        mean_ref[at, :] = jnp.broadcast_to(part, (size, lanes))
+        return carry
+
+    lax.fori_loop(0, count // size, chunk, 0)
+
+
+def norm_rows_back(
+    e_ref, source_ref, gain_ref, gain_row, scale_ref, mean_ref, mean_in, term_ref, model, first, count, use
+):
+    size, half = 64, e_ref.shape[1]
+
+    def chunk(i, carry):
+        at = pl.ds(pl.multiple_of(first + i * size, size), size)
+        e = e_ref[at, :]
+        source = source_ref[at, :half].astype(bf16).astype(f32)
+        scale = scale_ref[gain_row, at, 0:1]
+        inner = (mean_ref[at, 0:1] + mean_in[at, 0:1]) / model
+        weighted = e * gain_ref[gain_row : gain_row + 1, :half]
+        term_ref[gain_row : gain_row + 1, :] += jnp.sum(e * source * scale, axis=0, keepdims=True)
+        use(at, scale * weighted - source * (scale * scale * scale * inner))
+        return carry
+
+    lax.fori_loop(0, count // size, chunk, 0)
+
+
+def backward_kernel(
+    count,
+    d_mi, d_mo, e_theirs, e_mine, o_theirs, o_mine, low_ref,
+    middle_ref, scale_ref, gain_ref, w_ro, both_ref, state_ref, mask_ref, vec_ref, wr_ref, wi_ref,
+    land_mi, land_mo, total_mi, total_mo,
+    out_ref, dmid_ref, db_mine, db_theirs, dboth_ref, sums_ref, gr_ref, gi_ref, term_ref,
+    coef_ref, push_ref, dmix_ref, part_in, o_in, part_sum, y_out, y_in, oy_out, oy_in,
+    mean_ref, mean_in, stage_a, stage_b,
+    w_send, w_recv, m_send, m_recv, local_sem,
+):
+    at = Place(count)
+    size = w_ro.shape[1]
+    cols = at.columns(size)
+    own, half_model = middle_ref.shape
+    e_ref, low_left = dmid_ref, y_out
+    model = 2 * half_model
+    rows = own // 2
+    mi = Sums(at, d_mi, land_mi, total_mi, w_send.at[0], w_recv.at[0])
+    mo = Sums(at, d_mo, land_mo, total_mo, w_send.at[1], w_recv.at[1])
+    first, second = pl.ds(0, rows), pl.ds(rows, rows)
+    left, right = pl.ds(0, half_model), pl.ds(half_model, half_model)
+    halves = (first, second)
+
+    def move(k, src, dst, where):
+        return remote(src, dst, m_send.at[k], m_recv.at[k], where)
+
+    e_core = [move(i, e_theirs.at[h], part_in.at[h], at.core) for i, h in enumerate(halves)]
+    o_core = [move(2 + i, o_theirs.at[h], o_in.at[h], at.core) for i, h in enumerate(halves)]
+    e_y = [move(4 + i, y_out.at[h], y_in.at[h], at.over_y) for i, h in enumerate(halves)]
+    o_y = [move(6 + i, oy_out.at[h], oy_in.at[h], at.over_y) for i, h in enumerate(halves)]
+    mean_y = move(8, mean_ref, mean_in, at.over_y)
+    db_y = [
+        move(9 + i, db_mine.at[h, left], db_mine.at[h, right], at.over_y)
+        for i, h in enumerate(halves)
+    ]
+    db_core = [move(11 + i, db_mine.at[h], db_theirs.at[h], at.core) for i, h in enumerate(halves)]
+    out_move = move(13, out_ref.at[second], out_ref.at[first], at.behind)
+    low_load = pltpu.make_async_copy(low_ref.at[:, left], low_left, local_sem.at[0])
+
+    def fetch(src, dst, k):
+        return pltpu.make_async_copy(src, dst, local_sem.at[k])
+
+    def add(into, value):
+        count_rows, width = into.shape
+        a = stage_a.at[pl.ds(0, count_rows), pl.ds(0, width)]
+        b = stage_b.at[pl.ds(0, count_rows), pl.ds(0, width)]
+        loads = fetch(into, a, 1), fetch(value, b, 2)
+        for v in loads:
+            v.start()
+        for v in loads:
+            v.wait()
+        add_rows(a, b)
+        back = fetch(a, into, 3)
+        back.start()
+        back.wait()
+
+    def finish(w, parts):
+        count_rows, width = parts[0].shape
+        a = stage_a.at[pl.ds(0, count_rows), pl.ds(0, width)]
+        b = stage_b.at[pl.ds(0, count_rows), pl.ds(0, width)]
+        loads = fetch(parts[0], a, 1), fetch(parts[1], b, 2)
+        for v in loads:
+            v.start()
+        for v in loads:
+            v.wait()
+        add_rows(a, b)
+        if len(parts) == 3:
+            third = fetch(parts[2], b, 2)
+            third.start()
+            third.wait()
+            add_rows(a, b)
+        w.hop(11, a).start()
+        kept = fetch(a.at[w.rows_of(at.c)], w.total.at[0], 3)
+        kept.start()
+        kept.wait()
+        w.hop(11, a).wait()
+
+    def part_fetch(source, h):
+        return fetch(source.at[h], part_sum, 4)
+
+    def join(i, h, source, arrived, landed, keep_value, sent_ref, over):
+        part_fetch(source, h).wait()
+        arrived[i].wait_recv()
+        keep_value(i, part_sum[:, left] + landed[h, left].astype(f32))
+        sent_ref[h, :] = (part_sum[:, right] + landed[h, right].astype(f32)).astype(bf16)
+        over[i].start()
+
+    def keep_e(i, value):
+        e_ref[halves[i], :] = value
+
+    def o_place(i, k):
+        return k // 2, pl.ds(k % 2 * own + i * rows, rows)
+
+    def keep_o(i, value):
+        for k in range(half_model // lanes):
+            chunk, o_rows = o_place(i, k)
+            coef_ref[chunk, o_rows, :] = value[:, k * lanes : (k + 1) * lanes]
+
+    def kept_o(i):
+        parts = []
+        for k in range(half_model // lanes):
+            chunk, o_rows = o_place(i, k)
+            parts.append(coef_ref[chunk, o_rows, :])
+        return jnp.concatenate(parts, axis=1)
+
+    at.meet()
+
+    @pl.when(at.serves)
+    def _():
+        for w in (mo, mi):
+            w.received(5, 6)
+            w.start(10)
+        for w in (mo, mi):
+            w.received(9, 10)
+            finish(w, (w.land.at[2], w.land.at[3]))
+        out_move.wait_recv()
+        for w in (mo, mi):
+            w.sent(*serve_hops)
+
+    @pl.when(at.works)
+    def _():
+        for moved in e_core:
+            moved.start()
+        part_fetch(e_mine, first).start()
+        for w in (mo, mi):
+            w.start(1, 2, 0, 3, 5, 7)
+        term_ref[...] = jnp.zeros_like(term_ref)
+        join(0, first, e_mine, e_core, part_in, keep_e, y_out, e_y)
+        part_fetch(e_mine, second).start()
+        join(1, second, e_mine, e_core, part_in, keep_e, y_out, e_y)
+        part_fetch(o_mine, first).start()
+        for moved in o_core:
+            moved.start()
+        mo.step(4, add)
+        mo.step(6, add)
+        join(0, first, o_mine, o_core, o_in, keep_o, oy_out, o_y)
+        part_fetch(o_mine, second).start()
+        join(1, second, o_mine, o_core, o_in, keep_o, oy_out, o_y)
+        for i, h in enumerate(halves):
+            e_y[i].wait_recv()
+            norm_sums(e_ref, y_in, middle_ref, gain_ref, 1, mean_ref, i * rows, rows)
+        mean_y.start()
+        for moved in e_y:
+            moved.wait_send()
+        low_load.start()
+        mo.step(8, add)
+        low_load.wait()
+        mean_y.wait_recv()
+
+        def keep(row_at, back):
+            d_middle = back + low_left[row_at, :].astype(f32)
+            dmid_ref[row_at, :] = d_middle
+            db_mine[row_at, left] = d_middle.astype(bf16)
+
+        for i in range(2):
+            norm_rows_back(
+                e_ref, middle_ref, gain_ref, 1, scale_ref, mean_ref, mean_in, term_ref, model,
+                i * rows, rows, keep,
+            )
+            db_y[i].start()
+        mo.step(9, add)
+        mi.step(6, add)
+        mi.step(4, add)
+        for i, h in enumerate(halves):
+            o_y[i].wait_recv()
+            out_ref[h, :] = (
+                mask_ref[h, 4:5]
+                * (middle_ref[h, :] + kept_o(i) + oy_in[h, :].astype(f32))
+            ).astype(bf16)
+        out_move.start()
+        for i in range(2):
+            db_y[i].wait_recv()
+            db_core[i].start()
+        for i in range(2):
+            db_core[i].wait_recv()
+
+        def keep_mixed(start, value):
+            dmix_ref[pl.ds(start, chunk_rows), :] = value
+
+        project(db_mine, db_theirs, w_ro, cols, keep_mixed)
+        recur_first(
+            both_ref, state_ref, mask_ref, vec_ref, wr_ref, wi_ref, dmix_ref, dboth_ref, coef_ref, push_ref
+        )
+        mi.step(8, add)
+        scan_rows(coef_ref, push_ref, both_ref.shape[0] // held_buffers, True)
+        mi.step(9, add)
+        recur_last(
+            both_ref, state_ref, mask_ref, vec_ref, wr_ref, wi_ref, push_ref,
+            dboth_ref, sums_ref, gr_ref, gi_ref,
+        )
+        for w in (mo, mi):
+            w.received(7, 8)
+            finish(w, (w.partial.at[0], w.land.at[3], w.land.at[4]))
+        for w in (mo, mi):
+            w.sent(*work_hops)
+        for moved in (*e_core, *o_core, *o_y, mean_y, *db_y, *db_core, out_move):
+            moved.wait_send()
+
+
+def finish_kernel(
+    count,
+    one_mine, one_theirs, db_mine, db_theirs, dboth_ref, mixed_ref, w_ri, tok_ref, scale_ref, gain_ref,
+    dmid_ref, sums_ref, gates_ref, term_in,
+    total_ri, total_ro, out_ref, gates_out, sums_out, term_out,
+    d_ri, d_ro, land_ri, land_ro, tok_left, part_out, part_in, part_sum, y_out, y_in, e_ref,
+    mean_ref, mean_in, last_ri, last_ro, gates_in, sums_in, term_ref, term_land,
+    w_send, w_recv, m_send, m_recv, local_sem,
+):
+    at = Place(count)
+    size = w_ri.shape[1]
+    cols = at.columns(size)
+    own, half_model = dmid_ref.shape
+    model = 2 * half_model
+    rows = own // 2
+    ri = Sums(at, d_ri, land_ri, total_ri, w_send.at[0], w_recv.at[0])
+    ro = Sums(at, d_ro, land_ro, total_ro, w_send.at[1], w_recv.at[1])
+    first, second = pl.ds(0, rows), pl.ds(rows, rows)
+    left, right = pl.ds(0, half_model), pl.ds(half_model, half_model)
+    halves = (first, second)
+
+    def move(k, src, dst, where):
+        return remote(src, dst, m_send.at[k], m_recv.at[k], where)
+
+    e_core = [move(i, part_out.at[h], part_in.at[h], at.core) for i, h in enumerate(halves)]
+    e_y = [move(2 + i, y_out.at[h], y_in.at[h], at.over_y) for i, h in enumerate(halves)]
+    mean_y = move(4, mean_ref, mean_in, at.over_y)
+    out_move = move(5, out_ref.at[second], out_ref.at[first], at.behind)
+    gates_x = move(6, gates_ref, gates_in.at[0], at.beside)
+    gates_z = move(7, gates_in.at[0], gates_in.at[1], at.ahead)
+    gates_end = move(8, gates_out.at[0], gates_out.at[0], at.behind)
+    gates_core = move(9, gates_out.at[0], gates_out.at[1], at.core)
+    sums_x = move(10, sums_ref, sums_in.at[0], at.beside)
+    sums_z = move(11, sums_in.at[0], sums_in.at[1], at.ahead)
+    sums_end = move(12, sums_out.at[0], sums_out.at[0], at.behind)
+    sums_core = move(13, sums_out.at[0], sums_out.at[1], at.core)
+    term_x = move(14, term_ref, term_land.at[0], at.beside)
+    term_z = move(15, term_land.at[0], term_land.at[1], at.ahead)
+    term_core = move(16, term_land.at[1], term_land.at[2], at.core)
+    term_end = move(17, term_out, term_out, at.behind)
+    tok_load = pltpu.make_async_copy(tok_ref.at[:, left], tok_left, local_sem.at[0])
+
+    def add(into, value):
+        add_rows(into, value)
+
+    def finish(w, last, parts):
+        last[...] = parts[0][...]
+        add_rows(last, parts[1], parts[2] if len(parts) == 3 else None)
+        w.hop(11, last).start()
+        w.total[0] = last[w.rows_of(at.c), :]
+
+    at.meet()
+
+    @pl.when(at.serves)
+    def _():
+        for w in (ro, ri):
+            w.received(5, 6)
+            w.start(10)
+        sums_end.wait_recv()
+        sums_core.start()
+        gates_end.wait_recv()
+        gates_core.start()
+        for w, last in ((ro, last_ro), (ri, last_ri)):
+            w.received(9, 10)
+            finish(w, last, (w.land.at[2], w.land.at[3]))
+        for w, last in ((ro, last_ro), (ri, last_ri)):
+            w.hop(11, last).wait()
+            w.sent(*serve_hops)
+        out_move.wait_recv()
+        term_end.wait_recv()
+        sums_core.wait()
+        gates_core.wait()
+
+    @pl.when(at.works)
+    def _():
+        tok_load.start()
+        gates_x.start()
+        sums_x.start()
+
+        def partial(b):
+            here = columns_at(cols, b, size)
+
+            def product(mine_ref, theirs_ref, column_ref):
+                total = lax.dot_general(
+                    mine_ref[:, here], column_ref[:own, :], contract_rows, preferred_element_type=f32
+                )
+                total = total + lax.dot_general(
+                    theirs_ref[:, here], column_ref[own:, :], contract_rows, preferred_element_type=f32
+                )
+                return total.astype(bf16)
+
+            d_ro[b] = product(db_mine, db_theirs, mixed_ref)
+            d_ri[b] = product(one_mine, one_theirs, dboth_ref)
+
+        for b, hops in ((7, (1, 2)), (5, (0,)), (6, (3,)), (3, (5,)), (1, (7,))):
+            partial(b)
+            for w in (ro, ri):
+                w.start(*hops)
+
+        def back(start, out, out_at):
+            for b in range(blocks):
+                out[out_at, columns_at(cols, b, size)] = lax.dot_general(
+                    dboth_ref[pl.ds(start, rows), :], w_ri[b], contract_cols, preferred_element_type=f32
+                ).astype(out.dtype)
+
+        for i, h in enumerate(halves):
+            back(own + i * rows, part_out, h)
+            e_core[i].start()
+        for b in (4, 2, 0):
+            partial(b)
+        for w in (ro, ri):
+            w.step(4, add)
+            w.step(6, add)
+            w.step(8, add)
+        for i, h in enumerate(halves):
+            back(i * rows, part_sum, first)
+            e_core[i].wait_recv()
+            e_ref[h, :] = part_sum[:, left] + part_in[h, left].astype(f32)
+            y_out[h, :] = (part_sum[:, right] + part_in[h, right].astype(f32)).astype(bf16)
+            e_y[i].start()
+        sums_x.wait_recv()
+        sums_in[0] = sums_in[0] + sums_ref[...]
+        sums_z.start()
+        gates_x.wait_recv()
+        for k in range(2):
+            add_rows(gates_in.at[0, k], gates_ref.at[k])
+        gates_z.start()
+        for w in (ro, ri):
+            w.step(9, add)
+        sums_z.wait_recv()
+        sums_out[0] = sums_in[0] + sums_in[1]
+        sums_end.start()
+        sums_core.start()
+        gates_z.wait_recv()
+        for k in range(2):
+            gates_out[0, k] = gates_in[0, k]
+            add_rows(gates_out.at[0, k], gates_in.at[1, k])
+        gates_end.start()
+        gates_core.start()
+        term_ref[...] = term_in[...]
+        tok_load.wait()
+        for i in range(2):
+            e_y[i].wait_recv()
+            norm_sums(e_ref, y_in, tok_left, gain_ref, 0, mean_ref, i * rows, rows)
+        mean_y.start()
+        for w, last in ((ro, last_ro), (ri, last_ri)):
+            w.received(7, 8)
+            finish(w, last, (w.partial.at[0], w.land.at[3], w.land.at[4]))
+        mean_y.wait_recv()
+
+        def keep(row_at, value):
+            out_ref[row_at, :] = (value + dmid_ref[row_at, :]).astype(bf16)
+
+        for i in (1, 0):
+            norm_rows_back(
+                e_ref, tok_left, gain_ref, 0, scale_ref, mean_ref, mean_in, term_ref, model,
+                i * rows, rows, keep,
+            )
+            if i == 1:
+                out_move.start()
+        term_x.start()
+        term_x.wait_recv()
+        term_land[0] = term_land[0] + term_ref[...]
+        term_z.start()
+        term_z.wait_recv()
+        term_land[1] = term_land[0] + term_land[1]
+        term_core.start()
+        term_core.wait_recv()
+        term_out[...] = term_land[1] + term_land[2]
+        term_end.start()
+        for w, last in ((ro, last_ro), (ri, last_ri)):
+            w.hop(11, last).wait()
+            w.sent(*work_hops)
+        sums_core.wait_recv()
+        gates_core.wait_recv()
+        for moved in (
+            *e_core, *e_y, mean_y, out_move, gates_x, gates_z, gates_end, gates_core,
+            sums_x, sums_z, sums_end, sums_core, term_x, term_z, term_core, term_end,
+        ):
+            moved.wait_send()
+
+
 in_vmem = pl.BlockSpec(memory_space=pltpu.VMEM)
 in_smem = pl.BlockSpec(memory_space=pltpu.SMEM)
 in_any = pl.BlockSpec(memory_space=pl.ANY)
@@ -705,33 +1191,115 @@
             copy_sem((18,)),
             copy_sem((3,)),
         ],
-        compiler_params=pltpu.CompilerParams(
-            vmem_limit_bytes=60 * 2**20, collective_id=0, has_side_effects=True
-        ),
+        compiler_params=comm_params(0),
         cost_estimate=no_cost,
         name="gather_and_recur",
     )(*keeps, *gives, tokens, out_grad, mask, gains, vectors, wr, wi)
 
 
-def run_recur_backward(d_branch, weight, cols, both, state, mask, vectors, wr, wi):
-    rows, width = both.shape[0], wr.shape[0]
-    square = jax.ShapeDtypeStruct((width, width), f32)
+def comm_params(collective):
+    return pltpu.CompilerParams(
+        vmem_limit_bytes=63 * 2**20, collective_id=collective, has_side_effects=True
+    )
+
+
+def run_backward(
+    count, partials, e_parts, o_parts, low, middle, scales, gains, weight, both, state, mask, vectors, wr, wi
+):
+    own, half_model = middle.shape
+    model, width, rows = 2 * half_model, wr.shape[0], own // 2
+    size = weight.shape[1]
+    shape = jax.ShapeDtypeStruct
+    hidden = [v.shape[2] for v in partials]
+    square = shape((width, width), f32)
+    wide = shape((own, model), bf16)
     return pl.pallas_call(
-        recur_backward,
+        functools.partial(backward_kernel, count),
         out_shape=(
-            jax.ShapeDtypeStruct((rows, 2 * width), bf16),
-            jax.ShapeDtypeStruct((8, width), f32),
+            *[shape((5, size, n), bf16) for n in hidden],
+            *[shape((2, size // 2, n), bf16) for n in hidden],
+            shape((own, half_model), bf16),
+            shape((own, half_model), f32),
+            wide,
+            wide,
+            shape((2 * own, 2 * width), bf16),
+            shape((8, width), f32),
             square,
             square,
+            shape((8, half_model), f32),
         ),
-        in_specs=[in_vmem] * 3 + [in_smem] + [in_vmem] * 6,
-        out_specs=[in_vmem] * 4,
-        scratch_shapes=[pltpu.VMEM(lane_shape(rows, width), f32)] * 2
-        + [pltpu.VMEM((rows, width), f32)],
-        compiler_params=kernel_params,
+        in_specs=[in_any] * 7 + [in_vmem] * 10,
+        out_specs=[in_any] * 4 + [in_vmem] * 9,
+        scratch_shapes=[
+            pltpu.VMEM(lane_shape(2 * own, width), f32),
+            pltpu.VMEM(lane_shape(2 * own, width), f32),
+            pltpu.VMEM((2 * own, width), f32),
+            pltpu.VMEM((own, model), bf16),
+            pltpu.VMEM((own, model), bf16),
+            pltpu.VMEM((rows, model), f32),
+            *[pltpu.VMEM((own, half_model), bf16)] * 4,
+            pltpu.VMEM((own, lanes), f32),
+            pltpu.VMEM((own, lanes), f32),
+            pltpu.VMEM((size, max(hidden)), bf16),
+            pltpu.VMEM((size, max(hidden)), bf16),
+            copy_sem((2, 12)),
+            copy_sem((2, 12)),
+            copy_sem((14,)),
+            copy_sem((14,)),
+            copy_sem((5,)),
+        ],
+        compiler_params=comm_params(1),
         cost_estimate=no_cost,
-        name="recur_backward",
-    )(*d_branch, weight, cols, both, state, mask, vectors, wr, wi)
+        name="sum_and_recur_back",
+    )(*partials, *e_parts, *o_parts, low, middle, scales, gains, weight, both, state, mask, vectors, wr, wi)
+
+
+def run_finish(
+    count, normed, d_branch, d_both, mixed, weight, tokens, scales, gains, d_middle, sums, gates, term
+):
+    own, half_model = d_middle.shape
+    model, rows = 2 * half_model, own // 2
+    size = weight.shape[1]
+    widths = [weight.shape[2], mixed.shape[1]]
+    shape = jax.ShapeDtypeStruct
+    return pl.pallas_call(
+        functools.partial(finish_kernel, count),
+        out_shape=(
+            *[shape((2, size // 2, n), bf16) for n in widths],
+            shape((own, half_model), bf16),
+            shape((2, *gates.shape), bf16),
+            shape((2, *sums.shape), f32),
+            shape(term.shape, f32),
+        ),
+        in_specs=[in_vmem] * 7 + [in_any] + [in_vmem] * 6,
+        out_specs=[in_vmem] * 6,
+        scratch_shapes=[
+            *[pltpu.VMEM((blocks, size, n), bf16) for n in widths],
+            *[pltpu.VMEM((5, size, n), bf16) for n in widths],
+            pltpu.VMEM((own, half_model), bf16),
+            pltpu.VMEM((own, model), bf16),
+            pltpu.VMEM((own, model), bf16),
+            pltpu.VMEM((rows, model), f32),
+            pltpu.VMEM((own, half_model), bf16),
+            pltpu.VMEM((own, half_model), bf16),
+            pltpu.VMEM((own, half_model), f32),
+            pltpu.VMEM((own, lanes), f32),
+            pltpu.VMEM((own, lanes), f32),
+            *[pltpu.VMEM((size, n), bf16) for n in widths],
+            pltpu.VMEM((2, *gates.shape), bf16),
+            pltpu.VMEM((2, *sums.shape), f32),
+            pltpu.VMEM(term.shape, f32),
+            pltpu.VMEM((3, *term.shape), f32),
+            copy_sem((2, 12)),
+            copy_sem((2, 12)),
+            copy_sem((18,)),
+            copy_sem((18,)),
+            copy_sem((1,)),
+        ],
+        compiler_params=comm_params(2),
+        cost_estimate=no_cost,
+        name="sum_and_finish",
+    )(*normed, *d_branch, d_both, mixed, weight, tokens, scales, gains, d_middle, sums, gates, term)
 
 
 def run_mlp_forward(normed, weight, cols):
@@ -892,22 +1460,6 @@
     outer = jnp.where(z < 2, 0, 3)
     far = 3 - z
     far_outer = 3 - outer
-    worker = (z == 1) | (z == 2)
-
-    def mover(move):
-        table = pairs(n_dp, move)
-        return lambda value: lax.ppermute(value, "dp", table)
-
-    swap_c = mover(lambda z, x, c: (z, x, 1 - c))
-    swap_x = mover(lambda z, x, c: (z, 1 - x, c))
-    swap_x_work = mover(lambda z, x, c: (z, 1 - x, c) if z in (1, 2) else None)
-    swap_x_ends = mover(lambda z, x, c: (z, 1 - x, c) if z in (0, 3) else None)
-    inward = mover(lambda z, x, c: {0: (1, x, c), 3: (2, x, c)}.get(z))
-    outward = mover(lambda z, x, c: {1: (0, x, c), 2: (3, x, c)}.get(z))
-    across = mover(lambda z, x, c: {1: (2, x, c), 2: (1, x, c)}.get(z))
-
-    def swap_y(value):
-        return lax.ppermute(value, "mp", [(0, 1), (1, 0)])
 
     def pick_c(first, second):
         return jnp.where(c == 0, first, second)
@@ -933,29 +1485,9 @@
         ]
     ).astype(jnp.int32)
 
-    def added(*values):
-        return sum(v.astype(f32) for v in values).astype(bf16)
-
-    def scatter_grad(pieces, by_x):
-        own, own_x, near, near_x, across_one, across_x, across_near, across_near_x = pieces
-        if by_x:
-            across_near = added(across_near, swap_x_work(across_near_x))
-            across_one = added(across_one, swap_x_work(across_x))
-        else:
-            near_x = added(near_x, across(across_near_x))
-            across_one = added(across_one, swap_x_work(across_x))
-        near = added(near, across(across_near))
-        out_other = outward(near_x)
-        own_sum = swap_x_work(own_x)
-        far_sum = across(across_one)
-        out_near = outward(near)
-        worker_total = own.astype(f32) + own_sum.astype(f32) + far_sum.astype(f32)
-        end_total = out_near.astype(f32) + swap_x_ends(out_other).astype(f32)
-        total = jnp.where(worker, worker_total, end_total).astype(bf16)
-        top, bottom = total[:group_rows], total[group_rows:]
-        mine = pick_c(top, bottom)
-        arrived = swap_c(pick_c(bottom, top))
-        first, second = pick_c(mine, arrived).astype(f32), pick_c(arrived, mine).astype(f32)
+    def settle_grad(total):
+        first, second = pick_c(total[0], total[1]), pick_c(total[1], total[0])
+        first, second = first.astype(f32), second.astype(f32)
         if outer_count > 1:
             first, second = (
                 lax.psum_scatter(
@@ -965,28 +1497,12 @@
             )
         return first, second
 
-    def whole_features(half_rows):
-        return jnp.concatenate([half_rows, swap_y(half_rows)], axis=1)
-
-    def both_cores(rows_value):
-        return rows_value, swap_c(rows_value)
-
-    def sum_partials(name, parts, weight):
-        theirs = swap_c(run_rows_back(name + "_theirs", parts, weight, cols, 1, bf16))
-        mine = run_rows_back(name + "_mine", parts, weight, cols, 0, f32) + theirs.astype(f32)
-        arrived = swap_y(mine[:, half_model:].astype(bf16))
-        return mine[:, :half_model] + arrived.astype(f32)
+    def over_groups(value):
+        return lax.psum(value, "dp", axis_index_groups=outer_groups) if outer_count > 1 else value
 
     def relative(vector):
         first, second = vector[:half_model], vector[half_model:]
         return jnp.concatenate([pick_y(first, second), pick_y(second, first)])
-
-    def norm_back(source, scale_rows, gain, grad_rows):
-        weighted = grad_rows * gain
-        part = jnp.sum(weighted * source, axis=1, keepdims=True)
-        inner_mean = (part + swap_y(part)) / model
-        back_rows = scale_rows * weighted - source * (scale_rows * scale_rows * scale_rows) * inner_mean
-        return back_rows, jnp.sum(grad_rows * source * scale_rows, axis=0)
 
     def quarters(value, axis):
         size = value.shape[axis] // 2
@@ -1032,69 +1548,77 @@
         *rows_kept, scales,
     ) = run_forward(outer_count, keeps, gives, tokens, out_grad, mask, gains, vectors, wr, wi)
     normed, normed_two, grad_low = rows_kept[0:2], rows_kept[2:4], rows_kept[4:6]
-    scale_one, scale_two = scales[0, :, :1], scales[1, :, :1]
-    tokens_two = tokens_all[:, :half_model]
-    live = mask[:own_rows, 4:5]
-    live_grad = grad_low[0][:, :half_model].astype(f32)
-    middle_low = middle.astype(bf16)
 
     act, gate_slope, gate_value = run_mlp_forward(normed_two, mlp_in_all, cols)
-    mlp_out_grad = scatter_grad(
-        run_weight_partial("mlp_out_partial", grad_low, (act,), cols), True
+    d_pair = run_mlp_backward(grad_low, mlp_out_all, cols, gate_slope, gate_value)
+
+    def both_halves(name, parts, weight):
+        return (
+            run_rows_back(name + "_theirs", parts, weight, cols, 1, bf16),
+            run_rows_back(name + "_mine", parts, weight, cols, 0, f32),
+        )
+
+    partials = (
+        run_weight_partial("mlp_in_partial", normed_two, d_pair, cols),
+        run_weight_partial("mlp_out_partial", grad_low, (act,), cols),
     )
-    d_pair = run_mlp_backward(grad_low, mlp_out_all, cols, gate_slope, gate_value)
-    e_two = sum_partials("mlp_in_back", d_pair, mlp_in_all)
-    mlp_in_grad = scatter_grad(
-        run_weight_partial("mlp_in_partial", normed_two, d_pair, cols), False
+    (
+        _, _, mlp_in_total, mlp_out_total,
+        output_two, d_middle, d_branch, d_branch_theirs, d_both, sums, square_recur, square_input, term,
+    ) = run_backward(
+        outer_count,
+        partials,
+        both_halves("mlp_in_back", d_pair, mlp_in_all),
+        both_halves("mlp_out", (act,), mlp_out_all),
+        grad_low[0],
+        middle,
+        scales,
+        gains,
+        rnn_out_all,
+        both,
+        state,
+        mask,
+        vectors,
+        wr,
+        wi,
     )
-    back_two, gain_two_term = norm_back(
-        middle_low.astype(f32), scale_two, gain_two[:half_model], e_two
+    gates = jnp.stack(
+        [
+            diagonal_blocks(v, heads).reshape(-1, gate_recur.shape[1]).astype(bf16)
+            for v in (square_recur, square_input)
+        ]
     )
-    d_middle = live_grad + back_two
-    d_branch = both_cores(whole_features(d_middle.astype(bf16)))
-    rnn_out_grad = scatter_grad(
-        run_weight_partial("rnn_out_partial", d_branch, (mixed,), cols), True
+    rnn_in_total, rnn_out_total, tokens_grad_two, gates, sums, term = run_finish(
+        outer_count,
+        normed,
+        (d_branch, d_branch_theirs),
+        d_both,
+        mixed,
+        rnn_in_all,
+        tokens_all,
+        scales,
+        gains,
+        d_middle,
+        sums,
+        gates,
+        term,
     )
-    branch_two = sum_partials("mlp_out", (act,), mlp_out_all)
-    output_two = (live * (middle + branch_two)).astype(bf16)
-
-    d_both, sums, square_recur, square_input = run_recur_backward(
-        d_branch, rnn_out_all, cols, both, state, mask, vectors, wr, wi
+    layer_output, tokens_grad = output_two[:buffer_rows], tokens_grad_two[:buffer_rows]
+    mlp_in_grad, mlp_out_grad, rnn_in_grad, rnn_out_grad = (
+        settle_grad(v) for v in (mlp_in_total, mlp_out_total, rnn_in_total, rnn_out_total)
     )
-    rnn_in_grad = scatter_grad(run_weight_partial("rnn_in_partial", normed, (d_both,), cols), True)
-    e_one = sum_partials("rnn_in_back", (d_both,), rnn_in_all)
-    back_one, gain_one_term = norm_back(
-        tokens_two.astype(f32), scale_one, gain_one[:half_model], e_one
-    )
-    tokens_grad_two = (d_middle + back_one).astype(bf16)
-
-    def settle(two):
-        return jnp.where(worker, two[:buffer_rows], outward(two[buffer_rows:]))
-
-    layer_output = settle(output_two)
-    tokens_grad = settle(tokens_grad_two)
-
-    def total(value, dtype=f32):
-        value = jnp.where(worker, value, 0).astype(dtype)
-        if outer_count > 1:
-            value = lax.psum(value, "dp", axis_index_groups=outer_groups)
-        value = value + swap_x(value)
-        value = value + across(value)
-        return jnp.where(worker, value, outward(value))
-
-    def both_quarters(value, axis=0):
-        arrived = swap_c(value)
-        return pick_c(
-            jnp.concatenate([value, arrived], axis=axis), jnp.concatenate([arrived, value], axis=axis)
+
+    def both_quarters(pair, axis):
+        return over_groups(
+            pick_c(
+                jnp.concatenate([pair[0], pair[1]], axis=axis),
+                jnp.concatenate([pair[1], pair[0]], axis=axis),
+            )
         )
 
-    sums = both_quarters(total(sums), 1)
-    gate_grads = jnp.concatenate(
-        [diagonal_blocks(square_recur, heads), diagonal_blocks(square_input, heads)], axis=2
-    )
-    gate_grads = both_quarters(total(gate_grads, bf16)).astype(f32)
-    gains = total(jnp.stack([gain_one_term, gain_two_term]))
-    gains = gains + swap_c(gains)
+    sums = both_quarters(sums, 1)
+    gates = both_quarters(gates.astype(f32), 1)
+    gains_grad = over_groups(term[:2])
     size = gate_recur.shape[1]
 
     def pair_layout(halves):
@@ -1110,17 +1634,17 @@
     return (
         layer_output,
         tokens_grad,
-        gains[0],
+        gains_grad[0],
         pair_layout(rnn_in_grad),
-        gate_grads[:, :, :size],
-        gate_grads[:, :, size:],
+        gates[0].reshape(-1, size, size),
+        gates[1].reshape(-1, size, size),
         sums[5],
         sums[6],
         8.0 * jax.nn.sigmoid(-decay_param) * sums[7],
         sums[:4],
         sums[4],
         jnp.concatenate(rnn_out_grad, axis=1),
-        gains[1],
+        gains_grad[1],
         pair_layout(mlp_in_grad),
         jnp.concatenate(mlp_out_grad, axis=1),
     )

time: 845 us -> 704 us (0.83)
  waiting for transfers between devices: 275 us -> 0 us
  Pallas kernels: 395 us -> 648 us
  starting transfers between devices: 65.3 us -> 0 us
  other arithmetic: 50.6 us -> 23.2 us
  local copies, waits for them, and re-layouts: 50.6 us -> 25.5 us
    pallas_call x1 -> x2, Pallas kernels: 43.2 us -> 334 us  [the longest x1 201 us: run_backward(): pl.pallas_call(functools.partial(backward_kernel, count), out_shape=(*[sh...]
    ppermute x60 -> x0, waiting for transfers between devices: 275 us -> none  [the longest x54 210 us: mover(): return lambda value: lax.ppermute(value, 'dp', table)]
    ppermute x60 -> x0, starting transfers between devices: 65.3 us -> none  [the longest x54 56 us: mover(): return lambda value: lax.ppermute(value, 'dp', table)]
    convert_element_type x17 -> x5, other arithmetic: 26.3 us -> 2.92 us  [the longest x4 2.68 us: settle_grad(): first, second = (first.astype(f32), second.astype(f32))]
    pallas_call x4 -> x2, Pallas kernels: 50.9 us -> 30.4 us  [run_weight_partial(): pl.pallas_call(functools.partial(weight_partial, tiles), grid=(sum(tiles)...]
    pallas_call x6 -> x4, Pallas kernels: 63.5 us -> 45.6 us  [run_rows_back(): pl.pallas_call(functools.partial(rows_back, tiles), grid=(sum(tiles),), o...]
    another operation x4 -> x0, local copies, waits for them, and re-layouts: 14.5 us -> none  [scatter_grad(): own, own_x, near, near_x, across_one, across_x, across_near, across_near_...]
  transfers between devices with their start and end apart: 60 -> 0, of which waited for: 26 -> 0; matrix products, arithmetic and copies ran while one was open for 7% -> 0% of each run, Pallas kernels for 13% -> 0%
where the time goes in v3:
time: 704 us; the launch traced here: 698 us
  Pallas kernels  648 us (92%)
  local copies, waits for them, and re-layouts  25.5 us (4%)
  other arithmetic  23.2 us (3%)
    pallas_call x1, Pallas kernels, run_backward(): pl.pallas_call(functools.partial(backward_kernel, count), out_shape=(*[sh...  201 us
    pallas_call x1, Pallas kernels, run_forward(): pl.pallas_call(functools.partial(forward_kernel, count), out_shape=(*gath...  198 us
    pallas_call x1, Pallas kernels, run_finish(): pl.pallas_call(functools.partial(finish_kernel, count), out_shape=(*[shap...  133 us
    pallas_call x4, Pallas kernels, run_rows_back(): pl.pallas_call(functools.partial(rows_back, tiles), grid=(sum(tiles),), o...  45.6 us
    pallas_call x2, Pallas kernels, run_weight_partial(): pl.pallas_call(functools.partial(weight_partial, tiles), grid=(sum(tiles)...  30.4 us
    pallas_call x1, Pallas kernels, run_mlp_forward(): pl.pallas_call(mlp_forward, grid=(tiles,), out_shape=(out, out, out), in_...  24.9 us
    pallas_call x1, Pallas kernels, run_mlp_backward(): pl.pallas_call(mlp_backward, grid=(hidden // tile,), out_shape=(out, out)...  15.5 us

profile of v3, /device:TPU:0, one launch (start us, length us, event | category | flops | bytes accessed | tf_op | source)
XLA Modules:
  0.0 698.2 jit_solution(4704874448839714568)
XLA Ops:
  0.8 0.6 stack.139.cols_ref.refs_3_.refs_2_
  1.4 0.8 reduce_window_sum.11
  2.2 0.6 slice.281
  2.8 0.7 subtract_bitcast_fusion
  3.5 0.7 compare_convert_fusion.1
  4.2 0.7 convert_element_type.150
  4.9 0.7 convert_element_type.151
  5.6 0.6 pad_maximum_fusion.9.gain_ref
  6.2 0.8 slice_select_fusion.4
  7.1 0.9 compare_select_fusion
  8.0 0.9 slice_select_fusion.2
  8.8 0.6 concatenate.69.vec_ref
  9.6 0.7 pad.32.mask_in
  10.3 1.9 broadcast_select_fusion.6
  12.4 1.2 fusion.12.wr_ref
  13.5 1.2 fusion.15.wi_ref
  14.7 0.9 broadcast_select_fusion.2
  15.6 2.0 fusion.23
  17.8 1.1 broadcast_select_fusion.4
  19.2 2.2 fusion.20
  21.7 1.5 broadcast_select_fusion
  23.1 198.3 %gather_and_recur.1 = (bf16[8,256,1408]{2,1,0:T(8,128)(2,1)}, bf16[8,256,704]{2,1,0:T(8,128)(2,1)}, bf16[8,256,3072]{2,1,0:T(8,128)(2,1)}, bf16[8,256,1536]{2,1,...) custom-call(bf16[128,1408]{1,0:T(8,128)(2,1)} %get-tuple-element.186, ...), custom_call_target="tpu_custom_call" | custom-call | tf_op jit(solution)/shard_map/gather_and_recur/pallas_call | solution.py:1161
  221.4 24.9 %mlp_forward.1 = (bf16[1024,1536]{1,0:T(8,128)(2,1)}, bf16[1024,1536]{1,0:T(8,128)(2,1)}, bf16[1024,1536]{1,0:T(8,128)(2,1)}) custom-call(bf16[512,2048]{1,0:T(8,128)(2,1)} %get-tuple-element.54.mine_ref, bf16[512,2048]{1,0:T(8,128)(2,1)} %get-tuple-element.55.theirs_ref, bf16[8,256,3072]{2,1,0:T(8,128)(2,1)} %get-tuple-element.59.gate_weight.up_weight.refs_2_, ...), custom_call_target="tpu_custom_call" | custom-call | tf_op jit(solution)/shard_map/mlp_forward/pallas_call | solution.py:1311
  246.4 15.5 %mlp_backward.1 = (bf16[1024,1536]{1,0:T(8,128)(2,1)}, bf16[1024,1536]{1,0:T(8,128)(2,1)}) custom-call(bf16[512,2048]{1,0:T(8,128)(2,1)} %get-tuple-element.56.mine_ref.low_ref, bf16[512,2048]{1,0:T(8,128)(2,1)} %get-tuple-element.57.theirs_ref, bf16[8,256,1536]{2,1,0:T(8,128)(2,1)} %get-tuple-element.58.weight_ref.refs_1_, ...), custom_call_target="tpu_custom_call" | custom-call | tf_op jit(solution)/shard_map/mlp_backward/pallas_call | solution.py:1332
  261.9 13.5 %mlp_in_back_theirs.1.e_theirs = bf16[512,2048]{1,0:T(8,128)(2,1)} custom-call(bf16[1024,1536]{1,0:T(8,128)(2,1)} %get-tuple-element.62.refs_0_, bf16[1024,1536]{1,0:T(8,128)(2,1)} %get-tuple-element.63.refs_1_, bf16[8,256,3072]{2,1,0:T(8,128)(2,1)} %get-tuple-element.59.gate_weight.up_weight.refs_2_, s32[8]{0:T(128)} %stack.139.cols_ref.refs_3_.refs_2_), custom_call_target="tpu_custom_call" | custom-call | tf_op jit(solution)/shard_map/mlp_in_back_theirs/pallas_call | solution.py:1369
  275.4 14.2 %mlp_in_back_mine.1.e_mine = f32[512,2048]{1,0:T(8,128)} custom-call(bf16[1024,1536]{1,0:T(8,128)(2,1)} %get-tuple-element.62.refs_0_, bf16[1024,1536]{1,0:T(8,128)(2,1)} %get-tuple-element.63.refs_1_, bf16[8,256,3072]{2,1,0:T(8,128)(2,1)} %get-tuple-element.59.gate_weight.up_weight.refs_2_, s32[8]{0:T(128)} %stack.139.cols_ref.refs_3_.refs_2_), custom_call_target="tpu_custom_call" | custom-call | tf_op jit(solution)/shard_map/mlp_in_back_mine/pallas_call | solution.py:1369
  289.6 19.1 %mlp_in_partial.1.d_mi = bf16[8,256,3072]{2,1,0:T(8,128)(2,1)} custom-call(bf16[512,2048]{1,0:T(8,128)(2,1)} %get-tuple-element.54.mine_ref, bf16[512,2048]{1,0:T(8,128)(2,1)} %get-tuple-element.55.theirs_ref, s32[8]{0:T(128)} %stack.139.cols_ref.refs_3_.refs_2_, bf16[1024,1536]{1,0:T(8,128)(2,1)} %get-tuple-element.62.refs_0_, ...), custom_call_target="tpu_custom_call" | custom-call | tf_op jit(solution)/shard_map/mlp_in_partial/pallas_call | solution.py:1388
  308.8 8.6 %mlp_out_theirs.1.o_theirs = bf16[512,2048]{1,0:T(8,128)(2,1)} custom-call(bf16[1024,1536]{1,0:T(8,128)(2,1)} %get-tuple-element.64.refs_0_, bf16[8,256,1536]{2,1,0:T(8,128)(2,1)} %get-tuple-element.58.weight_ref.refs_1_, s32[8]{0:T(128)} %stack.139.cols_ref.refs_3_.refs_2_), custom_call_target="tpu_custom_call" | custom-call | tf_op jit(solution)/shard_map/mlp_out_theirs/pallas_call | solution.py:1369
  317.4 9.2 %mlp_out_mine.1.o_mine = f32[512,2048]{1,0:T(8,128)} custom-call(bf16[1024,1536]{1,0:T(8,128)(2,1)} %get-tuple-element.64.refs_0_, bf16[8,256,1536]{2,1,0:T(8,128)(2,1)} %get-tuple-element.58.weight_ref.refs_1_, s32[8]{0:T(128)} %stack.139.cols_ref.refs_3_.refs_2_), custom_call_target="tpu_custom_call" | custom-call | tf_op jit(solution)/shard_map/mlp_out_mine/pallas_call | solution.py:1369
  326.6 11.3 %mlp_out_partial.1.d_mo = bf16[8,256,1536]{2,1,0:T(8,128)(2,1)} custom-call(bf16[512,2048]{1,0:T(8,128)(2,1)} %get-tuple-element.56.mine_ref.low_ref, bf16[512,2048]{1,0:T(8,128)(2,1)} %get-tuple-element.57.theirs_ref, s32[8]{0:T(128)} %stack.139.cols_ref.refs_3_.refs_2_, bf16[1024,1536]{1,0:T(8,128)(2,1)} %get-tuple-element.64.refs_0_), custom_call_target="tpu_custom_call" | custom-call | tf_op jit(solution)/shard_map/mlp_out_partial/pallas_call | solution.py:1388
  337.8 200.8 %sum_and_recur_back.1 = (bf16[5,256,3072]{2,1,0:T(8,128)(2,1)}, bf16[5,256,1536]{2,1,0:T(8,128)(2,1)}, bf16[2,128,3072]{2,1,0:T(8,128)(2,1)}, bf16[2,128,1536]{2...) custom-call(bf16[8,256,3072]{2,1,0:T(8,128)(2,1)} %mlp_in_partial.1., ...), custom_call_target="tpu_custom_call" | custom-call | tf_op jit(solution)/shard_map/sum_and_recur_back/pallas_call | solution.py:1216
  538.7 1.9 slice.308
  540.5 1.3 select_bitcast_fusion.1
  541.9 1.3 maximum_convert_fusion
  543.5 1.3 copy-done.2
  545.1 1.0 pad_maximum_fusion.4.gates_ref
  546.1 132.7 %sum_and_finish.1 = (bf16[2,128,1408]{2,1,0:T(8,128)(2,1)}, bf16[2,128,704]{2,1,0:T(8,128)(2,1)}, bf16[512,1024]{1,0:T(8,128)(2,1)}, bf16[2,2,704,176]{3,2,1,0:T...) custom-call(bf16[512,2048]{1,0:T(8,128)(2,1)} %get-tuple-element.72.one_mine, ...), custom_call_target="tpu_custom_call" | custom-call | tf_op jit(solution)/shard_map/sum_and_finish/pallas_call | solution.py:1265
  678.9 1.9 slice.317
  680.8 1.4 fusion.24
  682.3 0.8 slice_bitcast_fusion.19
  683.1 0.6 slice.378
  683.7 0.7 slice_reduce_fusion
  684.4 0.6 multiply_multiply_fusion
  685.0 1.1 select_bitcast_fusion.3
  686.0 1.0 maximum_convert_fusion.1
  687.9 2.2 copy.75
  691.0 1.8 fusion.17
  693.9 4.1 copy.76
  (62 shorter events, 4.6 us)
Async XLA Ops:
  0.6 11.6 %copy-start.7 = (bf16[8,176,176]{2,1,0:T(8,128)(2,1)S(1)}, bf16[8,176,176]{2,1,0:T(8,128)(2,1)}, u32[]{:S(2)}) copy-start(bf16[8,176,176]{2,1,0:T(8,128)(2,1)} %param.20) | copy-start | bytes 1486852
  0.7 11.5 %copy-start.8 = (bf16[8,176,176]{2,1,0:T(8,128)(2,1)S(1)}, bf16[8,176,176]{2,1,0:T(8,128)(2,1)}, u32[]{:S(2)}) copy-start(bf16[8,176,176]{2,1,0:T(8,128)(2,1)} %param.19) | copy-start | bytes 1486852
  12.3 2.4 copy-start.6
  12.4 3.3 copy-start.1
  17.7 1.6 copy-start
  540.5 2.6 copy-start.3
  543.2 1.6 copy-start.2
  546.1 138.2 %copy-start.10 = (f32[1408]{0:T(1024)S(1)}, f32[1408]{0:T(1024)}, u32[]{:S(2)}) copy-start(f32[1408]{0:T(1024)} %param.23) | copy-start | bytes 16900
  678.9 8.2 %copy-start.9 = (bf16[2,128,1408]{2,1,0:T(8,128)(2,1)S(1)}, bf16[2,128,1408]{2,1,0:T(8,128)(2,1)}, u32[]{:S(2)}) copy-start(bf16[2,128,1408]{2,1,0:T(8,128)(2,1)} %get-tuple-element.87) | copy-start | bytes 2162692
  687.9 2.2 copy-start.5
  691.0 2.0 copy-start.4

commit v4 on v3

--- a/solution.py
+++ b/solution.py
@@ -265,12 +265,18 @@
     count,
     keep_ri, keep_ro, keep_mi, keep_mo, give_ri, give_ro, give_mi, give_mo,
     tokens_ref, grad_ref, mask_in, gain_ref, vec_ref, wr_ref, wi_ref,
-    g_ri, g_ro, g_mi, g_mo,
-    both_ref, state_ref, mixed_ref, mask_ref, middle_ref, tok_ref,
-    one_mine, one_theirs, two_mine, two_theirs, low_mine, low_theirs, scale_ref,
+    g_ri, g_ro, g_mi, g_mo, *refs,
+):
+    results, refs = refs[:13], refs[13:]
+    (
+        both_ref, state_ref, mixed_ref, mask_ref, middle_ref, tok_ref,
+        one_mine, one_theirs, two_mine, two_theirs, low_mine, low_theirs, scale_ref,
+    ) = held = refs[:13]
+    refs = refs[13:]
+    (
     coef_ref, w_ri, w_ro, grad_all, part_out, part_in, part_sum, y_out, y_in, mid_ref,
-    w_send, w_recv, w_local, load_sem, m_send, m_recv, m_local,
-):
+    w_send, w_recv, w_local, load_sem, m_send, m_recv, m_local, out_sem,
+    ) = refs
     at = Place(count)
     half_rows = keep_ri.shape[0]
     size = 2 * half_rows
@@ -348,6 +354,10 @@
 
     def load(w, target, b):
         return pltpu.make_async_copy(whole[w].at[b], target.at[b], load_sem.at[w, b])
+
+    def keep_out(k):
+        source = held[k].at[:, left] if k == 5 else held[k]
+        return pltpu.make_async_copy(source, results[k], out_sem.at[k])
 
     at.meet()
 
@@ -419,14 +429,21 @@
         def keep_both(start, value):
             both_ref[pl.ds(start, chunk_rows), :] = value
 
+        keep_out(3).start()
+        keep_out(5).start()
+        keep_out(6).start()
+        keep_out(7).start()
         project(one_mine, one_theirs, w_ri, cols, keep_both)
+        keep_out(0).start()
         grad_in.wait_recv()
         grad_y_two.start()
         recur_state(both_ref, mask_ref, vec_ref, wr_ref, wi_ref, coef_ref, state_ref)
+        keep_out(1).start()
         pass_on(mi, 2, 6)
         pass_on(mi, 4, 5)
         own_block(mo, (1, 4))
         recur_mixed(both_ref, state_ref, mixed_ref)
+        keep_out(2).start()
         for b in range(blocks):
             load(ro, w_ro, b).wait()
 
@@ -454,12 +471,14 @@
         grad_y_two.wait_recv()
         low_mine[...] = (grad_all[...].astype(f32) * mask_ref[mine_rows, 4:5]).astype(bf16)
         low_core.start()
+        keep_out(10).start()
         for i, h in enumerate(halves):
             part_y[i].wait_recv()
             middle = middle_ref[h, :] + y_in[h, :].astype(f32) + tok_ref[h, left].astype(f32)
             middle_ref[h, :] = middle
             mid_ref[h, left] = middle.astype(bf16)
             mid_y[i].start()
+        keep_out(4).start()
         pass_on(mi, 6, 8)
         pass_on(mo, 2, 6)
         pass_on(mo, 4, 5)
@@ -467,14 +486,18 @@
             mid_y[i].wait_recv()
             normed_rows(mid_ref, gain_ref, 1, scale_ref, 1, two_mine, i * rows, rows)
             two_core[i].start()
+        keep_out(8).start()
+        keep_out(12).start()
         pass_on(mo, 3, 7)
         pass_on(mo, 6, 8)
         for w in (mi, mo):
             for k in (1, 5, 7, 8):
                 hop(w, k).wait_recv()
         low_core.wait_recv()
+        keep_out(11).start()
         for moved in two_core:
             moved.wait_recv()
+        keep_out(9).start()
         for w in (ri, ro, mi, mo):
             for k in (1, 4, 5, 6, 7, 8):
                 hop(w, k).wait_send()
@@ -483,6 +506,8 @@
             *part_core, *part_y, *mid_y, *two_core,
         ):
             moved.wait_send()
+        for k in range(13):
+            keep_out(k).wait()
 
 
 def recur_first(both_ref, state_ref, mask_ref, vec_ref, wr_ref, wi_ref, dmix_ref, dboth_ref, coef_ref, push_ref):
@@ -589,66 +614,6 @@
         lax.fori_loop(0, own // chunk_rows, chunk, 0)
 
 
-def mlp_backward(mine_ref, theirs_ref, weight_ref, cols_ref, slope_ref, value_ref, d_gate_ref, d_up_ref):
-    def use(start, d_act):
-        at = pl.ds(start, chunk_rows)
-        d_gate_ref[at, :] = (d_act * slope_ref[at, :].astype(f32)).astype(bf16)
-        d_up_ref[at, :] = (d_act * value_ref[at, :].astype(f32)).astype(bf16)
-
-    project(mine_ref, theirs_ref, weight_ref, cols_ref, use)
-
-
-def rows_back(part_tiles, *refs):
-    count = len(part_tiles)
-    row_refs, (weight_ref, cols_ref, out_ref, total_ref) = refs[:count], refs[count:]
-    size = weight_ref.shape[1]
-    step = pl.program_id(0)
-
-    @pl.when(step == 0)
-    def _():
-        total_ref[...] = jnp.zeros_like(total_ref)
-
-    first = 0
-    for tiles, row_ref in zip(part_tiles, row_refs):
-
-        @pl.when((step >= first) & (step < first + tiles))
-        def _(row_ref=row_ref):
-            for b in range(blocks):
-                total_ref[:, columns_at(cols_ref, b, size)] += lax.dot_general(
-                    row_ref[...], weight_ref[b], contract_cols, preferred_element_type=f32
-                )
-
-        first += tiles
-
-    @pl.when(step == first - 1)
-    def _():
-        out_ref[...] = total_ref[...].astype(out_ref.dtype)
-
-
-def weight_partial(part_tiles, mine_ref, theirs_ref, cols_ref, *refs):
-    count = len(part_tiles)
-    column_refs, out_ref = refs[:count], refs[count]
-    size = out_ref.shape[1]
-    own = mine_ref.shape[0]
-    step = pl.program_id(0)
-    first = 0
-    for tiles, column_ref in zip(part_tiles, column_refs):
-
-        @pl.when((step >= first) & (step < first + tiles))
-        def _(column_ref=column_ref):
-            for b in range(blocks):
-                at = columns_at(cols_ref, b, size)
-                total = lax.dot_general(
-                    mine_ref[:, at], column_ref[:own, :], contract_rows, preferred_element_type=f32
-                )
-                total = total + lax.dot_general(
-                    theirs_ref[:, at], column_ref[own:, :], contract_rows, preferred_element_type=f32
-                )
-                out_ref[b] = total.astype(bf16)
-
-        first += tiles
-
-
 class Sums:
     def __init__(self, at, partial, land, total, send, recv):
         self.at, self.partial, self.land, self.total = at, partial, land, total
@@ -711,7 +676,7 @@
 
 
 def add_rows(into, value, other=None):
-    size = 32
+    size = 32 if into.shape[0] % 32 == 0 else 16
 
     def chunk(i, carry):
         at = pl.ds(pl.multiple_of(i * size, size), size)
@@ -758,23 +723,43 @@
     lax.fori_loop(0, count // size, chunk, 0)
 
 
+def stream_tiles(count, fetch, body):
+    fetch(0, 0).start()
+
+    def step(t, carry):
+        slot = t % 2
+
+        @pl.when(t + 1 < count)
+        def _():
+            fetch(t + 1, 1 - slot).start()
+
+        fetch(t, slot).wait()
+        body(t, slot)
+        return carry
+
+    lax.fori_loop(0, count, step, 0)
+
+
 def backward_kernel(
     count,
-    d_mi, d_mo, e_theirs, e_mine, o_theirs, o_mine, low_ref,
-    middle_ref, scale_ref, gain_ref, w_ro, both_ref, state_ref, mask_ref, vec_ref, wr_ref, wi_ref,
-    land_mi, land_mo, total_mi, total_mo,
-    out_ref, dmid_ref, db_mine, db_theirs, dboth_ref, sums_ref, gr_ref, gi_ref, term_ref,
-    coef_ref, push_ref, dmix_ref, part_in, o_in, part_sum, y_out, y_in, oy_out, oy_in,
-    mean_ref, mean_in, stage_a, stage_b,
-    w_send, w_recv, m_send, m_recv, local_sem,
+    weight_mi, weight_mo, act_in, slope_in, value_in, two_mine, two_theirs, low_mine, low_theirs,
+    middle_in, weight_in, both_in, state_in,
+    scale_ref, gain_ref, mask_ref, vec_ref, wr_ref, wi_ref,
+    d_mi, d_mo, land_mi, land_mo, total_mi, total_mo, dmid_out, mine_out, theirs_out, dboth_out,
+    out_ref, sums_ref, gates_ref, term_ref,
+    middle_ref, dmid_ref, db_mine, db_theirs,
+    part_out, part_in, o_in, y_out, y_in, oy_out, oy_in, mean_ref, mean_in, stage_a, stage_b,
+    w_send, w_recv, m_send, m_recv, local_sem, load_sem, out_sem, tile_sem, keep_sem,
 ):
     at = Place(count)
-    size = w_ro.shape[1]
+    size = weight_mi.shape[1]
     cols = at.columns(size)
     own, half_model = middle_ref.shape
-    e_ref, low_left = dmid_ref, y_out
     model = 2 * half_model
     rows = own // 2
+    hidden = act_in.shape[1]
+    width = weight_in.shape[2]
+    e_ref, low_left = dmid_ref, y_out
     mi = Sums(at, d_mi, land_mi, total_mi, w_send.at[0], w_recv.at[0])
     mo = Sums(at, d_mo, land_mo, total_mo, w_send.at[1], w_recv.at[1])
     first, second = pl.ds(0, rows), pl.ds(rows, rows)
@@ -784,8 +769,8 @@
     def move(k, src, dst, where):
         return remote(src, dst, m_send.at[k], m_recv.at[k], where)
 
-    e_core = [move(i, e_theirs.at[h], part_in.at[h], at.core) for i, h in enumerate(halves)]
-    o_core = [move(2 + i, o_theirs.at[h], o_in.at[h], at.core) for i, h in enumerate(halves)]
+    e_core = [move(i, part_out.at[h], part_in.at[h], at.core) for i, h in enumerate(halves)]
+    o_core = [move(2 + i, part_out.at[h], o_in.at[h], at.core) for i, h in enumerate(halves)]
     e_y = [move(4 + i, y_out.at[h], y_in.at[h], at.over_y) for i, h in enumerate(halves)]
     o_y = [move(6 + i, oy_out.at[h], oy_in.at[h], at.over_y) for i, h in enumerate(halves)]
     mean_y = move(8, mean_ref, mean_in, at.over_y)
@@ -795,15 +780,22 @@
     ]
     db_core = [move(11 + i, db_mine.at[h], db_theirs.at[h], at.core) for i, h in enumerate(halves)]
     out_move = move(13, out_ref.at[second], out_ref.at[first], at.behind)
-    low_load = pltpu.make_async_copy(low_ref.at[:, left], low_left, local_sem.at[0])
+    low_load = pltpu.make_async_copy(low_mine.at[:, left], low_left, local_sem.at[0])
+    middle_load = pltpu.make_async_copy(middle_in, middle_ref, local_sem.at[4])
+    keep_out = [
+        pltpu.make_async_copy(src, dst, out_sem.at[k])
+        for k, (src, dst) in enumerate(
+            ((dmid_ref, dmid_out), (db_mine, mine_out), (db_theirs, theirs_out))
+        )
+    ]
 
     def fetch(src, dst, k):
         return pltpu.make_async_copy(src, dst, local_sem.at[k])
 
     def add(into, value):
-        count_rows, width = into.shape
-        a = stage_a.at[pl.ds(0, count_rows), pl.ds(0, width)]
-        b = stage_b.at[pl.ds(0, count_rows), pl.ds(0, width)]
+        count_rows, wide = into.shape
+        a = stage_a.at[pl.ds(0, count_rows), pl.ds(0, wide)]
+        b = stage_b.at[pl.ds(0, count_rows), pl.ds(0, wide)]
         loads = fetch(into, a, 1), fetch(value, b, 2)
         for v in loads:
             v.start()
@@ -815,9 +807,9 @@
         back.wait()
 
     def finish(w, parts):
-        count_rows, width = parts[0].shape
-        a = stage_a.at[pl.ds(0, count_rows), pl.ds(0, width)]
-        b = stage_b.at[pl.ds(0, count_rows), pl.ds(0, width)]
+        count_rows, wide = parts[0].shape
+        a = stage_a.at[pl.ds(0, count_rows), pl.ds(0, wide)]
+        b = stage_b.at[pl.ds(0, count_rows), pl.ds(0, wide)]
         loads = fetch(parts[0], a, 1), fetch(parts[1], b, 2)
         for v in loads:
             v.start()
@@ -835,34 +827,6 @@
         kept.wait()
         w.hop(11, a).wait()
 
-    def part_fetch(source, h):
-        return fetch(source.at[h], part_sum, 4)
-
-    def join(i, h, source, arrived, landed, keep_value, sent_ref, over):
-        part_fetch(source, h).wait()
-        arrived[i].wait_recv()
-        keep_value(i, part_sum[:, left] + landed[h, left].astype(f32))
-        sent_ref[h, :] = (part_sum[:, right] + landed[h, right].astype(f32)).astype(bf16)
-        over[i].start()
-
-    def keep_e(i, value):
-        e_ref[halves[i], :] = value
-
-    def o_place(i, k):
-        return k // 2, pl.ds(k % 2 * own + i * rows, rows)
-
-    def keep_o(i, value):
-        for k in range(half_model // lanes):
-            chunk, o_rows = o_place(i, k)
-            coef_ref[chunk, o_rows, :] = value[:, k * lanes : (k + 1) * lanes]
-
-    def kept_o(i):
-        parts = []
-        for k in range(half_model // lanes):
-            chunk, o_rows = o_place(i, k)
-            parts.append(coef_ref[chunk, o_rows, :])
-        return jnp.concatenate(parts, axis=1)
-
     at.meet()
 
     @pl.when(at.serves)
@@ -877,25 +841,140 @@
         for w in (mo, mi):
             w.sent(*serve_hops)
 
-    @pl.when(at.works)
-    def _():
+    def partial_blocks(w, lhs, column_ref, room, order):
+        wide = column_ref.shape[1]
+        tile = 512
+        writes = []
+
+        def write(i, b):
+            return pltpu.make_async_copy(
+                room.at[i % 2, :, pl.ds(0, wide)], w.partial.at[b], keep_sem.at[i % 2]
+            )
+
+        for i, (b, hops) in enumerate(order):
+            if i >= 2:
+                write(i - 2, order[i - 2][0]).wait()
+                w.start(*order[i - 2][1])
+            here = columns_at(cols, b, size)
+
+            def column(t, carry, i=i, here=here):
+                wide_at = pl.ds(pl.multiple_of(t * tile, tile), tile)
+                total = lax.dot_general(
+                    lhs[0, :, here], column_ref[:own, wide_at], contract_rows, preferred_element_type=f32
+                )
+                total = total + lax.dot_general(
+                    lhs[1, :, here], column_ref[own:, wide_at], contract_rows, preferred_element_type=f32
+                )
+                room[i % 2, :, wide_at] = total.astype(bf16)
+                return carry
+
+            lax.fori_loop(0, wide // tile, column, 0)
+            write(i, b).start()
+        for i in (len(order) - 2, len(order) - 1):
+            write(i, order[i][0]).wait()
+            w.start(*order[i][1])
+
+    def rows_product(weight, row_ref, room, wide, which, out):
+        def block(b):
+            return pltpu.make_async_copy(
+                weight.at[b], room.at[b % 2, :, pl.ds(0, wide)], tile_sem.at[b % 2]
+            )
+
+        block(0).start()
+        for b in range(blocks):
+            if b + 1 < blocks:
+                block(b + 1).start()
+            block(b).wait()
+            here = columns_at(cols, b, size)
+
+            def chunk(i, carry, b=b, here=here):
+                start = pl.multiple_of(i * chunk_rows, chunk_rows)
+                out[pl.ds(start, chunk_rows), here] = lax.dot_general(
+                    row_ref[pl.ds(which * own + start, chunk_rows), :],
+                    room[b % 2, :, pl.ds(0, wide)],
+                    contract_cols,
+                    preferred_element_type=f32,
+                ).astype(out.dtype)
+                return carry
+
+            lax.fori_loop(0, own // chunk_rows, chunk, 0)
+
+    def join(i, h, mine_ref, arrived, landed, keep_value, sent_ref, over):
+        arrived[i].wait_recv()
+        keep_value(h, mine_ref[h, left] + landed[h, left].astype(f32))
+        sent_ref[h, :] = (mine_ref[h, right] + landed[h, right].astype(f32)).astype(bf16)
+        over[i].start()
+
+    def mlp_part(lhs, act_ref, pair_ref, tiles, room, mine_ref):
+        lhs_low = fetch(low_mine, lhs.at[0], 1), fetch(low_theirs, lhs.at[1], 2)
+        lhs_two = fetch(two_mine, lhs.at[0], 1), fetch(two_theirs, lhs.at[1], 2)
+        act_load = pltpu.make_async_copy(act_in, act_ref, load_sem.at[0])
+        pair_load = [
+            pltpu.make_async_copy(src, pair_ref.at[:, pl.ds(k * hidden, hidden)], load_sem.at[1 + k])
+            for k, src in enumerate((slope_in, value_in))
+        ]
+        for v in (*lhs_low, act_load, *pair_load):
+            v.start()
+        middle_load.start()
+        for v in (*lhs_low, act_load):
+            v.wait()
+        partial_blocks(
+            mo,
+            lhs,
+            act_ref,
+            room,
+            ((7, (1, 2)), (5, (0,)), (6, (3,)), (3, (5,)), (1, (7,)), (4, ()), (2, ()), (0, ())),
+        )
+        for v in pair_load:
+            v.wait()
+        tile = tiles.shape[3]
+
+        def back(t, slot):
+            gate_at = pl.ds(pl.multiple_of(t * tile, tile), tile)
+            up_at = pl.ds(pl.multiple_of(hidden + t * tile, tile), tile)
+
+            def use(start, d_act):
+                row_at = pl.ds(start, chunk_rows)
+                for where in (gate_at, up_at):
+                    pair_ref[row_at, where] = (d_act * pair_ref[row_at, where].astype(f32)).astype(bf16)
+
+            project(lhs.at[0], lhs.at[1], tiles.at[slot], cols, use)
+
+        stream_tiles(
+            hidden // tile,
+            lambda t, slot: pltpu.make_async_copy(
+                weight_mo.at[:, :, pl.ds(pl.multiple_of(t * tile, tile), tile)],
+                tiles.at[slot],
+                tile_sem.at[slot],
+            ),
+            back,
+        )
+        for v in lhs_two:
+            v.start()
+        mo.step(4, add_late)
+        mo.step(6, add_late)
+        for v in lhs_two:
+            v.wait()
+        rows_product(weight_mi, pair_ref, room, 2 * hidden, 1, part_out)
         for moved in e_core:
             moved.start()
-        part_fetch(e_mine, first).start()
-        for w in (mo, mi):
-            w.start(1, 2, 0, 3, 5, 7)
-        term_ref[...] = jnp.zeros_like(term_ref)
-        join(0, first, e_mine, e_core, part_in, keep_e, y_out, e_y)
-        part_fetch(e_mine, second).start()
-        join(1, second, e_mine, e_core, part_in, keep_e, y_out, e_y)
-        part_fetch(o_mine, first).start()
-        for moved in o_core:
-            moved.start()
-        mo.step(4, add)
-        mo.step(6, add)
-        join(0, first, o_mine, o_core, o_in, keep_o, oy_out, o_y)
-        part_fetch(o_mine, second).start()
-        join(1, second, o_mine, o_core, o_in, keep_o, oy_out, o_y)
+        mo.step(8, add)
+        rows_product(weight_mi, pair_ref, room, 2 * hidden, 0, mine_ref)
+
+        def keep_e(h, value):
+            e_ref[h, :] = value
+
+        for i, h in enumerate(halves):
+            join(i, h, mine_ref, e_core, part_in, keep_e, y_out, e_y)
+        mo.step(9, add)
+        partial_blocks(
+            mi,
+            lhs,
+            pair_ref,
+            room,
+            ((7, (1, 2)), (5, (0,)), (6, (3,)), (3, (5,)), (1, (7,)), (4, ()), (2, ()), (0, ())),
+        )
+        middle_load.wait()
         for i, h in enumerate(halves):
             e_y[i].wait_recv()
             norm_sums(e_ref, y_in, middle_ref, gain_ref, 1, mean_ref, i * rows, rows)
@@ -903,12 +982,12 @@
         for moved in e_y:
             moved.wait_send()
         low_load.start()
-        mo.step(8, add)
+        mi.step(6, add)
         low_load.wait()
         mean_y.wait_recv()
 
-        def keep(row_at, back):
-            d_middle = back + low_left[row_at, :].astype(f32)
+        def keep(row_at, value):
+            d_middle = value + low_left[row_at, :].astype(f32)
             dmid_ref[row_at, :] = d_middle
             db_mine[row_at, left] = d_middle.astype(bf16)
 
@@ -918,21 +997,52 @@
                 i * rows, rows, keep,
             )
             db_y[i].start()
-        mo.step(9, add)
-        mi.step(6, add)
+        for moved in e_core:
+            moved.wait_send()
+        rows_product(weight_mo, act_ref, room, hidden, 1, part_out)
+        for moved in o_core:
+            moved.start()
         mi.step(4, add)
-        for i, h in enumerate(halves):
-            o_y[i].wait_recv()
-            out_ref[h, :] = (
-                mask_ref[h, 4:5]
-                * (middle_ref[h, :] + kept_o(i) + oy_in[h, :].astype(f32))
-            ).astype(bf16)
-        out_move.start()
+        rows_product(weight_mo, act_ref, room, hidden, 0, mine_ref)
+
+        def keep_o(h, value):
+            middle_ref[h, :] = middle_ref[h, :] + value
+
         for i in range(2):
             db_y[i].wait_recv()
             db_core[i].start()
+        for i, h in enumerate(halves):
+            join(i, h, mine_ref, o_core, o_in, keep_o, oy_out, o_y)
+
+    def add_late(into, value):
+        count_rows, wide = into.shape
+        a = stage_a.at[pl.ds(0, count_rows), pl.ds(0, wide)]
+        b = stage_b.at[pl.ds(0, count_rows), pl.ds(0, wide)]
+        loads = fetch(into, a, 5), fetch(value, b, 6)
+        for v in loads:
+            v.start()
+        for v in loads:
+            v.wait()
+        add_rows(a, b)
+        back = fetch(a, into, 3)
+        back.start()
+        back.wait()
+
+    def recur_part(w_ro, both_ref, state_ref, dboth_ref, coef_ref, push_ref, dmix_ref, gr_ref, gi_ref):
+        loads = [
+            pltpu.make_async_copy(src, dst, load_sem.at[k])
+            for k, (src, dst) in enumerate(
+                ((weight_in, w_ro), (both_in, both_ref), (state_in, state_ref))
+            )
+        ]
+        for v in loads:
+            v.start()
         for i in range(2):
             db_core[i].wait_recv()
+        for v in keep_out:
+            v.start()
+        for v in loads:
+            v.wait()
 
         def keep_mixed(start, value):
             dmix_ref[pl.ds(start, chunk_rows), :] = value
@@ -941,6 +1051,12 @@
         recur_first(
             both_ref, state_ref, mask_ref, vec_ref, wr_ref, wi_ref, dmix_ref, dboth_ref, coef_ref, push_ref
         )
+        for i, h in enumerate(halves):
+            o_y[i].wait_recv()
+            out_ref[h, :] = (
+                mask_ref[h, 4:5] * (middle_ref[h, :] + oy_in[h, :].astype(f32))
+            ).astype(bf16)
+        out_move.start()
         mi.step(8, add)
         scan_rows(coef_ref, push_ref, both_ref.shape[0] // held_buffers, True)
         mi.step(9, add)
@@ -948,32 +1064,76 @@
             both_ref, state_ref, mask_ref, vec_ref, wr_ref, wi_ref, push_ref,
             dboth_ref, sums_ref, gr_ref, gi_ref,
         )
+        keep_both = pltpu.make_async_copy(dboth_ref, dboth_out, out_sem.at[3])
+        keep_both.start()
+        block = gates_ref.shape[0]
+        packed = [
+            ref[h * block : (h + 1) * block, h * block : (h + 1) * block].astype(bf16)
+            for ref in (gr_ref, gi_ref)
+            for h in range(width // block)
+        ]
+        gates_ref[...] = jnp.concatenate(packed, axis=1)
+        keep_both.wait()
+
+    @pl.when(at.works)
+    def _():
+        term_ref[...] = jnp.zeros_like(term_ref)
+        pl.run_scoped(
+            mlp_part,
+            pltpu.VMEM((2, own, model), bf16),
+            pltpu.VMEM((2 * own, hidden), bf16),
+            pltpu.VMEM((2 * own, 2 * hidden), bf16),
+            pltpu.VMEM((2, blocks, size, 256), bf16),
+            pltpu.VMEM((2, size, 2 * hidden), bf16),
+            pltpu.VMEM((own, model), f32),
+        )
+        pl.run_scoped(
+            recur_part,
+            pltpu.VMEM((blocks, size, width), bf16),
+            pltpu.VMEM(both_in.shape, f32),
+            pltpu.VMEM(state_in.shape, f32),
+            pltpu.VMEM(dboth_out.shape, bf16),
+            pltpu.VMEM(state_in.shape, f32),
+            pltpu.VMEM(state_in.shape, f32),
+            pltpu.VMEM((2 * own, width), f32),
+            pltpu.VMEM((width, width), f32),
+            pltpu.VMEM((width, width), f32),
+        )
         for w in (mo, mi):
             w.received(7, 8)
             finish(w, (w.partial.at[0], w.land.at[3], w.land.at[4]))
         for w in (mo, mi):
             w.sent(*work_hops)
-        for moved in (*e_core, *o_core, *o_y, mean_y, *db_y, *db_core, out_move):
+        for v in keep_out:
+            v.wait()
+        for moved in (*o_core, *o_y, mean_y, *db_y, *db_core, out_move):
             moved.wait_send()
 
 
 def finish_kernel(
     count,
-    one_mine, one_theirs, db_mine, db_theirs, dboth_ref, mixed_ref, w_ri, tok_ref, scale_ref, gain_ref,
-    dmid_ref, sums_ref, gates_ref, term_in,
-    total_ri, total_ro, out_ref, gates_out, sums_out, term_out,
-    d_ri, d_ro, land_ri, land_ro, tok_left, part_out, part_in, part_sum, y_out, y_in, e_ref,
-    mean_ref, mean_in, last_ri, last_ro, gates_in, sums_in, term_ref, term_land,
-    w_send, w_recv, m_send, m_recv, local_sem,
+    *refs,
 ):
+    sources, refs = refs[:9], refs[9:]
+    (
+        scale_ref, gain_ref, sums_ref, gates_ref, term_in,
+        total_r, out_ref, recur_out, input_out, sums_out, term_out,
+    ) = refs[:11]
+    refs = refs[11:]
+    one_mine, one_theirs, db_mine, db_theirs, dboth_ref, mixed_ref, w_ri, tok_left, dmid_ref = refs[:9]
+    (
+        d_r, land_r, part_out, part_in, part_sum, y_out, y_in, e_ref,
+        mean_ref, mean_in, last_r, gates_in, gates_out, sums_in, term_ref, term_land,
+        w_send, w_recv, m_send, m_recv, load_sem,
+    ) = refs[9:]
     at = Place(count)
     size = w_ri.shape[1]
     cols = at.columns(size)
     own, half_model = dmid_ref.shape
     model = 2 * half_model
     rows = own // 2
-    ri = Sums(at, d_ri, land_ri, total_ri, w_send.at[0], w_recv.at[0])
-    ro = Sums(at, d_ro, land_ro, total_ro, w_send.at[1], w_recv.at[1])
+    pair_width = dboth_ref.shape[1]
+    w = Sums(at, d_r, land_r, total_r, w_send, w_recv)
     first, second = pl.ds(0, rows), pl.ds(rows, rows)
     left, right = pl.ds(0, half_model), pl.ds(half_model, half_model)
     halves = (first, second)
@@ -997,44 +1157,55 @@
     term_z = move(15, term_land.at[0], term_land.at[1], at.ahead)
     term_core = move(16, term_land.at[1], term_land.at[2], at.core)
     term_end = move(17, term_out, term_out, at.behind)
-    tok_load = pltpu.make_async_copy(tok_ref.at[:, left], tok_left, local_sem.at[0])
+    loads = [
+        pltpu.make_async_copy(src, dst, load_sem.at[k]) for k, (src, dst) in enumerate(zip(sources, refs))
+    ]
 
     def add(into, value):
         add_rows(into, value)
 
-    def finish(w, last, parts):
-        last[...] = parts[0][...]
-        add_rows(last, parts[1], parts[2] if len(parts) == 3 else None)
-        w.hop(11, last).start()
-        w.total[0] = last[w.rows_of(at.c), :]
+    def finish(parts):
+        last_r[...] = parts[0][...]
+        add_rows(last_r, parts[1], parts[2] if len(parts) == 3 else None)
+        w.hop(11, last_r).start()
+        w.total[0] = last_r[w.rows_of(at.c), :]
+
+    def unpack(place, quarter):
+        block = recur_out.shape[1]
+        count_heads = recur_out.shape[0] // 2
+        for k, out in enumerate((recur_out, input_out)):
+            for h in range(count_heads):
+                start = (k * count_heads + h) * block
+                out[quarter * count_heads + h] = gates_out[place, :, start : start + block].astype(f32)
 
     at.meet()
 
     @pl.when(at.serves)
     def _():
-        for w in (ro, ri):
-            w.received(5, 6)
-            w.start(10)
         sums_end.wait_recv()
         sums_core.start()
+        w.received(5, 6)
+        w.start(10)
         gates_end.wait_recv()
         gates_core.start()
-        for w, last in ((ro, last_ro), (ri, last_ri)):
-            w.received(9, 10)
-            finish(w, last, (w.land.at[2], w.land.at[3]))
-        for w, last in ((ro, last_ro), (ri, last_ri)):
-            w.hop(11, last).wait()
-            w.sent(*serve_hops)
+        w.received(9, 10)
+        finish((w.land.at[2], w.land.at[3]))
+        w.hop(11, last_r).wait()
+        w.sent(*serve_hops)
         out_move.wait_recv()
         term_end.wait_recv()
         sums_core.wait()
+        unpack(0, at.c)
         gates_core.wait()
+        unpack(1, 1 - at.c)
 
     @pl.when(at.works)
     def _():
-        tok_load.start()
-        gates_x.start()
+        for k in (4, 0, 1, 5, 2, 3, 6, 7, 8):
+            loads[k].start()
         sums_x.start()
+        for k in (4, 0, 1, 5, 2, 3):
+            loads[k].wait()
 
         def partial(b):
             here = columns_at(cols, b, size)
@@ -1048,13 +1219,12 @@
                 )
                 return total.astype(bf16)
 
-            d_ro[b] = product(db_mine, db_theirs, mixed_ref)
-            d_ri[b] = product(one_mine, one_theirs, dboth_ref)
-
-        for b, hops in ((7, (1, 2)), (5, (0,)), (6, (3,)), (3, (5,)), (1, (7,))):
+            d_r[b, :, :pair_width] = product(one_mine, one_theirs, dboth_ref)
+            d_r[b, :, pair_width:] = product(db_mine, db_theirs, mixed_ref)
+
+        for b, hops in ((7, (1, 2)), (5, (0,)), (6, (3,)), (3, (5,))):
             partial(b)
-            for w in (ro, ri):
-                w.start(*hops)
+            w.start(*hops)
 
         def back(start, out, out_at):
             for b in range(blocks):
@@ -1062,49 +1232,49 @@
                     dboth_ref[pl.ds(start, rows), :], w_ri[b], contract_cols, preferred_element_type=f32
                 ).astype(out.dtype)
 
+        loads[6].wait()
         for i, h in enumerate(halves):
             back(own + i * rows, part_out, h)
             e_core[i].start()
-        for b in (4, 2, 0):
+        w.step(4, add)
+        w.step(6, add)
+        for b in (4, 1):
             partial(b)
-        for w in (ro, ri):
-            w.step(4, add)
-            w.step(6, add)
-            w.step(8, add)
         for i, h in enumerate(halves):
             back(i * rows, part_sum, first)
             e_core[i].wait_recv()
             e_ref[h, :] = part_sum[:, left] + part_in[h, left].astype(f32)
             y_out[h, :] = (part_sum[:, right] + part_in[h, right].astype(f32)).astype(bf16)
             e_y[i].start()
+        w.step(8, add)
+        gates_x.start()
+        w.start(7)
         sums_x.wait_recv()
         sums_in[0] = sums_in[0] + sums_ref[...]
         sums_z.start()
-        gates_x.wait_recv()
-        for k in range(2):
-            add_rows(gates_in.at[0, k], gates_ref.at[k])
-        gates_z.start()
-        for w in (ro, ri):
-            w.step(9, add)
+        for b in (2, 0):
+            partial(b)
+        w.step(9, add)
         sums_z.wait_recv()
         sums_out[0] = sums_in[0] + sums_in[1]
         sums_end.start()
         sums_core.start()
-        gates_z.wait_recv()
-        for k in range(2):
-            gates_out[0, k] = gates_in[0, k]
-            add_rows(gates_out.at[0, k], gates_in.at[1, k])
-        gates_end.start()
-        gates_core.start()
+        gates_x.wait_recv()
+        add_rows(gates_in.at[0], gates_ref)
+        gates_z.start()
         term_ref[...] = term_in[...]
-        tok_load.wait()
+        for k in (7, 8):
+            loads[k].wait()
         for i in range(2):
             e_y[i].wait_recv()
             norm_sums(e_ref, y_in, tok_left, gain_ref, 0, mean_ref, i * rows, rows)
         mean_y.start()
-        for w, last in ((ro, last_ro), (ri, last_ri)):
-            w.received(7, 8)
-            finish(w, last, (w.partial.at[0], w.land.at[3], w.land.at[4]))
+        gates_z.wait_recv()
+        gates_out[0] = gates_in[0]
+        add_rows(gates_out.at[0], gates_in.at[1])
+        gates_end.start()
+        gates_core.start()
+        unpack(0, at.c)
         mean_y.wait_recv()
 
         def keep(row_at, value):
@@ -1121,17 +1291,19 @@
         term_x.wait_recv()
         term_land[0] = term_land[0] + term_ref[...]
         term_z.start()
+        w.received(7, 8)
+        finish((w.partial.at[0], w.land.at[3], w.land.at[4]))
         term_z.wait_recv()
         term_land[1] = term_land[0] + term_land[1]
         term_core.start()
         term_core.wait_recv()
         term_out[...] = term_land[1] + term_land[2]
         term_end.start()
-        for w, last in ((ro, last_ro), (ri, last_ri)):
-            w.hop(11, last).wait()
-            w.sent(*work_hops)
+        w.hop(11, last_r).wait()
+        w.sent(*work_hops)
         sums_core.wait_recv()
         gates_core.wait_recv()
+        unpack(1, 1 - at.c)
         for moved in (
             *e_core, *e_y, mean_y, out_move, gates_x, gates_z, gates_end, gates_core,
             sums_x, sums_z, sums_end, sums_core, term_x, term_z, term_core, term_end,
@@ -1158,21 +1330,23 @@
     shape = jax.ShapeDtypeStruct
     gathered_shapes = [shape((blocks, size, v.shape[1]), bf16) for v in keeps]
     wide = shape((own, model), bf16)
+    kept = [
+        shape((2 * own, 2 * width), f32),
+        shape(lane_shape(2 * own, width), f32),
+        shape((2 * own, width), bf16),
+        shape((2 * own, lanes), f32),
+        shape((own, half_model), f32),
+        shape((own, half_model), bf16),
+        *[wide] * 6,
+        shape((2, own, lanes), f32),
+    ]
     return pl.pallas_call(
         functools.partial(forward_kernel, count),
-        out_shape=(
-            *gathered_shapes,
-            shape((2 * own, 2 * width), f32),
-            shape(lane_shape(2 * own, width), f32),
-            shape((2 * own, width), bf16),
-            shape((2 * own, lanes), f32),
-            shape((own, half_model), f32),
-            *[wide] * 7,
-            shape((2, own, lanes), f32),
-        ),
+        out_shape=(*gathered_shapes, *kept),
         in_specs=[in_any] * 11 + [in_vmem] * 4,
-        out_specs=[in_any] * 4 + [in_vmem] * 13,
+        out_specs=[in_any] * 17,
         scratch_shapes=[
+            *[pltpu.VMEM(wide.shape if i == 5 else v.shape, v.dtype) for i, v in enumerate(kept)],
             pltpu.VMEM(lane_shape(2 * own, width), f32),
             pltpu.VMEM((blocks, size, 2 * width), bf16),
             pltpu.VMEM((blocks, size, width), bf16),
@@ -1190,6 +1364,7 @@
             copy_sem((18,)),
             copy_sem((18,)),
             copy_sem((3,)),
+            copy_sem((13,)),
         ],
         compiler_params=comm_params(0),
         cost_estimate=no_cost,
@@ -1204,39 +1379,35 @@
 
 
 def run_backward(
-    count, partials, e_parts, o_parts, low, middle, scales, gains, weight, both, state, mask, vectors, wr, wi
+    count, weights, mlp_kept, normed_two, grad_low, middle, weight, both, state,
+    scales, gains, mask, vectors, wr, wi, block,
 ):
     own, half_model = middle.shape
     model, width, rows = 2 * half_model, wr.shape[0], own // 2
     size = weight.shape[1]
     shape = jax.ShapeDtypeStruct
-    hidden = [v.shape[2] for v in partials]
-    square = shape((width, width), f32)
+    hidden = [v.shape[2] for v in weights]
     wide = shape((own, model), bf16)
+    kept = (shape((own, half_model), f32), wide, wide)
     return pl.pallas_call(
         functools.partial(backward_kernel, count),
         out_shape=(
+            *[shape(v.shape, bf16) for v in weights],
             *[shape((5, size, n), bf16) for n in hidden],
             *[shape((2, size // 2, n), bf16) for n in hidden],
+            *kept,
+            shape((2 * own, 2 * width), bf16),
             shape((own, half_model), bf16),
-            shape((own, half_model), f32),
-            wide,
-            wide,
-            shape((2 * own, 2 * width), bf16),
             shape((8, width), f32),
-            square,
-            square,
+            shape((block, 2 * width), bf16),
             shape((8, half_model), f32),
         ),
-        in_specs=[in_any] * 7 + [in_vmem] * 10,
-        out_specs=[in_any] * 4 + [in_vmem] * 9,
+        in_specs=[in_any] * 13 + [in_vmem] * 6,
+        out_specs=[in_any] * 10 + [in_vmem] * 4,
         scratch_shapes=[
-            pltpu.VMEM(lane_shape(2 * own, width), f32),
-            pltpu.VMEM(lane_shape(2 * own, width), f32),
-            pltpu.VMEM((2 * own, width), f32),
-            pltpu.VMEM((own, model), bf16),
-            pltpu.VMEM((own, model), bf16),
-            pltpu.VMEM((rows, model), f32),
+            pltpu.VMEM((own, half_model), f32),
+            *[pltpu.VMEM(v.shape, v.dtype) for v in kept],
+            *[pltpu.VMEM((own, model), bf16)] * 3,
             *[pltpu.VMEM((own, half_model), bf16)] * 4,
             pltpu.VMEM((own, lanes), f32),
             pltpu.VMEM((own, lanes), f32),
@@ -1246,37 +1417,48 @@
             copy_sem((2, 12)),
             copy_sem((14,)),
             copy_sem((14,)),
-            copy_sem((5,)),
+            copy_sem((7,)),
+            copy_sem((4,)),
+            copy_sem((4,)),
+            copy_sem((2,)),
+            copy_sem((2,)),
         ],
         compiler_params=comm_params(1),
         cost_estimate=no_cost,
-        name="sum_and_recur_back",
-    )(*partials, *e_parts, *o_parts, low, middle, scales, gains, weight, both, state, mask, vectors, wr, wi)
+        name="sum_and_back",
+    )(
+        *weights, *mlp_kept, *normed_two, *grad_low, middle, weight, both, state,
+        scales, gains, mask, vectors, wr, wi,
+    )
 
 
 def run_finish(
-    count, normed, d_branch, d_both, mixed, weight, tokens, scales, gains, d_middle, sums, gates, term
+    count, normed, d_branch, d_both, mixed, weight, tokens, d_middle, scales, gains, sums, gates, term
 ):
     own, half_model = d_middle.shape
     model, rows = 2 * half_model, own // 2
     size = weight.shape[1]
-    widths = [weight.shape[2], mixed.shape[1]]
+    width = weight.shape[2] + mixed.shape[1]
     shape = jax.ShapeDtypeStruct
+    held = (*normed, *d_branch, d_both, mixed, weight, tokens, d_middle)
+    block = gates.shape[0]
+    square = shape((gates.shape[1] // block, block, block), f32)
     return pl.pallas_call(
         functools.partial(finish_kernel, count),
         out_shape=(
-            *[shape((2, size // 2, n), bf16) for n in widths],
+            shape((2, size // 2, width), bf16),
             shape((own, half_model), bf16),
-            shape((2, *gates.shape), bf16),
+            square,
+            square,
             shape((2, *sums.shape), f32),
             shape(term.shape, f32),
         ),
-        in_specs=[in_vmem] * 7 + [in_any] + [in_vmem] * 6,
+        in_specs=[in_any] * 9 + [in_vmem] * 5,
         out_specs=[in_vmem] * 6,
         scratch_shapes=[
-            *[pltpu.VMEM((blocks, size, n), bf16) for n in widths],
-            *[pltpu.VMEM((5, size, n), bf16) for n in widths],
-            pltpu.VMEM((own, half_model), bf16),
+            *[pltpu.VMEM(v.shape, v.dtype) for v in held],
+            pltpu.VMEM((blocks, size, width), bf16),
+            pltpu.VMEM((5, size, width), bf16),
             pltpu.VMEM((own, model), bf16),
             pltpu.VMEM((own, model), bf16),
             pltpu.VMEM((rows, model), f32),
@@ -1285,21 +1467,22 @@
             pltpu.VMEM((own, half_model), f32),
             pltpu.VMEM((own, lanes), f32),
             pltpu.VMEM((own, lanes), f32),
-            *[pltpu.VMEM((size, n), bf16) for n in widths],
+            pltpu.VMEM((size, width), bf16),
+            pltpu.VMEM((2, *gates.shape), bf16),
             pltpu.VMEM((2, *gates.shape), bf16),
             pltpu.VMEM((2, *sums.shape), f32),
             pltpu.VMEM(term.shape, f32),
             pltpu.VMEM((3, *term.shape), f32),
-            copy_sem((2, 12)),
-            copy_sem((2, 12)),
+            copy_sem((12,)),
+            copy_sem((12,)),
             copy_sem((18,)),
             copy_sem((18,)),
-            copy_sem((1,)),
+            copy_sem((9,)),
         ],
         compiler_params=comm_params(2),
         cost_estimate=no_cost,
         name="sum_and_finish",
-    )(*normed, *d_branch, d_both, mixed, weight, tokens, scales, gains, d_middle, sums, gates, term)
+    )(*held, scales, gains, sums, gates, term)
 
 
 def run_mlp_forward(normed, weight, cols):
@@ -1321,80 +1504,6 @@
         cost_estimate=no_cost,
         name="mlp_forward",
     )(*normed, weight, weight, cols)
-
-
-def run_mlp_backward(grad_low, weight, cols, slope, value):
-    own, model = grad_low[0].shape
-    size, hidden = weight.shape[1:]
-    tile = 256
-    out = jax.ShapeDtypeStruct((2 * own, hidden), bf16)
-    column = pl.BlockSpec((2 * own, tile), lambda n: (0, n))
-    return pl.pallas_call(
-        mlp_backward,
-        grid=(hidden // tile,),
-        out_shape=(out, out),
-        in_specs=[pl.BlockSpec((own, model), lambda n: (0, 0))] * 2
-        + [pl.BlockSpec((blocks, size, tile), lambda n: (0, 0, n))]
-        + [in_smem, column, column],
-        out_specs=[column, column],
-        compiler_params=kernel_params,
-        cost_estimate=no_cost,
-        name="mlp_backward",
-    )(*grad_low, weight, cols, slope, value)
-
-
-def tile_of(width):
-    return 512 if width % 512 == 0 else width
-
-
-def part_specs(parts, rows, row_block, tile):
-    specs, tiles, first = [], [], 0
-    for part in parts:
-        count = part.shape[1] // tile
-
-        def index(n, first=first, count=count):
-            return (row_block, jnp.clip(n - first, 0, count - 1))
-
-        specs.append(pl.BlockSpec((rows, tile), index))
-        tiles.append(count)
-        first += count
-    return specs, tuple(tiles)
-
-
-def run_rows_back(name, parts, weight, cols, row_block, dtype):
-    own = parts[0].shape[0] // 2
-    size = weight.shape[1]
-    tile = tile_of(parts[0].shape[1])
-    specs, tiles = part_specs(parts, own, row_block, tile)
-    return pl.pallas_call(
-        functools.partial(rows_back, tiles),
-        grid=(sum(tiles),),
-        out_shape=jax.ShapeDtypeStruct((own, size * blocks), dtype),
-        in_specs=specs
-        + [pl.BlockSpec((blocks, size, tile), lambda n: (0, 0, n)), in_smem],
-        out_specs=pl.BlockSpec((own, size * blocks), lambda n: (0, 0)),
-        scratch_shapes=[pltpu.VMEM((own, size * blocks), f32)],
-        compiler_params=kernel_params,
-        cost_estimate=no_cost,
-        name=name,
-    )(*parts, weight, cols)
-
-
-def run_weight_partial(name, rows, parts, cols):
-    own, model = rows[0].shape
-    size = model // blocks
-    tile = tile_of(parts[0].shape[1])
-    specs, tiles = part_specs(parts, 2 * own, 0, tile)
-    return pl.pallas_call(
-        functools.partial(weight_partial, tiles),
-        grid=(sum(tiles),),
-        out_shape=jax.ShapeDtypeStruct((blocks, size, sum(tiles) * tile), bf16),
-        in_specs=[pl.BlockSpec((own, model), lambda n: (0, 0))] * 2 + [in_smem] + specs,
-        out_specs=pl.BlockSpec((blocks, size, tile), lambda n: (0, 0, n)),
-        compiler_params=kernel_params,
-        cost_estimate=no_cost,
-        name=name,
-    )(*rows, cols, *parts)
 
 
 def block_diagonal(blocks):
@@ -1550,45 +1659,28 @@
     normed, normed_two, grad_low = rows_kept[0:2], rows_kept[2:4], rows_kept[4:6]
 
     act, gate_slope, gate_value = run_mlp_forward(normed_two, mlp_in_all, cols)
-    d_pair = run_mlp_backward(grad_low, mlp_out_all, cols, gate_slope, gate_value)
-
-    def both_halves(name, parts, weight):
-        return (
-            run_rows_back(name + "_theirs", parts, weight, cols, 1, bf16),
-            run_rows_back(name + "_mine", parts, weight, cols, 0, f32),
-        )
-
-    partials = (
-        run_weight_partial("mlp_in_partial", normed_two, d_pair, cols),
-        run_weight_partial("mlp_out_partial", grad_low, (act,), cols),
-    )
     (
-        _, _, mlp_in_total, mlp_out_total,
-        output_two, d_middle, d_branch, d_branch_theirs, d_both, sums, square_recur, square_input, term,
+        _, _, _, _, mlp_in_total, mlp_out_total, d_middle, d_branch, d_branch_theirs, d_both,
+        output_two, sums, gates, term,
     ) = run_backward(
         outer_count,
-        partials,
-        both_halves("mlp_in_back", d_pair, mlp_in_all),
-        both_halves("mlp_out", (act,), mlp_out_all),
-        grad_low[0],
+        (mlp_in_all, mlp_out_all),
+        (act, gate_slope, gate_value),
+        normed_two,
+        grad_low,
         middle,
-        scales,
-        gains,
         rnn_out_all,
         both,
         state,
+        scales,
+        gains,
         mask,
         vectors,
         wr,
         wi,
+        gate_recur.shape[1],
     )
-    gates = jnp.stack(
-        [
-            diagonal_blocks(v, heads).reshape(-1, gate_recur.shape[1]).astype(bf16)
-            for v in (square_recur, square_input)
-        ]
-    )
-    rnn_in_total, rnn_out_total, tokens_grad_two, gates, sums, term = run_finish(
+    rnn_total, tokens_grad_two, recur_grad, input_grad, sums, term = run_finish(
         outer_count,
         normed,
         (d_branch, d_branch_theirs),
@@ -1596,13 +1688,15 @@
         mixed,
         rnn_in_all,
         tokens_all,
+        d_middle,
         scales,
         gains,
-        d_middle,
         sums,
         gates,
         term,
     )
+    rnn_width = rnn_in.shape[2]
+    rnn_in_total, rnn_out_total = rnn_total[:, :, :rnn_width], rnn_total[:, :, rnn_width:]
     layer_output, tokens_grad = output_two[:buffer_rows], tokens_grad_two[:buffer_rows]
     mlp_in_grad, mlp_out_grad, rnn_in_grad, rnn_out_grad = (
         settle_grad(v) for v in (mlp_in_total, mlp_out_total, rnn_in_total, rnn_out_total)
@@ -1617,9 +1711,8 @@
         )
 
     sums = both_quarters(sums, 1)
-    gates = both_quarters(gates.astype(f32), 1)
+    recur_grad, input_grad = over_groups(recur_grad), over_groups(input_grad)
     gains_grad = over_groups(term[:2])
-    size = gate_recur.shape[1]
 
     def pair_layout(halves):
         columns = halves[0].shape[1] // 2
@@ -1636,8 +1729,8 @@
         tokens_grad,
         gains_grad[0],
         pair_layout(rnn_in_grad),
-        gates[0].reshape(-1, size, size),
-        gates[1].reshape(-1, size, size),
+        recur_grad,
+        input_grad,
         sums[5],
         sums[6],
         8.0 * jax.nn.sigmoid(-decay_param) * sums[7],

time: 704 us -> 627 us (0.89)
  Pallas kernels: 648 us -> 576 us
    pallas_call x8 -> x1, Pallas kernels: 224 us -> 117 us  [run_finish(): pl.pallas_call(functools.partial(finish_kernel, count), out_shape=(shape(...]
    pallas_call x1, Pallas kernels: 201 us -> 254 us  [run_backward(): pl.pallas_call(functools.partial(backward_kernel, count), out_shape=(*[sh...]
    pallas_call x1, Pallas kernels: 198 us -> 180 us  [run_forward(): pl.pallas_call(functools.partial(forward_kernel, count), out_shape=(*gath...]
where the time goes in v4:
time: 627 us; the launch traced here: 621 us
  Pallas kernels  576 us (92%)
  local copies, waits for them, and re-layouts  24.3 us (4%)
  other arithmetic  18.8 us (3%)
    pallas_call x1, Pallas kernels, run_backward(): pl.pallas_call(functools.partial(backward_kernel, count), out_shape=(*[sh...  254 us
    pallas_call x1, Pallas kernels, run_forward(): pl.pallas_call(functools.partial(forward_kernel, count), out_shape=(*gath...  180 us
    pallas_call x1, Pallas kernels, run_finish(): pl.pallas_call(functools.partial(finish_kernel, count), out_shape=(shape(...  117 us
    pallas_call x1, Pallas kernels, run_mlp_forward(): pl.pallas_call(mlp_forward, grid=(tiles,), out_shape=(out, out, out), in_...  24.9 us

profile of v4, /device:TPU:0, one launch (start us, length us, event | category | flops | bytes accessed | tf_op | source)
XLA Modules:
  0.0 620.9 jit_solution(1832303259042738370)
XLA Ops:
  0.8 0.7 stack.94.cols_ref
  1.4 0.8 reduce_window_sum.11
  2.3 0.6 slice.241
  2.9 0.7 subtract_bitcast_fusion
  3.6 0.7 compare_convert_fusion.1
  4.3 0.7 convert_element_type.125
  5.0 0.7 convert_element_type.126
  5.7 0.6 pad_maximum_fusion.6.gain_ref.refs_10_
  6.3 0.8 slice_select_fusion.4
  7.2 0.9 compare_select_fusion
  8.1 0.9 slice_select_fusion.2
  8.9 0.6 concatenate.63.vec_ref
  9.6 0.1 copy.74
  9.7 0.7 pad.32.mask_in
  10.4 1.9 broadcast_select_fusion.6
  12.4 1.2 fusion.12.wr_ref
  13.6 1.2 fusion.15.wi_ref
  14.8 0.9 broadcast_select_fusion.2
  15.7 2.0 fusion.22
  17.8 1.1 broadcast_select_fusion.4
  19.0 0.5 copy-done
  19.4 2.2 fusion.19
  21.9 1.5 broadcast_select_fusion
  23.4 180.5 %gather_and_recur.1 = (bf16[8,256,1408]{2,1,0:T(8,128)(2,1)}, bf16[8,256,704]{2,1,0:T(8,128)(2,1)}, bf16[8,256,3072]{2,1,0:T(8,128)(2,1)}, bf16[8,256,1536]{2,1,...) custom-call(bf16[128,1408]{1,0:T(8,128)(2,1)} %get-tuple-element.172, ...), custom_call_target="tpu_custom_call" | custom-call | tf_op jit(solution)/shard_map/gather_and_recur/pallas_call | solution.py:1343
  203.8 24.9 %mlp_forward.1 = (bf16[1024,1536]{1,0:T(8,128)(2,1)}, bf16[1024,1536]{1,0:T(8,128)(2,1)}, bf16[1024,1536]{1,0:T(8,128)(2,1)}) custom-call(bf16[512,2048]{1,0:T(8,128)(2,1)} %get-tuple-element.53.mine_ref.two_mine, bf16[512,2048]{1,0:T(8,128)(2,1)} %get-tuple-element.54.theirs_ref.two_theirs, ...), custom_call_target="tpu_custom_call" | custom-call | tf_op jit(solution)/shard_map/mlp_forward/pallas_call | solution.py:1494
  228.7 254.2 %sum_and_back.1 = (bf16[8,256,3072]{2,1,0:T(8,128)(2,1)}, bf16[8,256,1536]{2,1,0:T(8,128)(2,1)}, bf16[5,256,3072]{2,1,0:T(8,128)(2,1)}, bf16[5,256,1536]{2,1,0:T...) custom-call(bf16[8,256,3072]{2,1,0:T(8,128)(2,1)} %get-tuple-element, ...), custom_call_target="tpu_custom_call" | custom-call | tf_op jit(solution)/shard_map/sum_and_back/pallas_call | solution.py:1392
  483.0 116.8 %sum_and_finish.1 = (bf16[2,128,2112]{2,1,0:T(8,128)(2,1)}, bf16[512,1024]{1,0:T(8,128)(2,1)}, f32[8,176,176]{2,1,0:T(8,128)}, f32[8,176,176]{2,1,0:T(8,128)}, f32[2,8,704]{2,1,0:T(8,128)}, /*index=5*/f32[8,1024]{1,0:T(8,128)}) custom-call(bf16[512,2048]{1,0:T(8,128)(2,1)} %get-tuple-element.67.refs_0_, bf16[512,2048]{1,0:T(8,128)(2,1)} %get-tuple-element.68.refs_1_, ...), custom_call_target="tpu_custom_call" | custom-call | tf_op jit(solution)/shard_map/sum_and_finish/pallas_call | solution.py:1446
  599.9 2.0 slice.268
  601.9 1.9 slice.269
  603.7 1.4 fusion.23
  605.3 0.6 slice.314
  605.9 0.7 slice_reduce_fusion
  606.5 0.6 multiply_multiply_fusion
  607.3 1.0 maximum_convert_fusion.1
  608.4 0.2 fusion.20
  608.5 1.3 maximum_convert_fusion
  609.8 0.2 fusion.21
  610.0 0.2 maximum_bitcast_fusion.2
  610.2 0.2 maximum_bitcast_fusion.3
  610.5 2.2 copy.75
  612.7 0.2 bitcast_convert_fusion.1
  612.9 0.1 fusion.17
  613.0 0.1 fusion.18
  613.4 0.2 pad_maximum_fusion
  613.6 4.1 copy.76
  617.7 1.1 copy.95
  618.8 0.8 copy-done.3
  619.6 1.1 copy.96
  (48 shorter events, 1.2 us)
Async XLA Ops:
  0.6 11.6 %copy-start.8 = (bf16[8,176,176]{2,1,0:T(8,128)(2,1)S(1)}, bf16[8,176,176]{2,1,0:T(8,128)(2,1)}, u32[]{:S(2)}) copy-start(bf16[8,176,176]{2,1,0:T(8,128)(2,1)} %param.20) | copy-start | bytes 1486852
  0.7 11.6 %copy-start.9 = (bf16[8,176,176]{2,1,0:T(8,128)(2,1)S(1)}, bf16[8,176,176]{2,1,0:T(8,128)(2,1)}, u32[]{:S(2)}) copy-start(bf16[8,176,176]{2,1,0:T(8,128)(2,1)} %param.19) | copy-start | bytes 1486852
  12.4 2.3 copy-start.6
  13.6 2.1 copy-start.1
  17.8 1.7 copy-start
  599.8 5.4 copy-start.10
  599.8 6.7 %copy-start.11 = (f32[1408]{0:T(1024)S(1)}, f32[1408]{0:T(1024)}, u32[]{:S(2)}) copy-start(f32[1408]{0:T(1024)} %param.23) | copy-start | bytes 16900
  599.8 7.3 %copy-start.5 = (bf16[2,128,2112]{2,1,0:T(8,128)(2,1)S(1)}, bf16[2,128,2112]{2,1,0:T(8,128)(2,1)}, u32[]{:S(2)}) copy-start(bf16[2,128,2112]{2,1,0:T(8,128)(2,1)} %get-tuple-element.81) | copy-start | bytes 3244036
  599.9 7.3 %copy-start.7 = (bf16[2,128,1536]{2,1,0:T(8,128)(2,1)S(1)}, bf16[2,128,1536]{2,1,0:T(8,128)(2,1)}, u32[]{:S(2)}) copy-start(bf16[2,128,1536]{2,1,0:T(8,128)(2,1)} %get-tuple-element.86) | copy-start | bytes 2359300
  610.5 2.2 copy-start.2
  613.6 4.1 copy-start.4
  617.7 1.9 copy-start.3

commit v5 on v4

--- a/solution.py
+++ b/solution.py
@@ -18,7 +18,7 @@
 held_buffers = 4
 scan_unroll = 8
 blocks = 8
-chunk_rows = 256
+chunk_rows = 512
 lanes = 128
 by_mesh = pl.DeviceIdType.MESH
 
@@ -124,8 +124,7 @@
     return weight_ref[...].reshape(-1, weight_ref.shape[2])
 
 
-def project(mine_ref, theirs_ref, weight_ref, cols, use):
-    size = weight_ref.shape[1]
+def project(mine_ref, theirs_ref, weight, size, cols, use):
     own = mine_ref.shape[0]
     for part, ref in enumerate((mine_ref, theirs_ref)):
 
@@ -134,7 +133,7 @@
             rows = gathered(ref, at, cols, size)
             use(
                 pl.multiple_of(part * own + i * chunk_rows, chunk_rows),
-                jnp.dot(rows, stacked(weight_ref), preferred_element_type=f32),
+                jnp.dot(rows, weight(), preferred_element_type=f32),
             )
             return carry
 
@@ -192,6 +191,46 @@
         return carry
 
     lax.fori_loop(0, held_buffers, mix, 0)
+
+
+def stream_tiles(first, last, fetch, body):
+    fetch(first, first % 2).start()
+
+    def step(t, carry):
+        slot = t % 2
+
+        @pl.when(t + 1 < last)
+        def _():
+            fetch(t + 1, 1 - slot).start()
+
+        fetch(t, slot).wait()
+        body(t, slot)
+        return carry
+
+    lax.fori_loop(first, last, step, 0)
+
+
+class Tile:
+    def __init__(self, weight, room, sems, first_column, tile):
+        at = pl.ds(pl.multiple_of(first_column, tile), tile)
+        self.copies = [
+            pltpu.make_async_copy(
+                weight.at[b, :, at], room.at[:, pl.ds(b * tile, tile)], sems.at[b]
+            )
+            for b in range(blocks)
+        ]
+
+    def start(self):
+        for v in self.copies:
+            v.start()
+
+    def wait(self):
+        for v in self.copies:
+            v.wait()
+
+
+def tile_rows(room, tile):
+    return jnp.concatenate([room[:, b * tile : (b + 1) * tile] for b in range(blocks)], axis=0)
 
 
 class Place:
@@ -263,31 +302,32 @@
 
 def forward_kernel(
     count,
-    keep_ri, keep_ro, keep_mi, keep_mo, give_ri, give_ro, give_mi, give_mo,
+    s_ri, s_ro, s_mi, s_mo,
     tokens_ref, grad_ref, mask_in, gain_ref, vec_ref, wr_ref, wi_ref,
     g_ri, g_ro, g_mi, g_mo, *refs,
 ):
-    results, refs = refs[:13], refs[13:]
+    results, mlp_out_refs, refs = refs[:13], refs[13:16], refs[16:]
     (
-        both_ref, state_ref, mixed_ref, mask_ref, middle_ref, tok_ref,
+        state_ref, mask_ref, middle_ref, tok_ref,
         one_mine, one_theirs, two_mine, two_theirs, low_mine, low_theirs, scale_ref,
-    ) = held = refs[:13]
-    refs = refs[13:]
+    ) = refs[:11]
     (
-    coef_ref, w_ri, w_ro, grad_all, part_out, part_in, part_sum, y_out, y_in, mid_ref,
-    w_send, w_recv, w_local, load_sem, m_send, m_recv, m_local, out_sem,
-    ) = refs
+        grad_all, part_out, part_in, y_out, y_in, mid_ref,
+        w_send, w_recv, w_local, load_sem, m_send, m_recv, m_local, out_sem, tile_sem, mlp_sem,
+    ) = refs[11:]
+    held = (
+        None, state_ref, None, mask_ref, middle_ref, tok_ref,
+        one_mine, one_theirs, two_mine, two_theirs, low_mine, low_theirs, scale_ref,
+    )
     at = Place(count)
-    half_rows = keep_ri.shape[0]
+    half_rows = s_ri.shape[1]
     size = 2 * half_rows
     model = tok_ref.shape[1]
     half_model = model // 2
     rows = tokens_ref.shape[0]
     own = 2 * rows
     cols = at.columns(size)
-    whole, keeps, gives = (g_ri, g_ro, g_mi, g_mo), (keep_ri, keep_ro, keep_mi, keep_mo), (
-        give_ri, give_ro, give_mi, give_mo,
-    )
+    whole, splits = (g_ri, g_ro, g_mi, g_mo), (s_ri, s_ro, s_mi, s_mo)
     ri, ro, mi, mo = range(4)
     top, bottom = pl.ds(0, half_rows), pl.ds(half_rows, half_rows)
     core_rows = pl.ds(pl.multiple_of(at.c * half_rows, half_rows), half_rows)
@@ -295,7 +335,7 @@
     def hop(w, k):
         g = whole[w]
         src, dst, where = (
-            (gives[w], g.at[0, core_rows], at.core),
+            (splits[w].at[1 - at.c], g.at[0, core_rows], at.core),
             (g.at[0], g.at[1], at.beside),
             (g.at[0], g.at[2], at.ahead),
             (g.at[1], g.at[3], at.ahead),
@@ -308,7 +348,7 @@
         return remote(src, dst, w_send.at[w, k], w_recv.at[w, k], where)
 
     def kept(w):
-        return pltpu.make_async_copy(keeps[w], whole[w].at[0, core_rows], w_local.at[w])
+        return pltpu.make_async_copy(splits[w].at[at.c], whole[w].at[0, core_rows], w_local.at[w])
 
     def begin(w):
         kept(w).start()
@@ -355,8 +395,9 @@
     def load(w, target, b):
         return pltpu.make_async_copy(whole[w].at[b], target.at[b], load_sem.at[w, b])
 
-    def keep_out(k):
-        source = held[k].at[:, left] if k == 5 else held[k]
+    def keep_out(k, source=None):
+        if source is None:
+            source = held[k].at[:, left] if k == 5 else held[k]
         return pltpu.make_async_copy(source, results[k], out_sem.at[k])
 
     at.meet()
@@ -381,6 +422,116 @@
                 hop(w, k).wait_send()
         for moved in (mask_move, token_in, grad_in):
             moved.wait_send()
+
+    def recur_part(both_ref, mixed_ref, coef_ref, w_ri, w_ro, part_sum):
+        for w, target in ((ri, w_ri), (ro, w_ro)):
+            hop(w, 1).wait_recv()
+            for k in (5, 7, 8):
+                hop(w, k).wait_recv()
+            for b in range(blocks):
+                load(w, target, b).start()
+        for b in range(blocks):
+            load(ri, w_ri, b).wait()
+        one_core.wait_recv()
+        mask_core.wait_recv()
+
+        def keep_both(start, value):
+            both_ref[pl.ds(start, chunk_rows), :] = value
+
+        for k in (3, 5, 6, 7):
+            keep_out(k).start()
+        project(one_mine, one_theirs, lambda: stacked(w_ri), size, cols, keep_both)
+        keep_out(0, both_ref).start()
+        grad_in.wait_recv()
+        grad_y_two.start()
+        recur_state(both_ref, mask_ref, vec_ref, wr_ref, wi_ref, coef_ref, state_ref)
+        keep_out(1).start()
+        pass_on(mi, 2, 6)
+        pass_on(mi, 4, 5)
+        recur_mixed(both_ref, state_ref, mixed_ref)
+        keep_out(2, mixed_ref).start()
+        for b in range(blocks):
+            load(ro, w_ro, b).wait()
+
+        def branch(start, out_ref, out_at):
+            for b in range(blocks):
+                out_ref[out_at, columns_at(cols, b, size)] = lax.dot_general(
+                    mixed_ref[pl.ds(start, rows), :],
+                    w_ro[b],
+                    contract_cols,
+                    preferred_element_type=f32,
+                ).astype(out_ref.dtype)
+
+        for i, h in enumerate(halves):
+            branch(own + i * rows, part_out, h)
+            part_core[i].start()
+        for i, h in enumerate(halves):
+            branch(i * rows, part_sum, first)
+            part_core[i].wait_recv()
+            middle_ref[h, :] = part_sum[:, left] + part_in[h, left].astype(f32)
+            y_out[h, :] = (part_sum[:, right] + part_in[h, right].astype(f32)).astype(bf16)
+            part_y[i].start()
+        keep_out(0, both_ref).wait()
+        keep_out(2, mixed_ref).wait()
+
+    def mlp_part(gate_room, up_room, act_room, slope_room, value_room):
+        hidden = mlp_out_refs[0].shape[1]
+        tile = act_room.shape[2]
+        rooms = (act_room, slope_room, value_room)
+
+        class Both:
+            def __init__(self, t, slot):
+                self.tiles = (
+                    Tile(g_mi, gate_room.at[slot], tile_sem.at[slot, 0], t * tile, tile),
+                    Tile(g_mi, up_room.at[slot], tile_sem.at[slot, 1], hidden + t * tile, tile),
+                )
+
+            def start(self):
+                for v in self.tiles:
+                    v.start()
+
+            def wait(self):
+                for v in self.tiles:
+                    v.wait()
+
+        def results_of(t, slot):
+            columns = pl.ds(pl.multiple_of(t * tile, tile), tile)
+            return [
+                pltpu.make_async_copy(room.at[slot], out.at[:, columns], mlp_sem.at[slot, k])
+                for k, (room, out) in enumerate(zip(rooms, mlp_out_refs))
+            ]
+
+        def body(t, slot):
+            @pl.when(t >= 2)
+            def _():
+                for v in results_of(t - 2, slot):
+                    v.wait()
+
+            for part, ref in enumerate((two_mine, two_theirs)):
+                row_values = gathered(ref, slice(None), cols, size)
+                gate = jnp.dot(
+                    row_values, tile_rows(gate_room.at[slot], tile), preferred_element_type=f32
+                )
+                up = jnp.dot(
+                    row_values, tile_rows(up_room.at[slot], tile), preferred_element_type=f32
+                )
+                value, slope = gelu_parts(gate)
+                row_at = pl.ds(part * own, own)
+                act_room[slot, row_at, :] = (value * up).astype(bf16)
+                slope_room[slot, row_at, :] = (slope * up).astype(bf16)
+                value_room[slot, row_at, :] = value.astype(bf16)
+            for v in results_of(t, slot):
+                v.start()
+
+        count_tiles = hidden // tile
+        half_way = count_tiles // 2
+        stream_tiles(0, half_way, Both, body)
+        pass_on(mo, 3, 7)
+        pass_on(mo, 6, 8)
+        stream_tiles(half_way, count_tiles, Both, body)
+        for t in (count_tiles - 2, count_tiles - 1):
+            for v in results_of(t, t % 2):
+                v.wait()
 
     @pl.when(at.works)
     def _():
@@ -415,57 +566,16 @@
         pass_on(ro, 3, 7)
         pass_on(ro, 6, 8)
         grad_y.start()
-        for w, target in ((ri, w_ri), (ro, w_ro)):
-            hop(w, 1).wait_recv()
-            for k in (5, 7, 8):
-                hop(w, k).wait_recv()
-            for b in range(blocks):
-                load(w, target, b).start()
-        for b in range(blocks):
-            load(ri, w_ri, b).wait()
-        one_core.wait_recv()
-        mask_core.wait_recv()
-
-        def keep_both(start, value):
-            both_ref[pl.ds(start, chunk_rows), :] = value
-
-        keep_out(3).start()
-        keep_out(5).start()
-        keep_out(6).start()
-        keep_out(7).start()
-        project(one_mine, one_theirs, w_ri, cols, keep_both)
-        keep_out(0).start()
-        grad_in.wait_recv()
-        grad_y_two.start()
-        recur_state(both_ref, mask_ref, vec_ref, wr_ref, wi_ref, coef_ref, state_ref)
-        keep_out(1).start()
-        pass_on(mi, 2, 6)
-        pass_on(mi, 4, 5)
-        own_block(mo, (1, 4))
-        recur_mixed(both_ref, state_ref, mixed_ref)
-        keep_out(2).start()
-        for b in range(blocks):
-            load(ro, w_ro, b).wait()
-
-        def branch(start, out_ref, out_at):
-            for b in range(blocks):
-                out_ref[out_at, columns_at(cols, b, size)] = lax.dot_general(
-                    mixed_ref[pl.ds(start, rows), :],
-                    w_ro[b],
-                    contract_cols,
-                    preferred_element_type=f32,
-                ).astype(out_ref.dtype)
-
-        for i, h in enumerate(halves):
-            branch(own + i * rows, part_out, h)
-            part_core[i].start()
-        for i, h in enumerate(halves):
-            branch(i * rows, part_sum, first)
-            part_core[i].wait_recv()
-            middle_ref[h, :] = part_sum[:, left] + part_in[h, left].astype(f32)
-            y_out[h, :] = (part_sum[:, right] + part_in[h, right].astype(f32)).astype(bf16)
-            part_y[i].start()
-        pass_on(mi, 3, 7)
+        width = vec_ref.shape[1]
+        pl.run_scoped(
+            recur_part,
+            pltpu.VMEM((2 * own, 2 * width), f32),
+            pltpu.VMEM((2 * own, width), bf16),
+            pltpu.VMEM(state_ref.shape, f32),
+            pltpu.VMEM(g_ri.shape, bf16),
+            pltpu.VMEM(g_ro.shape, bf16),
+            pltpu.VMEM((rows, model), f32),
+        )
         grad_here.wait()
         grad_y.wait_recv()
         grad_y_two.wait_recv()
@@ -479,25 +589,32 @@
             mid_ref[h, left] = middle.astype(bf16)
             mid_y[i].start()
         keep_out(4).start()
+        pass_on(mi, 3, 7)
         pass_on(mi, 6, 8)
-        pass_on(mo, 2, 6)
-        pass_on(mo, 4, 5)
+        own_block(mo, (1, 4))
         for i, h in enumerate(halves):
             mid_y[i].wait_recv()
             normed_rows(mid_ref, gain_ref, 1, scale_ref, 1, two_mine, i * rows, rows)
             two_core[i].start()
         keep_out(8).start()
         keep_out(12).start()
-        pass_on(mo, 3, 7)
-        pass_on(mo, 6, 8)
-        for w in (mi, mo):
-            for k in (1, 5, 7, 8):
-                hop(w, k).wait_recv()
+        pass_on(mo, 2, 6)
+        pass_on(mo, 4, 5)
         low_core.wait_recv()
         keep_out(11).start()
         for moved in two_core:
             moved.wait_recv()
         keep_out(9).start()
+        for k in (1, 5, 7, 8):
+            hop(mi, k).wait_recv()
+        tile = 256
+        pl.run_scoped(
+            mlp_part,
+            *[pltpu.VMEM((2, size, blocks * tile), bf16)] * 2,
+            *[pltpu.VMEM((2, 2 * own, tile), bf16)] * 3,
+        )
+        for k in (1, 5, 7, 8):
+            hop(mo, k).wait_recv()
         for w in (ri, ro, mi, mo):
             for k in (1, 4, 5, 6, 7, 8):
                 hop(w, k).wait_send()
@@ -507,7 +624,8 @@
         ):
             moved.wait_send()
         for k in range(13):
-            keep_out(k).wait()
+            if k not in (0, 2):
+                keep_out(k).wait()
 
 
 def recur_first(both_ref, state_ref, mask_ref, vec_ref, wr_ref, wi_ref, dmix_ref, dboth_ref, coef_ref, push_ref):
@@ -593,27 +711,6 @@
     lax.fori_loop(0, held_buffers, last, 0)
 
 
-def mlp_forward(mine_ref, theirs_ref, gate_weight, up_weight, cols_ref, act_ref, slope_ref, value_ref):
-    size = gate_weight.shape[1]
-    own = mine_ref.shape[0]
-    for part, ref in enumerate((mine_ref, theirs_ref)):
-
-        def chunk(i, carry, part=part, ref=ref):
-            rows = gathered(
-                ref, pl.ds(pl.multiple_of(i * chunk_rows, chunk_rows), chunk_rows), cols_ref, size
-            )
-            gate = jnp.dot(rows, stacked(gate_weight), preferred_element_type=f32)
-            up = jnp.dot(rows, stacked(up_weight), preferred_element_type=f32)
-            value, slope = gelu_parts(gate)
-            at = pl.ds(pl.multiple_of(part * own + i * chunk_rows, chunk_rows), chunk_rows)
-            act_ref[at, :] = (value * up).astype(bf16)
-            slope_ref[at, :] = (slope * up).astype(bf16)
-            value_ref[at, :] = value.astype(bf16)
-            return carry
-
-        lax.fori_loop(0, own // chunk_rows, chunk, 0)
-
-
 class Sums:
     def __init__(self, at, partial, land, total, send, recv):
         self.at, self.partial, self.land, self.total = at, partial, land, total
@@ -639,7 +736,7 @@
             lambda: (land.at[0], land.at[4], at.ahead),
             lambda: (land.at[2], land.at[2], at.behind),
             lambda: (land.at[0], land.at[3], at.beside),
-            lambda: (last.at[self.rows_of(1 - at.c)], self.total.at[1], at.core),
+            lambda: (last.at[self.rows_of(1 - at.c)], self.total.at[at.c], at.core),
         )[k]()
         return remote(src, dst, self.send.at[k], self.recv.at[k], where)
 
@@ -655,20 +752,21 @@
         for k in hops:
             self.hop(k).wait_send()
 
+    def operands(self, k):
+        d, land, top, bottom = self.partial, self.land, self.top, self.bottom
+        return {
+            4: (land.at[1, top], d.at[6, bottom]),
+            6: (land.at[1, bottom], d.at[3, top]),
+            8: (land.at[0], d.at[4]),
+            9: (land.at[2], d.at[2]),
+        }[k]
+
+    def arrived(self, k):
+        self.received(*{4: (1,), 6: (2,), 8: (0,), 9: (3, 4)}[k])
+
     def step(self, k, add):
-        d, land, top, bottom = self.partial, self.land, self.top, self.bottom
-        if k == 4:
-            self.received(1)
-            add(land.at[1, top], d.at[6, bottom])
-        elif k == 6:
-            self.received(2)
-            add(land.at[1, bottom], d.at[3, top])
-        elif k == 8:
-            self.received(0)
-            add(land.at[0], d.at[4])
-        elif k == 9:
-            self.received(3, 4)
-            add(land.at[2], d.at[2])
+        self.arrived(k)
+        add(*self.operands(k))
         self.start(k)
 
 
@@ -721,23 +819,6 @@
         return carry
 
     lax.fori_loop(0, count // size, chunk, 0)
-
-
-def stream_tiles(count, fetch, body):
-    fetch(0, 0).start()
-
-    def step(t, carry):
-        slot = t % 2
-
-        @pl.when(t + 1 < count)
-        def _():
-            fetch(t + 1, 1 - slot).start()
-
-        fetch(t, slot).wait()
-        body(t, slot)
-        return carry
-
-    lax.fori_loop(0, count, step, 0)
 
 
 def backward_kernel(
@@ -780,8 +861,8 @@
     ]
     db_core = [move(11 + i, db_mine.at[h], db_theirs.at[h], at.core) for i, h in enumerate(halves)]
     out_move = move(13, out_ref.at[second], out_ref.at[first], at.behind)
-    low_load = pltpu.make_async_copy(low_mine.at[:, left], low_left, local_sem.at[0])
-    middle_load = pltpu.make_async_copy(middle_in, middle_ref, local_sem.at[4])
+    low_load = pltpu.make_async_copy(low_mine.at[:, left], low_left, local_sem.at[6])
+    middle_load = pltpu.make_async_copy(middle_in, middle_ref, local_sem.at[7])
     keep_out = [
         pltpu.make_async_copy(src, dst, out_sem.at[k])
         for k, (src, dst) in enumerate(
@@ -792,37 +873,52 @@
     def fetch(src, dst, k):
         return pltpu.make_async_copy(src, dst, local_sem.at[k])
 
-    def add(into, value):
+    def staged(w, k):
+        into, value = w.operands(k)
         count_rows, wide = into.shape
-        a = stage_a.at[pl.ds(0, count_rows), pl.ds(0, wide)]
-        b = stage_b.at[pl.ds(0, count_rows), pl.ds(0, wide)]
-        loads = fetch(into, a, 1), fetch(value, b, 2)
-        for v in loads:
-            v.start()
-        for v in loads:
-            v.wait()
-        add_rows(a, b)
-        back = fetch(a, into, 3)
-        back.start()
-        back.wait()
+        at_rows = pl.ds(0, count_rows) if k != 6 else pl.ds(count_rows, count_rows)
+        place = 3 if k == 6 else 0
+        a = stage_a.at[at_rows, pl.ds(0, wide)]
+        b = stage_b.at[at_rows, pl.ds(0, wide)]
+        return a, b, fetch(into, a, place), fetch(value, b, place + 1), fetch(a, into, place + 2)
+
+    def begin(w, *hops):
+        for k in hops:
+            w.arrived(k)
+            _, _, load_a, load_b, _ = staged(w, k)
+            load_a.start()
+            load_b.start()
+
+    def combine(w, *hops):
+        for k in hops:
+            a, b, load_a, load_b, back = staged(w, k)
+            load_a.wait()
+            load_b.wait()
+            add_rows(a, b)
+            back.start()
+
+    def send_on(w, *hops):
+        for k in hops:
+            staged(w, k)[4].wait()
+            w.start(k)
 
     def finish(w, parts):
         count_rows, wide = parts[0].shape
         a = stage_a.at[pl.ds(0, count_rows), pl.ds(0, wide)]
         b = stage_b.at[pl.ds(0, count_rows), pl.ds(0, wide)]
-        loads = fetch(parts[0], a, 1), fetch(parts[1], b, 2)
+        loads = fetch(parts[0], a, 0), fetch(parts[1], b, 1)
         for v in loads:
             v.start()
         for v in loads:
             v.wait()
         add_rows(a, b)
         if len(parts) == 3:
-            third = fetch(parts[2], b, 2)
+            third = fetch(parts[2], b, 1)
             third.start()
             third.wait()
             add_rows(a, b)
         w.hop(11, a).start()
-        kept = fetch(a.at[w.rows_of(at.c)], w.total.at[0], 3)
+        kept = fetch(a.at[w.rows_of(at.c)], w.total.at[at.c], 2)
         kept.start()
         kept.wait()
         w.hop(11, a).wait()
@@ -841,43 +937,43 @@
         for w in (mo, mi):
             w.sent(*serve_hops)
 
-    def partial_blocks(w, lhs, column_ref, room, order):
+    block_order = (
+        (7, (1, 2)), (5, (0,)), (6, (3,)), (3, (5,)), (1, (7,)), (4, ()), (2, ()), (0, ()),
+    )
+
+    def partial_blocks(w, lhs, column_ref, room, between=()):
         wide = column_ref.shape[1]
-        tile = 512
-        writes = []
-
-        def write(i, b):
+        between = dict(between)
+
+        def write(i):
             return pltpu.make_async_copy(
-                room.at[i % 2, :, pl.ds(0, wide)], w.partial.at[b], keep_sem.at[i % 2]
+                room.at[i % 2, :, pl.ds(0, wide)], w.partial.at[block_order[i][0]], keep_sem.at[i % 2]
             )
 
-        for i, (b, hops) in enumerate(order):
+        def leave(i):
+            write(i).wait()
+            w.start(*block_order[i][1])
+
+        for i in range(blocks):
             if i >= 2:
-                write(i - 2, order[i - 2][0]).wait()
-                w.start(*order[i - 2][1])
-            here = columns_at(cols, b, size)
-
-            def column(t, carry, i=i, here=here):
-                wide_at = pl.ds(pl.multiple_of(t * tile, tile), tile)
-                total = lax.dot_general(
-                    lhs[0, :, here], column_ref[:own, wide_at], contract_rows, preferred_element_type=f32
-                )
-                total = total + lax.dot_general(
-                    lhs[1, :, here], column_ref[own:, wide_at], contract_rows, preferred_element_type=f32
-                )
-                room[i % 2, :, wide_at] = total.astype(bf16)
-                return carry
-
-            lax.fori_loop(0, wide // tile, column, 0)
-            write(i, b).start()
-        for i in (len(order) - 2, len(order) - 1):
-            write(i, order[i][0]).wait()
-            w.start(*order[i][1])
-
-    def rows_product(weight, row_ref, room, wide, which, out):
+                leave(i - 2)
+            here = columns_at(cols, block_order[i][0], size)
+            rows_here = jnp.concatenate([lhs[0, :, here], lhs[1, :, here]], axis=0)
+            room[i % 2, :, :wide] = lax.dot_general(
+                rows_here, column_ref[...], contract_rows, preferred_element_type=f32
+            ).astype(bf16)
+            write(i).start()
+            if i in between:
+                between[i]()
+        leave(blocks - 2)
+        leave(blocks - 1)
+
+    def rows_product(weight, row_ref, room, wide, theirs_out, mine_out, between=()):
+        between = dict(between)
+
         def block(b):
             return pltpu.make_async_copy(
-                weight.at[b], room.at[b % 2, :, pl.ds(0, wide)], tile_sem.at[b % 2]
+                weight.at[b], room.at[b % 2, :, pl.ds(0, wide)], tile_sem.at[b % 2, 0]
             )
 
         block(0).start()
@@ -886,18 +982,19 @@
                 block(b + 1).start()
             block(b).wait()
             here = columns_at(cols, b, size)
-
-            def chunk(i, carry, b=b, here=here):
-                start = pl.multiple_of(i * chunk_rows, chunk_rows)
-                out[pl.ds(start, chunk_rows), here] = lax.dot_general(
-                    row_ref[pl.ds(which * own + start, chunk_rows), :],
-                    room[b % 2, :, pl.ds(0, wide)],
+            for which, out in ((1, theirs_out), (0, mine_out)):
+                out[:, here] = lax.dot_general(
+                    row_ref[which * own : (which + 1) * own, :],
+                    room[b % 2, :, :wide],
                     contract_cols,
                     preferred_element_type=f32,
                 ).astype(out.dtype)
-                return carry
-
-            lax.fori_loop(0, own // chunk_rows, chunk, 0)
+            if b in between:
+                between[b]()
+
+    def settle(w):
+        w.received(7, 8)
+        finish(w, (w.partial.at[0], w.land.at[3], w.land.at[4]))
 
     def join(i, h, mine_ref, arrived, landed, keep_value, sent_ref, over):
         arrived[i].wait_recv()
@@ -905,9 +1002,9 @@
         sent_ref[h, :] = (mine_ref[h, right] + landed[h, right].astype(f32)).astype(bf16)
         over[i].start()
 
-    def mlp_part(lhs, act_ref, pair_ref, tiles, room, mine_ref):
-        lhs_low = fetch(low_mine, lhs.at[0], 1), fetch(low_theirs, lhs.at[1], 2)
-        lhs_two = fetch(two_mine, lhs.at[0], 1), fetch(two_theirs, lhs.at[1], 2)
+    def mlp_part(lhs, act_ref, pair_ref, room, mine_ref):
+        lhs_low = fetch(low_mine, lhs.at[0], 8), fetch(low_theirs, lhs.at[1], 9)
+        lhs_two = fetch(two_mine, lhs.at[0], 8), fetch(two_theirs, lhs.at[1], 9)
         act_load = pltpu.make_async_copy(act_in, act_ref, load_sem.at[0])
         pair_load = [
             pltpu.make_async_copy(src, pair_ref.at[:, pl.ds(k * hidden, hidden)], load_sem.at[1 + k])
@@ -918,16 +1015,10 @@
         middle_load.start()
         for v in (*lhs_low, act_load):
             v.wait()
-        partial_blocks(
-            mo,
-            lhs,
-            act_ref,
-            room,
-            ((7, (1, 2)), (5, (0,)), (6, (3,)), (3, (5,)), (1, (7,)), (4, ()), (2, ()), (0, ())),
-        )
+        partial_blocks(mo, lhs, act_ref, room)
         for v in pair_load:
             v.wait()
-        tile = tiles.shape[3]
+        tile = 256
 
         def back(t, slot):
             gate_at = pl.ds(pl.multiple_of(t * tile, tile), tile)
@@ -938,41 +1029,54 @@
                 for where in (gate_at, up_at):
                     pair_ref[row_at, where] = (d_act * pair_ref[row_at, where].astype(f32)).astype(bf16)
 
-            project(lhs.at[0], lhs.at[1], tiles.at[slot], cols, use)
+            project(
+                lhs.at[0], lhs.at[1], lambda: tile_rows(room.at[slot], tile), size, cols, use
+            )
 
         stream_tiles(
+            0,
             hidden // tile,
-            lambda t, slot: pltpu.make_async_copy(
-                weight_mo.at[:, :, pl.ds(pl.multiple_of(t * tile, tile), tile)],
-                tiles.at[slot],
-                tile_sem.at[slot],
-            ),
+            lambda t, slot: Tile(weight_mo, room.at[slot], tile_sem.at[slot], t * tile, tile),
             back,
         )
         for v in lhs_two:
             v.start()
-        mo.step(4, add_late)
-        mo.step(6, add_late)
+        begin(mo, 4, 6)
+        rows_product(
+            weight_mi,
+            pair_ref,
+            room,
+            2 * hidden,
+            part_out,
+            mine_ref,
+            (
+                (1, lambda: combine(mo, 4, 6)),
+                (2, lambda: send_on(mo, 4, 6)),
+                (4, lambda: begin(mo, 8)),
+                (6, lambda: combine(mo, 8)),
+            ),
+        )
+        for moved in e_core:
+            moved.start()
+        send_on(mo, 8)
+
+        def keep_e(h, value):
+            e_ref[h, :] = value
+
+        for i, h in enumerate(halves):
+            join(i, h, mine_ref, e_core, part_in, keep_e, y_out, e_y)
         for v in lhs_two:
             v.wait()
-        rows_product(weight_mi, pair_ref, room, 2 * hidden, 1, part_out)
-        for moved in e_core:
-            moved.start()
-        mo.step(8, add)
-        rows_product(weight_mi, pair_ref, room, 2 * hidden, 0, mine_ref)
-
-        def keep_e(h, value):
-            e_ref[h, :] = value
-
-        for i, h in enumerate(halves):
-            join(i, h, mine_ref, e_core, part_in, keep_e, y_out, e_y)
-        mo.step(9, add)
         partial_blocks(
             mi,
             lhs,
             pair_ref,
             room,
-            ((7, (1, 2)), (5, (0,)), (6, (3,)), (3, (5,)), (1, (7,)), (4, ()), (2, ()), (0, ())),
+            (
+                (2, lambda: begin(mo, 9)),
+                (4, lambda: combine(mo, 9)),
+                (5, lambda: send_on(mo, 9)),
+            ),
         )
         middle_load.wait()
         for i, h in enumerate(halves):
@@ -982,7 +1086,8 @@
         for moved in e_y:
             moved.wait_send()
         low_load.start()
-        mi.step(6, add)
+        for moved in e_core:
+            moved.wait_send()
         low_load.wait()
         mean_y.wait_recv()
 
@@ -997,13 +1102,18 @@
                 i * rows, rows, keep,
             )
             db_y[i].start()
-        for moved in e_core:
-            moved.wait_send()
-        rows_product(weight_mo, act_ref, room, hidden, 1, part_out)
+        begin(mi, 4, 6)
+        rows_product(
+            weight_mo,
+            act_ref,
+            room,
+            hidden,
+            part_out,
+            mine_ref,
+            ((1, lambda: combine(mi, 4, 6)), (2, lambda: send_on(mi, 4, 6))),
+        )
         for moved in o_core:
             moved.start()
-        mi.step(4, add)
-        rows_product(weight_mo, act_ref, room, hidden, 0, mine_ref)
 
         def keep_o(h, value):
             middle_ref[h, :] = middle_ref[h, :] + value
@@ -1013,20 +1123,6 @@
             db_core[i].start()
         for i, h in enumerate(halves):
             join(i, h, mine_ref, o_core, o_in, keep_o, oy_out, o_y)
-
-    def add_late(into, value):
-        count_rows, wide = into.shape
-        a = stage_a.at[pl.ds(0, count_rows), pl.ds(0, wide)]
-        b = stage_b.at[pl.ds(0, count_rows), pl.ds(0, wide)]
-        loads = fetch(into, a, 5), fetch(value, b, 6)
-        for v in loads:
-            v.start()
-        for v in loads:
-            v.wait()
-        add_rows(a, b)
-        back = fetch(a, into, 3)
-        back.start()
-        back.wait()
 
     def recur_part(w_ro, both_ref, state_ref, dboth_ref, coef_ref, push_ref, dmix_ref, gr_ref, gi_ref):
         loads = [
@@ -1037,17 +1133,23 @@
         ]
         for v in loads:
             v.start()
+        begin(mi, 9)
         for i in range(2):
             db_core[i].wait_recv()
         for v in keep_out:
             v.start()
+        combine(mi, 9)
         for v in loads:
             v.wait()
+        send_on(mi, 9)
+        begin(mi, 8)
 
         def keep_mixed(start, value):
             dmix_ref[pl.ds(start, chunk_rows), :] = value
 
-        project(db_mine, db_theirs, w_ro, cols, keep_mixed)
+        project(db_mine, db_theirs, lambda: stacked(w_ro), size, cols, keep_mixed)
+        combine(mi, 8)
+        send_on(mi, 8)
         recur_first(
             both_ref, state_ref, mask_ref, vec_ref, wr_ref, wi_ref, dmix_ref, dboth_ref, coef_ref, push_ref
         )
@@ -1057,9 +1159,7 @@
                 mask_ref[h, 4:5] * (middle_ref[h, :] + oy_in[h, :].astype(f32))
             ).astype(bf16)
         out_move.start()
-        mi.step(8, add)
         scan_rows(coef_ref, push_ref, both_ref.shape[0] // held_buffers, True)
-        mi.step(9, add)
         recur_last(
             both_ref, state_ref, mask_ref, vec_ref, wr_ref, wi_ref, push_ref,
             dboth_ref, sums_ref, gr_ref, gi_ref,
@@ -1083,7 +1183,6 @@
             pltpu.VMEM((2, own, model), bf16),
             pltpu.VMEM((2 * own, hidden), bf16),
             pltpu.VMEM((2 * own, 2 * hidden), bf16),
-            pltpu.VMEM((2, blocks, size, 256), bf16),
             pltpu.VMEM((2, size, 2 * hidden), bf16),
             pltpu.VMEM((own, model), f32),
         )
@@ -1100,8 +1199,7 @@
             pltpu.VMEM((width, width), f32),
         )
         for w in (mo, mi):
-            w.received(7, 8)
-            finish(w, (w.partial.at[0], w.land.at[3], w.land.at[4]))
+            settle(w)
         for w in (mo, mi):
             w.sent(*work_hops)
         for v in keep_out:
@@ -1168,7 +1266,7 @@
         last_r[...] = parts[0][...]
         add_rows(last_r, parts[1], parts[2] if len(parts) == 3 else None)
         w.hop(11, last_r).start()
-        w.total[0] = last_r[w.rows_of(at.c), :]
+        w.total[at.c] = last_r[w.rows_of(at.c), :]
 
     def unpack(place, quarter):
         block = recur_out.shape[1]
@@ -1201,9 +1299,10 @@
 
     @pl.when(at.works)
     def _():
+        gates_x.start()
+        sums_x.start()
         for k in (4, 0, 1, 5, 2, 3, 6, 7, 8):
             loads[k].start()
-        sums_x.start()
         for k in (4, 0, 1, 5, 2, 3):
             loads[k].wait()
 
@@ -1222,7 +1321,16 @@
             d_r[b, :, :pair_width] = product(one_mine, one_theirs, dboth_ref)
             d_r[b, :, pair_width:] = product(db_mine, db_theirs, mixed_ref)
 
-        for b, hops in ((7, (1, 2)), (5, (0,)), (6, (3,)), (3, (5,))):
+        for b, hops in ((7, (1, 2)), (5, (0,))):
+            partial(b)
+            w.start(*hops)
+        sums_x.wait_recv()
+        sums_in[0] = sums_in[0] + sums_ref[...]
+        sums_z.start()
+        gates_x.wait_recv()
+        add_rows(gates_in.at[0], gates_ref)
+        gates_z.start()
+        for b, hops in ((6, (3,)), (3, (5,))):
             partial(b)
             w.start(*hops)
 
@@ -1246,22 +1354,20 @@
             e_ref[h, :] = part_sum[:, left] + part_in[h, left].astype(f32)
             y_out[h, :] = (part_sum[:, right] + part_in[h, right].astype(f32)).astype(bf16)
             e_y[i].start()
-        w.step(8, add)
-        gates_x.start()
-        w.start(7)
-        sums_x.wait_recv()
-        sums_in[0] = sums_in[0] + sums_ref[...]
-        sums_z.start()
-        for b in (2, 0):
-            partial(b)
-        w.step(9, add)
         sums_z.wait_recv()
         sums_out[0] = sums_in[0] + sums_in[1]
         sums_end.start()
         sums_core.start()
-        gates_x.wait_recv()
-        add_rows(gates_in.at[0], gates_ref)
-        gates_z.start()
+        gates_z.wait_recv()
+        gates_out[0] = gates_in[0]
+        add_rows(gates_out.at[0], gates_in.at[1])
+        gates_end.start()
+        gates_core.start()
+        w.step(8, add)
+        w.start(7)
+        for b in (2, 0):
+            partial(b)
+        w.step(9, add)
         term_ref[...] = term_in[...]
         for k in (7, 8):
             loads[k].wait()
@@ -1269,11 +1375,6 @@
             e_y[i].wait_recv()
             norm_sums(e_ref, y_in, tok_left, gain_ref, 0, mean_ref, i * rows, rows)
         mean_y.start()
-        gates_z.wait_recv()
-        gates_out[0] = gates_in[0]
-        add_rows(gates_out.at[0], gates_in.at[1])
-        gates_end.start()
-        gates_core.start()
         unpack(0, at.c)
         mean_y.wait_recv()
 
@@ -1323,12 +1424,12 @@
     return (pl.cdiv(width, lanes), rows, lanes)
 
 
-def run_forward(count, keeps, gives, tokens, out_grad, mask, gains, vectors, wr, wi):
+def run_forward(count, splits, tokens, out_grad, mask, gains, vectors, wr, wi):
     rows, half_model = tokens.shape
     own, model, width = 2 * rows, 2 * half_model, wr.shape[0]
-    size = 2 * keeps[0].shape[0]
+    size = 2 * splits[0].shape[1]
     shape = jax.ShapeDtypeStruct
-    gathered_shapes = [shape((blocks, size, v.shape[1]), bf16) for v in keeps]
+    gathered_shapes = [shape((blocks, size, v.shape[2]), bf16) for v in splits]
     wide = shape((own, model), bf16)
     kept = [
         shape((2 * own, 2 * width), f32),
@@ -1340,20 +1441,21 @@
         *[wide] * 6,
         shape((2, own, lanes), f32),
     ]
+    hidden = shape((2 * own, splits[3].shape[2]), bf16)
     return pl.pallas_call(
         functools.partial(forward_kernel, count),
-        out_shape=(*gathered_shapes, *kept),
-        in_specs=[in_any] * 11 + [in_vmem] * 4,
-        out_specs=[in_any] * 17,
+        out_shape=(*gathered_shapes, *kept, *[hidden] * 3),
+        in_specs=[in_any] * 7 + [in_vmem] * 4,
+        out_specs=[in_any] * 20,
         scratch_shapes=[
-            *[pltpu.VMEM(wide.shape if i == 5 else v.shape, v.dtype) for i, v in enumerate(kept)],
-            pltpu.VMEM(lane_shape(2 * own, width), f32),
-            pltpu.VMEM((blocks, size, 2 * width), bf16),
-            pltpu.VMEM((blocks, size, width), bf16),
+            *[
+                pltpu.VMEM(wide.shape if i == 5 else v.shape, v.dtype)
+                for i, v in enumerate(kept)
+                if i not in (0, 2)
+            ],
             pltpu.VMEM((own, model), bf16),
             pltpu.VMEM((own, model), bf16),
             pltpu.VMEM((own, model), bf16),
-            pltpu.VMEM((rows, model), f32),
             pltpu.VMEM((own, half_model), bf16),
             pltpu.VMEM((own, half_model), bf16),
             pltpu.VMEM((own, model), bf16),
@@ -1365,16 +1467,18 @@
             copy_sem((18,)),
             copy_sem((3,)),
             copy_sem((13,)),
+            copy_sem((2, 2, blocks)),
+            copy_sem((2, 3)),
         ],
         compiler_params=comm_params(0),
         cost_estimate=no_cost,
         name="gather_and_recur",
-    )(*keeps, *gives, tokens, out_grad, mask, gains, vectors, wr, wi)
+    )(*splits, tokens, out_grad, mask, gains, vectors, wr, wi)
 
 
 def comm_params(collective):
     return pltpu.CompilerParams(
-        vmem_limit_bytes=63 * 2**20, collective_id=collective, has_side_effects=True
+        vmem_limit_bytes=255 * 2**18, collective_id=collective, has_side_effects=True
     )
 
 
@@ -1417,10 +1521,10 @@
             copy_sem((2, 12)),
             copy_sem((14,)),
             copy_sem((14,)),
-            copy_sem((7,)),
+            copy_sem((10,)),
             copy_sem((4,)),
             copy_sem((4,)),
-            copy_sem((2,)),
+            copy_sem((2, blocks)),
             copy_sem((2,)),
         ],
         compiler_params=comm_params(1),
@@ -1485,27 +1589,6 @@
     )(*held, scales, gains, sums, gates, term)
 
 
-def run_mlp_forward(normed, weight, cols):
-    own, model = normed[0].shape
-    size, hidden = weight.shape[1], weight.shape[2] // 2
-    tile = 256
-    tiles = hidden // tile
-    out = jax.ShapeDtypeStruct((2 * own, hidden), bf16)
-    return pl.pallas_call(
-        mlp_forward,
-        grid=(tiles,),
-        out_shape=(out, out, out),
-        in_specs=[pl.BlockSpec((own, model), lambda n: (0, 0))] * 2
-        + [pl.BlockSpec((blocks, size, tile), lambda n: (0, 0, n))]
-        + [pl.BlockSpec((blocks, size, tile), lambda n: (0, 0, n + tiles))]
-        + [in_smem],
-        out_specs=[pl.BlockSpec((2 * own, tile), lambda n: (0, n))] * 3,
-        compiler_params=kernel_params,
-        cost_estimate=no_cost,
-        name="mlp_forward",
-    )(*normed, weight, weight, cols)
-
-
 def block_diagonal(blocks):
     count, size = blocks.shape[0], blocks.shape[1]
     rows = [
@@ -1584,7 +1667,7 @@
     def over_outer(value):
         if outer_count == 1:
             return value
-        return lax.all_gather(value, "dp", axis_index_groups=outer_groups, axis=0, tiled=True)
+        return lax.all_gather(value, "dp", axis_index_groups=outer_groups, axis=1, tiled=True)
 
     cols = jnp.stack(
         [
@@ -1595,16 +1678,20 @@
     ).astype(jnp.int32)
 
     def settle_grad(total):
-        first, second = pick_c(total[0], total[1]), pick_c(total[1], total[0])
-        first, second = first.astype(f32), second.astype(f32)
+        total = total.astype(f32)
         if outer_count > 1:
-            first, second = (
-                lax.psum_scatter(
-                    v, "dp", axis_index_groups=outer_groups, scatter_dimension=0, tiled=True
-                )
-                for v in (first, second)
+            total = lax.psum_scatter(
+                total, "dp", axis_index_groups=outer_groups, scatter_dimension=1, tiled=True
             )
-        return first, second
+        return total
+
+    def joined_pair(total):
+        _, row_count, columns = total.shape
+        parts = settle_grad(total).reshape(2, -1, 2, columns // 2).transpose(1, 2, 0, 3)
+        return parts.reshape(-1, 2, columns)
+
+    def joined_out(total):
+        return settle_grad(total).swapaxes(0, 1).reshape(-1, 2 * total.shape[2])
 
     def over_groups(value):
         return lax.psum(value, "dp", axis_index_groups=outer_groups) if outer_count > 1 else value
@@ -1619,10 +1706,6 @@
             lax.slice_in_dim(value, 0, size, axis=axis),
             lax.slice_in_dim(value, size, 2 * size, axis=axis),
         )
-
-    def pair_quarters(weight):
-        first, second = quarters(weight, 2)
-        return tuple(jnp.concatenate([v[:, 0], v[:, 1]], axis=1) for v in (first, second))
 
     def quarter(value, axis=0):
         return pick_c(*quarters(value, axis))
@@ -1641,24 +1724,24 @@
     heads = gate_recur.shape[0] // 2
     wr = block_diagonal(quarter(gate_recur))
     wi = block_diagonal(quarter(gate_input))
-    split = (
-        pair_quarters(rnn_in),
-        quarters(rnn_out, 1),
-        pair_quarters(mlp_in),
-        quarters(mlp_out, 1),
-    )
-    split = [(over_outer(first), over_outer(second)) for first, second in split]
-    keeps = [pick_c(first, second) for first, second in split]
-    gives = [pick_c(second, first) for first, second in split]
+    def split_pair(weight):
+        row_count, _, columns = weight.shape
+        parts = weight.reshape(row_count, 2, 2, columns // 2).transpose(2, 0, 1, 3)
+        return over_outer(parts.reshape(2, row_count, columns))
+
+    def split_out(weight):
+        row_count, columns = weight.shape
+        return over_outer(weight.reshape(row_count, 2, columns // 2).swapaxes(0, 1))
+
+    splits = (split_pair(rnn_in), split_out(rnn_out), split_pair(mlp_in), split_out(mlp_out))
     gains = jnp.stack([gain_one, gain_two])
     (
         rnn_in_all, rnn_out_all, mlp_in_all, mlp_out_all,
         both, state, mixed, mask, middle, tokens_all,
-        *rows_kept, scales,
-    ) = run_forward(outer_count, keeps, gives, tokens, out_grad, mask, gains, vectors, wr, wi)
+        *rows_kept, scales, act, gate_slope, gate_value,
+    ) = run_forward(outer_count, splits, tokens, out_grad, mask, gains, vectors, wr, wi)
     normed, normed_two, grad_low = rows_kept[0:2], rows_kept[2:4], rows_kept[4:6]
 
-    act, gate_slope, gate_value = run_mlp_forward(normed_two, mlp_in_all, cols)
     (
         _, _, _, _, mlp_in_total, mlp_out_total, d_middle, d_branch, d_branch_theirs, d_both,
         output_two, sums, gates, term,
@@ -1698,10 +1781,6 @@
     rnn_width = rnn_in.shape[2]
     rnn_in_total, rnn_out_total = rnn_total[:, :, :rnn_width], rnn_total[:, :, rnn_width:]
     layer_output, tokens_grad = output_two[:buffer_rows], tokens_grad_two[:buffer_rows]
-    mlp_in_grad, mlp_out_grad, rnn_in_grad, rnn_out_grad = (
-        settle_grad(v) for v in (mlp_in_total, mlp_out_total, rnn_in_total, rnn_out_total)
-    )
-
     def both_quarters(pair, axis):
         return over_groups(
             pick_c(
@@ -1714,21 +1793,11 @@
     recur_grad, input_grad = over_groups(recur_grad), over_groups(input_grad)
     gains_grad = over_groups(term[:2])
 
-    def pair_layout(halves):
-        columns = halves[0].shape[1] // 2
-        return jnp.stack(
-            [
-                jnp.concatenate([v[:, k * columns : (k + 1) * columns] for v in halves], axis=1)
-                for k in range(2)
-            ],
-            axis=1,
-        )
-
     return (
         layer_output,
         tokens_grad,
         gains_grad[0],
-        pair_layout(rnn_in_grad),
+        joined_pair(rnn_in_total),
         recur_grad,
         input_grad,
         sums[5],
@@ -1736,10 +1805,10 @@
         8.0 * jax.nn.sigmoid(-decay_param) * sums[7],
         sums[:4],
         sums[4],
-        jnp.concatenate(rnn_out_grad, axis=1),
+        joined_out(rnn_out_total),
         gains_grad[1],
-        pair_layout(mlp_in_grad),
-        jnp.concatenate(mlp_out_grad, axis=1),
+        joined_pair(mlp_in_total),
+        joined_out(mlp_out_total),
     )
 
 

time: 627 us -> 560 us (0.89)
  Pallas kernels: 576 us -> 507 us
  local copies, waits for them, and re-layouts: 24.3 us -> 35 us
  other arithmetic: 18.8 us -> 12.3 us
    pallas_call x1, Pallas kernels: 254 us -> 216 us  [run_backward(): pl.pallas_call(functools.partial(backward_kernel, count), out_shape=(*[sh...]
    pallas_call x1 -> x0, Pallas kernels: 24.9 us -> none  [run_mlp_forward(): pl.pallas_call(mlp_forward, grid=(tiles,), out_shape=(out, out, out), in_...]
    reshape x0 -> x11, local copies, waits for them, and re-layouts: none -> 14.4 us  [the longest x4 7.31 us: joined_pair(): return parts.reshape(-1, 2, columns)]
    pallas_call x1, Pallas kernels: 117 us -> 106 us  [run_finish(): pl.pallas_call(functools.partial(finish_kernel, count), out_shape=(shape(...]
where the time goes in v5:
time: 560 us; the launch traced here: 555 us
  Pallas kernels  507 us (91%)
  local copies, waits for them, and re-layouts  35 us (6%)
  other arithmetic  12.3 us (2%)
    pallas_call x1, Pallas kernels, run_backward(): pl.pallas_call(functools.partial(backward_kernel, count), out_shape=(*[sh...  216 us
    pallas_call x1, Pallas kernels, run_forward(): pl.pallas_call(functools.partial(forward_kernel, count), out_shape=(*gath...  185 us
    pallas_call x1, Pallas kernels, run_finish(): pl.pallas_call(functools.partial(finish_kernel, count), out_shape=(shape(...  106 us
    unnamed x26, local copies, waits for them, and re-layouts  11.9 us

profile of v5, /device:TPU:0, one launch (start us, length us, event | category | flops | bytes accessed | tf_op | source)
XLA Modules:
  0.0 555.4 jit_solution(14539680197915249156)
XLA Ops:
  0.7 0.8 reduce_window_sum.11
  1.5 0.6 slice.125
  2.1 0.7 subtract_bitcast_fusion
  2.7 0.1 select_reduce_fusion
  2.8 0.7 compare_convert_fusion.1
  3.5 0.7 convert_element_type.89
  4.2 0.7 convert_element_type.90
  4.9 0.6 pad_maximum_fusion.gain_ref.refs_10_
  5.5 0.8 slice_select_fusion.4
  6.4 0.9 compare_select_fusion
  7.3 0.9 slice_select_fusion.2
  8.2 0.6 concatenate.23.vec_ref
  8.8 0.1 copy.79
  8.9 0.7 pad.32.mask_in
  9.6 1.2 copy.74
  10.8 0.9 copy.75
  11.7 2.5 copy.72
  14.3 1.1 copy.80.s_ri
  15.6 1.2 fusion.12.wr_ref
  16.8 1.2 fusion.15.wi_ref
  18.0 0.4 copy.77
  18.3 1.2 copy.78
  19.5 1.1 copy.92
  20.6 2.1 reshape.299.s_mi
  22.6 185.4 %gather_and_recur.1 = (bf16[8,256,1408]{2,1,0:T(8,128)(2,1)}, bf16[8,256,704]{2,1,0:T(8,128)(2,1)}, bf16[8,256,3072]{2,1,0:T(8,128)(2,1)}, bf16[8,256,1536]{2,1,...) custom-call(bf16[2,128,1408]{2,1,0:T(8,128)(2,1)} %copy.80.s_ri, ...), custom_call_target="tpu_custom_call" | custom-call | tf_op jit(solution)/shard_map/gather_and_recur/pallas_call | solution.py:1445
  208.1 215.6 %sum_and_back.1 = (bf16[8,256,3072]{2,1,0:T(8,128)(2,1)}, bf16[8,256,1536]{2,1,0:T(8,128)(2,1)}, bf16[5,256,3072]{2,1,0:T(8,128)(2,1)}, bf16[5,256,1536]{2,1,0:T...) custom-call(bf16[8,256,3072]{2,1,0:T(8,128)(2,1)} %get-tuple-element, ...), custom_call_target="tpu_custom_call" | custom-call | tf_op jit(solution)/shard_map/sum_and_back/pallas_call | solution.py:1496
  423.7 105.9 %sum_and_finish.1 = (bf16[2,128,2112]{2,1,0:T(8,128)(2,1)}, bf16[512,1024]{1,0:T(8,128)(2,1)}, f32[8,176,176]{2,1,0:T(8,128)}, f32[8,176,176]{2,1,0:T(8,128)}, f32[2,8,704]{2,1,0:T(8,128)}, /*index=5*/f32[8,1024]{1,0:T(8,128)}) custom-call(bf16[512,2048]{1,0:T(8,128)(2,1)} %get-tuple-element.67.refs_0_, bf16[512,2048]{1,0:T(8,128)(2,1)} %get-tuple-element.68.refs_1_, ...), custom_call_target="tpu_custom_call" | custom-call | tf_op jit(solution)/shard_map/sum_and_finish/pallas_call | solution.py:1550
  529.7 1.9 slice.152
  531.6 1.9 slice.153
  533.4 1.4 fusion.17
  535.0 0.6 slice.180
  535.6 0.7 slice_reduce_fusion
  536.2 0.6 multiply_multiply_fusion
  536.9 1.0 convert_bitcast_fusion.1
  537.9 0.3 copy.83
  538.2 1.1 copy.87
  539.3 1.2 slice_convert_fusion
  540.5 0.4 copy.81
  540.9 0.1 copy.82
  541.1 2.1 copy.86
  543.1 0.2 convert_bitcast_fusion
  543.3 0.5 copy.85
  543.8 1.6 copy.88
  545.4 4.0 reshape.327
  549.5 2.7 copy.90
  552.2 1.1 copy.95
  553.3 0.8 copy-done.1
  554.1 1.1 copy.96
  (33 shorter events, 0.4 us)
Async XLA Ops:
  11.7 3.7 copy-start.5
  11.7 3.7 copy-start.6
  15.6 2.4 copy-start.3
  16.8 2.7 copy-start
  529.7 5.2 copy-start.7
  529.7 6.6 %copy-start.8 = (f32[1408]{0:T(1024)S(1)}, f32[1408]{0:T(1024)}, u32[]{:S(2)}) copy-start(f32[1408]{0:T(1024)} %param.23) | copy-start | bytes 16900
  541.0 2.1 copy-start.4
  549.4 2.8 copy-start.2
  552.2 1.9 copy-start.1

commit v6 on v5

--- a/solution.py
+++ b/solution.py
@@ -303,21 +303,23 @@
 def forward_kernel(
     count,
     s_ri, s_ro, s_mi, s_mo,
-    tokens_ref, grad_ref, mask_in, gain_ref, vec_ref, wr_ref, wi_ref,
+    tokens_ref, grad_ref, lengths_ref, gain_ref, taps_ref, biases_ref, recur_blocks, input_blocks,
     g_ri, g_ro, g_mi, g_mo, *refs,
 ):
-    results, mlp_out_refs, refs = refs[:13], refs[13:16], refs[16:]
+    results, mlp_out_refs, refs = refs[:16], refs[16:19], refs[19:]
     (
         state_ref, mask_ref, middle_ref, tok_ref,
         one_mine, one_theirs, two_mine, two_theirs, low_mine, low_theirs, scale_ref,
-    ) = refs[:11]
+        vec_ref, wr_ref, wi_ref,
+    ) = refs[:14]
     (
         grad_all, part_out, part_in, y_out, y_in, mid_ref,
         w_send, w_recv, w_local, load_sem, m_send, m_recv, m_local, out_sem, tile_sem, mlp_sem,
-    ) = refs[11:]
+    ) = refs[14:]
     held = (
         None, state_ref, None, mask_ref, middle_ref, tok_ref,
         one_mine, one_theirs, two_mine, two_theirs, low_mine, low_theirs, scale_ref,
+        vec_ref, wr_ref, wi_ref,
     )
     at = Place(count)
     half_rows = s_ri.shape[1]
@@ -332,10 +334,16 @@
     top, bottom = pl.ds(0, half_rows), pl.ds(half_rows, half_rows)
     core_rows = pl.ds(pl.multiple_of(at.c * half_rows, half_rows), half_rows)
 
+    def split(w, quarter):
+        if w == mo:
+            columns = whole[w].shape[2]
+            return s_mo.at[:, pl.ds(pl.multiple_of(quarter * columns, lanes), columns)]
+        return splits[w].at[quarter]
+
     def hop(w, k):
         g = whole[w]
         src, dst, where = (
-            (splits[w].at[1 - at.c], g.at[0, core_rows], at.core),
+            (split(w, 1 - at.c), g.at[0, core_rows], at.core),
             (g.at[0], g.at[1], at.beside),
             (g.at[0], g.at[2], at.ahead),
             (g.at[1], g.at[3], at.ahead),
@@ -348,7 +356,7 @@
         return remote(src, dst, w_send.at[w, k], w_recv.at[w, k], where)
 
     def kept(w):
-        return pltpu.make_async_copy(splits[w].at[at.c], whole[w].at[0, core_rows], w_local.at[w])
+        return pltpu.make_async_copy(split(w, at.c), whole[w].at[0, core_rows], w_local.at[w])
 
     def begin(w):
         kept(w).start()
@@ -376,7 +384,7 @@
     grad_in = move(3, grad_ref, grad_all.at[second, left], at.ahead)
     grad_y = move(4, grad_ref, grad_all.at[first, right], at.over_y)
     grad_y_two = move(5, grad_all.at[second, left], grad_all.at[second, right], at.over_y)
-    mask_move = move(6, mask_in, mask_ref.at[second], at.ahead)
+    mask_move = move(6, mask_ref.at[first], mask_ref.at[second], at.ahead)
     mask_core = move(7, mask_ref.at[mine_rows], mask_ref.at[their_rows], at.core)
     one_core = move(8, one_mine, one_theirs, at.core)
     low_core = move(9, low_mine, low_theirs, at.core)
@@ -390,7 +398,6 @@
     two_core = [move(16 + i, two_mine.at[h], two_theirs.at[h], at.core) for i, h in enumerate(halves)]
     token_here = pltpu.make_async_copy(tokens_ref, tok_ref.at[first, left], m_local.at[0])
     grad_here = pltpu.make_async_copy(grad_ref, grad_all.at[first, left], m_local.at[1])
-    mask_here = pltpu.make_async_copy(mask_in, mask_ref.at[first], m_local.at[2])
 
     def load(w, target, b):
         return pltpu.make_async_copy(whole[w].at[b], target.at[b], load_sem.at[w, b])
@@ -400,23 +407,61 @@
             source = held[k].at[:, left] if k == 5 else held[k]
         return pltpu.make_async_copy(source, results[k], out_sem.at[k])
 
+    def make_mask():
+        place = lax.broadcasted_iota(jnp.int32, (rows, lanes), 0)
+        lane = lax.broadcasted_iota(jnp.int32, (rows, lanes), 1)
+        ends = [lengths_ref[0, 0]]
+        for k in (1, 2):
+            ends.append(ends[-1] + lengths_ref[0, k])
+        start = jnp.zeros((rows, lanes), jnp.int32)
+        for end in ends:
+            start = jnp.where(place >= end, end, start)
+        offset = place - start
+        bound = jnp.where(lane == 0, 1, jnp.where(lane == 4, place + 1 - ends[2] + offset, lane))
+        mask_ref[first, :] = jnp.where((offset >= bound) & (lane < 5), 1.0, 0.0)
+
+    def make_parameters():
+        width = vec_ref.shape[1]
+
+        def quarter(ref, row):
+            value = ref[row : row + 1, :]
+            return jnp.where(at.c == 0, value[:, :width], value[:, width:])
+
+        for k in range(4):
+            vec_ref[k : k + 1, :] = quarter(taps_ref, k)
+        for k in range(3):
+            vec_ref[4 + k : 5 + k, :] = quarter(biases_ref, k)
+        turned = -quarter(biases_ref, 3)
+        vec_ref[7:8, :] = jnp.maximum(turned, 0.0) + jnp.log1p(jnp.exp(-jnp.abs(turned)))
+        block = recur_blocks.shape[1]
+        count_heads = width // block
+        for source, target in ((recur_blocks, wr_ref), (input_blocks, wi_ref)):
+            for h in range(count_heads):
+                parts = [source[at.c * count_heads + h]]
+                if h > 0:
+                    parts.insert(0, jnp.zeros((block, h * block), bf16))
+                if h + 1 < count_heads:
+                    parts.append(jnp.zeros((block, (count_heads - 1 - h) * block), bf16))
+                target[h * block : (h + 1) * block, :] = jnp.concatenate(parts, axis=1)
+
     at.meet()
 
     @pl.when(at.serves)
     def _():
-        mask_move.start()
-        token_in.start()
         for w in (ri, ro, mi, mo):
             begin(w)
-        for w in (ri, ro):
-            own_block(w, (1, 2))
-        for w in (ri, ro):
-            pass_on(w, 1, 3)
+        token_in.start()
+        make_mask()
+        mask_move.start()
+        own_block(ri, (1, 2))
+        pass_on(ri, 1, 3)
+        own_block(ro, (1, 2))
+        pass_on(ro, 1, 3)
+        own_block(mi, (1, 2))
         grad_in.start()
-        for w in (mi, mo):
-            own_block(w, (1, 2))
-        for w in (mi, mo):
-            pass_on(w, 1, 3)
+        pass_on(mi, 1, 3)
+        own_block(mo, (1, 2))
+        pass_on(mo, 1, 3)
         for w in (ri, ro, mi, mo):
             for k in (1, 2, 3):
                 hop(w, k).wait_send()
@@ -524,45 +569,49 @@
                 v.start()
 
         count_tiles = hidden // tile
-        half_way = count_tiles // 2
-        stream_tiles(0, half_way, Both, body)
+        stream_tiles(0, 2, Both, body)
+        pass_on(mo, 2, 6)
+        pass_on(mo, 4, 5)
+        stream_tiles(2, count_tiles, Both, body)
         pass_on(mo, 3, 7)
         pass_on(mo, 6, 8)
-        stream_tiles(half_way, count_tiles, Both, body)
         for t in (count_tiles - 2, count_tiles - 1):
             for v in results_of(t, t % 2):
                 v.wait()
 
     @pl.when(at.works)
     def _():
-        token_here.start()
-        mask_here.start()
-        token_y.start()
         begin(ri)
         begin(ro)
+        token_here.start()
+        token_y.start()
         grad_here.start()
         begin(mi)
         begin(mo)
         own_block(ri, (1, 4))
         own_block(ro, (1, 4))
-        mask_here.wait()
-        mask_move.wait_recv()
-        mask_core.start()
+        make_mask()
+        pass_on(ri, 4, 5)
         token_in.wait_recv()
         token_y_two.start()
         pass_on(ri, 2, 6)
-        pass_on(ri, 4, 5)
+        pass_on(ro, 4, 5)
         token_here.wait()
         token_y.wait_recv()
         normed_rows(tok_ref, gain_ref, 0, scale_ref, 0, one_mine, 0, rows)
         token_y_two.wait_recv()
         normed_rows(tok_ref, gain_ref, 0, scale_ref, 0, one_mine, rows, rows)
         one_core.start()
-        pass_on(ro, 2, 6)
-        pass_on(ro, 4, 5)
+        own_block(mi, (1, 4))
+        make_parameters()
+        keep_out(13).start()
+        keep_out(14).start()
+        keep_out(15).start()
+        mask_move.wait_recv()
+        mask_core.start()
         pass_on(ri, 3, 7)
         pass_on(ri, 6, 8)
-        own_block(mi, (1, 4))
+        pass_on(ro, 2, 6)
         pass_on(ro, 3, 7)
         pass_on(ro, 6, 8)
         grad_y.start()
@@ -598,8 +647,6 @@
             two_core[i].start()
         keep_out(8).start()
         keep_out(12).start()
-        pass_on(mo, 2, 6)
-        pass_on(mo, 4, 5)
         low_core.wait_recv()
         keep_out(11).start()
         for moved in two_core:
@@ -623,7 +670,7 @@
             *part_core, *part_y, *mid_y, *two_core,
         ):
             moved.wait_send()
-        for k in range(13):
+        for k in range(16):
             if k not in (0, 2):
                 keep_out(k).wait()
 
@@ -1424,12 +1471,13 @@
     return (pl.cdiv(width, lanes), rows, lanes)
 
 
-def run_forward(count, splits, tokens, out_grad, mask, gains, vectors, wr, wi):
+def run_forward(count, splits, tokens, out_grad, lengths, gains, taps, biases, recur_blocks, input_blocks):
     rows, half_model = tokens.shape
-    own, model, width = 2 * rows, 2 * half_model, wr.shape[0]
+    own, model, width = 2 * rows, 2 * half_model, taps.shape[1] // 2
     size = 2 * splits[0].shape[1]
+    columns = [v.shape[2] for v in splits[:3]] + [splits[3].shape[1] // 2]
     shape = jax.ShapeDtypeStruct
-    gathered_shapes = [shape((blocks, size, v.shape[2]), bf16) for v in splits]
+    gathered_shapes = [shape((blocks, size, n), bf16) for n in columns]
     wide = shape((own, model), bf16)
     kept = [
         shape((2 * own, 2 * width), f32),
@@ -1440,13 +1488,16 @@
         shape((own, half_model), bf16),
         *[wide] * 6,
         shape((2, own, lanes), f32),
+        shape((8, width), f32),
+        shape((width, width), bf16),
+        shape((width, width), bf16),
     ]
-    hidden = shape((2 * own, splits[3].shape[2]), bf16)
+    hidden = shape((2 * own, columns[3]), bf16)
     return pl.pallas_call(
         functools.partial(forward_kernel, count),
         out_shape=(*gathered_shapes, *kept, *[hidden] * 3),
-        in_specs=[in_any] * 7 + [in_vmem] * 4,
-        out_specs=[in_any] * 20,
+        in_specs=[in_any] * 6 + [in_smem] + [in_vmem] * 5,
+        out_specs=[in_any] * 23,
         scratch_shapes=[
             *[
                 pltpu.VMEM(wide.shape if i == 5 else v.shape, v.dtype)
@@ -1465,15 +1516,15 @@
             copy_sem((2, blocks)),
             copy_sem((18,)),
             copy_sem((18,)),
-            copy_sem((3,)),
-            copy_sem((13,)),
+            copy_sem((2,)),
+            copy_sem((16,)),
             copy_sem((2, 2, blocks)),
             copy_sem((2, 3)),
         ],
         compiler_params=comm_params(0),
         cost_estimate=no_cost,
         name="gather_and_recur",
-    )(*splits, tokens, out_grad, mask, gains, vectors, wr, wi)
+    )(*splits, tokens, out_grad, lengths, gains, taps, biases, recur_blocks, input_blocks)
 
 
 def comm_params(collective):
@@ -1589,36 +1640,6 @@
     )(*held, scales, gains, sums, gates, term)
 
 
-def block_diagonal(blocks):
-    count, size = blocks.shape[0], blocks.shape[1]
-    rows = [
-        jnp.pad(blocks[h], ((0, 0), (h * size, (count - 1 - h) * size))) for h in range(count)
-    ]
-    return jnp.concatenate(rows, axis=0)
-
-
-def diagonal_blocks(square, count):
-    size = square.shape[0] // count
-    return jnp.stack(
-        [square[h * size : (h + 1) * size, h * size : (h + 1) * size] for h in range(count)]
-    )
-
-
-def masks_of(lengths, rows):
-    ends = jnp.cumsum(lengths, axis=1)
-    starts = ends - lengths
-    places = jnp.arange(rows, dtype=jnp.int32)[None, :, None]
-    inside = (places >= starts[:, None, :]) & (places < ends[:, None, :])
-    first_place = jnp.sum(jnp.where(inside, starts[:, None, :], 0), axis=2)
-    places = places[:, :, 0]
-    live = (places < ends[:, 2:3]).astype(f32)
-    columns = [(places != first_place).astype(f32)]
-    for k in range(1, 4):
-        columns.append((places - k >= first_place).astype(f32))
-    columns += [live] + [jnp.zeros_like(live)] * 3
-    return jnp.stack(columns, axis=2).reshape(lengths.shape[0] * rows, 8), live
-
-
 def local(
     n_dp,
     tokens,
@@ -1686,12 +1707,21 @@
         return total
 
     def joined_pair(total):
-        _, row_count, columns = total.shape
-        parts = settle_grad(total).reshape(2, -1, 2, columns // 2).transpose(1, 2, 0, 3)
-        return parts.reshape(-1, 2, columns)
+        total = settle_grad(total)
+        columns = total.shape[2] // 2
+        return jnp.stack(
+            [
+                jnp.concatenate(
+                    [total[q, :, k * columns : (k + 1) * columns] for q in range(2)], axis=1
+                )
+                for k in range(2)
+            ],
+            axis=1,
+        )
 
     def joined_out(total):
-        return settle_grad(total).swapaxes(0, 1).reshape(-1, 2 * total.shape[2])
+        total = settle_grad(total)
+        return jnp.concatenate([total[0], total[1]], axis=1)
 
     def over_groups(value):
         return lax.psum(value, "dp", axis_index_groups=outer_groups) if outer_count > 1 else value
@@ -1711,19 +1741,6 @@
         return pick_c(*quarters(value, axis))
 
     gain_one, gain_two = relative(gain_rnn.astype(f32)), relative(gain_mlp.astype(f32))
-    mask, _ = masks_of(lengths, buffer_rows)
-    mask = jnp.pad(mask, ((0, 0), (0, lanes - mask.shape[1])))
-    softened = jax.nn.softplus(-quarter(decay_param))
-    vectors = jnp.concatenate(
-        [
-            quarter(conv_weight, 1),
-            jnp.stack([quarter(conv_bias), quarter(bias_recur), quarter(bias_input), softened]),
-        ],
-        axis=0,
-    )
-    heads = gate_recur.shape[0] // 2
-    wr = block_diagonal(quarter(gate_recur))
-    wi = block_diagonal(quarter(gate_input))
     def split_pair(weight):
         row_count, _, columns = weight.shape
         parts = weight.reshape(row_count, 2, 2, columns // 2).transpose(2, 0, 1, 3)
@@ -1733,13 +1750,21 @@
         row_count, columns = weight.shape
         return over_outer(weight.reshape(row_count, 2, columns // 2).swapaxes(0, 1))
 
-    splits = (split_pair(rnn_in), split_out(rnn_out), split_pair(mlp_in), split_out(mlp_out))
+    def split_none(weight):
+        if outer_count == 1:
+            return weight
+        return lax.all_gather(weight, "dp", axis_index_groups=outer_groups, axis=0, tiled=True)
+
+    splits = (split_pair(rnn_in), split_out(rnn_out), split_pair(mlp_in), split_none(mlp_out))
+    biases = jnp.stack([conv_bias, bias_recur, bias_input, decay_param])
     gains = jnp.stack([gain_one, gain_two])
     (
         rnn_in_all, rnn_out_all, mlp_in_all, mlp_out_all,
         both, state, mixed, mask, middle, tokens_all,
-        *rows_kept, scales, act, gate_slope, gate_value,
-    ) = run_forward(outer_count, splits, tokens, out_grad, mask, gains, vectors, wr, wi)
+        *rows_kept, scales, vectors, wr, wi, act, gate_slope, gate_value,
+    ) = run_forward(
+        outer_count, splits, tokens, out_grad, lengths, gains, conv_weight, biases, gate_recur, gate_input
+    )
     normed, normed_two, grad_low = rows_kept[0:2], rows_kept[2:4], rows_kept[4:6]
 
     (

time: 560 us -> 543 us (0.970)
  local copies, waits for them, and re-layouts: 35 us -> 28.1 us
    reshape x6 -> x0, local copies, waits for them, and re-layouts: 8.02 us -> none  [the longest x4 7.31 us: joined_pair(): return parts.reshape(-1, 2, columns)]
    unnamed x26 -> x24, local copies, waits for them, and re-layouts: 11.9 us -> 12.7 us
where the time goes in v6:
time: 543 us; the launch traced here: 538 us
  Pallas kernels  502 us (92%)
  local copies, waits for them, and re-layouts  28.1 us (5%)
  other arithmetic  7.15 us (1%)
    pallas_call x1, Pallas kernels, run_backward(): pl.pallas_call(functools.partial(backward_kernel, count), out_shape=(*[sh...  213 us
    pallas_call x1, Pallas kernels, run_forward(): pl.pallas_call(functools.partial(forward_kernel, count), out_shape=(*gath...  185 us
    pallas_call x1, Pallas kernels, run_finish(): pl.pallas_call(functools.partial(finish_kernel, count), out_shape=(shape(...  103 us
    unnamed x24, local copies, waits for them, and re-layouts  12.7 us

profile of v6, /device:TPU:0, one launch (start us, length us, event | category | flops | bytes accessed | tf_op | source)
XLA Modules:
  0.0 538.4 jit_solution(11264734940025932897)
XLA Ops:
  0.7 0.8 stack.46
  1.4 0.7 stack.47
  2.1 0.7 stack.45
  2.8 0.7 stack.48
  3.5 0.6 pad_maximum_fusion.4.biases_ref
  4.2 0.7 convert_element_type.18
  4.9 0.7 convert_element_type.19
  5.6 0.6 pad_maximum_fusion.5.gain_ref.refs_10_
  6.2 1.2 copy.37
  7.4 0.9 copy.38
  8.3 1.0 copy.35
  9.4 1.1 copy.40.s_ri
  10.6 0.5 copy-done
  11.0 1.1 copy.45
  12.1 2.1 reshape.49.s_mi
  14.2 185.4 %gather_and_recur.1 = (bf16[8,256,1408]{2,1,0:T(8,128)(2,1)}, bf16[8,256,704]{2,1,0:T(8,128)(2,1)}, bf16[8,256,3072]{2,1,0:T(8,128)(2,1)}, bf16[8,256,1536]{2,1,...) custom-call(bf16[2,128,1408]{2,1,0:T(8,128)(2,1)} %copy.40.s_ri, ...), custom_call_target="tpu_custom_call" | custom-call | tf_op jit(solution)/shard_map/gather_and_recur/pallas_call | solution.py:1496
  199.6 213.4 %sum_and_back.1 = (bf16[8,256,3072]{2,1,0:T(8,128)(2,1)}, bf16[8,256,1536]{2,1,0:T(8,128)(2,1)}, bf16[5,256,3072]{2,1,0:T(8,128)(2,1)}, bf16[5,256,1536]{2,1,0:T...) custom-call(bf16[8,256,3072]{2,1,0:T(8,128)(2,1)} %get-tuple-element, ...), custom_call_target="tpu_custom_call" | custom-call | tf_op jit(solution)/shard_map/sum_and_back/pallas_call | solution.py:1547
  413.0 103.3 %sum_and_finish.1 = (bf16[2,128,2112]{2,1,0:T(8,128)(2,1)}, bf16[512,1024]{1,0:T(8,128)(2,1)}, f32[8,176,176]{2,1,0:T(8,128)}, f32[8,176,176]{2,1,0:T(8,128)}, f32[2,8,704]{2,1,0:T(8,128)}, /*index=5*/f32[8,1024]{1,0:T(8,128)}) custom-call(bf16[512,2048]{1,0:T(8,128)(2,1)} %get-tuple-element.73.refs_0_, bf16[512,2048]{1,0:T(8,128)(2,1)} %get-tuple-element.74.refs_1_, ...), custom_call_target="tpu_custom_call" | custom-call | tf_op jit(solution)/shard_map/sum_and_finish/pallas_call | solution.py:1601
  516.3 0.0 copy-start.8
  516.3 2.0 slice.96
  518.3 1.9 slice.97
  520.1 1.4 fusion
  521.6 0.1 maximum_select_fusion
  521.7 0.6 slice.132
  522.3 0.7 slice_reduce_fusion
  523.0 0.6 multiply_multiply_fusion
  523.6 0.1 slice_convert_fusion.1
  523.6 0.1 slice_bitcast_fusion.7
  523.7 1.0 pad_maximum_fusion.3
  524.7 0.1 slice_convert_fusion
  524.8 0.3 slice_bitcast_fusion.11
  525.1 0.2 maximum_bitcast_fusion.2
  525.3 0.2 maximum_bitcast_fusion.3
  525.4 0.1 pad_maximum_fusion.2
  525.6 2.2 copy.41
  527.8 0.2 convert_element_type.23
  528.0 0.1 slice_bitcast_fusion.1
  528.1 1.3 pad_maximum_fusion.1
  529.3 0.7 copy-done.1
  530.0 0.4 convert_element_type.22
  530.4 0.3 slice_bitcast_fusion.5
  530.7 0.1 maximum_bitcast_fusion
  530.8 0.1 maximum_bitcast_fusion.1
  530.9 0.2 pad_maximum_fusion
  531.1 4.1 copy.42
  535.2 1.1 copy.48
  536.3 0.8 copy-done.2
  537.1 1.1 copy.49
  (19 shorter events, 0.1 us)
Async XLA Ops:
  0.6 7.7 %copy-start.6 = (bf16[128,2,1408]{2,1,0:T(2,128)(2,1)S(1)}, bf16[128,2,1408]{2,1,0:T(2,128)(2,1)}, u32[]{:S(2)}) copy-start(bf16[128,2,1408]{2,1,0:T(2,128)(2,1)} %param.18) | copy-start | bytes 2162692
  9.4 1.7 copy-start
  516.3 5.3 copy-start.7
  516.3 6.7 %copy-start.8 = (f32[1408]{0:T(1024)S(1)}, f32[1408]{0:T(1024)}, u32[]{:S(2)}) copy-start(f32[1408]{0:T(1024)} %param.23) | copy-start | bytes 16900
  516.3 7.3 %copy-start.4 = (bf16[2,128,2112]{2,1,0:T(8,128)(2,1)S(1)}, bf16[2,128,2112]{2,1,0:T(8,128)(2,1)}, u32[]{:S(2)}) copy-start(bf16[2,128,2112]{2,1,0:T(8,128)(2,1)} %get-tuple-element.87) | copy-start | bytes 3244036
  525.5 2.2 copy-start.5
  528.1 2.0 copy-start.1
  531.1 4.1 copy-start.3
  535.2 1.9 copy-start.2

commit v7 on v6

--- a/solution.py
+++ b/solution.py
@@ -772,7 +772,7 @@
     def hop(self, k, last=None):
         d, land, at, top, bottom = self.partial, self.land, self.at, self.top, self.bottom
         src, dst, where = (
-            lambda: (d.at[5], land.at[0], at.beside),
+            lambda: (d.at[5, top], land.at[0, top], at.beside),
             lambda: (d.at[7, bottom], land.at[1, top], at.beside),
             lambda: (d.at[7, top], land.at[1, bottom], at.ahead),
             lambda: (d.at[6, top], land.at[2, top], at.ahead),
@@ -780,10 +780,13 @@
             lambda: (d.at[3, bottom], land.at[0, bottom], at.behind),
             lambda: (land.at[1, bottom], land.at[0, top], at.behind),
             lambda: (d.at[1], land.at[3], at.beside),
-            lambda: (land.at[0], land.at[4], at.ahead),
-            lambda: (land.at[2], land.at[2], at.behind),
+            lambda: (land.at[0, top], land.at[4, top], at.ahead),
+            lambda: (land.at[2, bottom], land.at[2, bottom], at.behind),
             lambda: (land.at[0], land.at[3], at.beside),
             lambda: (last.at[self.rows_of(1 - at.c)], self.total.at[at.c], at.core),
+            lambda: (land.at[2, top], land.at[2, top], at.behind),
+            lambda: (land.at[0, bottom], land.at[4, bottom], at.ahead),
+            lambda: (d.at[5, bottom], land.at[0, bottom], at.beside),
         )[k]()
         return remote(src, dst, self.send.at[k], self.recv.at[k], where)
 
@@ -804,12 +807,14 @@
         return {
             4: (land.at[1, top], d.at[6, bottom]),
             6: (land.at[1, bottom], d.at[3, top]),
-            8: (land.at[0], d.at[4]),
-            9: (land.at[2], d.at[2]),
+            8: (land.at[0, top], d.at[4, top]),
+            9: (land.at[2, bottom], d.at[2, bottom]),
+            12: (land.at[2, top], d.at[2, top]),
+            13: (land.at[0, bottom], d.at[4, bottom]),
         }[k]
 
     def arrived(self, k):
-        self.received(*{4: (1,), 6: (2,), 8: (0,), 9: (3, 4)}[k])
+        self.received({4: 1, 6: 2, 8: 0, 9: 4, 12: 3, 13: 14}[k])
 
     def step(self, k, add):
         self.arrived(k)
@@ -817,7 +822,7 @@
         self.start(k)
 
 
-work_hops, serve_hops = (0, 1, 2, 3, 4, 5, 6, 7, 8, 9), (10,)
+work_hops, serve_hops = (0, 1, 2, 3, 4, 5, 6, 7, 8, 9, 12, 13, 14), (10,)
 
 
 def add_rows(into, value, other=None):
@@ -923,8 +928,9 @@
     def staged(w, k):
         into, value = w.operands(k)
         count_rows, wide = into.shape
-        at_rows = pl.ds(0, count_rows) if k != 6 else pl.ds(count_rows, count_rows)
-        place = 3 if k == 6 else 0
+        low = k in (6, 9, 13)
+        at_rows = pl.ds(count_rows, count_rows) if low else pl.ds(0, count_rows)
+        place = 3 if low else 0
         a = stage_a.at[at_rows, pl.ds(0, wide)]
         b = stage_b.at[at_rows, pl.ds(0, wide)]
         return a, b, fetch(into, a, place), fetch(value, b, place + 1), fetch(a, into, place + 2)
@@ -949,7 +955,7 @@
             staged(w, k)[4].wait()
             w.start(k)
 
-    def finish(w, parts):
+    def finish(w, parts, last_hop=None):
         count_rows, wide = parts[0].shape
         a = stage_a.at[pl.ds(0, count_rows), pl.ds(0, wide)]
         b = stage_b.at[pl.ds(0, count_rows), pl.ds(0, wide)]
@@ -960,6 +966,7 @@
             v.wait()
         add_rows(a, b)
         if len(parts) == 3:
+            w.received(*last_hop)
             third = fetch(parts[2], b, 1)
             third.start()
             third.wait()
@@ -978,14 +985,14 @@
             w.received(5, 6)
             w.start(10)
         for w in (mo, mi):
-            w.received(9, 10)
+            w.received(9, 12, 10)
             finish(w, (w.land.at[2], w.land.at[3]))
         out_move.wait_recv()
         for w in (mo, mi):
             w.sent(*serve_hops)
 
     block_order = (
-        (7, (1, 2)), (5, (0,)), (6, (3,)), (3, (5,)), (1, (7,)), (4, ()), (2, ()), (0, ()),
+        (7, (1, 2)), (5, (0, 14)), (6, (3,)), (3, (5,)), (1, (7,)), (4, ()), (2, ()), (0, ()),
     )
 
     def partial_blocks(w, lhs, column_ref, room, between=()):
@@ -1040,8 +1047,8 @@
                 between[b]()
 
     def settle(w):
-        w.received(7, 8)
-        finish(w, (w.partial.at[0], w.land.at[3], w.land.at[4]))
+        w.received(7)
+        finish(w, (w.partial.at[0], w.land.at[3], w.land.at[4]), (8, 13))
 
     def join(i, h, mine_ref, arrived, landed, keep_value, sent_ref, over):
         arrived[i].wait_recv()
@@ -1099,13 +1106,13 @@
             (
                 (1, lambda: combine(mo, 4, 6)),
                 (2, lambda: send_on(mo, 4, 6)),
-                (4, lambda: begin(mo, 8)),
-                (6, lambda: combine(mo, 8)),
+                (4, lambda: begin(mo, 8, 13)),
+                (6, lambda: combine(mo, 8, 13)),
             ),
         )
         for moved in e_core:
             moved.start()
-        send_on(mo, 8)
+        send_on(mo, 8, 13)
 
         def keep_e(h, value):
             e_ref[h, :] = value
@@ -1120,11 +1127,12 @@
             pair_ref,
             room,
             (
-                (2, lambda: begin(mo, 9)),
-                (4, lambda: combine(mo, 9)),
-                (5, lambda: send_on(mo, 9)),
+                (2, lambda: begin(mo, 12, 9)),
+                (4, lambda: combine(mo, 12, 9)),
+                (5, lambda: send_on(mo, 12, 9)),
             ),
         )
+        settle(mo)
         middle_load.wait()
         for i, h in enumerate(halves):
             e_y[i].wait_recv()
@@ -1157,7 +1165,15 @@
             hidden,
             part_out,
             mine_ref,
-            ((1, lambda: combine(mi, 4, 6)), (2, lambda: send_on(mi, 4, 6))),
+            (
+                (1, lambda: combine(mi, 4, 6)),
+                (2, lambda: send_on(mi, 4, 6)),
+                (3, lambda: begin(mi, 12)),
+                (4, lambda: combine(mi, 12)),
+                (5, lambda: (send_on(mi, 12), begin(mi, 8))),
+                (6, lambda: combine(mi, 8)),
+                (7, lambda: send_on(mi, 8)),
+            ),
         )
         for moved in o_core:
             moved.start()
@@ -1189,14 +1205,14 @@
         for v in loads:
             v.wait()
         send_on(mi, 9)
-        begin(mi, 8)
+        begin(mi, 13)
 
         def keep_mixed(start, value):
             dmix_ref[pl.ds(start, chunk_rows), :] = value
 
         project(db_mine, db_theirs, lambda: stacked(w_ro), size, cols, keep_mixed)
-        combine(mi, 8)
-        send_on(mi, 8)
+        combine(mi, 13)
+        send_on(mi, 13)
         recur_first(
             both_ref, state_ref, mask_ref, vec_ref, wr_ref, wi_ref, dmix_ref, dboth_ref, coef_ref, push_ref
         )
@@ -1245,8 +1261,7 @@
             pltpu.VMEM((width, width), f32),
             pltpu.VMEM((width, width), f32),
         )
-        for w in (mo, mi):
-            settle(w)
+        settle(mi)
         for w in (mo, mi):
             w.sent(*work_hops)
         for v in keep_out:
@@ -1309,9 +1324,12 @@
     def add(into, value):
         add_rows(into, value)
 
-    def finish(parts):
+    def finish(parts, last_hop=None):
         last_r[...] = parts[0][...]
-        add_rows(last_r, parts[1], parts[2] if len(parts) == 3 else None)
+        add_rows(last_r, parts[1])
+        if len(parts) == 3:
+            w.received(*last_hop)
+            add_rows(last_r, parts[2])
         w.hop(11, last_r).start()
         w.total[at.c] = last_r[w.rows_of(at.c), :]
 
@@ -1333,7 +1351,7 @@
         w.start(10)
         gates_end.wait_recv()
         gates_core.start()
-        w.received(9, 10)
+        w.received(9, 12, 10)
         finish((w.land.at[2], w.land.at[3]))
         w.hop(11, last_r).wait()
         w.sent(*serve_hops)
@@ -1368,7 +1386,7 @@
             d_r[b, :, :pair_width] = product(one_mine, one_theirs, dboth_ref)
             d_r[b, :, pair_width:] = product(db_mine, db_theirs, mixed_ref)
 
-        for b, hops in ((7, (1, 2)), (5, (0,))):
+        for b, hops in ((7, (1, 2)), (3, (5,)), (5, (0, 14))):
             partial(b)
             w.start(*hops)
         sums_x.wait_recv()
@@ -1377,7 +1395,7 @@
         gates_x.wait_recv()
         add_rows(gates_in.at[0], gates_ref)
         gates_z.start()
-        for b, hops in ((6, (3,)), (3, (5,))):
+        for b, hops in ((6, (3,)),):
             partial(b)
             w.start(*hops)
 
@@ -1411,9 +1429,11 @@
         gates_end.start()
         gates_core.start()
         w.step(8, add)
+        w.step(13, add)
         w.start(7)
         for b in (2, 0):
             partial(b)
+        w.step(12, add)
         w.step(9, add)
         term_ref[...] = term_in[...]
         for k in (7, 8):
@@ -1439,8 +1459,8 @@
         term_x.wait_recv()
         term_land[0] = term_land[0] + term_ref[...]
         term_z.start()
-        w.received(7, 8)
-        finish((w.partial.at[0], w.land.at[3], w.land.at[4]))
+        w.received(7)
+        finish((w.partial.at[0], w.land.at[3], w.land.at[4]), (8, 13))
         term_z.wait_recv()
         term_land[1] = term_land[0] + term_land[1]
         term_core.start()
@@ -1568,8 +1588,8 @@
             pltpu.VMEM((own, lanes), f32),
             pltpu.VMEM((size, max(hidden)), bf16),
             pltpu.VMEM((size, max(hidden)), bf16),
-            copy_sem((2, 12)),
-            copy_sem((2, 12)),
+            copy_sem((2, 15)),
+            copy_sem((2, 15)),
             copy_sem((14,)),
             copy_sem((14,)),
             copy_sem((10,)),
@@ -1628,8 +1648,8 @@
             pltpu.VMEM((2, *sums.shape), f32),
             pltpu.VMEM(term.shape, f32),
             pltpu.VMEM((3, *term.shape), f32),
-            copy_sem((12,)),
-            copy_sem((12,)),
+            copy_sem((15,)),
+            copy_sem((15,)),
             copy_sem((18,)),
             copy_sem((18,)),
             copy_sem((9,)),

time: 543 us -> 535 us (0.985)
  Pallas kernels: 502 us -> 494 us
    pallas_call x1, Pallas kernels: 213 us -> 204 us  [run_backward(): pl.pallas_call(functools.partial(backward_kernel, count), out_shape=(*[sh...]
where the time goes in v7:
time: 535 us; the launch traced here: 531 us
  Pallas kernels  494 us (92%)
  local copies, waits for them, and re-layouts  28.1 us (5%)
  other arithmetic  7.15 us (1%)
    pallas_call x1, Pallas kernels, run_backward(): pl.pallas_call(functools.partial(backward_kernel, count), out_shape=(*[sh...  204 us
    pallas_call x1, Pallas kernels, run_forward(): pl.pallas_call(functools.partial(forward_kernel, count), out_shape=(*gath...  185 us
    pallas_call x1, Pallas kernels, run_finish(): pl.pallas_call(functools.partial(finish_kernel, count), out_shape=(shape(...  105 us
    unnamed x24, local copies, waits for them, and re-layouts  12.7 us

profile of v7, /device:TPU:0, one launch (start us, length us, event | category | flops | bytes accessed | tf_op | source)
XLA Modules:
  0.0 530.9 jit_solution(4715130283106530911)
XLA Ops:
  0.7 0.8 stack.46
  1.4 0.7 stack.47
  2.1 0.7 stack.45
  2.8 0.7 stack.48
  3.5 0.6 pad_maximum_fusion.4.biases_ref
  4.2 0.7 convert_element_type.18
  4.9 0.7 convert_element_type.19
  5.6 0.6 pad_maximum_fusion.5.gain_ref.refs_10_
  6.2 1.2 copy.37
  7.4 0.9 copy.38
  8.3 1.0 copy.35
  9.4 0.0 copy-start
  9.4 1.1 copy.40.s_ri
  10.6 0.5 copy-done
  11.0 1.1 copy.45
  12.1 2.1 reshape.49.s_mi
  14.2 185.5 %gather_and_recur.1 = (bf16[8,256,1408]{2,1,0:T(8,128)(2,1)}, bf16[8,256,704]{2,1,0:T(8,128)(2,1)}, bf16[8,256,3072]{2,1,0:T(8,128)(2,1)}, bf16[8,256,1536]{2,1,...) custom-call(bf16[2,128,1408]{2,1,0:T(8,128)(2,1)} %copy.40.s_ri, ...), custom_call_target="tpu_custom_call" | custom-call | tf_op jit(solution)/shard_map/gather_and_recur/pallas_call | solution.py:1516
  199.7 203.9 %sum_and_back.1 = (bf16[8,256,3072]{2,1,0:T(8,128)(2,1)}, bf16[8,256,1536]{2,1,0:T(8,128)(2,1)}, bf16[5,256,3072]{2,1,0:T(8,128)(2,1)}, bf16[5,256,1536]{2,1,0:T...) custom-call(bf16[8,256,3072]{2,1,0:T(8,128)(2,1)} %get-tuple-element, ...), custom_call_target="tpu_custom_call" | custom-call | tf_op jit(solution)/shard_map/sum_and_back/pallas_call | solution.py:1567
  403.6 105.1 %sum_and_finish.1 = (bf16[2,128,2112]{2,1,0:T(8,128)(2,1)}, bf16[512,1024]{1,0:T(8,128)(2,1)}, f32[8,176,176]{2,1,0:T(8,128)}, f32[8,176,176]{2,1,0:T(8,128)}, f32[2,8,704]{2,1,0:T(8,128)}, /*index=5*/f32[8,1024]{1,0:T(8,128)}) custom-call(bf16[512,2048]{1,0:T(8,128)(2,1)} %get-tuple-element.73.refs_0_, bf16[512,2048]{1,0:T(8,128)(2,1)} %get-tuple-element.74.refs_1_, ...), custom_call_target="tpu_custom_call" | custom-call | tf_op jit(solution)/shard_map/sum_and_finish/pallas_call | solution.py:1621
  508.7 2.0 slice.96
  510.7 1.9 slice.97
  512.5 1.4 fusion
  514.0 0.1 maximum_select_fusion
  514.1 0.6 slice.132
  514.7 0.7 slice_reduce_fusion
  515.3 0.6 multiply_multiply_fusion
  516.0 0.1 slice_convert_fusion.1
  516.0 0.1 slice_bitcast_fusion.7
  516.1 1.0 pad_maximum_fusion.3
  517.1 0.1 slice_convert_fusion
  517.2 0.3 slice_bitcast_fusion.11
  517.5 0.2 maximum_bitcast_fusion.2
  517.7 0.2 maximum_bitcast_fusion.3
  517.8 0.1 pad_maximum_fusion.2
  517.9 2.2 copy.41
  520.2 0.2 convert_element_type.23
  520.3 0.1 slice_bitcast_fusion.1
  520.5 1.3 pad_maximum_fusion.1
  521.7 0.7 copy-done.1
  522.4 0.4 convert_element_type.22
  522.8 0.3 slice_bitcast_fusion.5
  523.1 0.1 maximum_bitcast_fusion
  523.2 0.1 maximum_bitcast_fusion.1
  523.3 0.2 pad_maximum_fusion
  523.5 4.1 copy.42
  527.6 1.1 copy.48
  528.7 0.8 copy-done.2
  529.5 1.1 copy.49
  (19 shorter events, 0.1 us)
Async XLA Ops:
  0.6 7.7 %copy-start.6 = (bf16[128,2,1408]{2,1,0:T(2,128)(2,1)S(1)}, bf16[128,2,1408]{2,1,0:T(2,128)(2,1)}, u32[]{:S(2)}) copy-start(bf16[128,2,1408]{2,1,0:T(2,128)(2,1)} %param.18) | copy-start | bytes 2162692
  9.4 1.7 copy-start
  508.7 5.3 copy-start.7
  508.7 6.7 %copy-start.8 = (f32[1408]{0:T(1024)S(1)}, f32[1408]{0:T(1024)}, u32[]{:S(2)}) copy-start(f32[1408]{0:T(1024)} %param.23) | copy-start | bytes 16900
  508.7 7.3 %copy-start.4 = (bf16[2,128,2112]{2,1,0:T(8,128)(2,1)S(1)}, bf16[2,128,2112]{2,1,0:T(8,128)(2,1)}, u32[]{:S(2)}) copy-start(bf16[2,128,2112]{2,1,0:T(8,128)(2,1)} %get-tuple-element.87) | copy-start | bytes 3244036
  517.9 2.2 copy-start.5
  520.5 2.0 copy-start.1
  523.5 4.1 copy-start.3
  527.6 1.9 copy-start.2
